TPU v7x, 32 devices: a whole 2x2x4 slice. The times are simulated.
32 devices in a mesh: req: 16 (over z, y, x), mlp: 2 (over core).
Axes of the slice: x: 2, y: 2, z: 4, core: 2. Of those that a mesh axis runs over, the one named last changes fastest.
Arguments:
- q_in: bfloat16 [8192, 4096], P('req', 'mlp'), may hold values from -6 to 6
- kv_in: bfloat16 [2, 8192, 1024], P(None, 'req', 'mlp'), may hold values from -6 to 6
- prefix_kv: bfloat16 [2, 1024, 1024], P(None, 'req', 'mlp'), may hold values from -1 to 1
- hidden_in: bfloat16 [8192, 2560], P(('req', 'mlp')), may hold values from -0.625 to 0.625
- q_gain: float32 [128], replicated, may hold values from 0.5 to 2.5
- k_gain: float32 [128], replicated, may hold values from 0.5 to 2.5
- post_gain: float32 [2560], replicated, may hold values from 0.1 to 1.9
- w_out: bfloat16 [4096, 2560], P('mlp'), may hold values from -0.09375 to 0.09375
- w_gate: bfloat16 [2560, 5120], P('req', 'mlp'), may hold values from -0.125 to 0.125
- w_up: bfloat16 [2560, 5120], P('req', 'mlp'), may hold values from -0.125 to 0.125
- w_down_t: bfloat16 [2560, 5120], P('req', 'mlp'), may hold values from -0.078125 to 0.078125
- lengths: int32 [16, 8], P('req'), may hold values from 1 to 256, 512 in all within a row
- row_group: int32 [16], P('req'), may hold values from 0 to 1
- owner_block: int32 [16], replicated, may hold values from 0 to 15, each once
Outputs:
- hidden_out: bfloat16 [8192, 2560], P(('req', 'mlp'))
Inputs may be any that keep to these rules, and one draw needn't show every extreme that they name: Each index's 8 lengths sum to 512; the largest is exactly 256. `owner_block`: A permutation; block b belongs to group b // 8, so every group has 8 blocks.
All inputs are finite; a program needn't handle non-finite values.
Results may differ from a plain program's by a relative error of at most 0.023.
Values may be sent and summed in bfloat16 or wider, within the bound.
No kernel may reach another device: no remote copies, remote signals or barrier semaphores. Data moves between devices by JAX's collectives and lax.ppermute only.
A program may use at most 128 MiB of HBM per device.

v0:
```python
import math

import jax
import jax.numpy as jnp
from jax import lax
from jax.sharding import PartitionSpec as P

HD = 128
PB = 64
PLEN = 512
BPG = 8


EPSILON = 1e-06
THETA = 1000000.0


def rms_scale(values, gains):
    mean_sq = jnp.mean(values * values, axis=-1, keepdims=True)
    return values * lax.rsqrt(mean_sq + EPSILON) * gains


def rotate(values, positions):
    half_width = values.shape[-1] // 2
    exponent = jnp.arange(half_width, dtype=jnp.float32) * (2.0 / values.shape[-1])
    inv_freq = jnp.power(jnp.float32(THETA), -exponent)
    angles = positions.astype(jnp.float32)[:, None] * inv_freq[None, :]
    cosine = jnp.cos(angles)[:, None, :]
    sine_part = jnp.sin(angles)[:, None, :]
    first_half = values[..., :half_width]
    second = values[..., half_width:]
    return jnp.concatenate(
        [first_half * cosine - second * sine_part, second * cosine + first_half * sine_part],
        axis=-1,
    )


def slot_layout(row_lengths, tok_count):
    req_ends = jnp.cumsum(row_lengths)
    starts = req_ends - row_lengths
    slot_ids = jnp.arange(tok_count, dtype=jnp.int32)
    request = jnp.sum((slot_ids[:, None] >= req_ends[None, :]).astype(jnp.int32), axis=1)
    member = request[:, None] == jnp.arange(row_lengths.shape[0], dtype=jnp.int32)[None, :]
    offset = slot_ids - jnp.sum(jnp.where(member, starts[None, :], 0), axis=1)
    return (request, offset)


def attention(queries, pre_keys, pre_vals, suffix_key_rows, suffix_value_rows, allowed):
    tok_count, head_count, head_width = queries.shape
    groups = pre_keys.shape[1]
    grouped_heads = queries.reshape(tok_count, groups, head_count // groups, head_width)
    logit_scale = 1.0 / math.sqrt(head_width)
    pre_weights = jnp.exp(
        jnp.einsum("tgrd,pgd->grtp", grouped_heads, pre_keys, preferred_element_type=jnp.float32)
        * logit_scale
    )
    suffix_logits = (
        jnp.einsum(
            "fknp,bkp->knfb", grouped_heads, suffix_key_rows, preferred_element_type=jnp.float32
        )
        * logit_scale
    )
    suf_weights = jnp.where(allowed[None, None, :, :], jnp.exp(suffix_logits), 0.0)
    total = jnp.sum(pre_weights, axis=-1) + jnp.sum(suf_weights, axis=-1)
    numerator = jnp.einsum(
        "grtp,pgd->grtd",
        pre_weights.astype(jnp.bfloat16),
        pre_vals,
        preferred_element_type=jnp.float32,
    )
    numerator = numerator + jnp.einsum(
        "mabi,ime->mabe",
        suf_weights.astype(jnp.bfloat16),
        suffix_value_rows,
        preferred_element_type=jnp.float32,
    )
    result = numerator / total[..., None]
    return (
        jnp.transpose(result, (2, 0, 1, 3))
        .reshape(tok_count, head_count * head_width)
        .astype(jnp.bfloat16)
    )


def activate(gate, upward):
    return (jax.nn.silu(gate) * upward).astype(jnp.bfloat16)


def per_device(
    q_in,
    kv_in,
    prefix_kv,
    hidden_in,
    q_gain,
    k_gain,
    post_gain,
    w_out,
    w_gate,
    w_up,
    w_down_t,
    lengths,
    row_group,
    owner_block,
):
    tok_count = q_in.shape[0]
    local_heads = q_in.shape[1] // HD
    local_groups = kv_in.shape[2] // HD
    request, offset = slot_layout(lengths[0], tok_count)
    positions = offset + PLEN
    queries = rotate(
        rms_scale(q_in.astype(jnp.float32).reshape(tok_count, local_heads, HD), q_gain), positions
    ).astype(jnp.bfloat16)
    suffix_key_rows = rotate(
        rms_scale(kv_in[0].astype(jnp.float32).reshape(tok_count, local_groups, HD), k_gain),
        positions,
    ).astype(jnp.bfloat16)
    suffix_value_rows = kv_in[1].reshape(tok_count, local_groups, HD)
    gathered = lax.all_gather(prefix_kv, "req", axis=1, tiled=True)
    blocks = gathered.reshape(2, -1, PB, local_groups * HD)
    inverse = jnp.argsort(owner_block)
    picked = lax.dynamic_slice_in_dim(inverse, row_group[0] * BPG, BPG, 0)
    chosen = jnp.take(blocks, picked, axis=1).reshape(2, PLEN, local_groups, HD)
    slot_ids = jnp.arange(tok_count, dtype=jnp.int32)
    allowed = (request[:, None] == request[None, :]) & (slot_ids[None, :] <= slot_ids[:, None])
    attn = attention(queries, chosen[0], chosen[1], suffix_key_rows, suffix_value_rows, allowed)
    summed = lax.psum_scatter(
        jnp.dot(attn, w_out, preferred_element_type=jnp.float32).astype(jnp.bfloat16),
        "mlp",
        scatter_dimension=0,
        tiled=True,
    ).astype(jnp.float32)
    resid = (hidden_in.astype(jnp.float32) + summed).astype(jnp.bfloat16)
    own_normed = rms_scale(resid.astype(jnp.float32), post_gain).astype(jnp.bfloat16)
    normed = lax.all_gather(own_normed, "mlp", axis=0, tiled=True)
    gate = jnp.dot(
        normed,
        lax.all_gather(w_gate, "req", axis=0, tiled=True),
        preferred_element_type=jnp.float32,
    )
    upward = jnp.dot(
        normed, lax.all_gather(w_up, "req", axis=0, tiled=True), preferred_element_type=jnp.float32
    )
    act = activate(gate, upward)
    terms = lax.dot_general(
        act,
        lax.all_gather(w_down_t, "req", axis=0, tiled=True),
        (((1,), (1,)), ((), ())),
        preferred_element_type=jnp.float32,
    )
    mixed = lax.psum_scatter(
        terms.astype(jnp.bfloat16), "mlp", scatter_dimension=0, tiled=True
    ).astype(jnp.float32)
    return (resid.astype(jnp.float32) + mixed).astype(jnp.bfloat16)


def solution(mesh):
    in_specs = (
        P("req", "mlp"),
        P(None, "req", "mlp"),
        P(None, "req", "mlp"),
        P(("req", "mlp"), None),
        P(),
        P(),
        P(),
        P("mlp", None),
        P("req", "mlp"),
        P("req", "mlp"),
        P("req", "mlp"),
        P("req", None),
        P("req"),
        P(),
    )
    out_specs = P(("req", "mlp"), None)
    return jax.shard_map(
        per_device, mesh=mesh, in_specs=in_specs, out_specs=out_specs, check_vma=False
    )
```

profile of v0, /device:TPU:0, one launch (start us, length us, event | category | flops | bytes accessed | tf_op | source)
XLA Modules:
  0.0 656.4 jit_solution(13133559369003266321)
XLA Ops:
  6.5 0.7 all-gather.6.cloned.1.call-update
  7.3 2.1 fusion.28
  9.4 0.8 reduce-window.4
  10.2 0.7 fusion.21
  10.9 2.1 convert_bitcast_fusion
  13.0 0.9 copy.67
  14.0 1.9 copy-done
  15.9 1.2 multiply_reduce_fusion
  17.1 0.1 copy.45
  17.2 0.1 copy.46
  17.5 4.4 multiply_multiply_fusion
  21.8 0.2 copy.54
  22.1 1.0 multiply_cosine_fusion
  23.1 4.9 subtract_convert_fusion
  28.0 0.5 copy.48
  28.6 1.9 copy.47
  30.4 1.3 copy.66
  31.7 1.2 copy.53
  33.5 1.3 sort.17
  34.9 0.1 multiply_reduce_fusion.1
  35.1 0.2 fusion.14
  35.3 1.7 multiply_multiply_fusion.1
  37.0 1.4 subtract_convert_fusion.1
  38.4 5.6 fusion
  44.0 4.7 fusion.2
  48.7 24.8 %all-gather.6.cloned.1.call-done = bf16[2,1024,512]{2,1,0:T(8,128)(2,1)} async-done(((bf16[2,64,512]{2,1,0:T(8,128)(2,1)}), bf16[2,1024,512]{2,1,0:T(8,128)(2,1)}) %all-gather.6.cloned.1.call-update) | async-done | bytes 2097168 | tf_op jit(solution)/shard_map/all_gather | solution.py:118
  73.5 2.2 gather_fusion
  75.7 0.2 select_bitcast_fusion
  75.9 0.1 fusion.27
  76.0 0.9 squeeze.4
  76.9 11.6 %bitcast_reduce_fusion = (f32[4,4,512]{2,1,0:T(4,128)S(1)}, f32[4,512,512,4]{2,1,3,0:T(8,128)}) fusion(bf16[512,4,4,64]{3,0,2,1:T(8,128)(2,1)S(1)} %bitcast.81, bf16[512,4,4,64]{3,0,2,1:T(8,128)(2,1)} %bitcast.82, bf16[512,4,128,1]{2,1,0,3:T(4,128)(2,1)} %bitcast.87), kind=kOutput, calls=%fused_computation.2 | convolution fusion | flops 1086316544 | bytes 19431424 | tf_op jit(solution)/shard_map/tgrd,pgd->grtp/dot_general | solution.py:54
  88.5 0.1 squeeze.10
  88.6 10.1 %fusion.9 = bf16[512,4,4,128]{0,3,2,1:T(8,128)(2,1)S(1)} fusion(f32[4,4,512,128]{2,3,1,0:T(8,128)} %fusion.2, f32[512,4,4]{0,2,1:T(4,128)S(1)} %add_bitcast_fusion, f32[4,512,512,4]{2,1,3,0:T(8,128)} %get-tuple-element.20, bf16[512,4,128,1]{2,1,0,3:T(4,128)(2,1)S(1)} %bitcast.89), kind=kOutput, calls=%fused_computation.17 | convolution fusion | flops 1085276160 | bytes 23625728 | tf_op jit(solution)/shard_map/grtp,pgd->grtd/dot_general | solution.py:65
  98.7 11.0 %convolution_convert_fusion.1 = bf16[512,2560]{1,0:T(8,128)(2,1)} fusion(bf16[512,2048]{0,1:T(8,128)(2,1)S(1)} %bitcast.92, bf16[2048,2560]{1,0:T(8,128)(2,1)} %param.21), kind=kOutput, calls=%fused_computation.15 | convolution fusion | flops 5370019840 | bytes 15204352 | tf_op jit(solution)/shard_map/dot_general | solution.py:127
  109.8 8.8 %reduce-scatter.3.cloned.1.call-done = bf16[256,2560]{1,0:T(8,128)(2,1)} async-done(((bf16[512,2560]{1,0:T(8,128)(2,1)}), bf16[256,2560]{1,0:T(8,128)(2,1)}) %reduce-scatter.3.cloned.1.call-update) | async-done | bytes 1310736 | tf_op jit(solution)/shard_map/reduce_scatter | solution.py:126
  118.7 1.8 fusion.10
  120.5 2.9 fusion.12
  123.5 0.5 all-gather.10.cloned.1.call-update
  124.1 0.5 all-gather.14.cloned.1.call-update
  124.7 0.5 all-gather.12.cloned.1.call-update
  125.2 11.0 %all-gather.8.cloned.1.call-done = bf16[512,2560]{1,0:T(8,128)(2,1)} async-done(((bf16[256,2560]{1,0:T(8,128)(2,1)}), bf16[512,2560]{1,0:T(8,128)(2,1)}) %all-gather.8.cloned.1.call-update) | async-done | bytes 2621456 | tf_op jit(solution)/shard_map/all_gather | solution.py:134
  136.2 161.2 %all-gather.10.cloned.1.call-done = bf16[2560,2560]{1,0:T(8,128)(2,1)} async-done(((bf16[160,2560]{1,0:T(8,128)(2,1)}), bf16[2560,2560]{1,0:T(8,128)(2,1)}) %all-gather.10.cloned.1.call-update) | async-done | bytes 13107216 | tf_op jit(solution)/shard_map/all_gather | solution.py:137
  297.4 12.3 %fusion.29 = f32[512,2560]{1,0:T(8,128)} fusion(bf16[512,2560]{1,0:T(8,128)(2,1)} %all-gather.8.cloned.1.call-done, bf16[2560,2560]{1,0:T(8,128)(2,1)} %all-gather.10.cloned.1.call-done), kind=kOutput, calls=%fused_computation.70 | convolution fusion | flops 6710886400 | bytes 20971520 | tf_op jit(solution)/shard_map/dot_general | solution.py:135
  309.7 145.9 %all-gather.14.cloned.1.call-done = bf16[2560,2560]{1,0:T(8,128)(2,1)} async-done(((bf16[160,2560]{1,0:T(8,128)(2,1)}), bf16[2560,2560]{1,0:T(8,128)(2,1)}) %all-gather.14.cloned.1.call-update) | async-done | bytes 13107216 | tf_op jit(solution)/shard_map/all_gather | solution.py:146
  455.6 158.2 %all-gather.12.cloned.1.call-done = bf16[2560,2560]{1,0:T(8,128)(2,1)} async-done(((bf16[160,2560]{1,0:T(8,128)(2,1)}), bf16[2560,2560]{1,0:T(8,128)(2,1)}) %all-gather.12.cloned.1.call-update) | async-done | bytes 13107216 | tf_op jit(solution)/shard_map/all_gather | solution.py:141
  613.8 24.4 %convolution_convert_fusion = bf16[512,2560]{1,0:T(8,128)(2,1)} fusion(bf16[2560,2560]{1,0:T(8,128)(2,1)} %all-gather.14.cloned.1.call-done, f32[512,2560]{1,0:T(8,128)} %fusion.29, bf16[512,2560]{1,0:T(8,128)(2,1)} %all-gather.8.cloned.1.call-done, bf16[2560,2560]{1,0:T(8,128)(2,1)} %all-gather.12.cloned.1.call-done), kind=kOutput, calls=%fused_computation.14 | convolution fusion | flops 13430947840 | bytes 36700160 | tf_op jit(solution)/shard_map/dot_general | solution.py:144
  638.2 8.5 %reduce-scatter.5.cloned.1.call-done = bf16[256,2560]{1,0:T(8,128)(2,1)} async-done(((bf16[512,2560]{1,0:T(8,128)(2,1)}), bf16[256,2560]{1,0:T(8,128)(2,1)}) %reduce-scatter.5.cloned.1.call-update) | async-done | bytes 1310736 | tf_op jit(solution)/shard_map/reduce_scatter | solution.py:150
  646.7 2.8 fusion.13
  (38 shorter events, 0.7 us)
Async XLA Ops:
  6.5 67.0 %all-gather.6.cloned.1.call-start = ((), (), s32[]{:S(2)}) async-start(), calls=%async_computation.2 | async-start | bytes 2228224 | tf_op jit(solution)/shard_map/all_gather | solution.py:118
  7.3 111.4 %reduce-scatter.3.cloned.1.call-start = ((), (), s32[]{:S(2)}) async-start(), calls=%async_computation.3 | async-start | bytes 3932160 | tf_op jit(solution)/shard_map/reduce_scatter | solution.py:126
  14.0 2.0 copy-start
  14.0 3.5 copy-start.6
  23.0 4.9 copy-start.4
  28.6 5.0 copy-start.8
  28.6 6.7 %copy-start.7 = (f32[128]{0:T(128)S(1)}, f32[128]{0:T(128)}, u32[]{:S(2)}) copy-start(f32[128]{0:T(128)} %param.19) | copy-start | bytes 1540
  34.8 3.6 copy-start.3
  98.7 20.0 %copy-start.1 = (bf16[256,2560]{1,0:T(8,128)(2,1)S(1)}, bf16[256,2560]{1,0:T(8,128)(2,1)}, u32[]{:S(2)}) copy-start(bf16[256,2560]{1,0:T(8,128)(2,1)} %param.17) | copy-start | bytes 3932164
  109.8 10.8 %copy-start.5 = (f32[2560]{0:T(1024)S(1)}, f32[2560]{0:T(1024)}, u32[]{:S(2)}) copy-start(f32[2560]{0:T(1024)} %param.20) | copy-start | bytes 30724
  109.8 26.4 %all-gather.8.cloned.1.call-start = ((), (), s32[]{:S(2)}) async-start(), calls=%async_computation.4 | async-start | bytes 3932160 | tf_op jit(solution)/shard_map/all_gather | solution.py:134
  123.4 173.9 %all-gather.10.cloned.1.call-start = ((), (), s32[]{:S(2)}) async-start(), calls=%async_computation.5 | async-start | bytes 13926400 | tf_op jit(solution)/shard_map/all_gather | solution.py:137
  124.0 331.5 %all-gather.14.cloned.1.call-start = ((), (), s32[]{:S(2)}) async-start(), calls=%async_computation.7 | async-start | bytes 13926400 | tf_op jit(solution)/shard_map/all_gather | solution.py:146
  124.6 489.2 %all-gather.12.cloned.1.call-start = ((), (), s32[]{:S(2)}) async-start(), calls=%async_computation.6 | async-start | bytes 13926400 | tf_op jit(solution)/shard_map/all_gather | solution.py:141
  125.2 521.5 %reduce-scatter.5.cloned.1.call-start = ((), (), s32[]{:S(2)}) async-start(), calls=%async_computation.8 | async-start | bytes 3932160 | tf_op jit(solution)/shard_map/reduce_scatter | solution.py:150
  309.7 337.1 %copy-start.2 = (bf16[256,2560]{1,0:T(8,128)(2,1)S(1)}, bf16[256,2560]{1,0:T(8,128)(2,1)}, u32[]{:S(2)}) copy-start(bf16[256,2560]{1,0:T(8,128)(2,1)} %reduce-scatter.3.cloned.1.call-done) | copy-start | bytes 3932164
Sparse Core Ops, SparseCore 0:
  10.1 63.3 all-gather.5
  109.9 8.7 reduce-scatter.2
  123.6 12.5 all-gather.7
  139.2 158.1 all-gather.9
  300.4 155.1 all-gather.13
  458.6 155.1 all-gather.11
  638.3 8.3 reduce-scatter.4
where the time goes:
time: 657 us; the launch traced here: 656 us
  waiting for transfers between devices  521 us (79%)
  matrix products  79.6 us (12%)
  other arithmetic  27.8 us (4%)
  between operations  14.4 us (2%)
  local copies, waits for them, and re-layouts  13.6 us (2%)
    all_gather x1, waiting for transfers between devices, per_device(): lax.all_gather(w_gate, 'req', axis=0, tiled=True)  161 us
    all_gather x1, waiting for transfers between devices, per_device(): lax.all_gather(w_up, 'req', axis=0, tiled=True)  158 us
    all_gather x1, waiting for transfers between devices, per_device(): lax.all_gather(w_down_t, 'req', axis=0, tiled=True)  146 us
    all_gather x1, waiting for transfers between devices, per_device(): gathered = lax.all_gather(prefix_kv, 'req', axis=1, tiled=True)  24.8 us
    dot_general x1, matrix products, per_device(): lax.dot_general(act, lax.all_gather(w_down_t, 'req', axis=0, tiled=True),...  24.4 us
  transfers between devices with their start and end apart: 7, of which 7 were waited for; matrix products, arithmetic and copies ran while one was open for 8% of the time, Pallas kernels for 0%

commit v1 on v0

--- a/solution.py
+++ b/solution.py
@@ -9,6 +9,7 @@
 PB = 64
 PLEN = 512
 BPG = 8
+GROUP = 4
 
 
 EPSILON = 1e-06
@@ -84,6 +85,10 @@
 
 def activate(gate, upward):
     return (jax.nn.silu(gate) * upward).astype(jnp.bfloat16)
+
+
+def swap(value, axis, size, bits):
+    return lax.ppermute(value, axis, [(i, i ^ bits) for i in range(size)])
 
 
 def per_device(
@@ -102,9 +107,43 @@
     row_group,
     owner_block,
 ):
+    n_req, n_mlp = lax.axis_size("req"), lax.axis_size("mlp")
+    me, core = lax.axis_index("req"), lax.axis_index("mlp")
+    seat = me % GROUP
     tok_count = q_in.shape[0]
     local_heads = q_in.shape[1] // HD
     local_groups = kv_in.shape[2] // HD
+    lines = [[line + GROUP * i for i in range(n_req // GROUP)] for line in range(GROUP)]
+
+    def spread(block):
+        width = block.shape[1] // GROUP
+        parts = []
+        for k in range(GROUP):
+            part = lax.dynamic_slice_in_dim(block, (seat ^ k) * width, width, 1)
+            parts.append(part if k == 0 else swap(part, "req", n_req, k))
+        ordered = jnp.take(jnp.stack(parts), jnp.arange(GROUP) ^ seat, axis=0)
+        rows = ordered.reshape(GROUP * block.shape[0], width)
+        return lax.all_gather(rows, "req", axis_index_groups=lines, axis=0, tiled=True)
+
+    def both(part):
+        return [part] + [swap(part, "mlp", n_mlp, k) for k in range(1, n_mlp)]
+
+    gate_w = spread(w_gate)
+    up_w = spread(w_up)
+    down_w = spread(w_down_t)
+
+    held = prefix_kv[None]
+    bit = GROUP
+    while bit < n_req:
+        held = jnp.concatenate([held, swap(held, "req", n_req, bit)], axis=0)
+        bit *= 2
+    held = jnp.stack([held] + [swap(held, "req", n_req, k) for k in range(1, GROUP)], axis=1)
+    held = held.reshape(n_req, 2, PB, local_groups * HD)
+    inverse = jnp.argsort(owner_block)
+    picked = lax.dynamic_slice_in_dim(inverse, row_group[0] * BPG, BPG, 0)
+    chosen = jnp.take(held, picked ^ me, axis=0)
+    chosen = jnp.transpose(chosen, (1, 0, 2, 3)).reshape(2, PLEN, local_groups, HD)
+
     request, offset = slot_layout(lengths[0], tok_count)
     positions = offset + PLEN
     queries = rotate(
@@ -115,41 +154,36 @@
         positions,
     ).astype(jnp.bfloat16)
     suffix_value_rows = kv_in[1].reshape(tok_count, local_groups, HD)
-    gathered = lax.all_gather(prefix_kv, "req", axis=1, tiled=True)
-    blocks = gathered.reshape(2, -1, PB, local_groups * HD)
-    inverse = jnp.argsort(owner_block)
-    picked = lax.dynamic_slice_in_dim(inverse, row_group[0] * BPG, BPG, 0)
-    chosen = jnp.take(blocks, picked, axis=1).reshape(2, PLEN, local_groups, HD)
     slot_ids = jnp.arange(tok_count, dtype=jnp.int32)
     allowed = (request[:, None] == request[None, :]) & (slot_ids[None, :] <= slot_ids[:, None])
     attn = attention(queries, chosen[0], chosen[1], suffix_key_rows, suffix_value_rows, allowed)
-    summed = lax.psum_scatter(
-        jnp.dot(attn, w_out, preferred_element_type=jnp.float32).astype(jnp.bfloat16),
-        "mlp",
-        scatter_dimension=0,
-        tiled=True,
-    ).astype(jnp.float32)
-    resid = (hidden_in.astype(jnp.float32) + summed).astype(jnp.bfloat16)
+
+    own_rows = hidden_in.shape[0]
+    summed = hidden_in.astype(jnp.float32)
+    for k in reversed(range(n_mlp)):
+        rows = lax.dynamic_slice_in_dim(attn, (core ^ k) * own_rows, own_rows, 0)
+        terms = jnp.dot(rows, w_out, preferred_element_type=jnp.float32)
+        if k > 0:
+            terms = swap(terms.astype(jnp.bfloat16), "mlp", n_mlp, k).astype(jnp.float32)
+        summed = summed + terms
+    resid = summed.astype(jnp.bfloat16)
     own_normed = rms_scale(resid.astype(jnp.float32), post_gain).astype(jnp.bfloat16)
-    normed = lax.all_gather(own_normed, "mlp", axis=0, tiled=True)
-    gate = jnp.dot(
-        normed,
-        lax.all_gather(w_gate, "req", axis=0, tiled=True),
-        preferred_element_type=jnp.float32,
-    )
-    upward = jnp.dot(
-        normed, lax.all_gather(w_up, "req", axis=0, tiled=True), preferred_element_type=jnp.float32
-    )
-    act = activate(gate, upward)
-    terms = lax.dot_general(
-        act,
-        lax.all_gather(w_down_t, "req", axis=0, tiled=True),
-        (((1,), (1,)), ((), ())),
-        preferred_element_type=jnp.float32,
-    )
-    mixed = lax.psum_scatter(
-        terms.astype(jnp.bfloat16), "mlp", scatter_dimension=0, tiled=True
-    ).astype(jnp.float32)
+
+    normed = jnp.concatenate(
+        [own_normed] + [swap(own_normed, "req", n_req, k) for k in range(1, GROUP)], axis=0
+    )
+    terms = 0.0
+    for gate_part, up_part, down_part in zip(both(gate_w), both(up_w), both(down_w)):
+        gate = jnp.dot(normed, gate_part, preferred_element_type=jnp.float32)
+        upward = jnp.dot(normed, up_part, preferred_element_type=jnp.float32)
+        act = activate(gate, upward)
+        terms = terms + lax.dot_general(
+            act, down_part, (((1,), (1,)), ((), ())), preferred_element_type=jnp.float32
+        )
+    terms = terms.reshape(GROUP, own_rows, -1)
+    mixed = terms[0]
+    for k in range(1, GROUP):
+        mixed = mixed + swap(terms[k].astype(jnp.bfloat16), "req", n_req, k).astype(jnp.float32)
     return (resid.astype(jnp.float32) + mixed).astype(jnp.bfloat16)
 
 

time: 657 us -> 387 us (0.59)
  waiting for transfers between devices: 521 us -> 174 us
  matrix products: 79.6 us -> 115 us
  starting transfers between devices: 0.24 us -> 29.9 us
  local copies, waits for them, and re-layouts: 13.6 us -> 21.2 us
    all_gather x5 -> x3, waiting for transfers between devices: 501 us -> 52.4 us  [spread(): lax.all_gather(rows, 'req', axis_index_groups=lines, axis=0, tiled=True)]
    ppermute x0 -> x24, waiting for transfers between devices: none -> 121 us  [swap(): return lax.ppermute(value, axis, [(i, i ^ bits) for i in range(size)])]
    ppermute x0 -> x24, starting transfers between devices: none -> 29.6 us  [swap(): return lax.ppermute(value, axis, [(i, i ^ bits) for i in range(size)])]
    dot_general x3 -> x6, matrix products: 47.7 us -> 72.2 us  [the longest x2 39.5 us: per_device(): lax.dot_general(act, down_part, (((1,), (1,)), ((), ())), preferred_eleme...]
    reduce_scatter x2 -> x0, waiting for transfers between devices: 17.4 us -> none  [the longest x1 8.85 us: per_device(): lax.psum_scatter(jnp.dot(attn, w_out, preferred_element_type=jnp.float32)...]
  transfers between devices with their start and end apart: 7 -> 27, of which waited for: 7 -> 15; matrix products, arithmetic and copies ran while one was open for 8% -> 34% of each run, Pallas kernels for 0% -> 0%
where the time goes in v1:
time: 387 us; the launch traced here: 382 us
  waiting for transfers between devices  174 us (45%)
  matrix products  115 us (30%)
  starting transfers between devices  29.9 us (8%)
  other arithmetic  28.4 us (7%)
  local copies, waits for them, and re-layouts  21.2 us (5%)
  between operations  14.4 us (4%)
    ppermute x24, waiting for transfers between devices, swap(): return lax.ppermute(value, axis, [(i, i ^ bits) for i in range(size)])  121 us
    all_gather x3, waiting for transfers between devices, spread(): lax.all_gather(rows, 'req', axis_index_groups=lines, axis=0, tiled=True)  52.4 us
    dot_general x2, matrix products, per_device(): lax.dot_general(act, down_part, (((1,), (1,)), ((), ())), preferred_eleme...  39.5 us
    ppermute x24, starting transfers between devices, swap(): return lax.ppermute(value, axis, [(i, i ^ bits) for i in range(size)])  29.6 us
    dot_general x2, matrix products, per_device(): upward = jnp.dot(normed, up_part, preferred_element_type=jnp.float32)  17.6 us
    dot_general x2, matrix products, per_device(): terms = jnp.dot(rows, w_out, preferred_element_type=jnp.float32)  15.1 us
    dot_general x1, matrix products, attention(): jnp.einsum('tgrd,pgd->grtp', grouped_heads, pre_keys, preferred_element_t...  11.6 us
    dot_general x1, matrix products, attention(): jnp.einsum('mabi,ime->mabe', suf_weights.astype(jnp.bfloat16), suffix_val...  10.9 us
  transfers between devices with their start and end apart: 27, of which 15 were waited for; matrix products, arithmetic and copies ran while one was open for 34% of the time, Pallas kernels for 0%

profile of v1, /device:TPU:0, one launch (start us, length us, event | category | flops | bytes accessed | tf_op | source)
XLA Modules:
  0.0 382.3 jit_solution(188340672797872241)
XLA Ops:
  6.5 1.4 dynamic-slice_bitcast_fusion.2
  7.9 4.0 %collective-permute-start.11 = (bf16[160,640]{1,0:T(8,128)(2,1)S(1)}, bf16[160,640]{1,0:T(8,128)(2,1)S(1)}, u32[]{:S(2)}, u32[]{:S(2)}) collective-permute-start(bf16[160,640]{1,0:T(8,128)(2,1)S(1)} %get-tuple-element.23), channel_id=1, source_target_pairs={{0,6},{2,4},{4,2},{6,0},{8,14},{10,12},{12,10},{14,8},{16,22},{18,... | collective-permute-start | bytes 614408 | tf_op jit(solution)/shard_map/ppermute | solution.py:91
  12.5 2.0 dynamic-slice_bitcast_fusion.1
  14.5 2.8 collective-permute-start.14
  19.8 2.4 collective-permute-done.10
  22.3 2.9 collective-permute-start.17
  26.7 2.0 collective-permute-start.15
  29.5 1.7 collective-permute-done.13
  33.7 1.9 collective-permute-done.17
  35.6 3.4 collective-permute-done.16
  41.4 1.6 broadcast_select_fusion.2
  43.1 1.6 collective-permute-start
  44.9 2.1 convert_bitcast_fusion
  48.0 2.0 copy-done
  52.9 4.1 %multiply_multiply_fusion = f32[512,16,128]{2,1,0:T(8,128)S(1)} fusion(f32[128]{0:T(128)S(1)} %copy-done.10, f32[512,16]{1,0:T(8,128)S(1)} %copy.58, f32[64,8,16,128]{3,2,1,0:T(8,128)} %copy-done), kind=kLoop, calls=%fused_computation.23 | loop fusion | flops 2097152 | bytes 8421888 | tf_op jit(solution)/shard_map/mul | solution.py:21
  57.0 1.6 subtract_convert_fusion
  59.1 1.9 copy.59
  62.0 1.3 copy.78
  64.6 1.7 multiply_multiply_fusion.1
  67.7 2.6 collective-permute-start.1
  70.4 9.7 %fusion = (f32[4,4,512]{2,1,0:T(4,128)}, f32[4,512,512,4]{2,1,3,0:T(8,128)}) fusion(pred[512,512]{0,1:T(8,128)(4,1)S(1)} %fusion.24, bf16[512,4,4,64]{3,0,2,1:T(8,128)(2,1)S(1)} %bitcast.102, bf16[512,4,4,64]{3,0,2,1:T(8,128)(2,1)S(1)} %bitcast.105, bf16[512,4,64]{2,0,1:T(8,128)(2,1)S(1)} %get-tuple-element.16, bf16[512,4,64]{2,0,1:T(8,128)(2,1)S(1)} %get-tuple-element.15), kind=kOutput, calls=%fused_computation.8 | convolution fusion | flops 1091559424 | bytes 19693568 | tf_op jit(solution)/shard_map/fknp,bkp->knfb/dot_general | solution.py:59
  80.3 19.4 %collective-permute-done.1 = bf16[2,2,64,512]{3,2,1,0:T(8,128)(2,1)} collective-permute-done((bf16[2,2,64,512]{3,2,1,0:T(8,128)(2,1)}, bf16[2,2,64,512]{3,2,1,0:T(8,128)(2,1)}, u32[]{:S(2)}, u32[]{:S(2)}) %collective-permute-start.1) | collective-permute-done | bytes 262176 | tf_op jit(solution)/shard_map/ppermute | solution.py:91
  99.7 1.9 fusion.41
  101.6 2.1 collective-permute-start.4
  105.0 10.9 %fusion.2 = f32[4,4,512,128]{2,3,1,0:T(8,128)} fusion(bf16[512,4,128,1]{0,2,3,1:T(8,128)(2,1)S(1)} %bitcast.112, f32[4,512,512,4]{2,1,3,0:T(8,128)} %get-tuple-element.43, pred[512,512]{0,1:T(8,128)(4,1)S(1)} %fusion.24), kind=kOutput, calls=%fused_computation.10 | convolution fusion | flops 1086324736 | bytes 21757952 | tf_op jit(solution)/shard_map/mabi,ime->mabe/dot_general | solution.py:72
  116.7 1.3 sort.17
  118.1 9.4 %collective-permute-done.3 = bf16[4,2,64,512]{3,2,1,0:T(8,128)(2,1)} collective-permute-done((bf16[4,2,64,512]{3,2,1,0:T(8,128)(2,1)}, bf16[4,2,64,512]{3,2,1,0:T(8,128)(2,1)}, u32[]{:S(2)}, u32[]{:S(2)}) %collective-permute-start.3) | collective-permute-done | bytes 524320 | tf_op jit(solution)/shard_map/ppermute | solution.py:91
  127.5 3.1 pad_maximum_fusion.1
  130.6 2.2 gather_fusion
  134.0 11.6 %bitcast_reduce_fusion = (f32[4,4,512]{2,1,0:T(4,128)S(1)}, f32[4,512,512,4]{2,1,3,0:T(8,128)}) fusion(bf16[512,4,4,64]{3,0,2,1:T(8,128)(2,1)S(1)} %bitcast.103, bf16[512,4,4,64]{3,0,2,1:T(8,128)(2,1)} %bitcast.104, bf16[512,4,128,1]{2,1,0,3:T(4,128)(2,1)} %bitcast.115), kind=kOutput, calls=%fused_computation.5 | convolution fusion | flops 1086316544 | bytes 19431424 | tf_op jit(solution)/shard_map/tgrd,pgd->grtp/dot_general | solution.py:55
  145.8 10.2 %fusion.9 = bf16[512,4,4,128]{0,3,2,1:T(8,128)(2,1)S(1)} fusion(f32[4,4,512,128]{2,3,1,0:T(8,128)} %fusion.2, f32[512,4,4]{0,2,1:T(4,128)S(1)} %add_bitcast_fusion, f32[4,512,512,4]{2,1,3,0:T(8,128)} %get-tuple-element.41, bf16[512,4,128,1]{2,1,0,3:T(4,128)(2,1)S(1)} %bitcast.116), kind=kOutput, calls=%fused_computation.19 | convolution fusion | flops 1085276160 | bytes 23625728 | tf_op jit(solution)/shard_map/grtp,pgd->grtd/dot_general | solution.py:66
  155.9 7.1 %convolution_convert_fusion = bf16[256,2560]{1,0:T(8,128)(2,1)S(1)} fusion(bf16[2048,2560]{1,0:T(8,128)(2,1)} %param.23, bf16[512,2048]{0,1:T(8,128)(2,1)S(1)} %bitcast.113, s32[]{:T(128)S(6)} %select_n.70), kind=kOutput, calls=%fused_computation.28 | convolution fusion | flops 2685009920 | bytes 12845060 | tf_op jit(solution)/shard_map/dot_general | solution.py:165
  163.2 3.1 collective-permute-done.5
  166.3 7.9 %fusion.10 = (f32[256]{0:T(256)S(1)}, bf16[256,2560]{1,0:T(8,128)(2,1)S(1)}) fusion(bf16[2048,2560]{1,0:T(8,128)(2,1)} %param.23, bf16[512,2048]{0,1:T(8,128)(2,1)S(1)} %bitcast.114, s32[]{:T(128)S(6)} %select_n.71, bf16[256,2560]{1,0:T(8,128)(2,1)} %collective-permute-done.5, bf16[256,2560]{1,0:T(8,128)(2,1)} %param.19), kind=kOutput, calls=%fused_computation.29 | convolution fusion | flops 2689597184 | bytes 15467524 | tf_op jit(solution)/shard_map/dot_general | solution.py:165
  174.7 1.8 collective-permute-start.8
  176.5 1.5 collective-permute-start.7
  178.2 7.8 %all-gather.6.cloned.1.call-done = bf16[2560,640]{1,0:T(8,128)(2,1)} async-done(((bf16[640,640]{1,0:T(8,128)(2,1)}), bf16[2560,640]{1,0:T(8,128)(2,1)}) %all-gather.6.cloned.1.call-update) | async-done | bytes 3276816 | tf_op jit(solution)/shard_map/all_gather | solution.py:126
  186.0 21.4 %collective-permute-done.8 = bf16[256,2560]{1,0:T(8,128)(2,1)} collective-permute-done((bf16[256,2560]{1,0:T(8,128)(2,1)S(1)}, bf16[256,2560]{1,0:T(8,128)(2,1)}, u32[]{:S(2)}, u32[]{:S(2)}) %collective-permute-start.8) | collective-permute-done | bytes 1310752 | tf_op jit(solution)/shard_map/ppermute | solution.py:91
  207.4 44.5 %all-gather.4.cloned.1.call-done = bf16[2560,640]{1,0:T(8,128)(2,1)} async-done(((bf16[640,640]{1,0:T(8,128)(2,1)}), bf16[2560,640]{1,0:T(8,128)(2,1)}) %all-gather.4.cloned.1.call-update) | async-done | bytes 3276816 | tf_op jit(solution)/shard_map/all_gather | solution.py:126
  252.0 8.8 %fusion.44 = f32[1024,640]{1,0:T(8,128)} fusion(bf16[2560,640]{1,0:T(8,128)(2,1)} %all-gather.6.cloned.1.call-done, bf16[256,2560]{1,0:T(8,128)(2,1)} %collective-permute-done.8, bf16[256,2560]{1,0:T(8,128)(2,1)} %collective-permute-done.7, bf16[256,2560]{1,0:T(8,128)(2,1)} %collective-permute-done.6, bf16[256,2560]{1,0:T(8,128)(2,1)S(1)} %fusion.12), kind=kOutput, calls=%fused_computation.113 | convolution fusion | flops 3376414720 | bytes 11141120 | tf_op jit(solution)/shard_map/dot_general | solution.py:178
  260.8 18.7 %fusion.16 = f32[1024,2560]{1,0:T(8,128)} fusion(bf16[2560,640]{1,0:T(8,128)(2,1)} %all-gather.8.cloned.1.call-done, f32[1024,640]{1,0:T(8,128)} %fusion.44, bf16[2560,640]{1,0:T(8,128)(2,1)} %all-gather.4.cloned.1.call-done, bf16[256,2560]{1,0:T(8,128)(2,1)} %collective-permute-done.8, bf16[256,2560]{1,0:T(8,128)(2,1)} %collective-permute-done.7, ...), kind=kOutput, calls=%fused_computation.41 | convolution fusion | flops 6735790080 | bytes 24903680 | tf_op jit(solution)/shard_map/dot_general | solution.py:180
  279.5 8.8 %fusion.42 = f32[1024,640]{1,0:T(8,128)} fusion(bf16[2560,640]{1,0:T(8,128)(2,1)} %collective-permute-done.19, bf16[256,2560]{1,0:T(8,128)(2,1)} %collective-permute-done.8, bf16[256,2560]{1,0:T(8,128)(2,1)} %collective-permute-done.7, bf16[256,2560]{1,0:T(8,128)(2,1)} %collective-permute-done.6, bf16[256,2560]{1,0:T(8,128)(2,1)S(1)} %fusion.12), kind=kOutput, calls=%fused_computation.111 | convolution fusion | flops 3376414720 | bytes 11141120 | tf_op jit(solution)/shard_map/dot_general | solution.py:178
  288.3 20.8 %fusion.49 = (bf16[1024,2560]{1,0:T(8,128)(2,1)}, f32[1024,2560]{1,0:T(8,128)}) fusion(f32[1024,2560]{1,0:T(8,128)} %fusion.16, bf16[2560,640]{1,0:T(8,128)(2,1)} %collective-permute-done.20, f32[1024,640]{1,0:T(8,128)} %fusion.42, bf16[2560,640]{1,0:T(8,128)(2,1)} %collective-permute-done.18, bf16[256,2560]{1,0:T(8,128)(2,1)} %collective-permute-done.8, ...), kind=kOutput, calls=%fused_computation.118 | convolution fusion | flops 6741032960 | bytes 40632320 | tf_op jit(solution)/shard_map/dot_general | solution.py:180
  309.1 2.4 fusion.46
  311.5 2.5 collective-permute-start.23
  315.0 29.0 %collective-permute-done.23 = bf16[256,2560]{1,0:T(8,128)(2,1)S(1)} collective-permute-done((bf16[256,2560]{1,0:T(8,128)(2,1)S(1)}, bf16[256,2560]{1,0:T(8,128)(2,1)S(1)}, u32[]{:S(2)}, u32[]{:S(2)}) %collective-permute-start.23) | collective-permute-done | bytes 1310752 | tf_op jit(solution)/shard_map/ppermute | solution.py:91
  344.1 27.7 %collective-permute-done.22 = bf16[256,2560]{1,0:T(8,128)(2,1)S(1)} collective-permute-done((bf16[256,2560]{1,0:T(8,128)(2,1)S(1)}, bf16[256,2560]{1,0:T(8,128)(2,1)S(1)}, u32[]{:S(2)}, u32[]{:S(2)}) %collective-permute-start.22) | collective-permute-done | bytes 1310752 | tf_op jit(solution)/shard_map/ppermute | solution.py:91
  371.8 3.7 fusion.13
  (103 shorter events, 23.4 us)
Async XLA Ops:
  6.5 11.3 %copy-start.4 = (bf16[160,2560]{1,0:T(8,128)(2,1)S(1)}, bf16[160,2560]{1,0:T(8,128)(2,1)}, u32[]{:S(2)}) copy-start(bf16[160,2560]{1,0:T(8,128)(2,1)} %param.26) | copy-start | bytes 2457604
  6.5 171.7 %all-gather.8.cloned.1.call-start = ((), (), s32[]{:S(2)}) async-start(), calls=%async_computation.2 | async-start | bytes 4096000 | tf_op jit(solution)/shard_map/all_gather | solution.py:126
  7.9 10.7 %collective-permute-start.11 = (bf16[160,640]{1,0:T(8,128)(2,1)S(1)}, bf16[160,640]{1,0:T(8,128)(2,1)S(1)}, u32[]{:S(2)}, u32[]{:S(2)}) collective-permute-start(bf16[160,640]{1,0:T(8,128)(2,1)S(1)} %get-tuple-element.23), channel_id=1, source_target_pairs={{0,6},{2,4},{4,2},{6,0},{8,14},{10,12},{12,10},{14,8},{16,22},{18,... | collective-permute-start | bytes 614408 | tf_op jit(solution)/shard_map/ppermute | solution.py:91
  11.9 10.4 %collective-permute-start.10 = (bf16[160,640]{1,0:T(8,128)(2,1)S(1)}, bf16[160,640]{1,0:T(8,128)(2,1)S(1)}, u32[]{:S(2)}, u32[]{:S(2)}) collective-permute-start(bf16[160,640]{1,0:T(8,128)(2,1)S(1)} %get-tuple-element.24), channel_id=1, source_target_pairs={{0,4},{2,6},{4,0},{6,2},{8,12},{10,14},{12,8},{14,10},{16,20},{18,... | collective-permute-start | bytes 614408 | tf_op jit(solution)/shard_map/ppermute | solution.py:91
  12.4 12.8 %collective-permute-start.9 = (bf16[160,640]{1,0:T(8,128)(2,1)S(1)}, bf16[160,640]{1,0:T(8,128)(2,1)S(1)}, u32[]{:S(2)}, u32[]{:S(2)}) collective-permute-start(bf16[160,640]{1,0:T(8,128)(2,1)S(1)} %get-tuple-element.22), channel_id=1, source_target_pairs={{0,2},{2,0},{4,6},{6,4},{8,10},{10,8},{12,14},{14,12},{16,18},{18,... | collective-permute-start | bytes 614408 | tf_op jit(solution)/shard_map/ppermute | solution.py:91
  14.5 12.1 %collective-permute-start.14 = (bf16[160,640]{1,0:T(8,128)(2,1)S(1)}, bf16[160,640]{1,0:T(8,128)(2,1)S(1)}, u32[]{:S(2)}, u32[]{:S(2)}) collective-permute-start(bf16[160,640]{1,0:T(8,128)(2,1)S(1)} %get-tuple-element.27), channel_id=1, source_target_pairs={{0,6},{2,4},{4,2},{6,0},{8,14},{10,12},{12,10},{14,8},{16,22},{18,... | collective-permute-start | bytes 614408 | tf_op jit(solution)/shard_map/ppermute | solution.py:91
  17.4 13.8 %collective-permute-start.13 = (bf16[160,640]{1,0:T(8,128)(2,1)}, bf16[160,640]{1,0:T(8,128)(2,1)}, u32[]{:S(2)}, u32[]{:S(2)}) collective-permute-start(bf16[160,640]{1,0:T(8,128)(2,1)} %get-tuple-element.28), channel_id=1, source_target_pairs={{0,4},{2,6},{4,0},{6,2},{8,12},{10,14},{12,8},{14,10},{16,20},{18,... | collective-permute-start | bytes 614408 | tf_op jit(solution)/shard_map/ppermute | solution.py:91
  18.6 13.1 %collective-permute-start.12 = (bf16[160,640]{1,0:T(8,128)(2,1)S(1)}, bf16[160,640]{1,0:T(8,128)(2,1)}, u32[]{:S(2)}, u32[]{:S(2)}) collective-permute-start(bf16[160,640]{1,0:T(8,128)(2,1)S(1)} %get-tuple-element.26), channel_id=1, source_target_pairs={{0,2},{2,0},{4,6},{6,4},{8,10},{10,8},{12,14},{14,12},{16,18},{18,... | collective-permute-start | bytes 614408 | tf_op jit(solution)/shard_map/ppermute | solution.py:91
  22.3 13.3 %collective-permute-start.17 = (bf16[160,640]{1,0:T(8,128)(2,1)}, bf16[160,640]{1,0:T(8,128)(2,1)}, u32[]{:S(2)}, u32[]{:S(2)}) collective-permute-start(bf16[160,640]{1,0:T(8,128)(2,1)} %get-tuple-element.31), channel_id=1, source_target_pairs={{0,6},{2,4},{4,2},{6,0},{8,14},{10,12},{12,10},{14,8},{16,22},{18,... | collective-permute-start | bytes 614408 | tf_op jit(solution)/shard_map/ppermute | solution.py:91
  25.2 13.8 %collective-permute-start.16 = (bf16[160,640]{1,0:T(8,128)(2,1)S(1)}, bf16[160,640]{1,0:T(8,128)(2,1)}, u32[]{:S(2)}, u32[]{:S(2)}) collective-permute-start(bf16[160,640]{1,0:T(8,128)(2,1)S(1)} %get-tuple-element.32), channel_id=1, source_target_pairs={{0,4},{2,6},{4,0},{6,2},{8,12},{10,14},{12,8},{14,10},{16,20},{18,... | collective-permute-start | bytes 614408 | tf_op jit(solution)/shard_map/ppermute | solution.py:91
  26.6 5.1 %copy-start.7 = (bf16[160,640]{1,0:T(8,128)(2,1)}, bf16[160,640]{1,0:T(8,128)(2,1)S(1)}, u32[]{:S(2)}) copy-start(bf16[160,640]{1,0:T(8,128)(2,1)S(1)} %collective-permute-done.14) | copy-start | bytes 614404
  26.7 12.7 %collective-permute-start.15 = (bf16[160,640]{1,0:T(8,128)(2,1)S(1)}, bf16[160,640]{1,0:T(8,128)(2,1)}, u32[]{:S(2)}, u32[]{:S(2)}) collective-permute-start(bf16[160,640]{1,0:T(8,128)(2,1)S(1)} %get-tuple-element.30), channel_id=1, source_target_pairs={{0,2},{2,0},{4,6},{6,4},{8,10},{10,8},{12,14},{14,12},{16,18},{18,... | collective-permute-start | bytes 614408 | tf_op jit(solution)/shard_map/ppermute | solution.py:91
  41.3 1.7 copy-start.5
  41.4 3.4 copy-start.12
  43.0 143.0 %all-gather.6.cloned.1.call-start = ((), (), s32[]{:S(2)}) async-start(), calls=%async_computation.1 | async-start | bytes 4096000 | tf_op jit(solution)/shard_map/all_gather | solution.py:126
  43.1 23.9 %collective-permute-start = (bf16[1,2,64,512]{3,2,1,0:T(8,128)(2,1)S(1)}, bf16[1,2,64,512]{3,2,1,0:T(8,128)(2,1)S(1)}, u32[]{:S(2)}, u32[]{:S(2)}) collective-permute-start(bf16[1,2,64,512]{3,2,1,0:T(8,128)(2,1)S(1)} %bitcast.117), channel_id=1, source_target_pairs={{0,8},{2,10},{4,12},{6,14},{8,0},{10,2},{12,4},{14,6},{16,24},{18,... | collective-permute-start | bytes 393224 | tf_op jit(solution)/shard_map/ppermute | solution.py:91
  47.9 2.1 copy-start
  47.9 4.9 %copy-start.10 = (f32[128]{0:T(128)S(1)}, f32[128]{0:T(128)}, u32[]{:S(2)}) copy-start(f32[128]{0:T(128)} %param.20) | copy-start | bytes 1540
  51.6 200.3 %all-gather.4.cloned.1.call-start = ((), (), s32[]{:S(2)}) async-start(), calls=%async_computation | async-start | bytes 4096000 | tf_op jit(solution)/shard_map/all_gather | solution.py:126
  58.6 2.4 copy-start.3
  61.0 3.6 copy-start.11
  64.6 5.8 %copy-start.1 = (bf16[512,16,64]{2,0,1:T(8,128)(2,1)S(1)}, bf16[512,16,64]{2,0,1:T(8,128)(2,1)}, u32[]{:S(2)}) copy-start(bf16[512,16,64]{2,0,1:T(8,128)(2,1)} %copy.59) | copy-start | bytes 3145732
  67.0 3.4 copy-start.6
  67.7 32.0 %collective-permute-start.1 = (bf16[2,2,64,512]{3,2,1,0:T(8,128)(2,1)}, bf16[2,2,64,512]{3,2,1,0:T(8,128)(2,1)}, u32[]{:S(2)}, u32[]{:S(2)}) collective-permute-start(bf16[2,2,64,512]{3,2,1,0:T(8,128)(2,1)} %pad_maximum_fusion.9), channel_id=1, source_target_pairs={{0,16},{2,18},{4,20},{6,22},{8,24},{10,26},{12,28},{14,30},{16,0},... | collective-permute-start | bytes 786440 | tf_op jit(solution)/shard_map/ppermute | solution.py:91
  70.4 9.7 %copy-start.2 = (bf16[1,512,512]{2,1,0:T(8,128)(2,1)S(1)}, bf16[1,512,512]{2,1,0:T(8,128)(2,1)}, u32[]{:S(2)}) copy-start(bf16[1,512,512]{2,1,0:T(8,128)(2,1)} %get-tuple-element.20) | copy-start | bytes 1572868
  101.6 16.5 %collective-permute-start.4 = (bf16[4,2,64,512]{3,2,1,0:T(8,128)(2,1)}, bf16[4,2,64,512]{3,2,1,0:T(8,128)(2,1)}, u32[]{:S(2)}, u32[]{:S(2)}) collective-permute-start(bf16[4,2,64,512]{3,2,1,0:T(8,128)(2,1)} %get-tuple-element.34), channel_id=1, source_target_pairs={{0,6},{2,4},{4,2},{6,0},{8,14},{10,12},{12,10},{14,8},{16,22},{18,... | collective-permute-start | bytes 1572872 | tf_op jit(solution)/shard_map/ppermute | solution.py:91
  103.7 23.8 %collective-permute-start.3 = (bf16[4,2,64,512]{3,2,1,0:T(8,128)(2,1)}, bf16[4,2,64,512]{3,2,1,0:T(8,128)(2,1)}, u32[]{:S(2)}, u32[]{:S(2)}) collective-permute-start(bf16[4,2,64,512]{3,2,1,0:T(8,128)(2,1)} %get-tuple-element.34), channel_id=1, source_target_pairs={{0,4},{2,6},{4,0},{6,2},{8,12},{10,14},{12,8},{14,10},{16,20},{18,... | collective-permute-start | bytes 1572872 | tf_op jit(solution)/shard_map/ppermute | solution.py:91
  104.6 22.9 %collective-permute-start.2 = (bf16[4,2,64,512]{3,2,1,0:T(8,128)(2,1)}, bf16[4,2,64,512]{3,2,1,0:T(8,128)(2,1)}, u32[]{:S(2)}, u32[]{:S(2)}) collective-permute-start(bf16[4,2,64,512]{3,2,1,0:T(8,128)(2,1)} %get-tuple-element.34), channel_id=1, source_target_pairs={{0,2},{2,0},{4,6},{6,4},{8,10},{10,8},{12,14},{14,12},{16,18},{18,... | collective-permute-start | bytes 1572872 | tf_op jit(solution)/shard_map/ppermute | solution.py:91
  105.0 11.6 %copy-start.13 = (s32[16]{0:T(128)S(1)}, s32[16]{0:T(128)}, u32[]{:S(2)}) copy-start(s32[16]{0:T(128)} %param.29) | copy-start | bytes 196
  134.0 11.8 %copy-start.8 = (f32[4,4,512]{2,1,0:T(4,128)S(1)}, f32[4,4,512]{2,1,0:T(4,128)}, u32[]{:S(2)}) copy-start(f32[4,4,512]{2,1,0:T(4,128)} %get-tuple-element.42) | copy-start | bytes 98308
  163.1 3.2 collective-permute-start.5
  163.2 11.1 %copy-start.9 = (f32[2560]{0:T(1024)S(1)}, f32[2560]{0:T(1024)}, u32[]{:S(2)}) copy-start(f32[2560]{0:T(1024)} %param.22) | copy-start | bytes 30724
  174.7 32.7 %collective-permute-start.8 = (bf16[256,2560]{1,0:T(8,128)(2,1)S(1)}, bf16[256,2560]{1,0:T(8,128)(2,1)}, u32[]{:S(2)}, u32[]{:S(2)}) collective-permute-start(bf16[256,2560]{1,0:T(8,128)(2,1)S(1)} %fusion.12), channel_id=1, source_target_pairs={{0,6},{2,4},{4,2},{6,0},{8,14},{10,12},{12,10},{14,8},{16,22},{18,... | collective-permute-start | bytes 3932168 | tf_op jit(solution)/shard_map/ppermute | solution.py:91
  176.5 75.5 %collective-permute-start.7 = (bf16[256,2560]{1,0:T(8,128)(2,1)S(1)}, bf16[256,2560]{1,0:T(8,128)(2,1)}, u32[]{:S(2)}, u32[]{:S(2)}) collective-permute-start(bf16[256,2560]{1,0:T(8,128)(2,1)S(1)} %fusion.12), channel_id=1, source_target_pairs={{0,4},{2,6},{4,0},{6,2},{8,12},{10,14},{12,8},{14,10},{16,20},{18,... | collective-permute-start | bytes 3932168 | tf_op jit(solution)/shard_map/ppermute | solution.py:91
  178.0 74.0 %collective-permute-start.6 = (bf16[256,2560]{1,0:T(8,128)(2,1)S(1)}, bf16[256,2560]{1,0:T(8,128)(2,1)}, u32[]{:S(2)}, u32[]{:S(2)}) collective-permute-start(bf16[256,2560]{1,0:T(8,128)(2,1)S(1)} %fusion.12), channel_id=1, source_target_pairs={{0,2},{2,0},{4,6},{6,4},{8,10},{10,8},{12,14},{14,12},{16,18},{18,... | collective-permute-start | bytes 3932168 | tf_op jit(solution)/shard_map/ppermute | solution.py:91
  178.2 110.1 %collective-permute-start.20 = (bf16[2560,640]{1,0:T(8,128)(2,1)}, bf16[2560,640]{1,0:T(8,128)(2,1)}, u32[]{:S(2)}, u32[]{:S(2)}) collective-permute-start(bf16[2560,640]{1,0:T(8,128)(2,1)} %all-gather.8.cloned.1.call-done), channel_id=1, source_target_pairs={{0,1},{1,0},{2,3},{3,2},{4,5},{5,4},{6,7},{7,6},{8,9},{9,8},{10,11... | collective-permute-start | bytes 9830408 | tf_op jit(solution)/shard_map/ppermute | solution.py:91
  186.0 93.5 %collective-permute-start.19 = (bf16[2560,640]{1,0:T(8,128)(2,1)}, bf16[2560,640]{1,0:T(8,128)(2,1)}, u32[]{:S(2)}, u32[]{:S(2)}) collective-permute-start(bf16[2560,640]{1,0:T(8,128)(2,1)} %all-gather.6.cloned.1.call-done), channel_id=1, source_target_pairs={{0,1},{1,0},{2,3},{3,2},{4,5},{5,4},{6,7},{7,6},{8,9},{9,8},{10,11... | collective-permute-start | bytes 9830408 | tf_op jit(solution)/shard_map/ppermute | solution.py:91
  251.9 36.4 %collective-permute-start.18 = (bf16[2560,640]{1,0:T(8,128)(2,1)}, bf16[2560,640]{1,0:T(8,128)(2,1)}, u32[]{:S(2)}, u32[]{:S(2)}) collective-permute-start(bf16[2560,640]{1,0:T(8,128)(2,1)} %all-gather.4.cloned.1.call-done), channel_id=1, source_target_pairs={{0,1},{1,0},{2,3},{3,2},{4,5},{5,4},{6,7},{7,6},{8,9},{9,8},{10,11... | collective-permute-start | bytes 9830408 | tf_op jit(solution)/shard_map/ppermute | solution.py:91
  311.5 32.6 %collective-permute-start.23 = (bf16[256,2560]{1,0:T(8,128)(2,1)S(1)}, bf16[256,2560]{1,0:T(8,128)(2,1)S(1)}, u32[]{:S(2)}, u32[]{:S(2)}) collective-permute-start(bf16[256,2560]{1,0:T(8,128)(2,1)S(1)} %get-tuple-element.11), channel_id=1, source_target_pairs={{0,6},{2,4},{4,2},{6,0},{8,14},{10,12},{12,10},{14,8},{16,22},{18,... | collective-permute-start | bytes 3932168 | tf_op jit(solution)/shard_map/ppermute | solution.py:91
  313.9 57.8 %collective-permute-start.22 = (bf16[256,2560]{1,0:T(8,128)(2,1)S(1)}, bf16[256,2560]{1,0:T(8,128)(2,1)S(1)}, u32[]{:S(2)}, u32[]{:S(2)}) collective-permute-start(bf16[256,2560]{1,0:T(8,128)(2,1)S(1)} %get-tuple-element.12), channel_id=1, source_target_pairs={{0,4},{2,6},{4,0},{6,2},{8,12},{10,14},{12,8},{14,10},{16,20},{18,... | collective-permute-start | bytes 3932168 | tf_op jit(solution)/shard_map/ppermute | solution.py:91
  314.5 57.3 %collective-permute-start.21 = (bf16[256,2560]{1,0:T(8,128)(2,1)S(1)}, bf16[256,2560]{1,0:T(8,128)(2,1)S(1)}, u32[]{:S(2)}, u32[]{:S(2)}) collective-permute-start(bf16[256,2560]{1,0:T(8,128)(2,1)S(1)} %get-tuple-element.10), channel_id=1, source_target_pairs={{0,2},{2,0},{4,6},{6,4},{8,10},{10,8},{12,14},{14,12},{16,18},{18,... | collective-permute-start | bytes 3932168 | tf_op jit(solution)/shard_map/ppermute | solution.py:91
Sparse Core Ops, SparseCore 0:
  43.1 76.9 all-gather.7
  121.6 64.3 all-gather.5
  187.6 64.2 all-gather.3

commit v2 on v0

v2 whole, which is shorter than its diff:
```python
import functools
import math

import jax
import jax.numpy as jnp
from jax import lax
from jax.experimental import pallas as pl
from jax.experimental.pallas import tpu as pltpu
from jax.sharding import PartitionSpec as P

HD = 128
PB = 64
PLEN = 512
BPG = 8
GROUP = 4
VMEM_LIMIT = 48 * 1024 * 1024


EPSILON = 1e-06
THETA = 1000000.0


def rotation(positions):
    half_width = HD // 2
    exponent = jnp.arange(half_width, dtype=jnp.float32) * (2.0 / HD)
    inv_freq = jnp.power(jnp.float32(THETA), -exponent)
    angles = positions.astype(jnp.float32)[:, None] * inv_freq[None, :]
    cosine, sine = jnp.cos(angles), jnp.sin(angles)
    return jnp.concatenate([cosine, cosine], axis=1), jnp.concatenate([-sine, sine], axis=1)


def slot_layout(row_lengths, tok_count):
    req_ends = jnp.cumsum(row_lengths)
    starts = req_ends - row_lengths
    slot_ids = jnp.arange(tok_count, dtype=jnp.int32)
    request = jnp.sum((slot_ids[:, None] >= req_ends[None, :]).astype(jnp.int32), axis=1)
    member = request[:, None] == jnp.arange(row_lengths.shape[0], dtype=jnp.int32)[None, :]
    offset = slot_ids - jnp.sum(jnp.where(member, starts[None, :], 0), axis=1)
    return (request, offset)


def dot_rows(left, right):
    return lax.dot_general(
        left, right, (((1,), (1,)), ((), ())), preferred_element_type=jnp.float32
    )


def attention_kernel(
    start_ref, cos_ref, sin_ref, q_gain, k_gain, q_ref, k_ref, v_ref, pk_ref, pv_ref, out_ref, bias
):
    tok_count = k_ref.shape[1]
    tile = min(256, tok_count)
    scale = math.log2(math.e) / math.sqrt(HD)

    @pl.when(pl.program_id(0) == 0)
    def _():
        keys = lax.broadcasted_iota(jnp.int32, (tok_count, tok_count), 1)
        slots = lax.broadcasted_iota(jnp.int32, (tok_count, tok_count), 0)
        seen = (keys >= start_ref[...]) & (keys <= slots)
        bias[...] = jnp.where(seen, 0.0, -1e30)

    def prepare(values, gain, rows):
        values = values.astype(jnp.float32)
        mean_sq = jnp.mean(values * values, axis=-1, keepdims=True)
        scaled = values * lax.rsqrt(mean_sq + EPSILON) * gain[...]
        turned = scaled * cos_ref[rows, :] + pltpu.roll(scaled, HD // 2, 1) * sin_ref[rows, :]
        return turned.astype(jnp.bfloat16)

    key = prepare(k_ref[0], k_gain, pl.ds(0, tok_count))
    value = v_ref[0]
    pre_key = pk_ref[...].reshape(-1, HD)
    pre_value = pv_ref[...].reshape(-1, HD)
    for head in range(q_ref.shape[1] // HD):
        lanes = pl.ds(head * HD, HD)
        for first in range(0, tok_count, tile):
            rows = pl.ds(first, tile)
            last = first + tile
            query = prepare(q_ref[rows, lanes], q_gain, rows)
            pre_w = jnp.exp2(dot_rows(query, pre_key) * scale)
            suf_w = jnp.exp2(dot_rows(query, key[:last]) * scale + bias[rows, :last])
            total = jnp.sum(pre_w, axis=-1, keepdims=True) + jnp.sum(suf_w, axis=-1, keepdims=True)
            top = jnp.dot(
                pre_w.astype(jnp.bfloat16), pre_value, preferred_element_type=jnp.float32
            ) + jnp.dot(
                suf_w.astype(jnp.bfloat16), value[:last], preferred_element_type=jnp.float32
            )
            out_ref[rows, lanes] = (top / total).astype(out_ref.dtype)


def attention(start, cosine, sine, q_gain, k_gain, q_in, kv_in, chosen, first, count):
    tok_count = q_in.shape[0]
    groups = kv_in.shape[2] // HD
    width = q_in.shape[1] // groups
    blocks = chosen.shape[0]

    def same(rows, columns):
        return pl.BlockSpec((rows, columns), lambda g: (0, 0))

    def suffix(which):
        return pl.BlockSpec((1, tok_count, HD), lambda g: (which, 0, g + first))

    def prefix(which):
        return pl.BlockSpec((blocks, 1, PB, HD), lambda g: (0, which, 0, g + first))

    keys = tok_count + PLEN
    return pl.pallas_call(
        attention_kernel,
        grid=(count,),
        in_specs=[
            same(tok_count, 1),
            same(tok_count, HD),
            same(tok_count, HD),
            same(1, HD),
            same(1, HD),
            pl.BlockSpec((tok_count, width), lambda g: (0, g + first)),
            suffix(0),
            suffix(1),
            prefix(0),
            prefix(1),
        ],
        out_specs=pl.BlockSpec((tok_count, width), lambda g: (0, g)),
        out_shape=jax.ShapeDtypeStruct((tok_count, count * width), jnp.bfloat16),
        scratch_shapes=[pltpu.VMEM((tok_count, tok_count), jnp.float32)],
        compiler_params=pltpu.CompilerParams(vmem_limit_bytes=VMEM_LIMIT),
        cost_estimate=pl.CostEstimate(
            flops=4 * tok_count * keys * width * count,
            bytes_accessed=4 * tok_count * width * count,
            transcendentals=tok_count * keys * width // HD * count,
        ),
        name="attention",
    )(start, cosine, sine, q_gain, k_gain, q_in, kv_in, kv_in, chosen, chosen)


def project_kernel(core, *refs, n_parts, n_mlp):
    parts, weights, outs = refs[:n_parts], refs[n_parts : 2 * n_parts], refs[2 * n_parts :]
    rows = outs[0].shape[0]
    for k in range(n_mlp - 1, -1, -1):
        part = pl.ds(pl.multiple_of((core[0] ^ k) * rows, rows), rows)
        total = 0.0
        for x, w in zip(parts, weights):
            total = total + jnp.dot(x[part, :], w[...], preferred_element_type=jnp.float32)
        outs[k][...] = total.astype(outs[k].dtype)


def project(core, parts, w_out, n_mlp):
    tok_count, depth = parts[0].shape
    columns = w_out.shape[1]
    rows, tile = tok_count // n_mlp, 512
    n_parts = len(parts)
    return pl.pallas_call(
        functools.partial(project_kernel, n_parts=n_parts, n_mlp=n_mlp),
        grid_spec=pltpu.PrefetchScalarGridSpec(
            num_scalar_prefetch=1,
            grid=(columns // tile,),
            in_specs=[pl.BlockSpec((tok_count, depth), lambda n, core: (0, 0))] * n_parts
            + [
                pl.BlockSpec((depth, tile), functools.partial(lambda i, n, core: (i, n), i))
                for i in range(n_parts)
            ],
            out_specs=[pl.BlockSpec((rows, tile), lambda n, core: (0, n))] * n_mlp,
        ),
        out_shape=[
            jax.ShapeDtypeStruct((rows, columns), jnp.bfloat16 if k else jnp.float32)
            for k in range(n_mlp)
        ],
        compiler_params=pltpu.CompilerParams(vmem_limit_bytes=VMEM_LIMIT),
        cost_estimate=pl.CostEstimate(
            flops=2 * tok_count * depth * n_parts * columns,
            bytes_accessed=2 * depth * n_parts * (tok_count + columns) + 3 * tok_count * columns,
            transcendentals=0,
        ),
        name="project",
    )(core, *parts, *[w_out] * n_parts)


def normalize_kernel(hidden, gain, own, *refs):
    parts, resid_ref, normed_ref = refs[:-2], refs[-2], refs[-1]
    total = hidden[...].astype(jnp.float32) + own[...]
    for part in parts:
        total = total + part[...].astype(jnp.float32)
    resid = total.astype(resid_ref.dtype)
    resid_ref[...] = resid
    values = resid.astype(jnp.float32)
    mean_sq = jnp.mean(values * values, axis=-1, keepdims=True)
    normed = values * lax.rsqrt(mean_sq + EPSILON) * gain[...]
    normed_ref[...] = normed.astype(normed_ref.dtype)


def normalize(hidden, gain, own, parts):
    rows, columns = hidden.shape
    tile = min(64, rows)
    spec = pl.BlockSpec((tile, columns), lambda i: (i, 0))
    return pl.pallas_call(
        normalize_kernel,
        grid=(rows // tile,),
        in_specs=[spec, pl.BlockSpec((1, columns), lambda i: (0, 0)), spec] + [spec] * len(parts),
        out_specs=[spec, spec],
        out_shape=[jax.ShapeDtypeStruct(hidden.shape, hidden.dtype)] * 2,
        compiler_params=pltpu.CompilerParams(vmem_limit_bytes=VMEM_LIMIT),
        cost_estimate=pl.CostEstimate(
            flops=rows * columns * 8, bytes_accessed=rows * columns * 12, transcendentals=rows
        ),
        name="normalize",
    )(hidden, gain, own, *parts)


def gate_up_kernel(pair, *refs):
    x_refs, w_refs, refs = refs[:GROUP], refs[GROUP : GROUP + 4], refs[GROUP + 4 :]
    act_ref, x_all, weight, gate_sum, up_sum, sems = refs
    width = act_ref.shape[1]
    rows, depth = x_refs[0].shape
    half = depth // 2
    packed = len(weight.shape) == 3
    x_copies = [
        pltpu.make_async_copy(x_ref, x_all.at[i], sems.at[i]) for i, x_ref in enumerate(x_refs)
    ]
    w_copies = []
    for i, w_ref in enumerate(w_refs):
        which, kind = i // 2, i % 2
        if packed:
            place = weight.at[which, :, pl.ds(kind * width, width)]
        else:
            place = weight.at[which, kind]
        w_copies.append(pltpu.make_async_copy(w_ref, place, sems.at[GROUP + i]))
    for copy in w_copies[:2] + x_copies + w_copies[2:]:
        copy.start()
    for copy in w_copies[:2] + x_copies:
        copy.wait()
    for which in range(2):
        start = pair[0] if which == 0 else 1 - pair[0]
        columns = pl.ds(pl.multiple_of(start * half, 128), half)
        if which == 1:
            for copy in w_copies[2:]:
                copy.wait()

        def step(i, carry):
            x = x_all[i, :, columns]
            if packed:
                terms = jnp.dot(x, weight[which], preferred_element_type=jnp.float32)
                gate, upward = terms[:, :width], terms[:, width:]
            else:
                gate = jnp.dot(x, weight[which, 0], preferred_element_type=jnp.float32)
                upward = jnp.dot(x, weight[which, 1], preferred_element_type=jnp.float32)
            if which == 0:
                gate_sum[i] = gate
                up_sum[i] = upward
            else:
                gate = gate + gate_sum[i]
                upward = upward + up_sum[i]
                here = pl.ds(pl.multiple_of(i * rows, rows), rows)
                act_ref[here, :] = (gate / (1.0 + jnp.exp(-gate)) * upward).astype(act_ref.dtype)
            return carry

        lax.fori_loop(0, GROUP, step, 0)


def gate_up(pair, normed, gate_w, up_w):
    rows, depth = normed[0].shape
    width = gate_w[0].shape[1]
    total = rows * len(normed)
    half = depth // 2
    shape = (2, half, 2 * width) if width % 128 == 0 else (2, 2, half, width)
    return pl.pallas_call(
        gate_up_kernel,
        in_specs=[pl.BlockSpec(memory_space=pltpu.SMEM)]
        + [pl.BlockSpec(memory_space=pl.ANY)] * (len(normed) + 4),
        out_specs=pl.BlockSpec(memory_space=pltpu.VMEM),
        out_shape=jax.ShapeDtypeStruct((total, width), jnp.bfloat16),
        scratch_shapes=[
            pltpu.VMEM((len(normed), rows, depth), jnp.bfloat16),
            pltpu.VMEM(shape, jnp.bfloat16),
            pltpu.VMEM((len(normed), rows, width), jnp.float32),
            pltpu.VMEM((len(normed), rows, width), jnp.float32),
            pltpu.SemaphoreType.DMA((len(normed) + 4,)),
        ],
        compiler_params=pltpu.CompilerParams(vmem_limit_bytes=VMEM_LIMIT),
        cost_estimate=pl.CostEstimate(
            flops=4 * total * depth * width,
            bytes_accessed=2 * (total * depth + 2 * depth * width + total * width),
            transcendentals=total * width,
        ),
        name="gate_up",
    )(pair, *normed, gate_w[0], up_w[0], gate_w[1], up_w[1])


def down_kernel(*refs, n_parts):
    act_refs, w_refs, outs = refs[:n_parts], refs[n_parts : 2 * n_parts], refs[2 * n_parts : -3]
    acts, weight, sems = refs[-3:]
    width = act_refs[0].shape[1]
    rows = outs[0].shape[0]
    packed = len(acts.shape) == 2
    copies = []
    for i in range(n_parts):
        if packed:
            lanes = pl.ds(i * width, width)
            places = acts.at[:, lanes], weight.at[:, lanes]
        else:
            places = acts.at[i], weight.at[i]
        copies.append(pltpu.make_async_copy(act_refs[i], places[0], sems.at[2 * i]))
        copies.append(pltpu.make_async_copy(w_refs[i], places[1], sems.at[2 * i + 1]))
    for copy in copies:
        copy.start()
    for copy in copies:
        copy.wait()
    for k in range(len(outs) - 1, -1, -1):
        here = pl.ds(k * rows, rows)
        if packed:
            total = dot_rows(acts[here, :], weight[...])
        else:
            total = sum(dot_rows(acts[i, here, :], weight[i]) for i in range(n_parts))
        outs[k][...] = total.astype(outs[k].dtype)


def down(acts, weights):
    total, width = acts[0].shape
    columns = weights[0].shape[0]
    rows = total // GROUP
    n_parts = len(acts)
    if width % 128 == 0:
        shapes = [(total, n_parts * width), (columns, n_parts * width)]
    else:
        shapes = [(n_parts, total, width), (n_parts, columns, width)]
    return pl.pallas_call(
        functools.partial(down_kernel, n_parts=n_parts),
        out_shape=[
            jax.ShapeDtypeStruct((rows, columns), jnp.bfloat16 if i else jnp.float32)
            for i in range(GROUP)
        ],
        in_specs=[pl.BlockSpec(memory_space=pl.ANY)] * (2 * n_parts),
        out_specs=[pl.BlockSpec(memory_space=pltpu.VMEM)] * GROUP,
        scratch_shapes=[pltpu.VMEM(shape, jnp.bfloat16) for shape in shapes]
        + [pltpu.SemaphoreType.DMA((2 * n_parts,))],
        compiler_params=pltpu.CompilerParams(vmem_limit_bytes=VMEM_LIMIT),
        cost_estimate=pl.CostEstimate(
            flops=2 * total * width * columns * n_parts,
            bytes_accessed=2 * n_parts * (total + columns) * width + 2 * total * columns,
            transcendentals=0,
        ),
        name="down",
    )(*acts, *weights)


def finish_kernel(order, resid, own, *refs):
    total = resid[...].astype(jnp.float32) + own[...]
    for part in refs[:-1]:
        total = total + part[...].astype(jnp.float32)
    refs[-1][...] = total.astype(refs[-1].dtype)


def finish(order, out, own, parts):
    rows, columns = own.shape
    chunk = out.shape[1] // 4
    placed = pl.BlockSpec((rows, chunk), lambda d, order: (0, order[d]))
    plain = pl.BlockSpec((rows, chunk), lambda d, order: (0, d))
    return pl.pallas_call(
        finish_kernel,
        grid_spec=pltpu.PrefetchScalarGridSpec(
            num_scalar_prefetch=1,
            grid=(columns // chunk,),
            in_specs=[placed] + [plain] * (1 + len(parts)),
            out_specs=placed,
        ),
        out_shape=jax.ShapeDtypeStruct(out.shape, out.dtype),
        input_output_aliases={1: 0},
        compiler_params=pltpu.CompilerParams(vmem_limit_bytes=VMEM_LIMIT),
        cost_estimate=pl.CostEstimate(
            flops=rows * columns * 5, bytes_accessed=rows * columns * 14, transcendentals=0
        ),
        name="finish",
    )(order, out, own, *parts)


def swap(value, axis, size, bits):
    return lax.ppermute(value, axis, [(i, i ^ bits) for i in range(size)])


def per_device(
    q_in,
    kv_in,
    prefix_kv,
    hidden_in,
    q_gain,
    k_gain,
    post_gain,
    w_out,
    w_gate,
    w_up,
    w_down_t,
    lengths,
    row_group,
    owner_block,
):
    n_req, n_mlp = lax.axis_size("req"), lax.axis_size("mlp")
    me, core = lax.axis_index("req"), lax.axis_index("mlp")
    seat, place = me % GROUP, me // GROUP
    n_line = n_req // GROUP
    tok_count = q_in.shape[0]
    local_groups = kv_in.shape[2] // HD

    def exchange(block):
        width = block.shape[1] // GROUP
        parts = []
        for k in range(GROUP):
            part = lax.dynamic_slice_in_dim(block, (seat ^ k) * width, width, 1)
            parts.append(part if k == 0 else swap(part, "req", n_req, k))
        rows = jnp.take(jnp.stack(parts), jnp.arange(GROUP) ^ seat, axis=0)
        return rows.reshape(GROUP * block.shape[0], width)

    if n_line == 4:
        pair = place // 2
        inner = (place == 1) | (place == 2)

        def hop(value, *edges):
            return lax.ppermute(
                value, "req", [(GROUP * a + i, GROUP * b + i) for a, b in edges for i in range(GROUP)]
            )

        def near(rows):
            other = swap(rows, "req", n_req, GROUP)
            return jnp.where(
                place % 2 == 0,
                jnp.concatenate([rows, other], axis=0),
                jnp.concatenate([other, rows], axis=0),
            )

        def over(base):
            return hop(base, (1, 2), (2, 1))

        def far(crossed):
            return jnp.where(inner, crossed, hop(crossed, (1, 0), (2, 3)))

    else:
        pair = 0
        lines = [[line + GROUP * i for i in range(n_line)] for line in range(GROUP)]

        def near(rows):
            return lax.all_gather(rows, "req", axis_index_groups=lines, axis=0, tiled=True)

        def over(base):
            return base

        def far(crossed):
            return crossed

    def cores(part):
        return [part] + [swap(part, "mlp", n_mlp, k) for k in range(1, n_mlp)]

    held, slot, bit, weight = prefix_kv[None], jnp.argsort(owner_block) ^ me, n_req // 2, 1
    spot = 0
    while bit >= GROUP:
        held = jnp.concatenate([held, swap(held, "req", n_req, bit)], axis=0)
        spot = spot + (slot // bit) % 2 * weight
        bit, weight = bit // 2, weight * 2
    spot = spot + slot % GROUP * weight

    gate_rows = exchange(w_gate)
    up_rows = exchange(w_up)
    held, w_down_t = lax.optimization_barrier((held, w_down_t))
    held = jnp.stack([held] + [swap(held, "req", n_req, k) for k in range(1, GROUP)])
    held = held.reshape(n_req, 2, PB, local_groups * HD)
    picked = lax.dynamic_slice_in_dim(spot, row_group[0] * BPG, BPG, 0)
    chosen = jnp.take(held, picked, axis=0)
    down_rows = exchange(w_down_t)

    _, offset = slot_layout(lengths[0], tok_count)
    cosine, sine = rotation(offset + PLEN)
    start = (jnp.arange(tok_count, dtype=jnp.int32) - offset)[:, None]
    gains = q_gain[None], k_gain[None]
    first = local_groups // 2

    gate_base = near(gate_rows)
    chosen, gate_base = lax.optimization_barrier((chosen, gate_base))
    up_base = near(up_rows)
    gate_over = over(gate_base)
    attn_low = attention(start, cosine, sine, *gains, q_in, kv_in, chosen, 0, first)
    attn_low, gate_over, up_base, down_rows = lax.optimization_barrier(
        (attn_low, gate_over, up_base, down_rows)
    )
    down_base = near(down_rows)
    up_over = over(up_base)
    attn_high = attention(
        start, cosine, sine, *gains, q_in, kv_in, chosen, first, local_groups - first
    )

    sums = project(core[None], [attn_low, attn_high], w_out, n_mlp)
    parts = [swap(sums[k], "mlp", n_mlp, k) for k in range(1, n_mlp)]
    resid, own_normed = normalize(hidden_in, post_gain[None], sums[0], parts)
    normed = [own_normed] + [swap(own_normed, "req", n_req, k) for k in range(1, GROUP)]

    if n_line == 4:
        down_over = over(down_base)
        gate_w, up_w = (gate_base, far(gate_over)), (up_base, far(up_over))
        chunk = down_rows.shape[0]
        down_w = down_base, far(down_over[:chunk]), far(down_over[chunk:])
        order = [2 * pair, 2 * pair + 1, 2 - 2 * pair, 3 - 2 * pair]
    else:
        half = up_base.shape[0] // 2
        gate_w, up_w, down_w = (
            (base[:half], base[half:]) for base in (gate_base, up_base, down_base)
        )
        order = [0, 1, 2, 3]
    order = jnp.stack([jnp.asarray(entry, jnp.int32) for entry in order])
    pair = jnp.asarray(pair, jnp.int32)[None]

    gate_w, up_w, down_w = ([cores(part) for part in parts] for parts in (gate_w, up_w, down_w))
    acts = [
        gate_up(pair, normed, [part[k] for part in gate_w], [part[k] for part in up_w])
        for k in range(n_mlp)
    ]
    out, done = resid, 0
    for weights in down_w:
        sums = down(acts, weights)
        parts = [swap(sums[k], "req", n_req, k) for k in range(1, GROUP)]
        blocks = 4 * sums[0].shape[1] // resid.shape[1]
        out = finish(order[done : done + blocks], out, sums[0], parts)
        done += blocks
    return out


def solution(mesh):
    in_specs = (
        P("req", "mlp"),
        P(None, "req", "mlp"),
        P(None, "req", "mlp"),
        P(("req", "mlp"), None),
        P(),
        P(),
        P(),
        P("mlp", None),
        P("req", "mlp"),
        P("req", "mlp"),
        P("req", "mlp"),
        P("req", None),
        P("req"),
        P(),
    )
    out_specs = P(("req", "mlp"), None)
    return jax.shard_map(
        per_device, mesh=mesh, in_specs=in_specs, out_specs=out_specs, check_vma=False
    )
```

time: 657 us -> 335 us (0.51)
  the two profiles are of different devices: /device:TPU:0 before, /device:TPU:12 now
where the time goes in v2:
time: 335 us; the launch traced here: 334 us
  waiting for transfers between devices  160 us (48%)
  Pallas kernels  67.6 us (20%)
  starting transfers between devices  55.1 us (16%)
  other arithmetic  27.6 us (8%)
  local copies, waits for them, and re-layouts  23.1 us (7%)
    ppermute x37, waiting for transfers between devices, swap(): return lax.ppermute(value, axis, [(i, i ^ bits) for i in range(size)])  98.6 us
    ppermute x7, waiting for transfers between devices, hop(): lax.ppermute(value, 'req', [(GROUP * a + i, GROUP * b + i) for a, b in ed...  61 us
    ppermute x37, starting transfers between devices, swap(): return lax.ppermute(value, axis, [(i, i ^ bits) for i in range(size)])  32.1 us
    ppermute x7, starting transfers between devices, hop(): lax.ppermute(value, 'req', [(GROUP * a + i, GROUP * b + i) for a, b in ed...  23 us
    pallas_call x2, Pallas kernels, gate_up(): pl.pallas_call(gate_up_kernel, in_specs=[pl.BlockSpec(memory_space=pltpu....  21.4 us
    unnamed x66, local copies, waits for them, and re-layouts  15.5 us
    pallas_call x2, Pallas kernels, attention(): pl.pallas_call(attention_kernel, grid=(count,), in_specs=[same(tok_count,...  14.1 us
    pallas_call x3, Pallas kernels, down(): pl.pallas_call(functools.partial(down_kernel, n_parts=n_parts), out_shape...  11.8 us
  transfers between devices with their start and end apart: 44, of which 17 were waited for; matrix products, arithmetic and copies ran while one was open for 9% of the time, Pallas kernels for 20%

profile of v2, /device:TPU:12, one launch (start us, length us, event | category | flops | bytes accessed | tf_op | source)
XLA Modules:
  0.0 334.2 jit_solution(8505083600693476672)
XLA Ops:
  0.0 2.6 collective-permute-start
  2.6 2.1 dynamic-slice_bitcast_fusion.1
  13.0 5.5 %collective-permute-done.1 = bf16[2,2,64,512]{3,2,1,0:T(8,128)(2,1)S(1)} collective-permute-done((bf16[2,2,64,512]{3,2,1,0:T(8,128)(2,1)S(1)}, bf16[2,2,64,512]{3,2,1,0:T(8,128)(2,1)S(1)}, u32[]{:S(2)}, u32[]{:S(2)}) %collective-permute-start.1) | collective-permute-done | bytes 262176 | tf_op jit(solution)/shard_map/ppermute | solution.py:374
  34.5 11.2 %collective-permute-done.15 = bf16[160,640]{1,0:T(8,128)(2,1)} collective-permute-done((bf16[160,640]{1,0:T(8,128)(2,1)}, bf16[160,640]{1,0:T(8,128)(2,1)}, u32[]{:S(2)}, u32[]{:S(2)}) %collective-permute-start.15) | collective-permute-done | bytes 204832 | tf_op jit(solution)/shard_map/ppermute | solution.py:374
  47.7 1.6 broadcast_select_fusion.3
  50.1 6.6 %collective-permute-done.3 = bf16[4,2,64,512]{3,2,1,0:T(8,128)(2,1)} collective-permute-done((bf16[4,2,64,512]{3,2,1,0:T(8,128)(2,1)}, bf16[4,2,64,512]{3,2,1,0:T(8,128)(2,1)}, u32[]{:S(2)}, u32[]{:S(2)}) %collective-permute-start.3) | collective-permute-done | bytes 524320 | tf_op jit(solution)/shard_map/ppermute | solution.py:374
  56.7 1.8 pad_maximum_fusion
  59.3 2.7 collective-permute-done.8
  62.0 3.5 %maximum_select_fusion.refs_4_ = bf16[1280,640]{1,0:T(8,128)(2,1)} fusion(bf16[640,640]{1,0:T(8,128)(2,1)} %collective-permute-done.8, bf16[640,640]{1,0:T(8,128)(2,1)} %bitcast.23, pred[]{:T(512)S(6)} %eq.36), kind=kLoop, calls=%fused_computation.5 | loop fusion | flops 7372800 | bytes 3276801 | tf_op jit(solution)/shard_map/jit(_where)/select_n | solution.py:420
  65.5 2.0 collective-permute-start.9
  69.7 1.7 copy-done.1
  71.4 7.0 %attention.2.refs_0_ = bf16[512,1024]{1,0:T(8,128)(2,1)S(1)} custom-call(s32[512,1]{1,0:T(8,128)S(1)} %subtract_subtract_fusion.start_ref, f32[512,128]{1,0:T(8,128)S(1)} %get-tuple-element.78.cos_ref, f32[512,128]{1,0:T(8,128)S(1)} %get-tuple-element.79.sin_ref, f32[1,128]{1,0:T(1,128)S(1)} %bitcast.42, f32[1,128]{1,0:T(1,128)S(1)} %bitcast.44, ...), custom_call_target="tpu_custom_call" | custom-call | flops 2147483648 | bytes 2097152 | tf_op jit(solution)/shard_map/attention/pallas_call | solution.py:106
  78.4 6.5 %collective-permute-done.13 = bf16[640,640]{1,0:T(8,128)(2,1)} collective-permute-done((bf16[640,640]{1,0:T(8,128)(2,1)}, bf16[640,640]{1,0:T(8,128)(2,1)}, u32[]{:S(2)}, u32[]{:S(2)}) %collective-permute-start.13) | collective-permute-done | bytes 819232 | tf_op jit(solution)/shard_map/ppermute | solution.py:374
  84.9 3.5 %maximum_select_fusion.1.refs_5_ = bf16[1280,640]{1,0:T(8,128)(2,1)} fusion(bf16[640,640]{1,0:T(8,128)(2,1)} %collective-permute-done.13, bf16[640,640]{1,0:T(8,128)(2,1)} %bitcast.28, pred[]{:T(512)S(6)} %eq.36), kind=kLoop, calls=%fused_computation.6 | loop fusion | flops 7372800 | bytes 3276801 | tf_op jit(solution)/shard_map/jit(_where)/select_n | solution.py:420
  88.4 13.2 %collective-permute-done.9 = bf16[1280,640]{1,0:T(8,128)(2,1)} collective-permute-done((bf16[1280,640]{1,0:T(8,128)(2,1)}, bf16[1280,640]{1,0:T(8,128)(2,1)}, u32[]{:S(2)}, u32[]{:S(2)}) %collective-permute-start.9) | collective-permute-done | bytes 1638432 | tf_op jit(solution)/shard_map/ppermute | solution.py:414
  101.6 3.0 collective-permute-start.22
  104.6 1.6 copy-done.2
  108.1 7.1 %attention.3.refs_1_ = bf16[512,1024]{1,0:T(8,128)(2,1)S(1)} custom-call(s32[512,1]{1,0:T(8,128)S(1)} %copy-done.7, f32[512,128]{1,0:T(8,128)S(1)} %get-tuple-element.78.cos_ref, f32[512,128]{1,0:T(8,128)S(1)} %copy-done.5, f32[1,128]{1,0:T(1,128)S(1)} %bitcast.43, f32[1,128]{1,0:T(1,128)S(1)} %bitcast.45, bf16[512,2048]{1,0:T(8,128)(2,1)S(1)} %copy-done.2, ...), custom_call_target="tpu_custom_call" | custom-call | flops 2147483648 | bytes 2097152 | tf_op jit(solution)/shard_map/attention/pallas_call | solution.py:106
  115.1 4.1 %collective-permute-start.21 = (bf16[1280,640]{1,0:T(8,128)(2,1)}, bf16[1280,640]{1,0:T(8,128)(2,1)}, u32[]{:S(2)}, u32[]{:S(2)}) collective-permute-start(bf16[1280,640]{1,0:T(8,128)(2,1)} %collective-permute-done.9), channel_id=1, source_target_pairs={{8,0},{10,2},{12,4},{14,6},{16,24},{18,26},{20,28},{22,30},{9,1},{... | collective-permute-start | bytes 4915208 | tf_op jit(solution)/shard_map/ppermute | solution.py:414
  119.2 3.6 %maximum_select_fusion.2.refs_2_ = bf16[1280,640]{1,0:T(8,128)(2,1)} fusion(bf16[640,640]{1,0:T(8,128)(2,1)} %collective-permute-done.28, bf16[640,640]{1,0:T(8,128)(2,1)} %bitcast.33, pred[]{:T(512)S(6)} %eq.36), kind=kLoop, calls=%fused_computation.7 | loop fusion | flops 7372800 | bytes 3276801 | tf_op jit(solution)/shard_map/jit(_where)/select_n | solution.py:420
  122.8 2.8 collective-permute-start.33
  125.6 9.5 %project.1 = (f32[256,2560]{1,0:T(8,128)S(1)}, bf16[256,2560]{1,0:T(8,128)(2,1)}) custom-call(s32[1]{0:T(128)} %bitcast.4.core, bf16[512,1024]{1,0:T(8,128)(2,1)S(1)} %attention.2.refs_0_, bf16[512,1024]{1,0:T(8,128)(2,1)S(1)} %attention.3.refs_1_, bf16[2048,2560]{1,0:T(8,128)(2,1)} %refs_3_.1, bf16[2048,2560]{1,0:T(8,128)(2,1)} %refs_3_.1), custom_call_target="tpu_custom_call" | custom-call | flops 5368709120 | bytes 16515072 | tf_op jit(solution)/shard_map/project/pallas_call | solution.py:150
  136.6 6.0 %collective-permute-done.22 = bf16[1280,640]{1,0:T(8,128)(2,1)} collective-permute-done((bf16[1280,640]{1,0:T(8,128)(2,1)}, bf16[1280,640]{1,0:T(8,128)(2,1)}, u32[]{:S(2)}, u32[]{:S(2)}) %collective-permute-start.22) | collective-permute-done | bytes 1638432 | tf_op jit(solution)/shard_map/ppermute | solution.py:414
  142.5 2.5 collective-permute-start.23
  145.0 26.7 %collective-permute-done.33 = bf16[1280,640]{1,0:T(8,128)(2,1)S(1)} collective-permute-done((bf16[1280,640]{1,0:T(8,128)(2,1)}, bf16[1280,640]{1,0:T(8,128)(2,1)S(1)}, u32[]{:S(2)}, u32[]{:S(2)}) %collective-permute-start.33) | collective-permute-done | bytes 1638432 | tf_op jit(solution)/shard_map/ppermute | solution.py:414
  173.9 2.2 collective-permute-start.39
  176.1 3.9 %normalize.1 = (bf16[256,2560]{1,0:T(8,128)(2,1)}, bf16[256,2560]{1,0:T(8,128)(2,1)S(1)}) custom-call(bf16[256,2560]{1,0:T(8,128)(2,1)S(1)} %copy-done.8, f32[1,2560]{1,0:T(1,128)S(1)} %broadcast_in_dim.61.gain, f32[256,2560]{1,0:T(8,128)} %copy-done.3, bf16[256,2560]{1,0:T(8,128)(2,1)S(1)} %collective-permute-done.17.refs_0_), custom_call_target="tpu_custom_call" | custom-call | flops 5242880 | bytes 7864320 | tf_op jit(solution)/shard_map/normalize/pallas_call | solution.py:193
  180.0 3.3 collective-permute-start.18
  184.8 2.8 broadcast_select_fusion.1.refs_6_
  187.6 15.1 %collective-permute-done.39 = bf16[640,640]{1,0:T(8,128)(2,1)} collective-permute-done((bf16[640,640]{1,0:T(8,128)(2,1)}, bf16[640,640]{1,0:T(8,128)(2,1)}, u32[]{:S(2)}, u32[]{:S(2)}) %collective-permute-start.39) | collective-permute-done | bytes 819232 | tf_op jit(solution)/shard_map/ppermute | solution.py:414
  202.9 6.6 %collective-permute-start.34 = (bf16[640,640]{1,0:T(8,128)(2,1)S(1)}, bf16[640,640]{1,0:T(8,128)(2,1)}, u32[]{:S(2)}, u32[]{:S(2)}) collective-permute-start(bf16[640,640]{1,0:T(8,128)(2,1)S(1)} %get-tuple-element.59), channel_id=1, source_target_pairs={{8,0},{10,2},{12,4},{14,6},{16,24},{18,26},{20,28},{22,30},{9,1},{... | collective-permute-start | bytes 2457608 | tf_op jit(solution)/shard_map/ppermute | solution.py:414
  209.5 2.8 broadcast_select_fusion.refs_7_
  213.0 24.3 %collective-permute-done.19.refs_2_ = bf16[256,2560]{1,0:T(8,128)(2,1)S(1)} collective-permute-done((bf16[256,2560]{1,0:T(8,128)(2,1)S(1)}, bf16[256,2560]{1,0:T(8,128)(2,1)S(1)}, u32[]{:S(2)}, u32[]{:S(2)}) %collective-permute-start.19) | collective-permute-done | bytes 1310752 | tf_op jit(solution)/shard_map/ppermute | solution.py:374
  241.3 10.7 %gate_up.2.refs_0_ = bf16[1024,640]{1,0:T(8,128)(2,1)S(1)} custom-call(s32[1]{0:T(128)} %bitcast.34.pair, bf16[256,2560]{1,0:T(8,128)(2,1)S(1)} %copy-done.20, bf16[256,2560]{1,0:T(8,128)(2,1)S(1)} %collective-permute-done.18.refs_1_, bf16[256,2560]{1,0:T(8,128)(2,1)S(1)} %copy-done.22, bf16[256,2560]{1,0:T(8,128)(2,1)} %copy-done.30, ...), custom_call_target="tpu_custom_call" | custom-call | flops 6710886400 | bytes 13107200 | tf_op jit(solution)/shard_map/gate_up/pallas_call | solution.py:263
  252.8 10.7 %gate_up.3.refs_1_ = bf16[1024,640]{1,0:T(8,128)(2,1)S(1)} custom-call(s32[1]{0:T(128)} %bitcast.34.pair, bf16[256,2560]{1,0:T(8,128)(2,1)S(1)} %copy-done.20, bf16[256,2560]{1,0:T(8,128)(2,1)S(1)} %collective-permute-done.18.refs_1_, bf16[256,2560]{1,0:T(8,128)(2,1)S(1)} %copy-done.22, bf16[256,2560]{1,0:T(8,128)(2,1)} %copy-done.30, ...), custom_call_target="tpu_custom_call" | custom-call | flops 6710886400 | bytes 13107200 | tf_op jit(solution)/shard_map/gate_up/pallas_call | solution.py:263
  263.5 5.7 %down.3 = (f32[256,1280]{1,0:T(8,128)S(1)}, bf16[256,1280]{1,0:T(8,128)(2,1)S(1)}, bf16[256,1280]{1,0:T(8,128)(2,1)S(1)}, bf16[256,1280]{1,0:T(8,128)(2,1)S(1)}) custom-call(bf16[1024,640]{1,0:T(8,128)(2,1)S(1)} %gate_up.2.refs_0_, bf16[1024,640]{1,0:T(8,128)(2,1)S(1)} %gate_up.3.refs_1_, bf16[1280,640]{1,0:T(8,128)(2,1)} %maximum_select_fusion.2.refs_2_, ...), custom_call_target="tpu_custom_call" | custom-call | flops 3355443200 | bytes 8519680 | tf_op jit(solution)/shard_map/down/pallas_call | solution.py:323
  269.6 3.1 collective-permute-start.32
  272.7 3.0 down.4
  276.4 3.0 down.5
  279.5 27.6 %collective-permute-done.36.refs_0_ = bf16[256,640]{1,0:T(8,128)(2,1)S(1)} collective-permute-done((bf16[256,640]{1,0:T(8,128)(2,1)S(1)}, bf16[256,640]{1,0:T(8,128)(2,1)S(1)}, u32[]{:S(2)}, u32[]{:S(2)}) %collective-permute-start.36) | collective-permute-done | bytes 327712 | tf_op jit(solution)/shard_map/ppermute | solution.py:374
  307.8 1.7 collective-permute-start.41
  310.4 1.7 collective-permute-start.42
  315.2 2.7 finish.3.resid
  317.9 1.8 collective-permute-done.38.refs_2_
  319.7 2.1 finish.4.resid
  321.8 3.8 %collective-permute-done.41.refs_0_ = bf16[256,640]{1,0:T(8,128)(2,1)} collective-permute-done((bf16[256,640]{1,0:T(8,128)(2,1)}, bf16[256,640]{1,0:T(8,128)(2,1)}, u32[]{:S(2)}, u32[]{:S(2)}) %collective-permute-start.41) | collective-permute-done | bytes 327712 | tf_op jit(solution)/shard_map/ppermute | solution.py:374
  326.6 5.4 %collective-permute-done.43.refs_2_ = bf16[256,640]{1,0:T(8,128)(2,1)} collective-permute-done((bf16[256,640]{1,0:T(8,128)(2,1)}, bf16[256,640]{1,0:T(8,128)(2,1)}, u32[]{:S(2)}, u32[]{:S(2)}) %collective-permute-start.43) | collective-permute-done | bytes 327712 | tf_op jit(solution)/shard_map/ppermute | solution.py:374
  332.0 2.2 finish.5
  (161 shorter events, 48.6 us)
Async XLA Ops:
  0.0 11.8 %collective-permute-start = (bf16[1,2,64,512]{3,2,1,0:T(8,128)(2,1)}, bf16[1,2,64,512]{3,2,1,0:T(8,128)(2,1)S(1)}, u32[]{:S(2)}, u32[]{:S(2)}) collective-permute-start(bf16[1,2,64,512]{3,2,1,0:T(8,128)(2,1)} %bitcast.47), channel_id=1, source_target_pairs={{0,16},{2,18},{4,20},{6,22},{8,24},{10,26},{12,28},{14,30},{16,0},... | collective-permute-start | bytes 393224 | tf_op jit(solution)/shard_map/ppermute | solution.py:374
  4.7 16.2 %collective-permute-start.12 = (bf16[160,640]{1,0:T(8,128)(2,1)S(1)}, bf16[160,640]{1,0:T(8,128)(2,1)S(1)}, u32[]{:S(2)}, u32[]{:S(2)}) collective-permute-start(bf16[160,640]{1,0:T(8,128)(2,1)S(1)} %get-tuple-element.66), channel_id=1, source_target_pairs={{0,6},{2,4},{4,2},{6,0},{8,14},{10,12},{12,10},{14,8},{16,22},{18,... | collective-permute-start | bytes 614408 | tf_op jit(solution)/shard_map/ppermute | solution.py:374
  6.1 16.2 %collective-permute-start.11 = (bf16[160,640]{1,0:T(8,128)(2,1)}, bf16[160,640]{1,0:T(8,128)(2,1)}, u32[]{:S(2)}, u32[]{:S(2)}) collective-permute-start(bf16[160,640]{1,0:T(8,128)(2,1)} %get-tuple-element.67), channel_id=1, source_target_pairs={{0,4},{2,6},{4,0},{6,2},{8,12},{10,14},{12,8},{14,10},{16,20},{18,... | collective-permute-start | bytes 614408 | tf_op jit(solution)/shard_map/ppermute | solution.py:374
  7.7 16.1 %collective-permute-start.10 = (bf16[160,640]{1,0:T(8,128)(2,1)}, bf16[160,640]{1,0:T(8,128)(2,1)}, u32[]{:S(2)}, u32[]{:S(2)}) collective-permute-start(bf16[160,640]{1,0:T(8,128)(2,1)} %get-tuple-element.65), channel_id=1, source_target_pairs={{0,2},{2,0},{4,6},{6,4},{8,10},{10,8},{12,14},{14,12},{16,18},{18,... | collective-permute-start | bytes 614408 | tf_op jit(solution)/shard_map/ppermute | solution.py:374
  9.0 16.2 %collective-permute-start.7 = (bf16[160,640]{1,0:T(8,128)(2,1)}, bf16[160,640]{1,0:T(8,128)(2,1)S(1)}, u32[]{:S(2)}, u32[]{:S(2)}) collective-permute-start(bf16[160,640]{1,0:T(8,128)(2,1)} %get-tuple-element.70), channel_id=1, source_target_pairs={{0,6},{2,4},{4,2},{6,0},{8,14},{10,12},{12,10},{14,8},{16,22},{18,... | collective-permute-start | bytes 614408 | tf_op jit(solution)/shard_map/ppermute | solution.py:374
  11.8 6.7 %collective-permute-start.1 = (bf16[2,2,64,512]{3,2,1,0:T(8,128)(2,1)S(1)}, bf16[2,2,64,512]{3,2,1,0:T(8,128)(2,1)S(1)}, u32[]{:S(2)}, u32[]{:S(2)}) collective-permute-start(bf16[2,2,64,512]{3,2,1,0:T(8,128)(2,1)S(1)} %pad_maximum_fusion.7), channel_id=1, source_target_pairs={{0,8},{2,10},{4,12},{6,14},{8,0},{10,2},{12,4},{14,6},{16,24},{18,... | collective-permute-start | bytes 786440 | tf_op jit(solution)/shard_map/ppermute | solution.py:374
  18.5 10.6 %collective-permute-start.6 = (bf16[160,640]{1,0:T(8,128)(2,1)}, bf16[160,640]{1,0:T(8,128)(2,1)}, u32[]{:S(2)}, u32[]{:S(2)}) collective-permute-start(bf16[160,640]{1,0:T(8,128)(2,1)} %get-tuple-element.71), channel_id=1, source_target_pairs={{0,4},{2,6},{4,0},{6,2},{8,12},{10,14},{12,8},{14,10},{16,20},{18,... | collective-permute-start | bytes 614408 | tf_op jit(solution)/shard_map/ppermute | solution.py:374
  20.9 8.2 %collective-permute-start.5 = (bf16[160,640]{1,0:T(8,128)(2,1)S(1)}, bf16[160,640]{1,0:T(8,128)(2,1)}, u32[]{:S(2)}, u32[]{:S(2)}) collective-permute-start(bf16[160,640]{1,0:T(8,128)(2,1)S(1)} %get-tuple-element.69), channel_id=1, source_target_pairs={{0,2},{2,0},{4,6},{6,4},{8,10},{10,8},{12,14},{14,12},{16,18},{18,... | collective-permute-start | bytes 614408 | tf_op jit(solution)/shard_map/ppermute | solution.py:374
  22.3 11.5 %collective-permute-start.16 = (bf16[160,640]{1,0:T(8,128)(2,1)}, bf16[160,640]{1,0:T(8,128)(2,1)}, u32[]{:S(2)}, u32[]{:S(2)}) collective-permute-start(bf16[160,640]{1,0:T(8,128)(2,1)} %get-tuple-element.61), channel_id=1, source_target_pairs={{0,6},{2,4},{4,2},{6,0},{8,14},{10,12},{12,10},{14,8},{16,22},{18,... | collective-permute-start | bytes 614408 | tf_op jit(solution)/shard_map/ppermute | solution.py:374
  23.7 22.0 %collective-permute-start.15 = (bf16[160,640]{1,0:T(8,128)(2,1)}, bf16[160,640]{1,0:T(8,128)(2,1)}, u32[]{:S(2)}, u32[]{:S(2)}) collective-permute-start(bf16[160,640]{1,0:T(8,128)(2,1)} %get-tuple-element.62), channel_id=1, source_target_pairs={{0,4},{2,6},{4,0},{6,2},{8,12},{10,14},{12,8},{14,10},{16,20},{18,... | collective-permute-start | bytes 614408 | tf_op jit(solution)/shard_map/ppermute | solution.py:374
  25.3 20.5 %collective-permute-start.14 = (bf16[160,640]{1,0:T(8,128)(2,1)}, bf16[160,640]{1,0:T(8,128)(2,1)}, u32[]{:S(2)}, u32[]{:S(2)}) collective-permute-start(bf16[160,640]{1,0:T(8,128)(2,1)} %get-tuple-element.63), channel_id=1, source_target_pairs={{0,2},{2,0},{4,6},{6,4},{8,10},{10,8},{12,14},{14,12},{16,18},{18,... | collective-permute-start | bytes 614408 | tf_op jit(solution)/shard_map/ppermute | solution.py:374
  31.0 19.1 %collective-permute-start.4 = (bf16[4,2,64,512]{3,2,1,0:T(8,128)(2,1)}, bf16[4,2,64,512]{3,2,1,0:T(8,128)(2,1)}, u32[]{:S(2)}, u32[]{:S(2)}) collective-permute-start(bf16[4,2,64,512]{3,2,1,0:T(8,128)(2,1)} %pad_maximum_fusion.4), channel_id=1, source_target_pairs={{0,6},{2,4},{4,2},{6,0},{8,14},{10,12},{12,10},{14,8},{16,22},{18,... | collective-permute-start | bytes 1572872 | tf_op jit(solution)/shard_map/ppermute | solution.py:374
  32.5 24.2 %collective-permute-start.3 = (bf16[4,2,64,512]{3,2,1,0:T(8,128)(2,1)}, bf16[4,2,64,512]{3,2,1,0:T(8,128)(2,1)}, u32[]{:S(2)}, u32[]{:S(2)}) collective-permute-start(bf16[4,2,64,512]{3,2,1,0:T(8,128)(2,1)} %pad_maximum_fusion.4), channel_id=1, source_target_pairs={{0,4},{2,6},{4,0},{6,2},{8,12},{10,14},{12,8},{14,10},{16,20},{18,... | collective-permute-start | bytes 1572872 | tf_op jit(solution)/shard_map/ppermute | solution.py:374
  33.8 22.9 %collective-permute-start.2 = (bf16[4,2,64,512]{3,2,1,0:T(8,128)(2,1)}, bf16[4,2,64,512]{3,2,1,0:T(8,128)(2,1)}, u32[]{:S(2)}, u32[]{:S(2)}) collective-permute-start(bf16[4,2,64,512]{3,2,1,0:T(8,128)(2,1)} %pad_maximum_fusion.4), channel_id=1, source_target_pairs={{0,2},{2,0},{4,6},{6,4},{8,10},{10,8},{12,14},{14,12},{16,18},{18,... | collective-permute-start | bytes 1572872 | tf_op jit(solution)/shard_map/ppermute | solution.py:374
  49.3 12.7 %collective-permute-start.8 = (bf16[640,640]{1,0:T(8,128)(2,1)}, bf16[640,640]{1,0:T(8,128)(2,1)}, u32[]{:S(2)}, u32[]{:S(2)}) collective-permute-start(bf16[640,640]{1,0:T(8,128)(2,1)} %bitcast.23), channel_id=1, source_target_pairs={{0,8},{2,10},{4,12},{6,14},{8,0},{10,2},{12,4},{14,6},{16,24},{18,... | collective-permute-start | bytes 2457608 | tf_op jit(solution)/shard_map/ppermute | solution.py:374
  65.5 36.1 %collective-permute-start.9 = (bf16[1280,640]{1,0:T(8,128)(2,1)}, bf16[1280,640]{1,0:T(8,128)(2,1)}, u32[]{:S(2)}, u32[]{:S(2)}) collective-permute-start(bf16[1280,640]{1,0:T(8,128)(2,1)} %maximum_select_fusion.refs_4_), channel_id=1, source_target_pairs={{8,16},{10,18},{12,20},{14,22},{16,8},{18,10},{20,12},{22,14},{9,1... | collective-permute-start | bytes 4915208 | tf_op jit(solution)/shard_map/ppermute | solution.py:414
  67.7 17.2 %collective-permute-start.13 = (bf16[640,640]{1,0:T(8,128)(2,1)}, bf16[640,640]{1,0:T(8,128)(2,1)}, u32[]{:S(2)}, u32[]{:S(2)}) collective-permute-start(bf16[640,640]{1,0:T(8,128)(2,1)} %bitcast.28), channel_id=1, source_target_pairs={{0,8},{2,10},{4,12},{6,14},{8,0},{10,2},{12,4},{14,6},{16,24},{18,... | collective-permute-start | bytes 2457608 | tf_op jit(solution)/shard_map/ppermute | solution.py:374
  101.6 17.6 %collective-permute-start.28 = (bf16[640,640]{1,0:T(8,128)(2,1)}, bf16[640,640]{1,0:T(8,128)(2,1)}, u32[]{:S(2)}, u32[]{:S(2)}) collective-permute-start(bf16[640,640]{1,0:T(8,128)(2,1)} %bitcast.33), channel_id=1, source_target_pairs={{0,8},{2,10},{4,12},{6,14},{8,0},{10,2},{12,4},{14,6},{16,24},{18,... | collective-permute-start | bytes 2457608 | tf_op jit(solution)/shard_map/ppermute | solution.py:374
  101.6 40.9 %collective-permute-start.22 = (bf16[1280,640]{1,0:T(8,128)(2,1)}, bf16[1280,640]{1,0:T(8,128)(2,1)}, u32[]{:S(2)}, u32[]{:S(2)}) collective-permute-start(bf16[1280,640]{1,0:T(8,128)(2,1)} %maximum_select_fusion.1.refs_5_), channel_id=1, source_target_pairs={{8,16},{10,18},{12,20},{14,22},{16,8},{18,10},{20,12},{22,14},{9,1... | collective-permute-start | bytes 4915208 | tf_op jit(solution)/shard_map/ppermute | solution.py:414
  115.1 68.2 %collective-permute-start.21 = (bf16[1280,640]{1,0:T(8,128)(2,1)}, bf16[1280,640]{1,0:T(8,128)(2,1)}, u32[]{:S(2)}, u32[]{:S(2)}) collective-permute-start(bf16[1280,640]{1,0:T(8,128)(2,1)} %collective-permute-done.9), channel_id=1, source_target_pairs={{8,0},{10,2},{12,4},{14,6},{16,24},{18,26},{20,28},{22,30},{9,1},{... | collective-permute-start | bytes 4915208 | tf_op jit(solution)/shard_map/ppermute | solution.py:414
  122.8 48.9 %collective-permute-start.33 = (bf16[1280,640]{1,0:T(8,128)(2,1)}, bf16[1280,640]{1,0:T(8,128)(2,1)S(1)}, u32[]{:S(2)}, u32[]{:S(2)}) collective-permute-start(bf16[1280,640]{1,0:T(8,128)(2,1)} %maximum_select_fusion.2.refs_2_), channel_id=1, source_target_pairs={{8,16},{10,18},{12,20},{14,22},{16,8},{18,10},{20,12},{22,14},{9,1... | collective-permute-start | bytes 4915208 | tf_op jit(solution)/shard_map/ppermute | solution.py:414
  136.5 39.5 %copy-start.29 = (f32[2560]{0:T(1024)S(1)}, f32[2560]{0:T(1024)}, u32[]{:S(2)}) copy-start(f32[2560]{0:T(1024)} %param.22) | copy-start | bytes 30724
  136.5 39.5 %copy-start.8 = (bf16[256,2560]{1,0:T(8,128)(2,1)S(1)}, bf16[256,2560]{1,0:T(8,128)(2,1)}, u32[]{:S(2)}) copy-start(bf16[256,2560]{1,0:T(8,128)(2,1)} %hidden.1) | copy-start | bytes 3932164
  136.5 39.5 %collective-permute-start.17 = (bf16[256,2560]{1,0:T(8,128)(2,1)}, bf16[256,2560]{1,0:T(8,128)(2,1)S(1)}, u32[]{:S(2)}, u32[]{:S(2)}) collective-permute-start(bf16[256,2560]{1,0:T(8,128)(2,1)} %get-tuple-element.38), channel_id=1, source_target_pairs={{0,1},{1,0},{2,3},{3,2},{4,5},{5,4},{6,7},{7,6},{8,9},{9,8},{10,11... | collective-permute-start | bytes 3932168 | tf_op jit(solution)/shard_map/ppermute | solution.py:374
  142.5 60.4 %collective-permute-start.23 = (bf16[1280,640]{1,0:T(8,128)(2,1)}, bf16[1280,640]{1,0:T(8,128)(2,1)}, u32[]{:S(2)}, u32[]{:S(2)}) collective-permute-start(bf16[1280,640]{1,0:T(8,128)(2,1)} %collective-permute-done.22), channel_id=1, source_target_pairs={{8,0},{10,2},{12,4},{14,6},{16,24},{18,26},{20,28},{22,30},{9,1},{... | collective-permute-start | bytes 4915208 | tf_op jit(solution)/shard_map/ppermute | solution.py:414
  173.9 28.9 %collective-permute-start.39 = (bf16[640,640]{1,0:T(8,128)(2,1)}, bf16[640,640]{1,0:T(8,128)(2,1)}, u32[]{:S(2)}, u32[]{:S(2)}) collective-permute-start(bf16[640,640]{1,0:T(8,128)(2,1)} %slice.17), channel_id=1, source_target_pairs={{8,0},{10,2},{12,4},{14,6},{16,24},{18,26},{20,28},{22,30},{9,1},{... | collective-permute-start | bytes 2457608 | tf_op jit(solution)/shard_map/ppermute | solution.py:414
  180.0 22.7 %copy-start.24 = (bf16[1280,640]{1,0:T(8,128)(2,1)S(1)}, bf16[1280,640]{1,0:T(8,128)(2,1)}, u32[]{:S(2)}) copy-start(bf16[1280,640]{1,0:T(8,128)(2,1)} %copy-done.23) | copy-start | bytes 4915204
  180.0 32.9 %collective-permute-start.18 = (bf16[256,2560]{1,0:T(8,128)(2,1)S(1)}, bf16[256,2560]{1,0:T(8,128)(2,1)S(1)}, u32[]{:S(2)}, u32[]{:S(2)}) collective-permute-start(bf16[256,2560]{1,0:T(8,128)(2,1)S(1)} %get-tuple-element.40.refs_0_), channel_id=1, source_target_pairs={{0,2},{2,0},{4,6},{6,4},{8,10},{10,8},{12,14},{14,12},{16,18},{18,... | collective-permute-start | bytes 3932168 | tf_op jit(solution)/shard_map/ppermute | solution.py:374
  183.3 54.0 %collective-permute-start.19 = (bf16[256,2560]{1,0:T(8,128)(2,1)S(1)}, bf16[256,2560]{1,0:T(8,128)(2,1)S(1)}, u32[]{:S(2)}, u32[]{:S(2)}) collective-permute-start(bf16[256,2560]{1,0:T(8,128)(2,1)S(1)} %get-tuple-element.40.refs_0_), channel_id=1, source_target_pairs={{0,4},{2,6},{4,0},{6,2},{8,12},{10,14},{12,8},{14,10},{16,20},{18,... | collective-permute-start | bytes 3932168 | tf_op jit(solution)/shard_map/ppermute | solution.py:374
  183.4 55.0 %collective-permute-start.20 = (bf16[256,2560]{1,0:T(8,128)(2,1)S(1)}, bf16[256,2560]{1,0:T(8,128)(2,1)S(1)}, u32[]{:S(2)}, u32[]{:S(2)}) collective-permute-start(bf16[256,2560]{1,0:T(8,128)(2,1)S(1)} %get-tuple-element.40.refs_0_), channel_id=1, source_target_pairs={{0,6},{2,4},{4,2},{6,0},{8,14},{10,12},{12,10},{14,8},{16,22},{18,... | collective-permute-start | bytes 3932168 | tf_op jit(solution)/shard_map/ppermute | solution.py:374
  202.7 49.4 %collective-permute-start.24 = (bf16[1280,640]{1,0:T(8,128)(2,1)}, bf16[1280,640]{1,0:T(8,128)(2,1)}, u32[]{:S(2)}, u32[]{:S(2)}) collective-permute-start(bf16[1280,640]{1,0:T(8,128)(2,1)} %maximum_select_fusion.refs_4_), channel_id=1, source_target_pairs={{0,1},{1,0},{2,3},{3,2},{4,5},{5,4},{6,7},{7,6},{8,9},{9,8},{10,11... | collective-permute-start | bytes 4915208 | tf_op jit(solution)/shard_map/ppermute | solution.py:374
  202.9 37.1 %copy-start.20 = (bf16[256,2560]{1,0:T(8,128)(2,1)S(1)}, bf16[256,2560]{1,0:T(8,128)(2,1)}, u32[]{:S(2)}) copy-start(bf16[256,2560]{1,0:T(8,128)(2,1)} %copy-done.19) | copy-start | bytes 3932164
  202.9 36.0 %collective-permute-start.34 = (bf16[640,640]{1,0:T(8,128)(2,1)S(1)}, bf16[640,640]{1,0:T(8,128)(2,1)}, u32[]{:S(2)}, u32[]{:S(2)}) collective-permute-start(bf16[640,640]{1,0:T(8,128)(2,1)S(1)} %get-tuple-element.59), channel_id=1, source_target_pairs={{8,0},{10,2},{12,4},{14,6},{16,24},{18,26},{20,28},{22,30},{9,1},{... | collective-permute-start | bytes 2457608 | tf_op jit(solution)/shard_map/ppermute | solution.py:414
  213.0 39.3 %collective-permute-start.25 = (bf16[1280,640]{1,0:T(8,128)(2,1)}, bf16[1280,640]{1,0:T(8,128)(2,1)}, u32[]{:S(2)}, u32[]{:S(2)}) collective-permute-start(bf16[1280,640]{1,0:T(8,128)(2,1)} %maximum_select_fusion.1.refs_5_), channel_id=1, source_target_pairs={{0,1},{1,0},{2,3},{3,2},{4,5},{5,4},{6,7},{7,6},{8,9},{9,8},{10,11... | collective-permute-start | bytes 4915208 | tf_op jit(solution)/shard_map/ppermute | solution.py:374
  238.4 14.4 %collective-permute-start.26 = (bf16[1280,640]{1,0:T(8,128)(2,1)}, bf16[1280,640]{1,0:T(8,128)(2,1)}, u32[]{:S(2)}, u32[]{:S(2)}) collective-permute-start(bf16[1280,640]{1,0:T(8,128)(2,1)} %broadcast_select_fusion.1.refs_6_), channel_id=1, source_target_pairs={{0,1},{1,0},{2,3},{3,2},{4,5},{5,4},{6,7},{7,6},{8,9},{9,8},{10,11... | collective-permute-start | bytes 4915208 | tf_op jit(solution)/shard_map/ppermute | solution.py:374
  238.4 14.4 %collective-permute-start.27 = (bf16[1280,640]{1,0:T(8,128)(2,1)}, bf16[1280,640]{1,0:T(8,128)(2,1)}, u32[]{:S(2)}, u32[]{:S(2)}) collective-permute-start(bf16[1280,640]{1,0:T(8,128)(2,1)} %broadcast_select_fusion.refs_7_), channel_id=1, source_target_pairs={{0,1},{1,0},{2,3},{3,2},{4,5},{5,4},{6,7},{7,6},{8,9},{9,8},{10,11... | collective-permute-start | bytes 4915208 | tf_op jit(solution)/shard_map/ppermute | solution.py:374
  239.5 24.0 %collective-permute-start.29 = (bf16[1280,640]{1,0:T(8,128)(2,1)}, bf16[1280,640]{1,0:T(8,128)(2,1)}, u32[]{:S(2)}, u32[]{:S(2)}) collective-permute-start(bf16[1280,640]{1,0:T(8,128)(2,1)} %maximum_select_fusion.2.refs_2_), channel_id=1, source_target_pairs={{0,1},{1,0},{2,3},{3,2},{4,5},{5,4},{6,7},{7,6},{8,9},{9,8},{10,11... | collective-permute-start | bytes 4915208 | tf_op jit(solution)/shard_map/ppermute | solution.py:374
  252.2 24.0 %collective-permute-start.40 = (bf16[640,640]{1,0:T(8,128)(2,1)S(1)}, bf16[640,640]{1,0:T(8,128)(2,1)S(1)}, u32[]{:S(2)}, u32[]{:S(2)}) collective-permute-start(bf16[640,640]{1,0:T(8,128)(2,1)S(1)} %get-tuple-element.58.refs_2_), channel_id=1, source_target_pairs={{0,1},{1,0},{2,3},{3,2},{4,5},{5,4},{6,7},{7,6},{8,9},{9,8},{10,11... | collective-permute-start | bytes 2457608 | tf_op jit(solution)/shard_map/ppermute | solution.py:374
  252.3 20.4 %collective-permute-start.35 = (bf16[640,640]{1,0:T(8,128)(2,1)S(1)}, bf16[640,640]{1,0:T(8,128)(2,1)S(1)}, u32[]{:S(2)}, u32[]{:S(2)}) collective-permute-start(bf16[640,640]{1,0:T(8,128)(2,1)S(1)} %broadcast_select_fusion.7.refs_2_), channel_id=1, source_target_pairs={{0,1},{1,0},{2,3},{3,2},{4,5},{5,4},{6,7},{7,6},{8,9},{9,8},{10,11... | collective-permute-start | bytes 2457608 | tf_op jit(solution)/shard_map/ppermute | solution.py:374
  269.2 38.6 %collective-permute-start.30 = (bf16[256,1280]{1,0:T(8,128)(2,1)S(1)}, bf16[256,1280]{1,0:T(8,128)(2,1)S(1)}, u32[]{:S(2)}, u32[]{:S(2)}) collective-permute-start(bf16[256,1280]{1,0:T(8,128)(2,1)S(1)} %get-tuple-element.45), channel_id=1, source_target_pairs={{0,2},{2,0},{4,6},{6,4},{8,10},{10,8},{12,14},{14,12},{16,18},{18,... | collective-permute-start | bytes 1966088 | tf_op jit(solution)/shard_map/ppermute | solution.py:374
  269.6 40.0 %collective-permute-start.31 = (bf16[256,1280]{1,0:T(8,128)(2,1)S(1)}, bf16[256,1280]{1,0:T(8,128)(2,1)S(1)}, u32[]{:S(2)}, u32[]{:S(2)}) collective-permute-start(bf16[256,1280]{1,0:T(8,128)(2,1)S(1)} %get-tuple-element.46), channel_id=1, source_target_pairs={{0,4},{2,6},{4,0},{6,2},{8,12},{10,14},{12,8},{14,10},{16,20},{18,... | collective-permute-start | bytes 1966088 | tf_op jit(solution)/shard_map/ppermute | solution.py:374
  269.6 42.5 %collective-permute-start.32 = (bf16[256,1280]{1,0:T(8,128)(2,1)S(1)}, bf16[256,1280]{1,0:T(8,128)(2,1)S(1)}, u32[]{:S(2)}, u32[]{:S(2)}) collective-permute-start(bf16[256,1280]{1,0:T(8,128)(2,1)S(1)} %get-tuple-element.47), channel_id=1, source_target_pairs={{0,6},{2,4},{4,2},{6,0},{8,14},{10,12},{12,10},{14,8},{16,22},{18,... | collective-permute-start | bytes 1966088 | tf_op jit(solution)/shard_map/ppermute | solution.py:374
  275.8 31.3 %collective-permute-start.36 = (bf16[256,640]{1,0:T(8,128)(2,1)S(1)}, bf16[256,640]{1,0:T(8,128)(2,1)S(1)}, u32[]{:S(2)}, u32[]{:S(2)}) collective-permute-start(bf16[256,640]{1,0:T(8,128)(2,1)S(1)} %get-tuple-element.49), channel_id=1, source_target_pairs={{0,2},{2,0},{4,6},{6,4},{8,10},{10,8},{12,14},{14,12},{16,18},{18,... | collective-permute-start | bytes 983048 | tf_op jit(solution)/shard_map/ppermute | solution.py:374
  276.2 41.7 %collective-permute-start.37 = (bf16[256,640]{1,0:T(8,128)(2,1)}, bf16[256,640]{1,0:T(8,128)(2,1)}, u32[]{:S(2)}, u32[]{:S(2)}) collective-permute-start(bf16[256,640]{1,0:T(8,128)(2,1)} %get-tuple-element.50), channel_id=1, source_target_pairs={{0,4},{2,6},{4,0},{6,2},{8,12},{10,14},{12,8},{14,10},{16,20},{18,... | collective-permute-start | bytes 983048 | tf_op jit(solution)/shard_map/ppermute | solution.py:374
  307.8 11.9 %collective-permute-start.38 = (bf16[256,640]{1,0:T(8,128)(2,1)}, bf16[256,640]{1,0:T(8,128)(2,1)}, u32[]{:S(2)}, u32[]{:S(2)}) collective-permute-start(bf16[256,640]{1,0:T(8,128)(2,1)} %get-tuple-element.51), channel_id=1, source_target_pairs={{0,6},{2,4},{4,2},{6,0},{8,14},{10,12},{12,10},{14,8},{16,22},{18,... | collective-permute-start | bytes 983048 | tf_op jit(solution)/shard_map/ppermute | solution.py:374
  307.8 17.7 %collective-permute-start.41 = (bf16[256,640]{1,0:T(8,128)(2,1)}, bf16[256,640]{1,0:T(8,128)(2,1)}, u32[]{:S(2)}, u32[]{:S(2)}) collective-permute-start(bf16[256,640]{1,0:T(8,128)(2,1)} %get-tuple-element.53), channel_id=1, source_target_pairs={{0,2},{2,0},{4,6},{6,4},{8,10},{10,8},{12,14},{14,12},{16,18},{18,... | collective-permute-start | bytes 983048 | tf_op jit(solution)/shard_map/ppermute | solution.py:374
  310.4 16.2 %collective-permute-start.42 = (bf16[256,640]{1,0:T(8,128)(2,1)}, bf16[256,640]{1,0:T(8,128)(2,1)}, u32[]{:S(2)}, u32[]{:S(2)}) collective-permute-start(bf16[256,640]{1,0:T(8,128)(2,1)} %get-tuple-element.54), channel_id=1, source_target_pairs={{0,4},{2,6},{4,0},{6,2},{8,12},{10,14},{12,8},{14,10},{16,20},{18,... | collective-permute-start | bytes 983048 | tf_op jit(solution)/shard_map/ppermute | solution.py:374
  313.0 19.1 %collective-permute-start.43 = (bf16[256,640]{1,0:T(8,128)(2,1)}, bf16[256,640]{1,0:T(8,128)(2,1)}, u32[]{:S(2)}, u32[]{:S(2)}) collective-permute-start(bf16[256,640]{1,0:T(8,128)(2,1)} %get-tuple-element.55), channel_id=1, source_target_pairs={{0,6},{2,4},{4,2},{6,0},{8,14},{10,12},{12,10},{14,8},{16,22},{18,... | collective-permute-start | bytes 983048 | tf_op jit(solution)/shard_map/ppermute | solution.py:374
  (29 other events, 121.2 us)

commit v3 on v2

v3 whole, which is shorter than its diff:
```python
import functools
import math

import jax
import jax.numpy as jnp
from jax import lax
from jax.experimental import pallas as pl
from jax.experimental.pallas import tpu as pltpu
from jax.sharding import PartitionSpec as P

HD = 128
PB = 64
PLEN = 512
BPG = 8
PARTNERS = (0, 1, 4, 5)
GROUP = len(PARTNERS)
VMEM_LIMIT = 48 * 1024 * 1024
SHORT = pl.CostEstimate(flops=1024, bytes_accessed=1024, transcendentals=0)


EPSILON = 1e-06
THETA = 1000000.0


def rotation(positions):
    half_width = HD // 2
    exponent = jnp.arange(half_width, dtype=jnp.float32) * (2.0 / HD)
    inv_freq = jnp.power(jnp.float32(THETA), -exponent)
    angles = positions.astype(jnp.float32)[:, None] * inv_freq[None, :]
    cosine, sine = jnp.cos(angles), jnp.sin(angles)
    return jnp.concatenate([cosine, cosine], axis=1), jnp.concatenate([-sine, sine], axis=1)


def slot_layout(row_lengths, tok_count):
    req_ends = jnp.cumsum(row_lengths)
    starts = req_ends - row_lengths
    slot_ids = jnp.arange(tok_count, dtype=jnp.int32)
    request = jnp.sum((slot_ids[:, None] >= req_ends[None, :]).astype(jnp.int32), axis=1)
    member = request[:, None] == jnp.arange(row_lengths.shape[0], dtype=jnp.int32)[None, :]
    offset = slot_ids - jnp.sum(jnp.where(member, starts[None, :], 0), axis=1)
    return (request, offset)


def dot_rows(left, right):
    return lax.dot_general(
        left, right, (((1,), (1,)), ((), ())), preferred_element_type=jnp.float32
    )


def attention_kernel(
    start_ref, cos_ref, sin_ref, q_gain, k_gain, q_ref, k_ref, v_ref, pk_ref, pv_ref, out_ref, bias
):
    tok_count = k_ref.shape[1]
    tile = min(256, tok_count)
    scale = math.log2(math.e) / math.sqrt(HD)

    @pl.when(pl.program_id(0) == 0)
    def _():
        keys = lax.broadcasted_iota(jnp.int32, (tok_count, tok_count), 1)
        slots = lax.broadcasted_iota(jnp.int32, (tok_count, tok_count), 0)
        seen = (keys >= start_ref[...]) & (keys <= slots)
        bias[...] = jnp.where(seen, 0.0, -1e30)

    def prepare(values, gain, rows):
        values = values.astype(jnp.float32)
        mean_sq = jnp.mean(values * values, axis=-1, keepdims=True)
        scaled = values * lax.rsqrt(mean_sq + EPSILON) * gain[...]
        turned = scaled * cos_ref[rows, :] + pltpu.roll(scaled, HD // 2, 1) * sin_ref[rows, :]
        return turned.astype(jnp.bfloat16)

    key = prepare(k_ref[0], k_gain, pl.ds(0, tok_count))
    value = v_ref[0]
    pre_key = pk_ref[...].reshape(-1, HD)
    pre_value = pv_ref[...].reshape(-1, HD)
    for head in range(q_ref.shape[1] // HD):
        lanes = pl.ds(head * HD, HD)
        for first in range(0, tok_count, tile):
            rows = pl.ds(first, tile)
            last = first + tile
            query = prepare(q_ref[rows, lanes], q_gain, rows)
            pre_w = jnp.exp2(dot_rows(query, pre_key) * scale)
            suf_w = jnp.exp2(dot_rows(query, key[:last]) * scale + bias[rows, :last])
            total = jnp.sum(pre_w, axis=-1, keepdims=True) + jnp.sum(suf_w, axis=-1, keepdims=True)
            top = jnp.dot(
                pre_w.astype(jnp.bfloat16), pre_value, preferred_element_type=jnp.float32
            ) + jnp.dot(
                suf_w.astype(jnp.bfloat16), value[:last], preferred_element_type=jnp.float32
            )
            out_ref[rows, lanes] = (top / total).astype(out_ref.dtype)


def attention(start, cosine, sine, q_gain, k_gain, q_in, kv_in, chosen, first, count):
    tok_count = q_in.shape[0]
    groups = kv_in.shape[2] // HD
    width = q_in.shape[1] // groups
    blocks = chosen.shape[0]

    def same(rows, columns):
        return pl.BlockSpec((rows, columns), lambda g: (0, 0))

    def suffix(which):
        return pl.BlockSpec((1, tok_count, HD), lambda g: (which, 0, g + first))

    def prefix(which):
        return pl.BlockSpec((blocks, 1, PB, HD), lambda g: (0, which, 0, g + first))

    keys = tok_count + PLEN
    return pl.pallas_call(
        attention_kernel,
        grid=(count,),
        in_specs=[
            same(tok_count, 1),
            same(tok_count, HD),
            same(tok_count, HD),
            same(1, HD),
            same(1, HD),
            pl.BlockSpec((tok_count, width), lambda g: (0, g + first)),
            suffix(0),
            suffix(1),
            prefix(0),
            prefix(1),
        ],
        out_specs=pl.BlockSpec((tok_count, width), lambda g: (0, g)),
        out_shape=jax.ShapeDtypeStruct((tok_count, count * width), jnp.bfloat16),
        scratch_shapes=[pltpu.VMEM((tok_count, tok_count), jnp.float32)],
        compiler_params=pltpu.CompilerParams(vmem_limit_bytes=VMEM_LIMIT),
        cost_estimate=SHORT,
        name="attention",
    )(start, cosine, sine, q_gain, k_gain, q_in, kv_in, kv_in, chosen, chosen)


def project_kernel(core, *refs, n_parts, n_mlp):
    parts, weights, outs = refs[:n_parts], refs[n_parts : 2 * n_parts], refs[2 * n_parts :]
    rows = outs[0].shape[0]
    for k in range(n_mlp - 1, -1, -1):
        part = pl.ds(pl.multiple_of((core[0] ^ k) * rows, rows), rows)
        total = 0.0
        for x, w in zip(parts, weights):
            total = total + jnp.dot(x[part, :], w[...], preferred_element_type=jnp.float32)
        outs[k][...] = total.astype(outs[k].dtype)


def project(core, parts, w_out, n_mlp):
    tok_count, depth = parts[0].shape
    columns = w_out.shape[1]
    rows, tile = tok_count // n_mlp, 512
    n_parts = len(parts)
    return pl.pallas_call(
        functools.partial(project_kernel, n_parts=n_parts, n_mlp=n_mlp),
        grid_spec=pltpu.PrefetchScalarGridSpec(
            num_scalar_prefetch=1,
            grid=(columns // tile,),
            in_specs=[pl.BlockSpec((tok_count, depth), lambda n, core: (0, 0))] * n_parts
            + [
                pl.BlockSpec((depth, tile), functools.partial(lambda i, n, core: (i, n), i))
                for i in range(n_parts)
            ],
            out_specs=[pl.BlockSpec((rows, tile), lambda n, core: (0, n))] * n_mlp,
        ),
        out_shape=[
            jax.ShapeDtypeStruct((rows, columns), jnp.bfloat16 if k else jnp.float32)
            for k in range(n_mlp)
        ],
        compiler_params=pltpu.CompilerParams(vmem_limit_bytes=VMEM_LIMIT),
        cost_estimate=SHORT,
        name="project",
    )(core, *parts, *[w_out] * n_parts)


def normalize_kernel(hidden, gain, own, *refs):
    parts, resid_ref, normed_ref = refs[:-2], refs[-2], refs[-1]
    total = hidden[...].astype(jnp.float32) + own[...]
    for part in parts:
        total = total + part[...].astype(jnp.float32)
    resid = total.astype(resid_ref.dtype)
    resid_ref[...] = resid
    values = resid.astype(jnp.float32)
    mean_sq = jnp.mean(values * values, axis=-1, keepdims=True)
    normed = values * lax.rsqrt(mean_sq + EPSILON) * gain[...]
    normed_ref[...] = normed.astype(normed_ref.dtype)


def normalize(hidden, gain, own, parts):
    rows, columns = hidden.shape
    tile = min(64, rows)
    spec = pl.BlockSpec((tile, columns), lambda i: (i, 0))
    return pl.pallas_call(
        normalize_kernel,
        grid=(rows // tile,),
        in_specs=[spec, pl.BlockSpec((1, columns), lambda i: (0, 0)), spec] + [spec] * len(parts),
        out_specs=[spec, spec],
        out_shape=[jax.ShapeDtypeStruct(hidden.shape, hidden.dtype)] * 2,
        compiler_params=pltpu.CompilerParams(vmem_limit_bytes=VMEM_LIMIT),
        cost_estimate=SHORT,
        name="normalize",
    )(hidden, gain, own, *parts)


def move_kernel(scalar, *refs, n_in, plan):
    sems = refs[-1]
    copies = [
        pltpu.make_async_copy(src, dst, sems.at[i])
        for i, (src, dst) in enumerate(plan(scalar[0], refs[:n_in], refs[n_in:-1]))
    ]
    for copy in copies:
        copy.start()
    for copy in copies:
        copy.wait()


def move(scalar, arrays, shapes, plan, n_copies, name):
    anywhere = pl.BlockSpec(memory_space=pl.ANY)
    return pl.pallas_call(
        functools.partial(move_kernel, n_in=len(arrays), plan=plan),
        in_specs=[pl.BlockSpec(memory_space=pltpu.SMEM)] + [anywhere] * len(arrays),
        out_specs=[pl.BlockSpec(memory_space=pltpu.VMEM)] * len(shapes),
        out_shape=[jax.ShapeDtypeStruct(shape, jnp.bfloat16) for shape in shapes],
        scratch_shapes=[pltpu.SemaphoreType.DMA((n_copies,))],
        compiler_params=pltpu.CompilerParams(vmem_limit_bytes=VMEM_LIMIT),
        cost_estimate=SHORT,
        name=name,
    )(scalar, *arrays)


def cut(seat, blocks):
    rows, columns = blocks[0].shape
    width = columns // GROUP
    if width % 128:
        return [
            jnp.stack(
                [lax.dynamic_slice_in_dim(x, (seat[0] ^ j) * width, width, 1) for x in blocks]
            )
            for j in range(GROUP)
        ]

    def plan(seat, sources, targets):
        return [
            (source.at[:, pl.ds(pl.multiple_of((seat ^ j) * width, 128), width)], targets[j].at[m])
            for j in range(GROUP)
            for m, source in enumerate(sources)
        ]

    shapes = [(len(blocks), rows, width)] * GROUP
    return move(seat, blocks, shapes, plan, GROUP * len(blocks), "cut")


def merge(seat, parts, groups):
    _, rows, width = parts[0].shape
    if width % 128:
        whole = jnp.stack(parts, axis=1)
        return [jnp.stack([whole[m] for m in group]) for group in groups]

    def plan(_, sources, targets):
        return [
            (source.at[m], target.at[i, j])
            for target, group in zip(targets, groups)
            for i, m in enumerate(group)
            for j, source in enumerate(sources)
        ]

    shapes = [(len(group), GROUP, rows, width) for group in groups]
    return move(seat, parts, shapes, plan, GROUP * sum(map(len, groups)), "merge")


def collect(seat, entries):
    shape = entries[0][0].shape[1:]
    if shape[-1] % 128:
        return jnp.stack([array[m] for array, m in entries])

    def plan(_, sources, targets):
        return [
            (source.at[m], targets[0].at[i])
            for i, (source, (_, m)) in enumerate(zip(sources, entries))
        ]

    arrays = [array for array, _ in entries]
    return move(seat, arrays, [(len(entries), *shape)], plan, len(entries), "collect")[0]


def weight_copies(me, refs, keys, target, mask, sems):
    copies = []
    for i, ref in enumerate(refs):
        part, entry = divmod(i, len(keys))
        rows, width = ref.shape[-2:]
        packed = len(target.shape) == 2
        lanes = pl.ds(part * width, width)
        if keys[entry] is None:
            place = target.at[:, lanes] if packed else target.at[part]
            copies.append(pltpu.make_async_copy(ref.at[0], place, sems.at[len(copies)]))
            continue
        for k, key in enumerate(keys[entry]):
            for j, partner in enumerate(PARTNERS):
                source = (me ^ (key ^ partner)) & mask
                here = pl.ds(pl.multiple_of(source * rows, 8), rows)
                place = target.at[here, lanes] if packed else target.at[part, here]
                copies.append(pltpu.make_async_copy(ref.at[k, j], place, sems.at[len(copies)]))
    return copies


def expand_kernel(me, *refs, n_parts, keys, second):
    n_weights = n_parts * len(keys)
    x_refs, refs = refs[: GROUP + 1], refs[GROUP + 1 :]
    w_refs, refs = refs[:n_weights], refs[n_weights:]
    before, refs = (refs[:n_parts], refs[n_parts:]) if second else ((), refs)
    outs, (x_all, weight, x_sems, w_sems) = refs[:n_parts], refs[n_parts:]
    width = outs[0].shape[1]
    rows, depth = x_refs[0].shape
    packed = len(weight.shape) == 2
    places = [x_all.at[i] for i in range(GROUP - 1)]
    places += [x_all.at[GROUP - 1, pl.ds(i * rows // 2, rows // 2)] for i in range(2)]
    copies = weight_copies(me[0], w_refs, keys, weight, -1, w_sems)
    copies += [
        pltpu.make_async_copy(x_ref, place, x_sems.at[i])
        for i, (x_ref, place) in enumerate(zip(x_refs, places))
    ]
    for copy in copies:
        copy.start()
    for copy in copies:
        copy.wait()

    def step(i, carry):
        x = x_all[i]
        lines = pl.ds(pl.multiple_of(i * rows, rows), rows)
        if packed:
            whole = jnp.dot(x, weight[...], preferred_element_type=jnp.float32)
        for part in range(n_parts):
            if packed:
                total = whole[:, part * width : (part + 1) * width]
            else:
                total = jnp.dot(x, weight[part], preferred_element_type=jnp.float32)
            if second:
                total = total * before[part][lines, :]
            else:
                total = total / (1.0 + jnp.exp(-total))
            outs[part][lines, :] = total.astype(outs[part].dtype)
        return carry

    lax.fori_loop(0, GROUP, step, 0)


def expand(me, normed, keys, weights, before=()):
    rows, depth = normed[0].shape
    n_parts = len(weights)
    width = weights[0][0].shape[-1]
    total = rows * GROUP
    n_copies = n_parts * GROUP * sum(len(entry or (0,)) for entry in keys)
    shape = (depth, n_parts * width) if width % 128 == 0 else (n_parts, depth, width)
    kind = jnp.bfloat16 if before else jnp.float32
    vmem, anywhere = pl.BlockSpec(memory_space=pltpu.VMEM), pl.BlockSpec(memory_space=pl.ANY)
    return pl.pallas_call(
        functools.partial(
            expand_kernel, n_parts=n_parts, keys=keys, second=bool(before)
        ),
        in_specs=[pl.BlockSpec(memory_space=pltpu.SMEM)]
        + [anywhere] * (len(normed) + n_parts * len(keys))
        + [vmem] * len(before),
        out_specs=[vmem] * n_parts,
        out_shape=[jax.ShapeDtypeStruct((total, width), kind)] * n_parts,
        scratch_shapes=[
            pltpu.VMEM((GROUP, rows, depth), jnp.bfloat16),
            pltpu.VMEM(shape, jnp.bfloat16),
            pltpu.SemaphoreType.DMA((len(normed),)),
            pltpu.SemaphoreType.DMA((n_copies,)),
        ],
        compiler_params=pltpu.CompilerParams(vmem_limit_bytes=VMEM_LIMIT),
        cost_estimate=SHORT,
        name="up" if before else "gate",
    )(me, *normed, *[array for part in weights for array in part], *before)


def down_kernel(me, *refs, n_parts, keys, mask):
    n_weights = n_parts * len(keys)
    act_refs, w_refs = refs[:n_parts], refs[n_parts : n_parts + n_weights]
    own, to_x, to_y, keep_x, keep_y, acts, weight, a_sems, w_sems = refs[n_parts + n_weights :]
    width = act_refs[0].shape[1]
    rows = own.shape[0]
    half = rows // 2
    packed = len(acts.shape) == 2
    copies = weight_copies(me[0], w_refs, keys, weight, mask, w_sems)
    for i in range(n_parts):
        place = acts.at[:, pl.ds(i * width, width)] if packed else acts.at[i]
        copies.append(pltpu.make_async_copy(act_refs[i], place, a_sems.at[i]))
    for copy in copies:
        copy.start()
    for copy in copies:
        copy.wait()

    def sums(block):
        here = pl.ds(block * rows, rows)
        if packed:
            return dot_rows(acts[here, :], weight[...])
        return sum(dot_rows(acts[i, here, :], weight[i]) for i in range(n_parts))

    total = sums(3).astype(jnp.bfloat16)
    to_x[half:, :] = total[:half]
    to_y[half:, :] = total[half:]
    total = sums(1)
    to_x[:half, :] = total[:half].astype(jnp.bfloat16)
    keep_x[...] = total[half:]
    total = sums(2)
    to_y[:half, :] = total[half:].astype(jnp.bfloat16)
    keep_y[...] = total[:half]
    own[...] = sums(0)


def down(me, acts, keys, weights, mask):
    total, width = acts[0].shape
    n_parts = len(acts)
    columns = sum(math.prod(array.shape[:-1]) for array in weights[0])
    rows = total // GROUP
    if width % 128 == 0:
        shapes = [(total, n_parts * width), (columns, n_parts * width)]
    else:
        shapes = [(n_parts, total, width), (n_parts, columns, width)]
    outs = [(rows, jnp.float32), (rows, jnp.bfloat16), (rows, jnp.bfloat16)]
    outs += [(rows // 2, jnp.float32)] * 2
    return pl.pallas_call(
        functools.partial(down_kernel, n_parts=n_parts, keys=keys, mask=mask),
        out_shape=[jax.ShapeDtypeStruct((length, columns), dtype) for length, dtype in outs],
        in_specs=[pl.BlockSpec(memory_space=pltpu.SMEM)]
        + [pl.BlockSpec(memory_space=pl.ANY)] * (n_parts + n_parts * len(keys)),
        out_specs=[pl.BlockSpec(memory_space=pltpu.VMEM)] * 5,
        scratch_shapes=[pltpu.VMEM(shape, jnp.bfloat16) for shape in shapes]
        + [
            pltpu.SemaphoreType.DMA((n_parts,)),
            pltpu.SemaphoreType.DMA((n_parts * GROUP * sum(len(entry or (0,)) for entry in keys),)),
        ],
        compiler_params=pltpu.CompilerParams(vmem_limit_bytes=VMEM_LIMIT),
        cost_estimate=SHORT,
        name="down",
    )(me, *acts, *[array for part in weights for array in part])


def finish_kernel(upper, resid, *refs):
    out_ref = refs[-1]
    half, width = resid.shape[0] // 2, resid.shape[1] // 2
    for piece in range(2):
        own, from_x, from_y, late_x, late_y = refs[5 * piece : 5 * piece + 5]
        here = pl.ds(pl.multiple_of((upper[0] ^ piece) * width, 128), width)
        for rows, first, late in (
            (pl.ds(0, half), from_x, late_y),
            (pl.ds(half, half), from_y, late_x),
        ):
            total = resid[rows, here].astype(jnp.float32) + own[rows, :]
            total = total + first[:half, :].astype(jnp.float32) + late[...].astype(jnp.float32)
            out_ref[rows, here] = total.astype(out_ref.dtype)


def finish(upper, resid, pieces):
    vmem = pl.BlockSpec(memory_space=pltpu.VMEM)
    return pl.pallas_call(
        finish_kernel,
        in_specs=[pl.BlockSpec(memory_space=pltpu.SMEM)] + [vmem] * 11,
        out_specs=vmem,
        out_shape=jax.ShapeDtypeStruct(resid.shape, resid.dtype),
        compiler_params=pltpu.CompilerParams(vmem_limit_bytes=VMEM_LIMIT),
        cost_estimate=SHORT,
        name="finish",
    )(upper, resid, *[part for piece in pieces for part in piece])


def swap(value, axis, size, bits):
    return lax.ppermute(value, axis, [(i, i ^ bits) for i in range(size)])


def per_device(
    q_in,
    kv_in,
    prefix_kv,
    hidden_in,
    q_gain,
    k_gain,
    post_gain,
    w_out,
    w_gate,
    w_up,
    w_down_t,
    lengths,
    row_group,
    owner_block,
):
    n_req, n_mlp = lax.axis_size("req"), lax.axis_size("mlp")
    me, core = lax.axis_index("req"), lax.axis_index("mlp")
    tok_count = q_in.shape[0]
    local_groups = kv_in.shape[2] // HD

    def tie(tree):
        leaves, shape = jax.tree.flatten(tree)
        fixed = [isinstance(leaf, int) for leaf in leaves]
        held = iter(lax.optimization_barrier([x for x, f in zip(leaves, fixed) if not f]))
        return jax.tree.unflatten(shape, [x if f else next(held) for x, f in zip(leaves, fixed)])

    top = n_req // 2
    others = [1 << i for i in range(n_req.bit_length()) if 1 << i < n_req and 1 << i not in PARTNERS]
    others = others[::-1]
    seat = ((me & 1) + (me >> 2 & 1) * 2)[None]
    place, upper = me[None], (me // top)[None]

    def req(value, key):
        return swap(value, "req", n_req, key)

    def cores(part):
        return [part] + [swap(part, "mlp", n_mlp, k) for k in range(1, n_mlp)]

    def trade(parts):
        return [parts[0]] + [req(part, key) for part, key in zip(parts[1:], PARTNERS[1:])]

    def relay(entry, key):
        array, m = entry
        return (req(array if array.shape[0] == 1 else array[m : m + 1], key), 0)

    def complete(entries):
        for key in others[1:]:
            for held_key in list(entries):
                if held_key ^ key not in entries:
                    entries[held_key ^ key] = relay(entries[held_key], key)
        return entries

    def share(entries, *keys):
        return [(keys, cores(collect(seat, [entries[key] for key in keys])))]

    def gather(shares, count):
        keys, parts = [keys for keys, _ in shares], list(zip(*[parts for _, parts in shares]))
        if parts[0][0].shape[2] % 16 == 0:
            return keys, [list(part) for part in parts]
        spots = [(key ^ partner) % count for entry in keys for key in entry for partner in PARTNERS]
        spots = jnp.asarray([spots.index(i) for i in range(count)])
        spots = spots[(me ^ jnp.arange(count)) % count]
        ordered = []
        for part in parts:
            whole = jnp.concatenate(part, axis=0)
            whole = whole.reshape(count, *whole.shape[2:])
            ordered.append([jnp.take(whole, spots, axis=0).reshape(1, -1, whole.shape[-1])])
        return [None], ordered

    planes = [prefix_kv] + [req(prefix_kv, 4 * k) for k in range(1, n_req // 4)]
    held = jnp.stack(planes)
    slot = jnp.argsort(owner_block) ^ me
    spot = slot // 4 + slot % 4 * (n_req // 4)
    picked = lax.dynamic_slice_in_dim(spot, row_group[0] * BPG, BPG, 0)

    parts = list(cut(seat, [w_gate, w_up]))
    held, parts[3] = tie((held, parts[3]))
    open_w, gate_own, up_own = merge(seat, trade(parts), [(0, 1), (0,), (1,)])
    last = others[-1]
    held = jnp.stack([held] + [req(held, k) for k in range(1, 4)])
    held = held.reshape(n_req, 2, PB, local_groups * HD)
    chosen = jnp.take(held, picked, axis=0)
    gate_top, open_last = req(gate_own, top), req(open_w, last)

    _, offset = slot_layout(lengths[0], tok_count)
    cosine, sine = rotation(offset + PLEN)
    start = (jnp.arange(tok_count, dtype=jnp.int32) - offset)[:, None]
    gains = q_gain[None], k_gain[None]

    chosen, cosine, sine, start = tie((chosen, cosine, sine, start))
    attn = attention(start, cosine, sine, *gains, q_in, kv_in, chosen, 0, local_groups)
    attn, gate_top, up_own, w_down_t = tie((attn, gate_top, up_own, w_down_t))
    down_parts = trade(cut(seat, [w_down_t]))

    own_rows = hidden_in.shape[0]
    sums = project(core[None], [attn], w_out, n_mlp)
    parts = [swap(sums[k], "mlp", n_mlp, k) for k in range(1, n_mlp)]
    resid, own_normed = normalize(hidden_in, post_gain[None], sums[0], parts)

    own_normed, open_last, down_parts, up_own = tie((own_normed, open_last, down_parts, up_own))
    gate_w = {0: (gate_own, 0), last: (open_last, 0), top: (gate_top, 0)}

    half = own_rows // 2
    key_x, key_y = PARTNERS[1:3]
    next_x, next_y = req(own_normed, key_x), req(own_normed, key_y)
    up_top = req(up_own, top)
    (down_own,) = merge(seat, down_parts, [(0,)])
    gate_all = share(gate_w, *gate_w)
    gate_rest = {key: v for key, v in complete(dict(gate_w)).items() if key not in gate_w}
    next_x, next_y, up_top, down_own, gate_all, gate_rest = tie(
        (next_x, next_y, up_top, down_own, gate_all, gate_rest)
    )
    diag = [req(next_x[:half], key_y), req(next_y[half:], key_x)]
    up_w = {0: (up_own, 0), last: (open_last, 1), top: (up_top, 0)}
    up_all = share(up_w, *up_w)
    up_rest = {key: v for key, v in complete(dict(up_w)).items() if key not in up_w}
    gate_all = gate_all + [([key], cores(v[0])) for key, v in gate_rest.items()]
    diag, up_all, up_rest, gate_all, down_own = tie((diag, up_all, up_rest, gate_all, down_own))
    normed = [own_normed, next_x, next_y] + diag

    opened = expand(place, normed, *gather(gate_all, n_req))
    up_all = up_all + [([key], cores(v[0])) for key, v in up_rest.items()]
    down_top, down_last = req(down_own, top), req(down_own, last)
    near = [([0], cores(down_own))]
    opened, up_all, near = tie((opened, up_all, near))
    acts = expand(place, normed, *gather(up_all, n_req), opened)
    acts, down_top, down_last = tie((acts, down_top, down_last))
    down_w = complete({0: (down_own, 0), last: (down_last, 0), top: (down_top, 0)})
    near = near + [([key], cores(v[0])) for key, v in down_w.items() if key and not key & top]
    far = [([key], v[0]) for key, v in down_w.items() if key & top]

    sums, parts = [], down(place, acts, *gather(near, top), top - 1)
    for piece in range(2):
        own, to_x, to_y, keep_x, keep_y = parts
        from_x, from_y = req(to_x, key_x), req(to_y, key_y)
        if piece == 0:
            far, from_x, from_y = tie((far, from_x, from_y))
            far = [(keys, cores(array)) for keys, array in far]
            parts = down(place, acts, *gather(far, top), top - 1)
        late_y = keep_y + from_x[half:].astype(jnp.float32)
        late_x = keep_x + from_y[half:].astype(jnp.float32)
        late_y = req(late_y.astype(jnp.bfloat16), key_y)
        late_x = req(late_x.astype(jnp.bfloat16), key_x)
        sums.append([own, from_x, from_y, late_x, late_y])
    return finish(upper, resid, sums)


def solution(mesh):
    in_specs = (
        P("req", "mlp"),
        P(None, "req", "mlp"),
        P(None, "req", "mlp"),
        P(("req", "mlp"), None),
        P(),
        P(),
        P(),
        P("mlp", None),
        P("req", "mlp"),
        P("req", "mlp"),
        P("req", "mlp"),
        P("req", None),
        P("req"),
        P(),
    )
    out_specs = P(("req", "mlp"), None)
    return jax.shard_map(
        per_device, mesh=mesh, in_specs=in_specs, out_specs=out_specs, check_vma=False
    )
```

time: 335 us -> 291 us (0.87)
  the two profiles are of different devices: /device:TPU:12 before, /device:TPU:0 now
where the time goes in v3:
time: 291 us; the launch traced here: 290 us
  waiting for transfers between devices  138 us (47%)
  Pallas kernels  79.1 us (27%)
  starting transfers between devices  41.3 us (14%)
  local copies, waits for them, and re-layouts  17.1 us (6%)
  other arithmetic  13.3 us (5%)
    ppermute x41, waiting for transfers between devices, swap(): return lax.ppermute(value, axis, [(i, i ^ bits) for i in range(size)])  138 us
    ppermute x41, starting transfers between devices, swap(): return lax.ppermute(value, axis, [(i, i ^ bits) for i in range(size)])  41.3 us
    pallas_call x2, Pallas kernels, expand(): pl.pallas_call(functools.partial(expand_kernel, n_parts=n_parts, keys=key...  26.8 us
    pallas_call x1, Pallas kernels, attention(): pl.pallas_call(attention_kernel, grid=(count,), in_specs=[same(tok_count,...  14.6 us
    pallas_call x2, Pallas kernels, down(): pl.pallas_call(functools.partial(down_kernel, n_parts=n_parts, keys=keys,...  13.7 us
    unnamed x50, local copies, waits for them, and re-layouts  13.6 us
    pallas_call x1, Pallas kernels, project(): pl.pallas_call(functools.partial(project_kernel, n_parts=n_parts, n_mlp=n...  8.87 us
    pallas_call x6, Pallas kernels, move(): pl.pallas_call(functools.partial(move_kernel, n_in=len(arrays), plan=plan...  8.48 us
  transfers between devices with their start and end apart: 41, of which 24 were waited for; matrix products, arithmetic and copies ran while one was open for 6% of the time, Pallas kernels for 23%

profile of v3, /device:TPU:0, one launch (start us, length us, event | category | flops | bytes accessed | tf_op | source)
XLA Modules:
  0.0 290.3 jit_solution(11762160695590836980)
XLA Ops:
  0.0 3.0 %collective-permute-start = (bf16[2,64,512]{2,1,0:T(8,128)(2,1)}, bf16[2,64,512]{2,1,0:T(8,128)(2,1)S(1)}, u32[]{:S(2)}, u32[]{:S(2)}) collective-permute-start(bf16[2,64,512]{2,1,0:T(8,128)(2,1)} %param.16), channel_id=1, source_target_pairs={{0,8},{2,10},{4,12},{6,14},{8,0},{10,2},{12,4},{14,6},{16,24},{18,... | collective-permute-start | bytes 393224 | tf_op jit(solution)/shard_map/ppermute | solution.py:463
  3.0 2.6 collective-permute-start.1
  8.2 1.8 collective-permute-start.6
  12.3 1.9 sort.17
  14.2 2.0 collective-permute-done.1
  17.2 3.0 %collective-permute-start.8 = (bf16[2,160,640]{2,1,0:T(8,128)(2,1)S(1)}, bf16[2,160,640]{2,1,0:T(8,128)(2,1)S(1)}, u32[]{:S(2)}, u32[]{:S(2)}) collective-permute-start(bf16[2,160,640]{2,1,0:T(8,128)(2,1)S(1)} %get-tuple-element.95), channel_id=1, source_target_pairs={{0,10},{2,8},{4,14},{6,12},{8,2},{10,0},{12,6},{14,4},{16,26},{18,... | collective-permute-start | bytes 1228808 | tf_op jit(solution)/shard_map/ppermute | solution.py:463
  21.1 1.6 collective-permute-start.4
  23.2 1.5 collective-permute-start.3
  25.6 7.0 %collective-permute-done.8.refs_3_ = bf16[2,160,640]{2,1,0:T(8,128)(2,1)S(1)} collective-permute-done((bf16[2,160,640]{2,1,0:T(8,128)(2,1)S(1)}, bf16[2,160,640]{2,1,0:T(8,128)(2,1)S(1)}, u32[]{:S(2)}, u32[]{:S(2)}) %collective-permute-start.8) | collective-permute-done | bytes 409632 | tf_op jit(solution)/shard_map/ppermute | solution.py:463
  32.5 5.2 %merge.2 = (bf16[2,4,160,640]{3,2,1,0:T(8,128)(2,1)S(1)}, bf16[1,4,160,640]{3,2,1,0:T(8,128)(2,1)}, bf16[1,4,160,640]{3,2,1,0:T(8,128)(2,1)S(1)}) custom-call(s32[1]{0:T(128)} %bitcast.7.scalar, bf16[2,160,640]{2,1,0:T(8,128)(2,1)S(1)} %get-tuple-element.92.refs_0_, bf16[2,160,640]{2,1,0:T(8,128)(2,1)S(1)} %collective-permute-done.6.refs_1_, ...), custom_call_target="tpu_custom_call" | custom-call | flops 1024 | bytes 1024 | tf_op jit(solution)/shard_map/merge/pallas_call | solution.py:213
  41.4 1.6 collective-permute-start.11
  43.0 2.5 collective-permute-done.4
  45.5 8.8 %collective-permute-done.3 = bf16[4,2,64,512]{3,2,1,0:T(8,128)(2,1)} collective-permute-done((bf16[4,2,64,512]{3,2,1,0:T(8,128)(2,1)S(1)}, bf16[4,2,64,512]{3,2,1,0:T(8,128)(2,1)}, u32[]{:S(2)}, u32[]{:S(2)}) %collective-permute-start.3) | collective-permute-done | bytes 524320 | tf_op jit(solution)/shard_map/ppermute | solution.py:463
  54.3 3.0 %pad_maximum_fusion = bf16[4,4,2,64,512]{4,3,2,1,0:T(8,128)(2,1)} fusion(bf16[1,4,2,64,512]{4,3,2,1,0:T(8,128)(2,1)} %bitcast.11, bf16[1,4,2,64,512]{4,3,2,1,0:T(8,128)(2,1)} %bitcast.10, bf16[1,4,2,64,512]{4,3,2,1,0:T(8,128)(2,1)} %bitcast.9, bf16[1,4,2,64,512]{4,3,2,1,0:T(8,128)(2,1)S(1)} %bitcast.28), kind=kLoop, calls=%fused_computation.1 | loop fusion | flops 3145728 | bytes 4194304 | tf_op jit(solution)/shard_map/stack | solution.py:546
  57.3 3.3 %gather_fusion = bf16[8,2,64,512]{3,2,1,0:T(8,128)(2,1)} fusion(bf16[16,2,64,512]{3,2,1,0:T(8,128)(2,1)} %bitcast.27, s32[1024]{0:T(1024)S(1)} %pad_clamp_fusion), kind=kCustom, calls=%fused_computation | custom fusion | bytes 2097184 | tf_op jit(solution)/shard_map/jit(_take)/gather | solution.py:548
  62.0 14.6 %attention.1.refs_0_ = bf16[512,2048]{1,0:T(8,128)(2,1)S(1)} custom-call(s32[512,1]{1,0:T(8,128)S(1)} %subtract_subtract_fusion.start_ref, f32[512,128]{1,0:T(8,128)S(1)} %get-tuple-element.89.cos_ref, f32[512,128]{1,0:T(8,128)S(1)} %get-tuple-element.90.sin_ref, f32[1,128]{1,0:T(1,128)S(1)} %bitcast.25, f32[1,128]{1,0:T(1,128)S(1)} %bitcast.26, ...), custom_call_target="tpu_custom_call" | custom-call | flops 1024 | bytes 1024 | tf_op jit(solution)/shard_map/attention/pallas_call | solution.py:108
  77.6 8.9 %project.1 = (f32[256,2560]{1,0:T(8,128)S(1)}, bf16[256,2560]{1,0:T(8,128)(2,1)S(1)}) custom-call(s32[1]{0:T(128)} %bitcast.1.core, bf16[512,2048]{1,0:T(8,128)(2,1)S(1)} %attention.1.refs_0_, bf16[2048,2560]{1,0:T(8,128)(2,1)} %refs_1_.3), custom_call_target="tpu_custom_call" | custom-call | flops 1024 | bytes 1024 | tf_op jit(solution)/shard_map/project/pallas_call | solution.py:148
  86.5 1.5 copy-done.7
  89.6 2.1 collective-permute-start.14
  91.7 3.1 %normalize.1 = (bf16[256,2560]{1,0:T(8,128)(2,1)S(1)}, bf16[256,2560]{1,0:T(8,128)(2,1)S(1)}) custom-call(bf16[256,2560]{1,0:T(8,128)(2,1)S(1)} %copy-done.10, f32[1,2560]{1,0:T(1,128)S(1)} %broadcast_in_dim.56.gain, f32[256,2560]{1,0:T(8,128)} %copy-done.7, bf16[256,2560]{1,0:T(8,128)(2,1)S(1)} %collective-permute-done.10.refs_0_), custom_call_target="tpu_custom_call" | custom-call | flops 1024 | bytes 1024 | tf_op jit(solution)/shard_map/normalize/pallas_call | solution.py:187
  95.9 1.6 collective-permute-done.13.refs_2_
  97.5 3.8 %collective-permute-done.14.refs_3_ = bf16[1,160,640]{2,1,0:T(8,128)(2,1)S(1)} collective-permute-done((bf16[1,160,640]{2,1,0:T(8,128)(2,1)S(1)}, bf16[1,160,640]{2,1,0:T(8,128)(2,1)S(1)}, u32[]{:S(2)}, u32[]{:S(2)}) %collective-permute-start.14) | collective-permute-done | bytes 204832 | tf_op jit(solution)/shard_map/ppermute | solution.py:463
  101.3 1.5 collect.2.refs_5_
  102.9 1.5 collective-permute-start.15
  104.6 1.5 collective-permute-start.19
  106.1 2.3 collective-permute-start.17
  109.5 15.3 %collective-permute-done.19.refs_6_ = bf16[1,4,160,640]{3,2,1,0:T(8,128)(2,1)S(1)} collective-permute-done((bf16[1,4,160,640]{3,2,1,0:T(8,128)(2,1)}, bf16[1,4,160,640]{3,2,1,0:T(8,128)(2,1)S(1)}, u32[]{:S(2)}, u32[]{:S(2)}) %collective-permute-start.19) | collective-permute-done | bytes 819232 | tf_op jit(solution)/shard_map/ppermute | solution.py:463
  124.9 25.7 %collective-permute-done.17.refs_2_ = bf16[1,4,160,640]{3,2,1,0:T(8,128)(2,1)S(1)} collective-permute-done((bf16[1,4,160,640]{3,2,1,0:T(8,128)(2,1)S(1)}, bf16[1,4,160,640]{3,2,1,0:T(8,128)(2,1)S(1)}, u32[]{:S(2)}, u32[]{:S(2)}) %collective-permute-start.17) | collective-permute-done | bytes 819232 | tf_op jit(solution)/shard_map/ppermute | solution.py:463
  150.5 2.2 collective-permute-done.16.refs_2_
  153.2 1.6 collective-permute-start.23
  156.8 15.2 %collective-permute-done.20.refs_3_ = bf16[128,2560]{1,0:T(8,128)(2,1)S(1)} collective-permute-done((bf16[128,2560]{1,0:T(8,128)(2,1)S(1)}, bf16[128,2560]{1,0:T(8,128)(2,1)S(1)}, u32[]{:S(2)}, u32[]{:S(2)}) %collective-permute-start.20) | collective-permute-done | bytes 655392 | tf_op jit(solution)/shard_map/ppermute | solution.py:463
  175.6 1.5 collective-permute-start.28
  177.1 12.8 %gate.1 = (f32[1024,640]{1,0:T(8,128)}, f32[1024,640]{1,0:T(8,128)}) custom-call(s32[1]{0:T(128)} %bitcast.20.me, bf16[256,2560]{1,0:T(8,128)(2,1)S(1)} %get-tuple-element.110.refs_0_, bf16[256,2560]{1,0:T(8,128)(2,1)S(1)} %collective-permute-done.15.refs_1_, bf16[256,2560]{1,0:T(8,128)(2,1)} %copy-done.23, ...), custom_call_target="tpu_custom_call" | custom-call | flops 1024 | bytes 1024 | tf_op jit(solution)/shard_map/gate/pallas_call | solution.py:350
  193.1 14.0 %up.1 = (bf16[1024,640]{1,0:T(8,128)(2,1)S(1)}, bf16[1024,640]{1,0:T(8,128)(2,1)S(1)}) custom-call(s32[1]{0:T(128)} %bitcast.20.me, bf16[256,2560]{1,0:T(8,128)(2,1)} %copy-done.3, bf16[256,2560]{1,0:T(8,128)(2,1)} %copy-done.2, bf16[256,2560]{1,0:T(8,128)(2,1)} %copy-done.23, bf16[128,2560]{1,0:T(8,128)(2,1)S(1)} %collective-permute-done.20.refs_3_, ...), custom_call_target="tpu_custom_call" | custom-call | flops 1024 | bytes 1024 | tf_op jit(solution)/shard_map/up/pallas_call | solution.py:350
  209.3 3.8 %collective-permute-done.27.refs_2_ = bf16[1,4,160,640]{3,2,1,0:T(8,128)(2,1)S(1)} collective-permute-done((bf16[1,4,160,640]{3,2,1,0:T(8,128)(2,1)S(1)}, bf16[1,4,160,640]{3,2,1,0:T(8,128)(2,1)S(1)}, u32[]{:S(2)}, u32[]{:S(2)}) %collective-permute-start.27) | collective-permute-done | bytes 819232 | tf_op jit(solution)/shard_map/ppermute | solution.py:463
  213.1 1.5 collective-permute-start.30
  215.4 6.9 %down.2 = (f32[256,1280]{1,0:T(8,128)}, bf16[256,1280]{1,0:T(8,128)(2,1)S(1)}, bf16[256,1280]{1,0:T(8,128)(2,1)S(1)}, f32[128,1280]{1,0:T(8,128)S(1)}, f32[128,1280]{1,0:T(8,128)S(1)}) custom-call(s32[1]{0:T(128)} %bitcast.20.me, bf16[1024,640]{1,0:T(8,128)(2,1)} %copy-done.4, bf16[1024,640]{1,0:T(8,128)(2,1)} %copy-done.5, ...), custom_call_target="tpu_custom_call" | custom-call | flops 1024 | bytes 1024 | tf_op jit(solution)/shard_map/down/pallas_call | solution.py:417
  223.0 10.7 %collective-permute-done.30.refs_3_ = bf16[1,4,160,640]{3,2,1,0:T(8,128)(2,1)S(1)} collective-permute-done((bf16[1,4,160,640]{3,2,1,0:T(8,128)(2,1)S(1)}, bf16[1,4,160,640]{3,2,1,0:T(8,128)(2,1)S(1)}, u32[]{:S(2)}, u32[]{:S(2)}) %collective-permute-start.30) | collective-permute-done | bytes 819232 | tf_op jit(solution)/shard_map/ppermute | solution.py:463
  233.8 5.4 %collective-permute-done.31.refs_1_ = bf16[256,1280]{1,0:T(8,128)(2,1)S(1)} collective-permute-done((bf16[256,1280]{1,0:T(8,128)(2,1)S(1)}, bf16[256,1280]{1,0:T(8,128)(2,1)S(1)}, u32[]{:S(2)}, u32[]{:S(2)}) %collective-permute-start.31) | collective-permute-done | bytes 655392 | tf_op jit(solution)/shard_map/ppermute | solution.py:463
  240.0 1.8 collective-permute-done.35.refs_4_
  243.0 6.9 %down.3 = (f32[256,1280]{1,0:T(8,128)}, bf16[256,1280]{1,0:T(8,128)(2,1)S(1)}, bf16[256,1280]{1,0:T(8,128)(2,1)S(1)}, f32[128,1280]{1,0:T(8,128)S(1)}, f32[128,1280]{1,0:T(8,128)S(1)}) custom-call(s32[1]{0:T(128)} %bitcast.20.me, bf16[1024,640]{1,0:T(8,128)(2,1)} %copy-done.4, bf16[1024,640]{1,0:T(8,128)(2,1)} %copy-done.5, ...), custom_call_target="tpu_custom_call" | custom-call | flops 1024 | bytes 1024 | tf_op jit(solution)/shard_map/down/pallas_call | solution.py:417
  249.9 1.5 collective-permute-start.37
  252.4 1.7 collective-permute-start.38
  255.5 12.0 %collective-permute-done.37.refs_6_ = bf16[256,1280]{1,0:T(8,128)(2,1)S(1)} collective-permute-done((bf16[256,1280]{1,0:T(8,128)(2,1)S(1)}, bf16[256,1280]{1,0:T(8,128)(2,1)S(1)}, u32[]{:S(2)}, u32[]{:S(2)}) %collective-permute-start.37) | collective-permute-done | bytes 655392 | tf_op jit(solution)/shard_map/ppermute | solution.py:463
  268.6 8.4 %collective-permute-done.38.refs_7_ = bf16[256,1280]{1,0:T(8,128)(2,1)S(1)} collective-permute-done((bf16[256,1280]{1,0:T(8,128)(2,1)S(1)}, bf16[256,1280]{1,0:T(8,128)(2,1)S(1)}, u32[]{:S(2)}, u32[]{:S(2)}) %collective-permute-start.38) | collective-permute-done | bytes 655392 | tf_op jit(solution)/shard_map/ppermute | solution.py:463
  278.4 4.6 %collective-permute-done.40.refs_9_ = bf16[128,1280]{1,0:T(8,128)(2,1)} collective-permute-done((bf16[128,1280]{1,0:T(8,128)(2,1)}, bf16[128,1280]{1,0:T(8,128)(2,1)}, u32[]{:S(2)}, u32[]{:S(2)}) %collective-permute-start.40) | collective-permute-done | bytes 327712 | tf_op jit(solution)/shard_map/ppermute | solution.py:463
  283.0 2.6 collective-permute-done.39.refs_8_
  286.8 3.5 %finish.1 = bf16[256,2560]{1,0:T(8,128)(2,1)} custom-call(s32[1]{0:T(128)} %bitcast.upper, bf16[256,2560]{1,0:T(8,128)(2,1)S(1)} %copy-done.9, f32[256,1280]{1,0:T(8,128)} %get-tuple-element.150.refs_0_, bf16[256,1280]{1,0:T(8,128)(2,1)S(1)} %collective-permute-done.31.refs_1_, bf16[256,1280]{1,0:T(8,128)(2,1)S(1)} %collective-permute-done.32.refs_2_, ...), custom_call_target="tpu_custom_call" | custom-call | flops 1024 | bytes 1024 | tf_op jit(solution)/shard_map/finish/pallas_call | solution.py:451
  (124 shorter events, 38.9 us)
Async XLA Ops:
  0.0 14.2 %collective-permute-start = (bf16[2,64,512]{2,1,0:T(8,128)(2,1)}, bf16[2,64,512]{2,1,0:T(8,128)(2,1)S(1)}, u32[]{:S(2)}, u32[]{:S(2)}) collective-permute-start(bf16[2,64,512]{2,1,0:T(8,128)(2,1)} %param.16), channel_id=1, source_target_pairs={{0,8},{2,10},{4,12},{6,14},{8,0},{10,2},{12,4},{14,6},{16,24},{18,... | collective-permute-start | bytes 393224 | tf_op jit(solution)/shard_map/ppermute | solution.py:463
  3.0 13.2 %collective-permute-start.1 = (bf16[2,64,512]{2,1,0:T(8,128)(2,1)}, bf16[2,64,512]{2,1,0:T(8,128)(2,1)S(1)}, u32[]{:S(2)}, u32[]{:S(2)}) collective-permute-start(bf16[2,64,512]{2,1,0:T(8,128)(2,1)} %param.16), channel_id=1, source_target_pairs={{0,16},{2,18},{4,20},{6,22},{8,24},{10,26},{12,28},{14,30},{16,0},... | collective-permute-start | bytes 393224 | tf_op jit(solution)/shard_map/ppermute | solution.py:463
  5.6 10.6 %collective-permute-start.2 = (bf16[2,64,512]{2,1,0:T(8,128)(2,1)}, bf16[2,64,512]{2,1,0:T(8,128)(2,1)S(1)}, u32[]{:S(2)}, u32[]{:S(2)}) collective-permute-start(bf16[2,64,512]{2,1,0:T(8,128)(2,1)} %param.16), channel_id=1, source_target_pairs={{0,24},{2,26},{4,28},{6,30},{8,16},{10,18},{12,20},{14,22},{16,8},... | collective-permute-start | bytes 393224 | tf_op jit(solution)/shard_map/ppermute | solution.py:463
  8.2 15.0 %collective-permute-start.6 = (bf16[2,160,640]{2,1,0:T(8,128)(2,1)S(1)}, bf16[2,160,640]{2,1,0:T(8,128)(2,1)S(1)}, u32[]{:S(2)}, u32[]{:S(2)}) collective-permute-start(bf16[2,160,640]{2,1,0:T(8,128)(2,1)S(1)} %get-tuple-element.93), channel_id=1, source_target_pairs={{0,2},{2,0},{4,6},{6,4},{8,10},{10,8},{12,14},{14,12},{16,18},{18,... | collective-permute-start | bytes 1228808 | tf_op jit(solution)/shard_map/ppermute | solution.py:463
  9.9 15.6 %collective-permute-start.7 = (bf16[2,160,640]{2,1,0:T(8,128)(2,1)S(1)}, bf16[2,160,640]{2,1,0:T(8,128)(2,1)S(1)}, u32[]{:S(2)}, u32[]{:S(2)}) collective-permute-start(bf16[2,160,640]{2,1,0:T(8,128)(2,1)S(1)} %get-tuple-element.94), channel_id=1, source_target_pairs={{0,8},{2,10},{4,12},{6,14},{8,0},{10,2},{12,4},{14,6},{16,24},{18,... | collective-permute-start | bytes 1228808 | tf_op jit(solution)/shard_map/ppermute | solution.py:463
  17.2 15.4 %collective-permute-start.8 = (bf16[2,160,640]{2,1,0:T(8,128)(2,1)S(1)}, bf16[2,160,640]{2,1,0:T(8,128)(2,1)S(1)}, u32[]{:S(2)}, u32[]{:S(2)}) collective-permute-start(bf16[2,160,640]{2,1,0:T(8,128)(2,1)S(1)} %get-tuple-element.95), channel_id=1, source_target_pairs={{0,10},{2,8},{4,14},{6,12},{8,2},{10,0},{12,6},{14,4},{16,26},{18,... | collective-permute-start | bytes 1228808 | tf_op jit(solution)/shard_map/ppermute | solution.py:463
  21.1 24.4 %collective-permute-start.4 = (bf16[4,2,64,512]{3,2,1,0:T(8,128)(2,1)S(1)}, bf16[4,2,64,512]{3,2,1,0:T(8,128)(2,1)}, u32[]{:S(2)}, u32[]{:S(2)}) collective-permute-start(bf16[4,2,64,512]{3,2,1,0:T(8,128)(2,1)S(1)} %pad_maximum_fusion.1), channel_id=1, source_target_pairs={{0,4},{2,6},{4,0},{6,2},{8,12},{10,14},{12,8},{14,10},{16,20},{18,... | collective-permute-start | bytes 1572872 | tf_op jit(solution)/shard_map/ppermute | solution.py:463
  22.7 22.8 %collective-permute-start.5 = (bf16[4,2,64,512]{3,2,1,0:T(8,128)(2,1)S(1)}, bf16[4,2,64,512]{3,2,1,0:T(8,128)(2,1)}, u32[]{:S(2)}, u32[]{:S(2)}) collective-permute-start(bf16[4,2,64,512]{3,2,1,0:T(8,128)(2,1)S(1)} %pad_maximum_fusion.1), channel_id=1, source_target_pairs={{0,6},{2,4},{4,2},{6,0},{8,14},{10,12},{12,10},{14,8},{16,22},{18,... | collective-permute-start | bytes 1572872 | tf_op jit(solution)/shard_map/ppermute | solution.py:463
  23.2 31.1 %collective-permute-start.3 = (bf16[4,2,64,512]{3,2,1,0:T(8,128)(2,1)S(1)}, bf16[4,2,64,512]{3,2,1,0:T(8,128)(2,1)}, u32[]{:S(2)}, u32[]{:S(2)}) collective-permute-start(bf16[4,2,64,512]{3,2,1,0:T(8,128)(2,1)S(1)} %pad_maximum_fusion.1), channel_id=1, source_target_pairs={{0,2},{2,0},{4,6},{6,4},{8,10},{10,8},{12,14},{14,12},{16,18},{18,... | collective-permute-start | bytes 1572872 | tf_op jit(solution)/shard_map/ppermute | solution.py:463
  39.9 37.8 %collective-permute-start.9 = (bf16[1,4,160,640]{3,2,1,0:T(8,128)(2,1)}, bf16[1,4,160,640]{3,2,1,0:T(8,128)(2,1)}, u32[]{:S(2)}, u32[]{:S(2)}) collective-permute-start(bf16[1,4,160,640]{3,2,1,0:T(8,128)(2,1)} %get-tuple-element.96.refs_0_), channel_id=1, source_target_pairs={{0,16},{2,18},{4,20},{6,22},{8,24},{10,26},{12,28},{14,30},{16,0},... | collective-permute-start | bytes 2457608 | tf_op jit(solution)/shard_map/ppermute | solution.py:463
  41.4 59.9 %collective-permute-start.11 = (bf16[2,4,160,640]{3,2,1,0:T(8,128)(2,1)}, bf16[2,4,160,640]{3,2,1,0:T(8,128)(2,1)S(1)}, u32[]{:S(2)}, u32[]{:S(2)}) collective-permute-start(bf16[2,4,160,640]{3,2,1,0:T(8,128)(2,1)} %copy-done.22), channel_id=1, source_target_pairs={{0,4},{2,6},{4,0},{6,2},{8,12},{10,14},{12,8},{14,10},{16,20},{18,... | collective-permute-start | bytes 4915208 | tf_op jit(solution)/shard_map/ppermute | solution.py:463
  77.6 14.0 %copy-start.24 = (f32[2560]{0:T(1024)S(1)}, f32[2560]{0:T(1024)}, u32[]{:S(2)}) copy-start(f32[2560]{0:T(1024)} %param.20) | copy-start | bytes 30724
  77.6 14.1 %copy-start.10 = (bf16[256,2560]{1,0:T(8,128)(2,1)S(1)}, bf16[256,2560]{1,0:T(8,128)(2,1)}, u32[]{:S(2)}) copy-start(bf16[256,2560]{1,0:T(8,128)(2,1)} %hidden.1) | copy-start | bytes 3932164
  88.0 3.7 %collective-permute-start.10 = (bf16[256,2560]{1,0:T(8,128)(2,1)S(1)}, bf16[256,2560]{1,0:T(8,128)(2,1)S(1)}, u32[]{:S(2)}, u32[]{:S(2)}) collective-permute-start(bf16[256,2560]{1,0:T(8,128)(2,1)S(1)} %get-tuple-element.100), channel_id=1, source_target_pairs={{0,1},{1,0},{2,3},{3,2},{4,5},{5,4},{6,7},{7,6},{8,9},{9,8},{10,11... | collective-permute-start | bytes 3932168 | tf_op jit(solution)/shard_map/ppermute | solution.py:463
  88.1 7.8 %collective-permute-start.12 = (bf16[1,160,640]{2,1,0:T(8,128)(2,1)S(1)}, bf16[1,160,640]{2,1,0:T(8,128)(2,1)S(1)}, u32[]{:S(2)}, u32[]{:S(2)}) collective-permute-start(bf16[1,160,640]{2,1,0:T(8,128)(2,1)S(1)} %get-tuple-element.106), channel_id=1, source_target_pairs={{0,2},{2,0},{4,6},{6,4},{8,10},{10,8},{12,14},{14,12},{16,18},{18,... | collective-permute-start | bytes 614408 | tf_op jit(solution)/shard_map/ppermute | solution.py:463
  89.6 7.9 %collective-permute-start.13 = (bf16[1,160,640]{2,1,0:T(8,128)(2,1)S(1)}, bf16[1,160,640]{2,1,0:T(8,128)(2,1)S(1)}, u32[]{:S(2)}, u32[]{:S(2)}) collective-permute-start(bf16[1,160,640]{2,1,0:T(8,128)(2,1)S(1)} %get-tuple-element.107), channel_id=1, source_target_pairs={{0,8},{2,10},{4,12},{6,14},{8,0},{10,2},{12,4},{14,6},{16,24},{18,... | collective-permute-start | bytes 614408 | tf_op jit(solution)/shard_map/ppermute | solution.py:463
  89.6 11.7 %collective-permute-start.14 = (bf16[1,160,640]{2,1,0:T(8,128)(2,1)S(1)}, bf16[1,160,640]{2,1,0:T(8,128)(2,1)S(1)}, u32[]{:S(2)}, u32[]{:S(2)}) collective-permute-start(bf16[1,160,640]{2,1,0:T(8,128)(2,1)S(1)} %get-tuple-element.108), channel_id=1, source_target_pairs={{0,10},{2,8},{4,14},{6,12},{8,2},{10,0},{12,6},{14,4},{16,26},{18,... | collective-permute-start | bytes 614408 | tf_op jit(solution)/shard_map/ppermute | solution.py:463
  95.9 81.2 %copy-start.3 = (bf16[256,2560]{1,0:T(8,128)(2,1)}, bf16[256,2560]{1,0:T(8,128)(2,1)S(1)}, u32[]{:S(2)}) copy-start(bf16[256,2560]{1,0:T(8,128)(2,1)S(1)} %get-tuple-element.110.refs_0_) | copy-start | bytes 3932164
  102.8 50.3 %copy-start = (bf16[3,4,160,640]{3,2,1,0:T(8,128)(2,1)}, bf16[3,4,160,640]{3,2,1,0:T(8,128)(2,1)S(1)}, u32[]{:S(2)}) copy-start(bf16[3,4,160,640]{3,2,1,0:T(8,128)(2,1)S(1)} %collect.2.refs_5_) | copy-start | bytes 7372804
  102.8 50.0 %collective-permute-start.18 = (bf16[3,4,160,640]{3,2,1,0:T(8,128)(2,1)S(1)}, bf16[3,4,160,640]{3,2,1,0:T(8,128)(2,1)}, u32[]{:S(2)}, u32[]{:S(2)}) collective-permute-start(bf16[3,4,160,640]{3,2,1,0:T(8,128)(2,1)S(1)} %collect.2.refs_5_), channel_id=1, source_target_pairs={{0,1},{1,0},{2,3},{3,2},{4,5},{5,4},{6,7},{7,6},{8,9},{9,8},{10,11... | collective-permute-start | bytes 7372808 | tf_op jit(solution)/shard_map/ppermute | solution.py:463
  102.9 47.7 %collective-permute-start.15 = (bf16[256,2560]{1,0:T(8,128)(2,1)S(1)}, bf16[256,2560]{1,0:T(8,128)(2,1)S(1)}, u32[]{:S(2)}, u32[]{:S(2)}) collective-permute-start(bf16[256,2560]{1,0:T(8,128)(2,1)S(1)} %get-tuple-element.110.refs_0_), channel_id=1, source_target_pairs={{0,2},{2,0},{4,6},{6,4},{8,10},{10,8},{12,14},{14,12},{16,18},{18,... | collective-permute-start | bytes 3932168 | tf_op jit(solution)/shard_map/ppermute | solution.py:463
  104.3 48.4 %collective-permute-start.16 = (bf16[256,2560]{1,0:T(8,128)(2,1)S(1)}, bf16[256,2560]{1,0:T(8,128)(2,1)S(1)}, u32[]{:S(2)}, u32[]{:S(2)}) collective-permute-start(bf16[256,2560]{1,0:T(8,128)(2,1)S(1)} %get-tuple-element.110.refs_0_), channel_id=1, source_target_pairs={{0,8},{2,10},{4,12},{6,14},{8,0},{10,2},{12,4},{14,6},{16,24},{18,... | collective-permute-start | bytes 3932168 | tf_op jit(solution)/shard_map/ppermute | solution.py:463
  104.6 20.2 %collective-permute-start.19 = (bf16[1,4,160,640]{3,2,1,0:T(8,128)(2,1)}, bf16[1,4,160,640]{3,2,1,0:T(8,128)(2,1)S(1)}, u32[]{:S(2)}, u32[]{:S(2)}) collective-permute-start(bf16[1,4,160,640]{3,2,1,0:T(8,128)(2,1)} %collective-permute-done.9.refs_2_), channel_id=1, source_target_pairs={{0,4},{2,6},{4,0},{6,2},{8,12},{10,14},{12,8},{14,10},{16,20},{18,... | collective-permute-start | bytes 2457608 | tf_op jit(solution)/shard_map/ppermute | solution.py:463
  106.1 44.4 %collective-permute-start.17 = (bf16[1,4,160,640]{3,2,1,0:T(8,128)(2,1)S(1)}, bf16[1,4,160,640]{3,2,1,0:T(8,128)(2,1)S(1)}, u32[]{:S(2)}, u32[]{:S(2)}) collective-permute-start(bf16[1,4,160,640]{3,2,1,0:T(8,128)(2,1)S(1)} %copy-done.15), channel_id=1, source_target_pairs={{0,16},{2,18},{4,20},{6,22},{8,24},{10,26},{12,28},{14,30},{16,0},... | collective-permute-start | bytes 2457608 | tf_op jit(solution)/shard_map/ppermute | solution.py:463
  150.5 26.6 %copy-start.2 = (bf16[256,2560]{1,0:T(8,128)(2,1)}, bf16[256,2560]{1,0:T(8,128)(2,1)S(1)}, u32[]{:S(2)}) copy-start(bf16[256,2560]{1,0:T(8,128)(2,1)S(1)} %collective-permute-done.15.refs_1_) | copy-start | bytes 3932164
  153.1 36.9 %copy-start.1 = (bf16[3,4,160,640]{3,2,1,0:T(8,128)(2,1)}, bf16[3,4,160,640]{3,2,1,0:T(8,128)(2,1)S(1)}, u32[]{:S(2)}) copy-start(bf16[3,4,160,640]{3,2,1,0:T(8,128)(2,1)S(1)} %collect.3.refs_5_) | copy-start | bytes 7372804
  153.1 20.7 %collective-permute-start.22 = (bf16[3,4,160,640]{3,2,1,0:T(8,128)(2,1)S(1)}, bf16[3,4,160,640]{3,2,1,0:T(8,128)(2,1)}, u32[]{:S(2)}, u32[]{:S(2)}) collective-permute-start(bf16[3,4,160,640]{3,2,1,0:T(8,128)(2,1)S(1)} %collect.3.refs_5_), channel_id=1, source_target_pairs={{0,1},{1,0},{2,3},{3,2},{4,5},{5,4},{6,7},{7,6},{8,9},{9,8},{10,11... | collective-permute-start | bytes 7372808 | tf_op jit(solution)/shard_map/ppermute | solution.py:463
  153.2 20.7 %collective-permute-start.23 = (bf16[1,4,160,640]{3,2,1,0:T(8,128)(2,1)S(1)}, bf16[1,4,160,640]{3,2,1,0:T(8,128)(2,1)S(1)}, u32[]{:S(2)}, u32[]{:S(2)}) collective-permute-start(bf16[1,4,160,640]{3,2,1,0:T(8,128)(2,1)S(1)} %collective-permute-done.17.refs_2_), channel_id=1, source_target_pairs={{0,4},{2,6},{4,0},{6,2},{8,12},{10,14},{12,8},{14,10},{16,20},{18,... | collective-permute-start | bytes 2457608 | tf_op jit(solution)/shard_map/ppermute | solution.py:463
  154.7 19.1 %collective-permute-start.24 = (bf16[1,4,160,640]{3,2,1,0:T(8,128)(2,1)S(1)}, bf16[1,4,160,640]{3,2,1,0:T(8,128)(2,1)S(1)}, u32[]{:S(2)}, u32[]{:S(2)}) collective-permute-start(bf16[1,4,160,640]{3,2,1,0:T(8,128)(2,1)S(1)} %collective-permute-done.19.refs_6_), channel_id=1, source_target_pairs={{0,1},{1,0},{2,3},{3,2},{4,5},{5,4},{6,7},{7,6},{8,9},{9,8},{10,11... | collective-permute-start | bytes 2457608 | tf_op jit(solution)/shard_map/ppermute | solution.py:463
  155.0 17.0 %collective-permute-start.20 = (bf16[128,2560]{1,0:T(8,128)(2,1)S(1)}, bf16[128,2560]{1,0:T(8,128)(2,1)S(1)}, u32[]{:S(2)}, u32[]{:S(2)}) collective-permute-start(bf16[128,2560]{1,0:T(8,128)(2,1)S(1)} %slice.18), channel_id=1, source_target_pairs={{0,8},{2,10},{4,12},{6,14},{8,0},{10,2},{12,4},{14,6},{16,24},{18,... | collective-permute-start | bytes 1966088 | tf_op jit(solution)/shard_map/ppermute | solution.py:463
  156.0 16.8 %collective-permute-start.21 = (bf16[128,2560]{1,0:T(8,128)(2,1)S(1)}, bf16[128,2560]{1,0:T(8,128)(2,1)S(1)}, u32[]{:S(2)}, u32[]{:S(2)}) collective-permute-start(bf16[128,2560]{1,0:T(8,128)(2,1)S(1)} %slice.19), channel_id=1, source_target_pairs={{0,2},{2,0},{4,6},{6,4},{8,10},{10,8},{12,14},{14,12},{16,18},{18,... | collective-permute-start | bytes 1966088 | tf_op jit(solution)/shard_map/ppermute | solution.py:463
  173.8 16.1 %copy-start.16 = (bf16[1,4,160,640]{3,2,1,0:T(8,128)(2,1)}, bf16[1,4,160,640]{3,2,1,0:T(8,128)(2,1)S(1)}, u32[]{:S(2)}) copy-start(bf16[1,4,160,640]{3,2,1,0:T(8,128)(2,1)S(1)} %collective-permute-done.23.refs_6_) | copy-start | bytes 2457604
  173.8 16.1 %collective-permute-start.25 = (bf16[1,4,160,640]{3,2,1,0:T(8,128)(2,1)S(1)}, bf16[1,4,160,640]{3,2,1,0:T(8,128)(2,1)S(1)}, u32[]{:S(2)}, u32[]{:S(2)}) collective-permute-start(bf16[1,4,160,640]{3,2,1,0:T(8,128)(2,1)S(1)} %collective-permute-done.23.refs_6_), channel_id=1, source_target_pairs={{0,1},{1,0},{2,3},{3,2},{4,5},{5,4},{6,7},{7,6},{8,9},{9,8},{10,11... | collective-permute-start | bytes 2457608 | tf_op jit(solution)/shard_map/ppermute | solution.py:463
  173.9 16.9 %collective-permute-start.26 = (bf16[1,4,160,640]{3,2,1,0:T(8,128)(2,1)S(1)}, bf16[1,4,160,640]{3,2,1,0:T(8,128)(2,1)S(1)}, u32[]{:S(2)}, u32[]{:S(2)}) collective-permute-start(bf16[1,4,160,640]{3,2,1,0:T(8,128)(2,1)S(1)} %merge.3.refs_2_), channel_id=1, source_target_pairs={{0,1},{1,0},{2,3},{3,2},{4,5},{5,4},{6,7},{7,6},{8,9},{9,8},{10,11... | collective-permute-start | bytes 2457608 | tf_op jit(solution)/shard_map/ppermute | solution.py:463
  174.4 38.7 %collective-permute-start.27 = (bf16[1,4,160,640]{3,2,1,0:T(8,128)(2,1)S(1)}, bf16[1,4,160,640]{3,2,1,0:T(8,128)(2,1)S(1)}, u32[]{:S(2)}, u32[]{:S(2)}) collective-permute-start(bf16[1,4,160,640]{3,2,1,0:T(8,128)(2,1)S(1)} %merge.3.refs_2_), channel_id=1, source_target_pairs={{0,16},{2,18},{4,20},{6,22},{8,24},{10,26},{12,28},{14,30},{16,0},... | collective-permute-start | bytes 2457608 | tf_op jit(solution)/shard_map/ppermute | solution.py:463
  175.6 37.5 %collective-permute-start.28 = (bf16[1,4,160,640]{3,2,1,0:T(8,128)(2,1)S(1)}, bf16[1,4,160,640]{3,2,1,0:T(8,128)(2,1)S(1)}, u32[]{:S(2)}, u32[]{:S(2)}) collective-permute-start(bf16[1,4,160,640]{3,2,1,0:T(8,128)(2,1)S(1)} %merge.3.refs_2_), channel_id=1, source_target_pairs={{0,4},{2,6},{4,0},{6,2},{8,12},{10,14},{12,8},{14,10},{16,20},{18,... | collective-permute-start | bytes 2457608 | tf_op jit(solution)/shard_map/ppermute | solution.py:463
  213.1 2.3 collective-permute-start.29
  213.1 20.7 %collective-permute-start.30 = (bf16[1,4,160,640]{3,2,1,0:T(8,128)(2,1)S(1)}, bf16[1,4,160,640]{3,2,1,0:T(8,128)(2,1)S(1)}, u32[]{:S(2)}, u32[]{:S(2)}) collective-permute-start(bf16[1,4,160,640]{3,2,1,0:T(8,128)(2,1)S(1)} %collective-permute-done.27.refs_2_), channel_id=1, source_target_pairs={{0,4},{2,6},{4,0},{6,2},{8,12},{10,14},{12,8},{14,10},{16,20},{18,... | collective-permute-start | bytes 2457608 | tf_op jit(solution)/shard_map/ppermute | solution.py:463
  222.3 16.8 %collective-permute-start.31 = (bf16[256,1280]{1,0:T(8,128)(2,1)S(1)}, bf16[256,1280]{1,0:T(8,128)(2,1)S(1)}, u32[]{:S(2)}, u32[]{:S(2)}) collective-permute-start(bf16[256,1280]{1,0:T(8,128)(2,1)S(1)} %get-tuple-element.152), channel_id=1, source_target_pairs={{0,2},{2,0},{4,6},{6,4},{8,10},{10,8},{12,14},{14,12},{16,18},{18,... | collective-permute-start | bytes 1966088 | tf_op jit(solution)/shard_map/ppermute | solution.py:463
  223.0 16.5 %collective-permute-start.32 = (bf16[256,1280]{1,0:T(8,128)(2,1)S(1)}, bf16[256,1280]{1,0:T(8,128)(2,1)S(1)}, u32[]{:S(2)}, u32[]{:S(2)}) collective-permute-start(bf16[256,1280]{1,0:T(8,128)(2,1)S(1)} %get-tuple-element.153), channel_id=1, source_target_pairs={{0,8},{2,10},{4,12},{6,14},{8,0},{10,2},{12,4},{14,6},{16,24},{18,... | collective-permute-start | bytes 1966088 | tf_op jit(solution)/shard_map/ppermute | solution.py:463
  239.5 2.3 collective-permute-start.35
  239.5 3.5 %collective-permute-start.36 = (bf16[1,4,160,640]{3,2,1,0:T(8,128)(2,1)S(1)}, bf16[1,4,160,640]{3,2,1,0:T(8,128)(2,1)S(1)}, u32[]{:S(2)}, u32[]{:S(2)}) collective-permute-start(bf16[1,4,160,640]{3,2,1,0:T(8,128)(2,1)S(1)} %collective-permute-done.30.refs_3_), channel_id=1, source_target_pairs={{0,1},{1,0},{2,3},{3,2},{4,5},{5,4},{6,7},{7,6},{8,9},{9,8},{10,11... | collective-permute-start | bytes 2457608 | tf_op jit(solution)/shard_map/ppermute | solution.py:463
  249.9 17.6 %collective-permute-start.37 = (bf16[256,1280]{1,0:T(8,128)(2,1)S(1)}, bf16[256,1280]{1,0:T(8,128)(2,1)S(1)}, u32[]{:S(2)}, u32[]{:S(2)}) collective-permute-start(bf16[256,1280]{1,0:T(8,128)(2,1)S(1)} %get-tuple-element.161), channel_id=1, source_target_pairs={{0,2},{2,0},{4,6},{6,4},{8,10},{10,8},{12,14},{14,12},{16,18},{18,... | collective-permute-start | bytes 1966088 | tf_op jit(solution)/shard_map/ppermute | solution.py:463
  252.1 26.3 %collective-permute-start.34 = (bf16[128,1280]{1,0:T(8,128)(2,1)}, bf16[128,1280]{1,0:T(8,128)(2,1)S(1)}, u32[]{:S(2)}, u32[]{:S(2)}) collective-permute-start(bf16[128,1280]{1,0:T(8,128)(2,1)} %add_convert_fusion.2), channel_id=1, source_target_pairs={{0,8},{2,10},{4,12},{6,14},{8,0},{10,2},{12,4},{14,6},{16,24},{18,... | collective-permute-start | bytes 983048 | tf_op jit(solution)/shard_map/ppermute | solution.py:463
  252.4 24.6 %collective-permute-start.38 = (bf16[256,1280]{1,0:T(8,128)(2,1)S(1)}, bf16[256,1280]{1,0:T(8,128)(2,1)S(1)}, u32[]{:S(2)}, u32[]{:S(2)}) collective-permute-start(bf16[256,1280]{1,0:T(8,128)(2,1)S(1)} %get-tuple-element.162), channel_id=1, source_target_pairs={{0,8},{2,10},{4,12},{6,14},{8,0},{10,2},{12,4},{14,6},{16,24},{18,... | collective-permute-start | bytes 1966088 | tf_op jit(solution)/shard_map/ppermute | solution.py:463
  254.9 23.5 %collective-permute-start.33 = (bf16[128,1280]{1,0:T(8,128)(2,1)}, bf16[128,1280]{1,0:T(8,128)(2,1)S(1)}, u32[]{:S(2)}, u32[]{:S(2)}) collective-permute-start(bf16[128,1280]{1,0:T(8,128)(2,1)} %add_convert_fusion.3), channel_id=1, source_target_pairs={{0,2},{2,0},{4,6},{6,4},{8,10},{10,8},{12,14},{14,12},{16,18},{18,... | collective-permute-start | bytes 983048 | tf_op jit(solution)/shard_map/ppermute | solution.py:463
  268.3 14.7 %collective-permute-start.40 = (bf16[128,1280]{1,0:T(8,128)(2,1)}, bf16[128,1280]{1,0:T(8,128)(2,1)}, u32[]{:S(2)}, u32[]{:S(2)}) collective-permute-start(bf16[128,1280]{1,0:T(8,128)(2,1)} %add_convert_fusion), channel_id=1, source_target_pairs={{0,8},{2,10},{4,12},{6,14},{8,0},{10,2},{12,4},{14,6},{16,24},{18,... | collective-permute-start | bytes 983048 | tf_op jit(solution)/shard_map/ppermute | solution.py:463
  277.7 7.8 %collective-permute-start.39 = (bf16[128,1280]{1,0:T(8,128)(2,1)}, bf16[128,1280]{1,0:T(8,128)(2,1)}, u32[]{:S(2)}, u32[]{:S(2)}) collective-permute-start(bf16[128,1280]{1,0:T(8,128)(2,1)} %add_convert_fusion.1), channel_id=1, source_target_pairs={{0,2},{2,0},{4,6},{6,4},{8,10},{10,8},{12,14},{14,12},{16,18},{18,... | collective-permute-start | bytes 983048 | tf_op jit(solution)/shard_map/ppermute | solution.py:463
  (18 other events, 46.0 us)

commit v4 on v3

--- a/solution.py
+++ b/solution.py
@@ -244,40 +244,23 @@
     return move(seat, blocks, shapes, plan, GROUP * len(blocks), "cut")
 
 
-def merge(seat, parts, groups):
-    _, rows, width = parts[0].shape
+def merge(seat, parts):
+    n_mats, rows, width = parts[0].shape
     if width % 128:
-        whole = jnp.stack(parts, axis=1)
-        return [jnp.stack([whole[m] for m in group]) for group in groups]
+        return jnp.stack(parts, axis=1)
 
     def plan(_, sources, targets):
         return [
-            (source.at[m], target.at[i, j])
-            for target, group in zip(targets, groups)
-            for i, m in enumerate(group)
+            (source.at[m], targets[0].at[m, j])
             for j, source in enumerate(sources)
+            for m in range(n_mats)
         ]
 
-    shapes = [(len(group), GROUP, rows, width) for group in groups]
-    return move(seat, parts, shapes, plan, GROUP * sum(map(len, groups)), "merge")
-
-
-def collect(seat, entries):
-    shape = entries[0][0].shape[1:]
-    if shape[-1] % 128:
-        return jnp.stack([array[m] for array, m in entries])
-
-    def plan(_, sources, targets):
-        return [
-            (source.at[m], targets[0].at[i])
-            for i, (source, (_, m)) in enumerate(zip(sources, entries))
-        ]
-
-    arrays = [array for array, _ in entries]
-    return move(seat, arrays, [(len(entries), *shape)], plan, len(entries), "collect")[0]
-
-
-def weight_copies(me, refs, keys, target, mask, sems):
+    shapes = [(n_mats, GROUP, rows, width)]
+    return move(seat, parts, shapes, plan, GROUP * n_mats, "merge")[0]
+
+
+def weight_copies(me, refs, keys, matrix, target, mask, sems):
     copies = []
     for i, ref in enumerate(refs):
         part, entry = divmod(i, len(keys))
@@ -286,86 +269,89 @@
         lanes = pl.ds(part * width, width)
         if keys[entry] is None:
             place = target.at[:, lanes] if packed else target.at[part]
-            copies.append(pltpu.make_async_copy(ref.at[0], place, sems.at[len(copies)]))
+            copies.append(pltpu.make_async_copy(ref.at[matrix], place, sems.at[len(copies)]))
             continue
         for k, key in enumerate(keys[entry]):
             for j, partner in enumerate(PARTNERS):
                 source = (me ^ (key ^ partner)) & mask
                 here = pl.ds(pl.multiple_of(source * rows, 8), rows)
                 place = target.at[here, lanes] if packed else target.at[part, here]
-                copies.append(pltpu.make_async_copy(ref.at[k, j], place, sems.at[len(copies)]))
+                copies.append(pltpu.make_async_copy(ref.at[matrix * len(keys[entry]) + k, j], place, sems.at[len(copies)]))
     return copies
 
 
-def expand_kernel(me, *refs, n_parts, keys, second):
+def expand_kernel(me, *refs, n_parts, keys):
     n_weights = n_parts * len(keys)
     x_refs, refs = refs[: GROUP + 1], refs[GROUP + 1 :]
-    w_refs, refs = refs[:n_weights], refs[n_weights:]
-    before, refs = (refs[:n_parts], refs[n_parts:]) if second else ((), refs)
-    outs, (x_all, weight, x_sems, w_sems) = refs[:n_parts], refs[n_parts:]
+    w_refs, outs, refs = refs[:n_weights], refs[n_weights : n_weights + n_parts], refs[n_weights + n_parts :]
+    x_all, gate_w, up_w, opened, x_sems, gate_sems, up_sems = refs
     width = outs[0].shape[1]
     rows, depth = x_refs[0].shape
-    packed = len(weight.shape) == 2
     places = [x_all.at[i] for i in range(GROUP - 1)]
     places += [x_all.at[GROUP - 1, pl.ds(i * rows // 2, rows // 2)] for i in range(2)]
-    copies = weight_copies(me[0], w_refs, keys, weight, -1, w_sems)
-    copies += [
+    first = weight_copies(me[0], w_refs, keys, 0, gate_w, -1, gate_sems)
+    first += [
         pltpu.make_async_copy(x_ref, place, x_sems.at[i])
         for i, (x_ref, place) in enumerate(zip(x_refs, places))
     ]
-    for copy in copies:
+    second = weight_copies(me[0], w_refs, keys, 1, up_w, -1, up_sems)
+    for copy in first + second:
         copy.start()
-    for copy in copies:
+
+    def product(x, weight):
+        if len(weight.shape) == 2:
+            whole = jnp.dot(x, weight[...], preferred_element_type=jnp.float32)
+            return [whole[:, part * width : (part + 1) * width] for part in range(n_parts)]
+        return [
+            jnp.dot(x, weight[part], preferred_element_type=jnp.float32) for part in range(n_parts)
+        ]
+
+    def gate_step(i, carry):
+        for part, gate in enumerate(product(x_all[i], gate_w)):
+            opened[i, part] = gate / (1.0 + jnp.exp(-gate))
+        return carry
+
+    def up_step(i, carry):
+        lines = pl.ds(pl.multiple_of(i * rows, rows), rows)
+        for part, upward in enumerate(product(x_all[i], up_w)):
+            outs[part][lines, :] = (opened[i, part] * upward).astype(outs[part].dtype)
+        return carry
+
+    for copy in first:
         copy.wait()
-
-    def step(i, carry):
-        x = x_all[i]
-        lines = pl.ds(pl.multiple_of(i * rows, rows), rows)
-        if packed:
-            whole = jnp.dot(x, weight[...], preferred_element_type=jnp.float32)
-        for part in range(n_parts):
-            if packed:
-                total = whole[:, part * width : (part + 1) * width]
-            else:
-                total = jnp.dot(x, weight[part], preferred_element_type=jnp.float32)
-            if second:
-                total = total * before[part][lines, :]
-            else:
-                total = total / (1.0 + jnp.exp(-total))
-            outs[part][lines, :] = total.astype(outs[part].dtype)
-        return carry
-
-    lax.fori_loop(0, GROUP, step, 0)
-
-
-def expand(me, normed, keys, weights, before=()):
+    lax.fori_loop(0, GROUP, gate_step, 0)
+    for copy in second:
+        copy.wait()
+    lax.fori_loop(0, GROUP, up_step, 0)
+
+
+def expand(me, normed, keys, weights):
     rows, depth = normed[0].shape
     n_parts = len(weights)
     width = weights[0][0].shape[-1]
     total = rows * GROUP
     n_copies = n_parts * GROUP * sum(len(entry or (0,)) for entry in keys)
     shape = (depth, n_parts * width) if width % 128 == 0 else (n_parts, depth, width)
-    kind = jnp.bfloat16 if before else jnp.float32
     vmem, anywhere = pl.BlockSpec(memory_space=pltpu.VMEM), pl.BlockSpec(memory_space=pl.ANY)
     return pl.pallas_call(
-        functools.partial(
-            expand_kernel, n_parts=n_parts, keys=keys, second=bool(before)
-        ),
+        functools.partial(expand_kernel, n_parts=n_parts, keys=keys),
         in_specs=[pl.BlockSpec(memory_space=pltpu.SMEM)]
-        + [anywhere] * (len(normed) + n_parts * len(keys))
-        + [vmem] * len(before),
+        + [anywhere] * (len(normed) + n_parts * len(keys)),
         out_specs=[vmem] * n_parts,
-        out_shape=[jax.ShapeDtypeStruct((total, width), kind)] * n_parts,
+        out_shape=[jax.ShapeDtypeStruct((total, width), jnp.bfloat16)] * n_parts,
         scratch_shapes=[
             pltpu.VMEM((GROUP, rows, depth), jnp.bfloat16),
             pltpu.VMEM(shape, jnp.bfloat16),
+            pltpu.VMEM(shape, jnp.bfloat16),
+            pltpu.VMEM((GROUP, n_parts, rows, width), jnp.float32),
             pltpu.SemaphoreType.DMA((len(normed),)),
+            pltpu.SemaphoreType.DMA((n_copies,)),
             pltpu.SemaphoreType.DMA((n_copies,)),
         ],
         compiler_params=pltpu.CompilerParams(vmem_limit_bytes=VMEM_LIMIT),
         cost_estimate=SHORT,
-        name="up" if before else "gate",
-    )(me, *normed, *[array for part in weights for array in part], *before)
+        name="gate_up",
+    )(me, *normed, *[array for part in weights for array in part])
 
 
 def down_kernel(me, *refs, n_parts, keys, mask):
@@ -376,7 +362,7 @@
     rows = own.shape[0]
     half = rows // 2
     packed = len(acts.shape) == 2
-    copies = weight_copies(me[0], w_refs, keys, weight, mask, w_sems)
+    copies = weight_copies(me[0], w_refs, keys, 0, weight, mask, w_sems)
     for i in range(n_parts):
         place = acts.at[:, pl.ds(i * width, width)] if packed else acts.at[i]
         copies.append(pltpu.make_async_copy(act_refs[i], place, a_sems.at[i]))
@@ -505,21 +491,17 @@
     def trade(parts):
         return [parts[0]] + [req(part, key) for part, key in zip(parts[1:], PARTNERS[1:])]
 
-    def relay(entry, key):
-        array, m = entry
-        return (req(array if array.shape[0] == 1 else array[m : m + 1], key), 0)
-
-    def complete(entries):
+    def complete(arrays):
         for key in others[1:]:
-            for held_key in list(entries):
-                if held_key ^ key not in entries:
-                    entries[held_key ^ key] = relay(entries[held_key], key)
-        return entries
-
-    def share(entries, *keys):
-        return [(keys, cores(collect(seat, [entries[key] for key in keys])))]
-
-    def gather(shares, count):
+            for held_key in list(arrays):
+                if held_key ^ key not in arrays:
+                    arrays[held_key ^ key] = req(arrays[held_key], key)
+        return arrays
+
+    def single(arrays):
+        return [([key], cores(array)) for key, array in arrays.items()]
+
+    def gather(shares, count, n_mats):
         keys, parts = [keys for keys, _ in shares], list(zip(*[parts for _, parts in shares]))
         if parts[0][0].shape[2] % 16 == 0:
             return keys, [list(part) for part in parts]
@@ -528,9 +510,10 @@
         spots = spots[(me ^ jnp.arange(count)) % count]
         ordered = []
         for part in parts:
-            whole = jnp.concatenate(part, axis=0)
-            whole = whole.reshape(count, *whole.shape[2:])
-            ordered.append([jnp.take(whole, spots, axis=0).reshape(1, -1, whole.shape[-1])])
+            width = part[0].shape[-1]
+            whole = [x.reshape(n_mats, -1, *x.shape[2:]) for x in part]
+            whole = jnp.take(jnp.concatenate(whole, axis=1), spots, axis=1)
+            ordered.append([whole.reshape(n_mats, -1, width)])
         return [None], ordered
 
     planes = [prefix_kv] + [req(prefix_kv, 4 * k) for k in range(1, n_req // 4)]
@@ -541,12 +524,12 @@
 
     parts = list(cut(seat, [w_gate, w_up]))
     held, parts[3] = tie((held, parts[3]))
-    open_w, gate_own, up_own = merge(seat, trade(parts), [(0, 1), (0,), (1,)])
+    open_w = merge(seat, trade(parts))
     last = others[-1]
     held = jnp.stack([held] + [req(held, k) for k in range(1, 4)])
     held = held.reshape(n_req, 2, PB, local_groups * HD)
     chosen = jnp.take(held, picked, axis=0)
-    gate_top, open_last = req(gate_own, top), req(open_w, last)
+    open_top, open_last = req(open_w, top), req(open_w, last)
 
     _, offset = slot_layout(lengths[0], tok_count)
     cosine, sine = rotation(offset + PLEN)
@@ -555,7 +538,7 @@
 
     chosen, cosine, sine, start = tie((chosen, cosine, sine, start))
     attn = attention(start, cosine, sine, *gains, q_in, kv_in, chosen, 0, local_groups)
-    attn, gate_top, up_own, w_down_t = tie((attn, gate_top, up_own, w_down_t))
+    attn, w_down_t = tie((attn, w_down_t))
     down_parts = trade(cut(seat, [w_down_t]))
 
     own_rows = hidden_in.shape[0]
@@ -563,50 +546,49 @@
     parts = [swap(sums[k], "mlp", n_mlp, k) for k in range(1, n_mlp)]
     resid, own_normed = normalize(hidden_in, post_gain[None], sums[0], parts)
 
-    own_normed, open_last, down_parts, up_own = tie((own_normed, open_last, down_parts, up_own))
-    gate_w = {0: (gate_own, 0), last: (open_last, 0), top: (gate_top, 0)}
+    own_normed, open_top, open_last, down_parts = tie(
+        (own_normed, open_top, open_last, down_parts)
+    )
 
     half = own_rows // 2
     key_x, key_y = PARTNERS[1:3]
     next_x, next_y = req(own_normed, key_x), req(own_normed, key_y)
-    up_top = req(up_own, top)
-    (down_own,) = merge(seat, down_parts, [(0,)])
-    gate_all = share(gate_w, *gate_w)
-    gate_rest = {key: v for key, v in complete(dict(gate_w)).items() if key not in gate_w}
-    next_x, next_y, up_top, down_own, gate_all, gate_rest = tie(
-        (next_x, next_y, up_top, down_own, gate_all, gate_rest)
+    early = {0: open_w, last: open_last, top: open_top}
+    late = {key: array for key, array in complete(dict(early)).items() if key not in early}
+    open_all = single({0: open_w, last: open_last})
+    down_own = merge(seat, down_parts)
+    next_x, next_y, open_all, late, open_top, down_own = tie(
+        (next_x, next_y, open_all, late, open_top, down_own)
     )
     diag = [req(next_x[:half], key_y), req(next_y[half:], key_x)]
-    up_w = {0: (up_own, 0), last: (open_last, 1), top: (up_top, 0)}
-    up_all = share(up_w, *up_w)
-    up_rest = {key: v for key, v in complete(dict(up_w)).items() if key not in up_w}
-    gate_all = gate_all + [([key], cores(v[0])) for key, v in gate_rest.items()]
-    diag, up_all, up_rest, gate_all, down_own = tie((diag, up_all, up_rest, gate_all, down_own))
+    open_all = open_all + single({top: open_top, **late})
+    down_last = req(down_own, last)
+    diag, open_all, down_own, down_last = tie((diag, open_all, down_own, down_last))
     normed = [own_normed, next_x, next_y] + diag
 
-    opened = expand(place, normed, *gather(gate_all, n_req))
-    up_all = up_all + [([key], cores(v[0])) for key, v in up_rest.items()]
-    down_top, down_last = req(down_own, top), req(down_own, last)
-    near = [([0], cores(down_own))]
-    opened, up_all, near = tie((opened, up_all, near))
-    acts = expand(place, normed, *gather(up_all, n_req), opened)
-    acts, down_top, down_last = tie((acts, down_top, down_last))
-    down_w = complete({0: (down_own, 0), last: (down_last, 0), top: (down_top, 0)})
-    near = near + [([key], cores(v[0])) for key, v in down_w.items() if key and not key & top]
-    far = [([key], v[0]) for key, v in down_w.items() if key & top]
-
-    sums, parts = [], down(place, acts, *gather(near, top), top - 1)
+    acts = expand(place, normed, *gather(open_all, n_req, 2))
+    down_top = req(down_own, top)
+    near = single({0: down_own, last: down_last})
+    acts, near = tie((acts, near))
+    down_w = complete({0: down_own, last: down_last}) if n_req > 16 else {}
+    near = near + single({key: v for key, v in down_w.items() if key not in (0, last)})
+    parts = down(place, acts, *gather(near, top, 1), top - 1)
+    parts, down_top = tie((parts, down_top))
+    down_w = complete({top: down_top})
+    far = {key: v for key, v in down_w.items() if key & top}
+
+    sums = []
     for piece in range(2):
         own, to_x, to_y, keep_x, keep_y = parts
         from_x, from_y = req(to_x, key_x), req(to_y, key_y)
+        late_y = (keep_y + from_x[half:].astype(jnp.float32)).astype(jnp.bfloat16)
+        late_x = (keep_x + from_y[half:].astype(jnp.float32)).astype(jnp.bfloat16)
         if piece == 0:
-            far, from_x, from_y = tie((far, from_x, from_y))
-            far = [(keys, cores(array)) for keys, array in far]
-            parts = down(place, acts, *gather(far, top), top - 1)
-        late_y = keep_y + from_x[half:].astype(jnp.float32)
-        late_x = keep_x + from_y[half:].astype(jnp.float32)
-        late_y = req(late_y.astype(jnp.bfloat16), key_y)
-        late_x = req(late_x.astype(jnp.bfloat16), key_x)
+            far, late_x, late_y = tie((far, late_x, late_y))
+            parts = down(place, acts, *gather(single(far), top, 1), top - 1)
+        late_y, late_x = req(late_y, key_y), req(late_x, key_x)
+        if piece == 0:
+            parts, late_y, late_x = tie((parts, late_y, late_x))
         sums.append([own, from_x, from_y, late_x, late_y])
     return finish(upper, resid, sums)
 

time: 291 us -> 283 us (0.973)
  Pallas kernels: 79.1 us -> 67.5 us
  waiting for transfers between devices: 138 us -> 142 us
    pallas_call x2 -> x1, Pallas kernels: 26.8 us -> 19.7 us  [expand(): pl.pallas_call(functools.partial(expand_kernel, n_parts=n_parts, keys=key...]
    pallas_call x6 -> x4, Pallas kernels: 8.48 us -> 3.6 us  [move(): pl.pallas_call(functools.partial(move_kernel, n_in=len(arrays), plan=plan...]
    ppermute x41 -> x39, waiting for transfers between devices: 138 us -> 142 us  [swap(): return lax.ppermute(value, axis, [(i, i ^ bits) for i in range(size)])]
    unnamed x50 -> x56, local copies, waits for them, and re-layouts: 13.6 us -> 11.1 us
    ppermute x41 -> x39, starting transfers between devices: 41.3 us -> 42.8 us  [swap(): return lax.ppermute(value, axis, [(i, i ^ bits) for i in range(size)])]
  transfers between devices with their start and end apart: 41 -> 39, of which waited for: 24 -> 21; matrix products, arithmetic and copies ran while one was open for 6% -> 6% of each run, Pallas kernels for 23% -> 23%
where the time goes in v4:
time: 283 us; the launch traced here: 282 us
  waiting for transfers between devices  142 us (50%)
  Pallas kernels  67.5 us (24%)
  starting transfers between devices  42.8 us (15%)
  local copies, waits for them, and re-layouts  15.3 us (5%)
  other arithmetic  13 us (5%)
    ppermute x39, waiting for transfers between devices, swap(): return lax.ppermute(value, axis, [(i, i ^ bits) for i in range(size)])  142 us
    ppermute x39, starting transfers between devices, swap(): return lax.ppermute(value, axis, [(i, i ^ bits) for i in range(size)])  42.8 us
    pallas_call x1, Pallas kernels, expand(): pl.pallas_call(functools.partial(expand_kernel, n_parts=n_parts, keys=key...  19.7 us
    pallas_call x1, Pallas kernels, attention(): pl.pallas_call(attention_kernel, grid=(count,), in_specs=[same(tok_count,...  14.6 us
    pallas_call x2, Pallas kernels, down(): pl.pallas_call(functools.partial(down_kernel, n_parts=n_parts, keys=keys,...  13.9 us
    unnamed x56, local copies, waits for them, and re-layouts  11.1 us
    pallas_call x1, Pallas kernels, project(): pl.pallas_call(functools.partial(project_kernel, n_parts=n_parts, n_mlp=n...  8.99 us
  transfers between devices with their start and end apart: 39, of which 21 were waited for; matrix products, arithmetic and copies ran while one was open for 6% of the time, Pallas kernels for 23%

profile of v4, /device:TPU:0, one launch (start us, length us, event | category | flops | bytes accessed | tf_op | source)
XLA Modules:
  0.0 281.9 jit_solution(6695311516175075936)
XLA Ops:
  0.0 3.0 %collective-permute-start = (bf16[2,64,512]{2,1,0:T(8,128)(2,1)}, bf16[2,64,512]{2,1,0:T(8,128)(2,1)S(1)}, u32[]{:S(2)}, u32[]{:S(2)}) collective-permute-start(bf16[2,64,512]{2,1,0:T(8,128)(2,1)} %param.16), channel_id=1, source_target_pairs={{0,8},{2,10},{4,12},{6,14},{8,0},{10,2},{12,4},{14,6},{16,24},{18,... | collective-permute-start | bytes 393224 | tf_op jit(solution)/shard_map/ppermute | solution.py:449
  3.0 2.6 collective-permute-start.1
  8.2 1.8 collective-permute-start.7
  12.9 1.8 fusion
  14.8 1.4 collective-permute-done.1
  17.0 1.5 collective-permute-start.4
  18.6 1.4 collective-permute-start.5
  20.6 2.9 %collective-permute-start.9 = (bf16[2,160,640]{2,1,0:T(8,128)(2,1)S(1)}, bf16[2,160,640]{2,1,0:T(8,128)(2,1)S(1)}, u32[]{:S(2)}, u32[]{:S(2)}) collective-permute-start(bf16[2,160,640]{2,1,0:T(8,128)(2,1)S(1)} %get-tuple-element.104), channel_id=1, source_target_pairs={{0,10},{2,8},{4,14},{6,12},{8,2},{10,0},{12,6},{14,4},{16,26},{18,... | collective-permute-start | bytes 1228808 | tf_op jit(solution)/shard_map/ppermute | solution.py:449
  27.5 5.1 %collective-permute-done.9.refs_3_ = bf16[2,160,640]{2,1,0:T(8,128)(2,1)S(1)} collective-permute-done((bf16[2,160,640]{2,1,0:T(8,128)(2,1)S(1)}, bf16[2,160,640]{2,1,0:T(8,128)(2,1)S(1)}, u32[]{:S(2)}, u32[]{:S(2)}) %collective-permute-start.9) | collective-permute-done | bytes 409632 | tf_op jit(solution)/shard_map/ppermute | solution.py:449
  35.3 2.2 merge.2.refs_5_
  37.5 1.6 collective-permute-start.10
  39.0 1.5 collective-permute-start.11
  40.5 2.9 %collective-permute-done.5 = bf16[4,2,64,512]{3,2,1,0:T(8,128)(2,1)} collective-permute-done((bf16[4,2,64,512]{3,2,1,0:T(8,128)(2,1)}, bf16[4,2,64,512]{3,2,1,0:T(8,128)(2,1)}, u32[]{:S(2)}, u32[]{:S(2)}) %collective-permute-start.5) | collective-permute-done | bytes 524320 | tf_op jit(solution)/shard_map/ppermute | solution.py:449
  43.4 6.9 %collective-permute-done.3 = bf16[4,2,64,512]{3,2,1,0:T(8,128)(2,1)} collective-permute-done((bf16[4,2,64,512]{3,2,1,0:T(8,128)(2,1)}, bf16[4,2,64,512]{3,2,1,0:T(8,128)(2,1)}, u32[]{:S(2)}, u32[]{:S(2)}) %collective-permute-start.3) | collective-permute-done | bytes 524320 | tf_op jit(solution)/shard_map/ppermute | solution.py:449
  50.3 3.2 %pad_maximum_fusion = bf16[4,4,2,64,512]{4,3,2,1,0:T(8,128)(2,1)} fusion(bf16[1,4,2,64,512]{4,3,2,1,0:T(8,128)(2,1)} %bitcast.11, bf16[1,4,2,64,512]{4,3,2,1,0:T(8,128)(2,1)} %bitcast.10, bf16[1,4,2,64,512]{4,3,2,1,0:T(8,128)(2,1)} %bitcast.9, bf16[1,4,2,64,512]{4,3,2,1,0:T(8,128)(2,1)} %bitcast.8), kind=kLoop, calls=%fused_computation.1 | loop fusion | flops 3145728 | bytes 4194304 | tf_op jit(solution)/shard_map/stack | solution.py:529
  53.5 3.3 %gather_fusion = bf16[8,2,64,512]{3,2,1,0:T(8,128)(2,1)} fusion(bf16[16,2,64,512]{3,2,1,0:T(8,128)(2,1)} %bitcast.27, s32[1024]{0:T(1024)S(1)} %pad_clamp_fusion), kind=kCustom, calls=%fused_computation | custom fusion | bytes 2097184 | tf_op jit(solution)/shard_map/jit(_take)/gather | solution.py:531
  56.8 1.4 broadcast_select_fusion.pk_ref.pv_ref
  58.2 14.6 %attention.1.refs_0_ = bf16[512,2048]{1,0:T(8,128)(2,1)S(1)} custom-call(s32[512,1]{1,0:T(8,128)S(1)} %subtract_subtract_fusion.start_ref, f32[512,128]{1,0:T(8,128)S(1)} %get-tuple-element.93.cos_ref, f32[512,128]{1,0:T(8,128)S(1)} %get-tuple-element.94.sin_ref, f32[1,128]{1,0:T(1,128)S(1)} %bitcast.25, f32[1,128]{1,0:T(1,128)S(1)} %bitcast.26, ...), custom_call_target="tpu_custom_call" | custom-call | flops 1024 | bytes 1024 | tf_op jit(solution)/shard_map/attention/pallas_call | solution.py:108
  72.9 9.0 %project.1 = (f32[256,2560]{1,0:T(8,128)S(1)}, bf16[256,2560]{1,0:T(8,128)(2,1)S(1)}) custom-call(s32[1]{0:T(128)} %bitcast.1.core, bf16[512,2048]{1,0:T(8,128)(2,1)S(1)} %attention.1.refs_0_, bf16[2048,2560]{1,0:T(8,128)(2,1)} %refs_1_.3), custom_call_target="tpu_custom_call" | custom-call | flops 1024 | bytes 1024 | tf_op jit(solution)/shard_map/project/pallas_call | solution.py:148
  81.9 1.5 copy-done.4
  83.5 1.6 collective-permute-start.12
  85.1 2.8 %collective-permute-start.13 = (bf16[1,160,640]{2,1,0:T(8,128)(2,1)S(1)}, bf16[1,160,640]{2,1,0:T(8,128)(2,1)S(1)}, u32[]{:S(2)}, u32[]{:S(2)}) collective-permute-start(bf16[1,160,640]{2,1,0:T(8,128)(2,1)S(1)} %get-tuple-element.108), channel_id=1, source_target_pairs={{0,8},{2,10},{4,12},{6,14},{8,0},{10,2},{12,4},{14,6},{16,24},{18,... | collective-permute-start | bytes 614408 | tf_op jit(solution)/shard_map/ppermute | solution.py:449
  87.9 2.3 collective-permute-start.14
  90.2 3.2 %normalize.1 = (bf16[256,2560]{1,0:T(8,128)(2,1)S(1)}, bf16[256,2560]{1,0:T(8,128)(2,1)S(1)}) custom-call(bf16[256,2560]{1,0:T(8,128)(2,1)S(1)} %copy-done.7, f32[1,2560]{1,0:T(1,128)S(1)} %broadcast_in_dim.56.gain, f32[256,2560]{1,0:T(8,128)} %copy-done.4, bf16[256,2560]{1,0:T(8,128)(2,1)S(1)} %collective-permute-done.6.refs_0_), custom_call_target="tpu_custom_call" | custom-call | flops 1024 | bytes 1024 | tf_op jit(solution)/shard_map/normalize/pallas_call | solution.py:187
  93.5 20.8 %collective-permute-done.13.refs_2_ = bf16[1,160,640]{2,1,0:T(8,128)(2,1)S(1)} collective-permute-done((bf16[1,160,640]{2,1,0:T(8,128)(2,1)S(1)}, bf16[1,160,640]{2,1,0:T(8,128)(2,1)S(1)}, u32[]{:S(2)}, u32[]{:S(2)}) %collective-permute-start.13) | collective-permute-done | bytes 204832 | tf_op jit(solution)/shard_map/ppermute | solution.py:449
  114.3 3.5 %collective-permute-done.14.refs_3_ = bf16[1,160,640]{2,1,0:T(8,128)(2,1)S(1)} collective-permute-done((bf16[1,160,640]{2,1,0:T(8,128)(2,1)S(1)}, bf16[1,160,640]{2,1,0:T(8,128)(2,1)S(1)}, u32[]{:S(2)}, u32[]{:S(2)}) %collective-permute-start.14) | collective-permute-done | bytes 204832 | tf_op jit(solution)/shard_map/ppermute | solution.py:449
  117.9 1.5 collective-permute-start.19
  119.4 2.3 collective-permute-start.15
  122.8 28.0 %collective-permute-done.15.refs_1_ = bf16[256,2560]{1,0:T(8,128)(2,1)S(1)} collective-permute-done((bf16[256,2560]{1,0:T(8,128)(2,1)S(1)}, bf16[256,2560]{1,0:T(8,128)(2,1)S(1)}, u32[]{:S(2)}, u32[]{:S(2)}) %collective-permute-start.15) | collective-permute-done | bytes 1310752 | tf_op jit(solution)/shard_map/ppermute | solution.py:449
  150.8 1.5 collective-permute-done.16.refs_2_
  152.3 4.0 %collective-permute-done.19.refs_8_ = bf16[2,4,160,640]{3,2,1,0:T(8,128)(2,1)S(1)} collective-permute-done((bf16[2,4,160,640]{3,2,1,0:T(8,128)(2,1)}, bf16[2,4,160,640]{3,2,1,0:T(8,128)(2,1)S(1)}, u32[]{:S(2)}, u32[]{:S(2)}) %collective-permute-start.19) | collective-permute-done | bytes 1638432 | tf_op jit(solution)/shard_map/ppermute | solution.py:449
  156.8 1.5 collective-permute-start.24
  158.9 2.0 collective-permute-start.21
  160.8 14.0 %collective-permute-done.20.refs_3_ = bf16[128,2560]{1,0:T(8,128)(2,1)S(1)} collective-permute-done((bf16[128,2560]{1,0:T(8,128)(2,1)S(1)}, bf16[128,2560]{1,0:T(8,128)(2,1)S(1)}, u32[]{:S(2)}, u32[]{:S(2)}) %collective-permute-start.20) | collective-permute-done | bytes 655392 | tf_op jit(solution)/shard_map/ppermute | solution.py:449
  175.5 1.5 collective-permute-done.24.refs_3_
  178.7 19.7 %gate_up.1 = (bf16[1024,640]{1,0:T(8,128)(2,1)S(1)}, bf16[1024,640]{1,0:T(8,128)(2,1)S(1)}) custom-call(s32[1]{0:T(128)} %bitcast.20.me, bf16[256,2560]{1,0:T(8,128)(2,1)S(1)} %get-tuple-element.110.refs_0_, bf16[256,2560]{1,0:T(8,128)(2,1)} %copy-done.17, bf16[256,2560]{1,0:T(8,128)(2,1)} %copy-done.18, ...), custom_call_target="tpu_custom_call" | custom-call | flops 1024 | bytes 1024 | tf_op jit(solution)/shard_map/gate_up/pallas_call | solution.py:336
  200.6 7.1 %down.2 = (f32[256,1280]{1,0:T(8,128)}, bf16[256,1280]{1,0:T(8,128)(2,1)S(1)}, bf16[256,1280]{1,0:T(8,128)(2,1)S(1)}, f32[128,1280]{1,0:T(8,128)S(1)}, f32[128,1280]{1,0:T(8,128)S(1)}) custom-call(s32[1]{0:T(128)} %bitcast.20.me, bf16[1024,640]{1,0:T(8,128)(2,1)} %copy-done.1, bf16[1024,640]{1,0:T(8,128)(2,1)} %copy-done.2, ...), custom_call_target="tpu_custom_call" | custom-call | flops 1024 | bytes 1024 | tf_op jit(solution)/shard_map/down/pallas_call | solution.py:403
  207.6 8.6 %collective-permute-done.27.refs_2_ = bf16[1,4,160,640]{3,2,1,0:T(8,128)(2,1)S(1)} collective-permute-done((bf16[1,4,160,640]{3,2,1,0:T(8,128)(2,1)S(1)}, bf16[1,4,160,640]{3,2,1,0:T(8,128)(2,1)S(1)}, u32[]{:S(2)}, u32[]{:S(2)}) %collective-permute-start.27) | collective-permute-done | bytes 819232 | tf_op jit(solution)/shard_map/ppermute | solution.py:449
  216.2 1.4 collective-permute-start.28
  218.6 14.3 %collective-permute-done.28.refs_1_ = bf16[256,1280]{1,0:T(8,128)(2,1)S(1)} collective-permute-done((bf16[256,1280]{1,0:T(8,128)(2,1)S(1)}, bf16[256,1280]{1,0:T(8,128)(2,1)S(1)}, u32[]{:S(2)}, u32[]{:S(2)}) %collective-permute-start.28) | collective-permute-done | bytes 655392 | tf_op jit(solution)/shard_map/ppermute | solution.py:449
  234.1 3.4 %collective-permute-done.30.refs_3_ = bf16[1,4,160,640]{3,2,1,0:T(8,128)(2,1)S(1)} collective-permute-done((bf16[1,4,160,640]{3,2,1,0:T(8,128)(2,1)S(1)}, bf16[1,4,160,640]{3,2,1,0:T(8,128)(2,1)S(1)}, u32[]{:S(2)}, u32[]{:S(2)}) %collective-permute-start.30) | collective-permute-done | bytes 819232 | tf_op jit(solution)/shard_map/ppermute | solution.py:449
  238.1 1.7 collective-permute-start.33
  241.1 6.9 %down.3 = (f32[256,1280]{1,0:T(8,128)}, bf16[256,1280]{1,0:T(8,128)(2,1)S(1)}, bf16[256,1280]{1,0:T(8,128)(2,1)S(1)}, f32[128,1280]{1,0:T(8,128)S(1)}, f32[128,1280]{1,0:T(8,128)S(1)}) custom-call(s32[1]{0:T(128)} %bitcast.20.me, bf16[1024,640]{1,0:T(8,128)(2,1)} %copy-done.1, bf16[1024,640]{1,0:T(8,128)(2,1)} %copy-done.2, ...), custom_call_target="tpu_custom_call" | custom-call | flops 1024 | bytes 1024 | tf_op jit(solution)/shard_map/down/pallas_call | solution.py:403
  250.4 14.4 %collective-permute-done.35.refs_6_ = bf16[256,1280]{1,0:T(8,128)(2,1)S(1)} collective-permute-done((bf16[256,1280]{1,0:T(8,128)(2,1)S(1)}, bf16[256,1280]{1,0:T(8,128)(2,1)S(1)}, u32[]{:S(2)}, u32[]{:S(2)}) %collective-permute-start.35) | collective-permute-done | bytes 655392 | tf_op jit(solution)/shard_map/ppermute | solution.py:449
  265.6 1.7 collective-permute-start.38
  268.7 6.1 %collective-permute-done.38.refs_9_ = bf16[128,1280]{1,0:T(8,128)(2,1)} collective-permute-done((bf16[128,1280]{1,0:T(8,128)(2,1)}, bf16[128,1280]{1,0:T(8,128)(2,1)}, u32[]{:S(2)}, u32[]{:S(2)}) %collective-permute-start.38) | collective-permute-done | bytes 327712 | tf_op jit(solution)/shard_map/ppermute | solution.py:449
  274.8 2.3 collective-permute-done.37.refs_8_
  278.4 3.5 %finish.1 = bf16[256,2560]{1,0:T(8,128)(2,1)} custom-call(s32[1]{0:T(128)} %bitcast.upper, bf16[256,2560]{1,0:T(8,128)(2,1)S(1)} %copy-done.6, f32[256,1280]{1,0:T(8,128)} %get-tuple-element.151.refs_0_, bf16[256,1280]{1,0:T(8,128)(2,1)S(1)} %collective-permute-done.28.refs_1_, bf16[256,1280]{1,0:T(8,128)(2,1)S(1)} %collective-permute-done.29.refs_2_, ...), custom_call_target="tpu_custom_call" | custom-call | flops 1024 | bytes 1024 | tf_op jit(solution)/shard_map/finish/pallas_call | solution.py:437
  (123 shorter events, 29.8 us)
Async XLA Ops:
  0.0 11.7 %copy-start.27 = (s32[16]{0:T(128)S(1)}, s32[16]{0:T(128)}, u32[]{:S(2)}) copy-start(s32[16]{0:T(128)} %param.27) | copy-start | bytes 196
  0.0 14.7 %collective-permute-start = (bf16[2,64,512]{2,1,0:T(8,128)(2,1)}, bf16[2,64,512]{2,1,0:T(8,128)(2,1)S(1)}, u32[]{:S(2)}, u32[]{:S(2)}) collective-permute-start(bf16[2,64,512]{2,1,0:T(8,128)(2,1)} %param.16), channel_id=1, source_target_pairs={{0,8},{2,10},{4,12},{6,14},{8,0},{10,2},{12,4},{14,6},{16,24},{18,... | collective-permute-start | bytes 393224 | tf_op jit(solution)/shard_map/ppermute | solution.py:449
  3.0 13.2 %collective-permute-start.1 = (bf16[2,64,512]{2,1,0:T(8,128)(2,1)}, bf16[2,64,512]{2,1,0:T(8,128)(2,1)S(1)}, u32[]{:S(2)}, u32[]{:S(2)}) collective-permute-start(bf16[2,64,512]{2,1,0:T(8,128)(2,1)} %param.16), channel_id=1, source_target_pairs={{0,16},{2,18},{4,20},{6,22},{8,24},{10,26},{12,28},{14,30},{16,0},... | collective-permute-start | bytes 393224 | tf_op jit(solution)/shard_map/ppermute | solution.py:449
  5.6 10.6 %collective-permute-start.2 = (bf16[2,64,512]{2,1,0:T(8,128)(2,1)}, bf16[2,64,512]{2,1,0:T(8,128)(2,1)S(1)}, u32[]{:S(2)}, u32[]{:S(2)}) collective-permute-start(bf16[2,64,512]{2,1,0:T(8,128)(2,1)} %param.16), channel_id=1, source_target_pairs={{0,24},{2,26},{4,28},{6,30},{8,16},{10,18},{12,20},{14,22},{16,8},... | collective-permute-start | bytes 393224 | tf_op jit(solution)/shard_map/ppermute | solution.py:449
  8.2 12.5 %collective-permute-start.7 = (bf16[2,160,640]{2,1,0:T(8,128)(2,1)S(1)}, bf16[2,160,640]{2,1,0:T(8,128)(2,1)S(1)}, u32[]{:S(2)}, u32[]{:S(2)}) collective-permute-start(bf16[2,160,640]{2,1,0:T(8,128)(2,1)S(1)} %get-tuple-element.102), channel_id=1, source_target_pairs={{0,2},{2,0},{4,6},{6,4},{8,10},{10,8},{12,14},{14,12},{16,18},{18,... | collective-permute-start | bytes 1228808 | tf_op jit(solution)/shard_map/ppermute | solution.py:449
  9.9 16.8 %collective-permute-start.8 = (bf16[2,160,640]{2,1,0:T(8,128)(2,1)S(1)}, bf16[2,160,640]{2,1,0:T(8,128)(2,1)S(1)}, u32[]{:S(2)}, u32[]{:S(2)}) collective-permute-start(bf16[2,160,640]{2,1,0:T(8,128)(2,1)S(1)} %get-tuple-element.103), channel_id=1, source_target_pairs={{0,8},{2,10},{4,12},{6,14},{8,0},{10,2},{12,4},{14,6},{16,24},{18,... | collective-permute-start | bytes 1228808 | tf_op jit(solution)/shard_map/ppermute | solution.py:449
  17.0 23.5 %collective-permute-start.4 = (bf16[4,2,64,512]{3,2,1,0:T(8,128)(2,1)}, bf16[4,2,64,512]{3,2,1,0:T(8,128)(2,1)}, u32[]{:S(2)}, u32[]{:S(2)}) collective-permute-start(bf16[4,2,64,512]{3,2,1,0:T(8,128)(2,1)} %pad_maximum_fusion.1), channel_id=1, source_target_pairs={{0,4},{2,6},{4,0},{6,2},{8,12},{10,14},{12,8},{14,10},{16,20},{18,... | collective-permute-start | bytes 1572872 | tf_op jit(solution)/shard_map/ppermute | solution.py:449
  18.6 24.9 %collective-permute-start.5 = (bf16[4,2,64,512]{3,2,1,0:T(8,128)(2,1)}, bf16[4,2,64,512]{3,2,1,0:T(8,128)(2,1)}, u32[]{:S(2)}, u32[]{:S(2)}) collective-permute-start(bf16[4,2,64,512]{3,2,1,0:T(8,128)(2,1)} %pad_maximum_fusion.1), channel_id=1, source_target_pairs={{0,6},{2,4},{4,2},{6,0},{8,14},{10,12},{12,10},{14,8},{16,22},{18,... | collective-permute-start | bytes 1572872 | tf_op jit(solution)/shard_map/ppermute | solution.py:449
  20.0 30.3 %collective-permute-start.3 = (bf16[4,2,64,512]{3,2,1,0:T(8,128)(2,1)}, bf16[4,2,64,512]{3,2,1,0:T(8,128)(2,1)}, u32[]{:S(2)}, u32[]{:S(2)}) collective-permute-start(bf16[4,2,64,512]{3,2,1,0:T(8,128)(2,1)} %pad_maximum_fusion.1), channel_id=1, source_target_pairs={{0,2},{2,0},{4,6},{6,4},{8,10},{10,8},{12,14},{14,12},{16,18},{18,... | collective-permute-start | bytes 1572872 | tf_op jit(solution)/shard_map/ppermute | solution.py:449
  20.6 11.9 %collective-permute-start.9 = (bf16[2,160,640]{2,1,0:T(8,128)(2,1)S(1)}, bf16[2,160,640]{2,1,0:T(8,128)(2,1)S(1)}, u32[]{:S(2)}, u32[]{:S(2)}) collective-permute-start(bf16[2,160,640]{2,1,0:T(8,128)(2,1)S(1)} %get-tuple-element.104), channel_id=1, source_target_pairs={{0,10},{2,8},{4,14},{6,12},{8,2},{10,0},{12,6},{14,4},{16,26},{18,... | collective-permute-start | bytes 1228808 | tf_op jit(solution)/shard_map/ppermute | solution.py:449
  37.5 55.9 %copy-start = (bf16[2,4,160,640]{3,2,1,0:T(8,128)(2,1)}, bf16[2,4,160,640]{3,2,1,0:T(8,128)(2,1)S(1)}, u32[]{:S(2)}) copy-start(bf16[2,4,160,640]{3,2,1,0:T(8,128)(2,1)S(1)} %merge.2.refs_5_) | copy-start | bytes 4915204
  37.5 80.4 %collective-permute-start.10 = (bf16[2,4,160,640]{3,2,1,0:T(8,128)(2,1)S(1)}, bf16[2,4,160,640]{3,2,1,0:T(8,128)(2,1)}, u32[]{:S(2)}, u32[]{:S(2)}) collective-permute-start(bf16[2,4,160,640]{3,2,1,0:T(8,128)(2,1)S(1)} %merge.2.refs_5_), channel_id=1, source_target_pairs={{0,16},{2,18},{4,20},{6,22},{8,24},{10,26},{12,28},{14,30},{16,0},... | collective-permute-start | bytes 4915208 | tf_op jit(solution)/shard_map/ppermute | solution.py:449
  39.0 78.8 %collective-permute-start.11 = (bf16[2,4,160,640]{3,2,1,0:T(8,128)(2,1)S(1)}, bf16[2,4,160,640]{3,2,1,0:T(8,128)(2,1)}, u32[]{:S(2)}, u32[]{:S(2)}) collective-permute-start(bf16[2,4,160,640]{3,2,1,0:T(8,128)(2,1)S(1)} %merge.2.refs_5_), channel_id=1, source_target_pairs={{0,4},{2,6},{4,0},{6,2},{8,12},{10,14},{12,8},{14,10},{16,20},{18,... | collective-permute-start | bytes 4915208 | tf_op jit(solution)/shard_map/ppermute | solution.py:449
  72.8 17.3 %copy-start.25 = (f32[2560]{0:T(1024)S(1)}, f32[2560]{0:T(1024)}, u32[]{:S(2)}) copy-start(f32[2560]{0:T(1024)} %param.20) | copy-start | bytes 30724
  72.9 17.3 %copy-start.7 = (bf16[256,2560]{1,0:T(8,128)(2,1)S(1)}, bf16[256,2560]{1,0:T(8,128)(2,1)}, u32[]{:S(2)}) copy-start(bf16[256,2560]{1,0:T(8,128)(2,1)} %hidden.1) | copy-start | bytes 3932164
  83.4 4.5 %collective-permute-start.6 = (bf16[256,2560]{1,0:T(8,128)(2,1)S(1)}, bf16[256,2560]{1,0:T(8,128)(2,1)S(1)}, u32[]{:S(2)}, u32[]{:S(2)}) collective-permute-start(bf16[256,2560]{1,0:T(8,128)(2,1)S(1)} %get-tuple-element.98), channel_id=1, source_target_pairs={{0,1},{1,0},{2,3},{3,2},{4,5},{5,4},{6,7},{7,6},{8,9},{9,8},{10,11... | collective-permute-start | bytes 3932168 | tf_op jit(solution)/shard_map/ppermute | solution.py:449
  83.5 9.9 %collective-permute-start.12 = (bf16[1,160,640]{2,1,0:T(8,128)(2,1)S(1)}, bf16[1,160,640]{2,1,0:T(8,128)(2,1)S(1)}, u32[]{:S(2)}, u32[]{:S(2)}) collective-permute-start(bf16[1,160,640]{2,1,0:T(8,128)(2,1)S(1)} %get-tuple-element.107), channel_id=1, source_target_pairs={{0,2},{2,0},{4,6},{6,4},{8,10},{10,8},{12,14},{14,12},{16,18},{18,... | collective-permute-start | bytes 614408 | tf_op jit(solution)/shard_map/ppermute | solution.py:449
  85.1 29.2 %collective-permute-start.13 = (bf16[1,160,640]{2,1,0:T(8,128)(2,1)S(1)}, bf16[1,160,640]{2,1,0:T(8,128)(2,1)S(1)}, u32[]{:S(2)}, u32[]{:S(2)}) collective-permute-start(bf16[1,160,640]{2,1,0:T(8,128)(2,1)S(1)} %get-tuple-element.108), channel_id=1, source_target_pairs={{0,8},{2,10},{4,12},{6,14},{8,0},{10,2},{12,4},{14,6},{16,24},{18,... | collective-permute-start | bytes 614408 | tf_op jit(solution)/shard_map/ppermute | solution.py:449
  87.9 30.0 %collective-permute-start.14 = (bf16[1,160,640]{2,1,0:T(8,128)(2,1)S(1)}, bf16[1,160,640]{2,1,0:T(8,128)(2,1)S(1)}, u32[]{:S(2)}, u32[]{:S(2)}) collective-permute-start(bf16[1,160,640]{2,1,0:T(8,128)(2,1)S(1)} %get-tuple-element.109), channel_id=1, source_target_pairs={{0,10},{2,8},{4,14},{6,12},{8,2},{10,0},{12,6},{14,4},{16,26},{18,... | collective-permute-start | bytes 614408 | tf_op jit(solution)/shard_map/ppermute | solution.py:449
  93.4 65.5 %copy-start.5 = (bf16[256,2560]{1,0:T(8,128)(2,1)}, bf16[256,2560]{1,0:T(8,128)(2,1)S(1)}, u32[]{:S(2)}) copy-start(bf16[256,2560]{1,0:T(8,128)(2,1)S(1)} %get-tuple-element.99.resid) | copy-start | bytes 3932164
  93.4 29.4 %collective-permute-start.17 = (bf16[2,4,160,640]{3,2,1,0:T(8,128)(2,1)S(1)}, bf16[2,4,160,640]{3,2,1,0:T(8,128)(2,1)S(1)}, u32[]{:S(2)}, u32[]{:S(2)}) collective-permute-start(bf16[2,4,160,640]{3,2,1,0:T(8,128)(2,1)S(1)} %merge.2.refs_5_), channel_id=1, source_target_pairs={{0,1},{1,0},{2,3},{3,2},{4,5},{5,4},{6,7},{7,6},{8,9},{9,8},{10,11... | collective-permute-start | bytes 4915208 | tf_op jit(solution)/shard_map/ppermute | solution.py:449
  117.9 34.4 %collective-permute-start.18 = (bf16[2,4,160,640]{3,2,1,0:T(8,128)(2,1)}, bf16[2,4,160,640]{3,2,1,0:T(8,128)(2,1)S(1)}, u32[]{:S(2)}, u32[]{:S(2)}) collective-permute-start(bf16[2,4,160,640]{3,2,1,0:T(8,128)(2,1)} %collective-permute-done.11.refs_6_), channel_id=1, source_target_pairs={{0,1},{1,0},{2,3},{3,2},{4,5},{5,4},{6,7},{7,6},{8,9},{9,8},{10,11... | collective-permute-start | bytes 4915208 | tf_op jit(solution)/shard_map/ppermute | solution.py:449
  117.9 38.4 %collective-permute-start.19 = (bf16[2,4,160,640]{3,2,1,0:T(8,128)(2,1)}, bf16[2,4,160,640]{3,2,1,0:T(8,128)(2,1)S(1)}, u32[]{:S(2)}, u32[]{:S(2)}) collective-permute-start(bf16[2,4,160,640]{3,2,1,0:T(8,128)(2,1)} %collective-permute-done.10.refs_7_), channel_id=1, source_target_pairs={{0,4},{2,6},{4,0},{6,2},{8,12},{10,14},{12,8},{14,10},{16,20},{18,... | collective-permute-start | bytes 4915208 | tf_op jit(solution)/shard_map/ppermute | solution.py:449
  119.4 31.4 %collective-permute-start.15 = (bf16[256,2560]{1,0:T(8,128)(2,1)S(1)}, bf16[256,2560]{1,0:T(8,128)(2,1)S(1)}, u32[]{:S(2)}, u32[]{:S(2)}) collective-permute-start(bf16[256,2560]{1,0:T(8,128)(2,1)S(1)} %get-tuple-element.110.refs_0_), channel_id=1, source_target_pairs={{0,2},{2,0},{4,6},{6,4},{8,10},{10,8},{12,14},{14,12},{16,18},{18,... | collective-permute-start | bytes 3932168 | tf_op jit(solution)/shard_map/ppermute | solution.py:449
  121.7 30.6 %collective-permute-start.16 = (bf16[256,2560]{1,0:T(8,128)(2,1)S(1)}, bf16[256,2560]{1,0:T(8,128)(2,1)S(1)}, u32[]{:S(2)}, u32[]{:S(2)}) collective-permute-start(bf16[256,2560]{1,0:T(8,128)(2,1)S(1)} %get-tuple-element.110.refs_0_), channel_id=1, source_target_pairs={{0,8},{2,10},{4,12},{6,14},{8,0},{10,2},{12,4},{14,6},{16,24},{18,... | collective-permute-start | bytes 3932168 | tf_op jit(solution)/shard_map/ppermute | solution.py:449
  122.8 55.7 %copy-start.19 = (bf16[2,4,160,640]{3,2,1,0:T(8,128)(2,1)}, bf16[2,4,160,640]{3,2,1,0:T(8,128)(2,1)S(1)}, u32[]{:S(2)}) copy-start(bf16[2,4,160,640]{3,2,1,0:T(8,128)(2,1)S(1)} %collective-permute-done.17.refs_9_) | copy-start | bytes 4915204
  150.8 27.7 %copy-start.17 = (bf16[256,2560]{1,0:T(8,128)(2,1)}, bf16[256,2560]{1,0:T(8,128)(2,1)S(1)}, u32[]{:S(2)}) copy-start(bf16[256,2560]{1,0:T(8,128)(2,1)S(1)} %collective-permute-done.15.refs_1_) | copy-start | bytes 3932164
  152.3 26.2 %copy-start.18 = (bf16[256,2560]{1,0:T(8,128)(2,1)}, bf16[256,2560]{1,0:T(8,128)(2,1)S(1)}, u32[]{:S(2)}) copy-start(bf16[256,2560]{1,0:T(8,128)(2,1)S(1)} %collective-permute-done.16.refs_2_) | copy-start | bytes 3932164
  156.3 20.7 %copy-start.21 = (bf16[2,4,160,640]{3,2,1,0:T(8,128)(2,1)}, bf16[2,4,160,640]{3,2,1,0:T(8,128)(2,1)S(1)}, u32[]{:S(2)}) copy-start(bf16[2,4,160,640]{3,2,1,0:T(8,128)(2,1)S(1)} %collective-permute-done.19.refs_8_) | copy-start | bytes 4915204
  156.3 20.7 %collective-permute-start.22 = (bf16[2,4,160,640]{3,2,1,0:T(8,128)(2,1)}, bf16[2,4,160,640]{3,2,1,0:T(8,128)(2,1)S(1)}, u32[]{:S(2)}, u32[]{:S(2)}) collective-permute-start(bf16[2,4,160,640]{3,2,1,0:T(8,128)(2,1)} %collective-permute-done.10.refs_7_), channel_id=1, source_target_pairs={{0,1},{1,0},{2,3},{3,2},{4,5},{5,4},{6,7},{7,6},{8,9},{9,8},{10,11... | collective-permute-start | bytes 4915208 | tf_op jit(solution)/shard_map/ppermute | solution.py:449
  156.3 20.7 %collective-permute-start.23 = (bf16[2,4,160,640]{3,2,1,0:T(8,128)(2,1)S(1)}, bf16[2,4,160,640]{3,2,1,0:T(8,128)(2,1)S(1)}, u32[]{:S(2)}, u32[]{:S(2)}) collective-permute-start(bf16[2,4,160,640]{3,2,1,0:T(8,128)(2,1)S(1)} %collective-permute-done.19.refs_8_), channel_id=1, source_target_pairs={{0,1},{1,0},{2,3},{3,2},{4,5},{5,4},{6,7},{7,6},{8,9},{9,8},{10,11... | collective-permute-start | bytes 4915208 | tf_op jit(solution)/shard_map/ppermute | solution.py:449
  156.8 20.2 %collective-permute-start.24 = (bf16[1,4,160,640]{3,2,1,0:T(8,128)(2,1)S(1)}, bf16[1,4,160,640]{3,2,1,0:T(8,128)(2,1)S(1)}, u32[]{:S(2)}, u32[]{:S(2)}) collective-permute-start(bf16[1,4,160,640]{3,2,1,0:T(8,128)(2,1)S(1)} %merge.3.refs_2_), channel_id=1, source_target_pairs={{0,4},{2,6},{4,0},{6,2},{8,12},{10,14},{12,8},{14,10},{16,20},{18,... | collective-permute-start | bytes 2457608 | tf_op jit(solution)/shard_map/ppermute | solution.py:449
  158.4 16.4 %collective-permute-start.20 = (bf16[128,2560]{1,0:T(8,128)(2,1)S(1)}, bf16[128,2560]{1,0:T(8,128)(2,1)S(1)}, u32[]{:S(2)}, u32[]{:S(2)}) collective-permute-start(bf16[128,2560]{1,0:T(8,128)(2,1)S(1)} %slice.18), channel_id=1, source_target_pairs={{0,8},{2,10},{4,12},{6,14},{8,0},{10,2},{12,4},{14,6},{16,24},{18,... | collective-permute-start | bytes 1966088 | tf_op jit(solution)/shard_map/ppermute | solution.py:449
  158.9 16.6 %collective-permute-start.21 = (bf16[128,2560]{1,0:T(8,128)(2,1)S(1)}, bf16[128,2560]{1,0:T(8,128)(2,1)S(1)}, u32[]{:S(2)}, u32[]{:S(2)}) collective-permute-start(bf16[128,2560]{1,0:T(8,128)(2,1)S(1)} %slice.19), channel_id=1, source_target_pairs={{0,2},{2,0},{4,6},{6,4},{8,10},{10,8},{12,14},{14,12},{16,18},{18,... | collective-permute-start | bytes 1966088 | tf_op jit(solution)/shard_map/ppermute | solution.py:449
  177.0 23.6 %collective-permute-start.25 = (bf16[1,4,160,640]{3,2,1,0:T(8,128)(2,1)S(1)}, bf16[1,4,160,640]{3,2,1,0:T(8,128)(2,1)S(1)}, u32[]{:S(2)}, u32[]{:S(2)}) collective-permute-start(bf16[1,4,160,640]{3,2,1,0:T(8,128)(2,1)S(1)} %merge.3.refs_2_), channel_id=1, source_target_pairs={{0,1},{1,0},{2,3},{3,2},{4,5},{5,4},{6,7},{7,6},{8,9},{9,8},{10,11... | collective-permute-start | bytes 2457608 | tf_op jit(solution)/shard_map/ppermute | solution.py:449
  177.1 23.5 %collective-permute-start.26 = (bf16[1,4,160,640]{3,2,1,0:T(8,128)(2,1)S(1)}, bf16[1,4,160,640]{3,2,1,0:T(8,128)(2,1)S(1)}, u32[]{:S(2)}, u32[]{:S(2)}) collective-permute-start(bf16[1,4,160,640]{3,2,1,0:T(8,128)(2,1)S(1)} %collective-permute-done.24.refs_3_), channel_id=1, source_target_pairs={{0,1},{1,0},{2,3},{3,2},{4,5},{5,4},{6,7},{7,6},{8,9},{9,8},{10,11... | collective-permute-start | bytes 2457608 | tf_op jit(solution)/shard_map/ppermute | solution.py:449
  177.6 38.7 %collective-permute-start.27 = (bf16[1,4,160,640]{3,2,1,0:T(8,128)(2,1)S(1)}, bf16[1,4,160,640]{3,2,1,0:T(8,128)(2,1)S(1)}, u32[]{:S(2)}, u32[]{:S(2)}) collective-permute-start(bf16[1,4,160,640]{3,2,1,0:T(8,128)(2,1)S(1)} %merge.3.refs_2_), channel_id=1, source_target_pairs={{0,16},{2,18},{4,20},{6,22},{8,24},{10,26},{12,28},{14,30},{16,0},... | collective-permute-start | bytes 2457608 | tf_op jit(solution)/shard_map/ppermute | solution.py:449
  216.2 16.7 %collective-permute-start.28 = (bf16[256,1280]{1,0:T(8,128)(2,1)S(1)}, bf16[256,1280]{1,0:T(8,128)(2,1)S(1)}, u32[]{:S(2)}, u32[]{:S(2)}) collective-permute-start(bf16[256,1280]{1,0:T(8,128)(2,1)S(1)} %get-tuple-element.152), channel_id=1, source_target_pairs={{0,2},{2,0},{4,6},{6,4},{8,10},{10,8},{12,14},{14,12},{16,18},{18,... | collective-permute-start | bytes 1966088 | tf_op jit(solution)/shard_map/ppermute | solution.py:449
  217.7 16.4 %collective-permute-start.29 = (bf16[256,1280]{1,0:T(8,128)(2,1)S(1)}, bf16[256,1280]{1,0:T(8,128)(2,1)S(1)}, u32[]{:S(2)}, u32[]{:S(2)}) collective-permute-start(bf16[256,1280]{1,0:T(8,128)(2,1)S(1)} %get-tuple-element.153), channel_id=1, source_target_pairs={{0,8},{2,10},{4,12},{6,14},{8,0},{10,2},{12,4},{14,6},{16,24},{18,... | collective-permute-start | bytes 1966088 | tf_op jit(solution)/shard_map/ppermute | solution.py:449
  217.7 19.9 %collective-permute-start.30 = (bf16[1,4,160,640]{3,2,1,0:T(8,128)(2,1)S(1)}, bf16[1,4,160,640]{3,2,1,0:T(8,128)(2,1)S(1)}, u32[]{:S(2)}, u32[]{:S(2)}) collective-permute-start(bf16[1,4,160,640]{3,2,1,0:T(8,128)(2,1)S(1)} %collective-permute-done.27.refs_2_), channel_id=1, source_target_pairs={{0,4},{2,6},{4,0},{6,2},{8,12},{10,14},{12,8},{14,10},{16,20},{18,... | collective-permute-start | bytes 2457608 | tf_op jit(solution)/shard_map/ppermute | solution.py:449
  237.6 2.9 %collective-permute-start.31 = (bf16[1,4,160,640]{3,2,1,0:T(8,128)(2,1)S(1)}, bf16[1,4,160,640]{3,2,1,0:T(8,128)(2,1)S(1)}, u32[]{:S(2)}, u32[]{:S(2)}) collective-permute-start(bf16[1,4,160,640]{3,2,1,0:T(8,128)(2,1)S(1)} %collective-permute-done.27.refs_2_), channel_id=1, source_target_pairs={{0,1},{1,0},{2,3},{3,2},{4,5},{5,4},{6,7},{7,6},{8,9},{9,8},{10,11... | collective-permute-start | bytes 2457608 | tf_op jit(solution)/shard_map/ppermute | solution.py:449
  237.6 3.5 %collective-permute-start.32 = (bf16[1,4,160,640]{3,2,1,0:T(8,128)(2,1)S(1)}, bf16[1,4,160,640]{3,2,1,0:T(8,128)(2,1)S(1)}, u32[]{:S(2)}, u32[]{:S(2)}) collective-permute-start(bf16[1,4,160,640]{3,2,1,0:T(8,128)(2,1)S(1)} %collective-permute-done.30.refs_3_), channel_id=1, source_target_pairs={{0,1},{1,0},{2,3},{3,2},{4,5},{5,4},{6,7},{7,6},{8,9},{9,8},{10,11... | collective-permute-start | bytes 2457608 | tf_op jit(solution)/shard_map/ppermute | solution.py:449
  238.1 9.9 %collective-permute-start.33 = (bf16[128,1280]{1,0:T(8,128)(2,1)S(1)}, bf16[128,1280]{1,0:T(8,128)(2,1)S(1)}, u32[]{:S(2)}, u32[]{:S(2)}) collective-permute-start(bf16[128,1280]{1,0:T(8,128)(2,1)S(1)} %add_convert_fusion.2), channel_id=1, source_target_pairs={{0,8},{2,10},{4,12},{6,14},{8,0},{10,2},{12,4},{14,6},{16,24},{18,... | collective-permute-start | bytes 983048 | tf_op jit(solution)/shard_map/ppermute | solution.py:449
  239.8 9.3 %collective-permute-start.34 = (bf16[128,1280]{1,0:T(8,128)(2,1)S(1)}, bf16[128,1280]{1,0:T(8,128)(2,1)S(1)}, u32[]{:S(2)}, u32[]{:S(2)}) collective-permute-start(bf16[128,1280]{1,0:T(8,128)(2,1)S(1)} %add_convert_fusion.3), channel_id=1, source_target_pairs={{0,2},{2,0},{4,6},{6,4},{8,10},{10,8},{12,14},{14,12},{16,18},{18,... | collective-permute-start | bytes 983048 | tf_op jit(solution)/shard_map/ppermute | solution.py:449
  249.2 15.6 %collective-permute-start.35 = (bf16[256,1280]{1,0:T(8,128)(2,1)S(1)}, bf16[256,1280]{1,0:T(8,128)(2,1)S(1)}, u32[]{:S(2)}, u32[]{:S(2)}) collective-permute-start(bf16[256,1280]{1,0:T(8,128)(2,1)S(1)} %get-tuple-element.169), channel_id=1, source_target_pairs={{0,2},{2,0},{4,6},{6,4},{8,10},{10,8},{12,14},{14,12},{16,18},{18,... | collective-permute-start | bytes 1966088 | tf_op jit(solution)/shard_map/ppermute | solution.py:449
  249.8 17.6 %collective-permute-start.36 = (bf16[256,1280]{1,0:T(8,128)(2,1)S(1)}, bf16[256,1280]{1,0:T(8,128)(2,1)S(1)}, u32[]{:S(2)}, u32[]{:S(2)}) collective-permute-start(bf16[256,1280]{1,0:T(8,128)(2,1)S(1)} %get-tuple-element.170), channel_id=1, source_target_pairs={{0,8},{2,10},{4,12},{6,14},{8,0},{10,2},{12,4},{14,6},{16,24},{18,... | collective-permute-start | bytes 1966088 | tf_op jit(solution)/shard_map/ppermute | solution.py:449
  265.6 9.2 %collective-permute-start.38 = (bf16[128,1280]{1,0:T(8,128)(2,1)}, bf16[128,1280]{1,0:T(8,128)(2,1)}, u32[]{:S(2)}, u32[]{:S(2)}) collective-permute-start(bf16[128,1280]{1,0:T(8,128)(2,1)} %add_convert_fusion), channel_id=1, source_target_pairs={{0,8},{2,10},{4,12},{6,14},{8,0},{10,2},{12,4},{14,6},{16,24},{18,... | collective-permute-start | bytes 983048 | tf_op jit(solution)/shard_map/ppermute | solution.py:449
  268.1 9.0 %collective-permute-start.37 = (bf16[128,1280]{1,0:T(8,128)(2,1)}, bf16[128,1280]{1,0:T(8,128)(2,1)}, u32[]{:S(2)}, u32[]{:S(2)}) collective-permute-start(bf16[128,1280]{1,0:T(8,128)(2,1)} %add_convert_fusion.1), channel_id=1, source_target_pairs={{0,2},{2,0},{4,6},{6,4},{8,10},{10,8},{12,14},{14,12},{16,18},{18,... | collective-permute-start | bytes 983048 | tf_op jit(solution)/shard_map/ppermute | solution.py:449
  (19 other events, 64.2 us)

commit v5 on v4

--- a/solution.py
+++ b/solution.py
@@ -168,7 +168,8 @@
 
 
 def normalize_kernel(hidden, gain, own, *refs):
-    parts, resid_ref, normed_ref = refs[:-2], refs[-2], refs[-1]
+    parts, (resid_ref, low_ref, high_ref) = refs[:-3], refs[-3:]
+    step, middle = pl.program_id(0), pl.num_programs(0) // 2
     total = hidden[...].astype(jnp.float32) + own[...]
     for part in parts:
         total = total + part[...].astype(jnp.float32)
@@ -176,20 +177,31 @@
     resid_ref[...] = resid
     values = resid.astype(jnp.float32)
     mean_sq = jnp.mean(values * values, axis=-1, keepdims=True)
-    normed = values * lax.rsqrt(mean_sq + EPSILON) * gain[...]
-    normed_ref[...] = normed.astype(normed_ref.dtype)
+    normed = (values * lax.rsqrt(mean_sq + EPSILON) * gain[...]).astype(low_ref.dtype)
+
+    @pl.when(step < middle)
+    def _():
+        low_ref[...] = normed
+
+    @pl.when(step >= middle)
+    def _():
+        high_ref[...] = normed
 
 
 def normalize(hidden, gain, own, parts):
     rows, columns = hidden.shape
-    tile = min(64, rows)
+    tile = min(64, rows // 2)
+    middle = rows // 2 // tile
     spec = pl.BlockSpec((tile, columns), lambda i: (i, 0))
+    low = pl.BlockSpec((tile, columns), lambda i: (jnp.minimum(i, middle - 1), 0))
+    high = pl.BlockSpec((tile, columns), lambda i: (jnp.maximum(i - middle, 0), 0))
+    halves = jax.ShapeDtypeStruct((rows // 2, columns), hidden.dtype)
     return pl.pallas_call(
         normalize_kernel,
-        grid=(rows // tile,),
+        grid=(2 * middle,),
         in_specs=[spec, pl.BlockSpec((1, columns), lambda i: (0, 0)), spec] + [spec] * len(parts),
-        out_specs=[spec, spec],
-        out_shape=[jax.ShapeDtypeStruct(hidden.shape, hidden.dtype)] * 2,
+        out_specs=[spec, low, high],
+        out_shape=[jax.ShapeDtypeStruct(hidden.shape, hidden.dtype), halves, halves],
         compiler_params=pltpu.CompilerParams(vmem_limit_bytes=VMEM_LIMIT),
         cost_estimate=SHORT,
         name="normalize",
@@ -282,13 +294,13 @@
 
 def expand_kernel(me, *refs, n_parts, keys):
     n_weights = n_parts * len(keys)
-    x_refs, refs = refs[: GROUP + 1], refs[GROUP + 1 :]
+    x_refs, refs = refs[: 2 * GROUP], refs[2 * GROUP :]
     w_refs, outs, refs = refs[:n_weights], refs[n_weights : n_weights + n_parts], refs[n_weights + n_parts :]
     x_all, gate_w, up_w, opened, x_sems, gate_sems, up_sems = refs
     width = outs[0].shape[1]
-    rows, depth = x_refs[0].shape
-    places = [x_all.at[i] for i in range(GROUP - 1)]
-    places += [x_all.at[GROUP - 1, pl.ds(i * rows // 2, rows // 2)] for i in range(2)]
+    half, depth = x_refs[0].shape
+    rows = 2 * half
+    places = [x_all.at[i // 2, pl.ds(i % 2 * half, half)] for i in range(2 * GROUP)]
     first = weight_copies(me[0], w_refs, keys, 0, gate_w, -1, gate_sems)
     first += [
         pltpu.make_async_copy(x_ref, place, x_sems.at[i])
@@ -326,7 +338,7 @@
 
 
 def expand(me, normed, keys, weights):
-    rows, depth = normed[0].shape
+    rows, depth = 2 * normed[0].shape[0], normed[0].shape[1]
     n_parts = len(weights)
     width = weights[0][0].shape[-1]
     total = rows * GROUP
@@ -525,6 +537,7 @@
     parts = list(cut(seat, [w_gate, w_up]))
     held, parts[3] = tie((held, parts[3]))
     open_w = merge(seat, trade(parts))
+    open_w, w_down_t = tie((open_w, w_down_t))
     last = others[-1]
     held = jnp.stack([held] + [req(held, k) for k in range(1, 4)])
     held = held.reshape(n_req, 2, PB, local_groups * HD)
@@ -538,33 +551,35 @@
 
     chosen, cosine, sine, start = tie((chosen, cosine, sine, start))
     attn = attention(start, cosine, sine, *gains, q_in, kv_in, chosen, 0, local_groups)
-    attn, w_down_t = tie((attn, w_down_t))
-    down_parts = trade(cut(seat, [w_down_t]))
+    attn, down_parts = tie((attn, trade(cut(seat, [w_down_t]))))
+    down_own = merge(seat, down_parts)
+    down_last = req(down_own, last)
 
     own_rows = hidden_in.shape[0]
     sums = project(core[None], [attn], w_out, n_mlp)
     parts = [swap(sums[k], "mlp", n_mlp, k) for k in range(1, n_mlp)]
-    resid, own_normed = normalize(hidden_in, post_gain[None], sums[0], parts)
-
-    own_normed, open_top, open_last, down_parts = tie(
-        (own_normed, open_top, open_last, down_parts)
+    resid, *own_normed = normalize(hidden_in, post_gain[None], sums[0], parts)
+
+    own_normed, open_top, open_last, down_own, down_last = tie(
+        (own_normed, open_top, open_last, down_own, down_last)
     )
 
     half = own_rows // 2
     key_x, key_y = PARTNERS[1:3]
-    next_x, next_y = req(own_normed, key_x), req(own_normed, key_y)
-    early = {0: open_w, last: open_last, top: open_top}
-    late = {key: array for key, array in complete(dict(early)).items() if key not in early}
-    open_all = single({0: open_w, last: open_last})
-    down_own = merge(seat, down_parts)
-    next_x, next_y, open_all, late, open_top, down_own = tie(
-        (next_x, next_y, open_all, late, open_top, down_own)
+    low, high = own_normed
+    low_x, high_y = req(low, key_x), req(high, key_y)
+    late = complete({0: open_w, last: open_last, top: open_top})
+    late = {key: late[key] for key in late if key not in (0, last, top)}
+    open_all = single({0: open_w})
+    low_x, high_y = tie((low_x, high_y))
+    high_x, low_y = req(high, key_x), req(low, key_y)
+    diag = [req(low_x, key_y), req(high_y, key_x)]
+    open_all = open_all + single({last: open_last, top: open_top})
+    diag, high_x, low_y, open_all, late, down_own, down_last = tie(
+        (diag, high_x, low_y, open_all, late, down_own, down_last)
     )
-    diag = [req(next_x[:half], key_y), req(next_y[half:], key_x)]
-    open_all = open_all + single({top: open_top, **late})
-    down_last = req(down_own, last)
-    diag, open_all, down_own, down_last = tie((diag, open_all, down_own, down_last))
-    normed = [own_normed, next_x, next_y] + diag
+    open_all = open_all + single(late)
+    normed = [low, high, low_x, high_x, low_y, high_y] + diag
 
     acts = expand(place, normed, *gather(open_all, n_req, 2))
     down_top = req(down_own, top)

time: 283 us -> 269 us (0.951)
  waiting for transfers between devices: 142 us -> 124 us
    ppermute x39 -> x41, waiting for transfers between devices: 142 us -> 124 us  [swap(): return lax.ppermute(value, axis, [(i, i ^ bits) for i in range(size)])]
    unnamed x56 -> x60, local copies, waits for them, and re-layouts: 11.1 us -> 13.7 us
    ppermute x39 -> x41, starting transfers between devices: 42.8 us -> 44.1 us  [swap(): return lax.ppermute(value, axis, [(i, i ^ bits) for i in range(size)])]
  transfers between devices with their start and end apart: 39 -> 41, of which waited for: 21 -> 22; matrix products, arithmetic and copies ran while one was open for 6% -> 6% of each run, Pallas kernels for 23% -> 24%
where the time goes in v5:
time: 269 us; the launch traced here: 268 us
  waiting for transfers between devices  124 us (46%)
  Pallas kernels  68.8 us (26%)
  starting transfers between devices  44.1 us (16%)
  local copies, waits for them, and re-layouts  17.9 us (7%)
  other arithmetic  11.9 us (4%)
    ppermute x41, waiting for transfers between devices, swap(): return lax.ppermute(value, axis, [(i, i ^ bits) for i in range(size)])  124 us
    ppermute x41, starting transfers between devices, swap(): return lax.ppermute(value, axis, [(i, i ^ bits) for i in range(size)])  44.1 us
    pallas_call x1, Pallas kernels, expand(): pl.pallas_call(functools.partial(expand_kernel, n_parts=n_parts, keys=key...  20.2 us
    pallas_call x1, Pallas kernels, attention(): pl.pallas_call(attention_kernel, grid=(count,), in_specs=[same(tok_count,...  14.6 us
    pallas_call x2, Pallas kernels, down(): pl.pallas_call(functools.partial(down_kernel, n_parts=n_parts, keys=keys,...  13.8 us
    unnamed x60, local copies, waits for them, and re-layouts  13.7 us
    pallas_call x1, Pallas kernels, project(): pl.pallas_call(functools.partial(project_kernel, n_parts=n_parts, n_mlp=n...  8.76 us
  transfers between devices with their start and end apart: 41, of which 22 were waited for; matrix products, arithmetic and copies ran while one was open for 6% of the time, Pallas kernels for 24%

profile of v5, /device:TPU:0, one launch (start us, length us, event | category | flops | bytes accessed | tf_op | source)
XLA Modules:
  0.0 267.8 jit_solution(6141638717950148108)
XLA Ops:
  0.0 3.0 %collective-permute-start = (bf16[2,64,512]{2,1,0:T(8,128)(2,1)}, bf16[2,64,512]{2,1,0:T(8,128)(2,1)S(1)}, u32[]{:S(2)}, u32[]{:S(2)}) collective-permute-start(bf16[2,64,512]{2,1,0:T(8,128)(2,1)} %param.16), channel_id=1, source_target_pairs={{0,8},{2,10},{4,12},{6,14},{8,0},{10,2},{12,4},{14,6},{16,24},{18,... | collective-permute-start | bytes 393224 | tf_op jit(solution)/shard_map/ppermute | solution.py:461
  3.0 2.6 collective-permute-start.1
  8.9 1.7 collective-permute-start.6
  13.6 1.8 fusion
  16.3 1.6 collective-permute-start.4
  17.9 1.4 collective-permute-start.5
  21.3 1.6 collective-permute-start.8
  26.8 6.2 %collective-permute-done.8.refs_3_ = bf16[2,160,640]{2,1,0:T(8,128)(2,1)S(1)} collective-permute-done((bf16[2,160,640]{2,1,0:T(8,128)(2,1)S(1)}, bf16[2,160,640]{2,1,0:T(8,128)(2,1)S(1)}, u32[]{:S(2)}, u32[]{:S(2)}) %collective-permute-start.8) | collective-permute-done | bytes 409632 | tf_op jit(solution)/shard_map/ppermute | solution.py:461
  37.8 2.2 merge.2.refs_8_
  40.8 1.5 collective-permute-start.14
  43.3 2.7 %collective-permute-start.10 = (bf16[1,160,640]{2,1,0:T(8,128)(2,1)}, bf16[1,160,640]{2,1,0:T(8,128)(2,1)}, u32[]{:S(2)}, u32[]{:S(2)}) collective-permute-start(bf16[1,160,640]{2,1,0:T(8,128)(2,1)} %get-tuple-element.102), channel_id=1, source_target_pairs={{0,8},{2,10},{4,12},{6,14},{8,0},{10,2},{12,4},{14,6},{16,24},{18,... | collective-permute-start | bytes 614408 | tf_op jit(solution)/shard_map/ppermute | solution.py:461
  46.2 9.2 %collective-permute-done.3 = bf16[4,2,64,512]{3,2,1,0:T(8,128)(2,1)} collective-permute-done((bf16[4,2,64,512]{3,2,1,0:T(8,128)(2,1)S(1)}, bf16[4,2,64,512]{3,2,1,0:T(8,128)(2,1)}, u32[]{:S(2)}, u32[]{:S(2)}) %collective-permute-start.3) | collective-permute-done | bytes 524320 | tf_op jit(solution)/shard_map/ppermute | solution.py:461
  55.4 1.5 collective-permute-start.9
  56.9 3.0 %pad_maximum_fusion = bf16[4,4,2,64,512]{4,3,2,1,0:T(8,128)(2,1)} fusion(bf16[1,4,2,64,512]{4,3,2,1,0:T(8,128)(2,1)} %bitcast.11, bf16[1,4,2,64,512]{4,3,2,1,0:T(8,128)(2,1)} %bitcast.10, bf16[1,4,2,64,512]{4,3,2,1,0:T(8,128)(2,1)} %bitcast.9, bf16[1,4,2,64,512]{4,3,2,1,0:T(8,128)(2,1)S(1)} %bitcast.28), kind=kLoop, calls=%fused_computation.1 | loop fusion | flops 3145728 | bytes 4194304 | tf_op jit(solution)/shard_map/stack | solution.py:542
  59.8 3.3 %gather_fusion = bf16[8,2,64,512]{3,2,1,0:T(8,128)(2,1)} fusion(bf16[16,2,64,512]{3,2,1,0:T(8,128)(2,1)} %bitcast.27, s32[1024]{0:T(1024)S(1)} %pad_clamp_fusion), kind=kCustom, calls=%fused_computation | custom fusion | bytes 2097184 | tf_op jit(solution)/shard_map/jit(_take)/gather | solution.py:544
  64.5 14.6 %attention.1.refs_0_ = bf16[512,2048]{1,0:T(8,128)(2,1)S(1)} custom-call(s32[512,1]{1,0:T(8,128)S(1)} %subtract_subtract_fusion.start_ref, f32[512,128]{1,0:T(8,128)S(1)} %get-tuple-element.92.cos_ref, f32[512,128]{1,0:T(8,128)S(1)} %get-tuple-element.93.sin_ref, f32[1,128]{1,0:T(1,128)S(1)} %bitcast.25, f32[1,128]{1,0:T(1,128)S(1)} %bitcast.26, ...), custom_call_target="tpu_custom_call" | custom-call | flops 1024 | bytes 1024 | tf_op jit(solution)/shard_map/attention/pallas_call | solution.py:108
  79.2 1.7 collective-permute-done.10.refs_2_
  80.8 2.2 collective-permute-done.11.refs_3_
  83.0 8.8 %project.1 = (f32[256,2560]{1,0:T(8,128)S(1)}, bf16[256,2560]{1,0:T(8,128)(2,1)S(1)}) custom-call(s32[1]{0:T(128)} %bitcast.1.core, bf16[512,2048]{1,0:T(8,128)(2,1)S(1)} %attention.1.refs_0_, bf16[2048,2560]{1,0:T(8,128)(2,1)} %refs_1_.3), custom_call_target="tpu_custom_call" | custom-call | flops 1024 | bytes 1024 | tf_op jit(solution)/shard_map/project/pallas_call | solution.py:148
  91.8 1.5 copy-done.2
  93.9 1.4 merge.3.refs_2_
  95.3 1.6 collective-permute-start.15
  96.9 3.2 %normalize.1 = (bf16[256,2560]{1,0:T(8,128)(2,1)S(1)}, bf16[128,2560]{1,0:T(8,128)(2,1)S(1)}, bf16[128,2560]{1,0:T(8,128)(2,1)S(1)}) custom-call(bf16[256,2560]{1,0:T(8,128)(2,1)S(1)} %copy-done.5, f32[1,2560]{1,0:T(1,128)S(1)} %broadcast_in_dim.56.gain, f32[256,2560]{1,0:T(8,128)} %copy-done.2, bf16[256,2560]{1,0:T(8,128)(2,1)S(1)} %collective-permute-done.12.refs_0_), custom_call_target="tpu_custom_call" | custom-call | flops 1024 | bytes 1024 | tf_op jit(solution)/shard_map/normalize/pallas_call | solution.py:199
  101.1 14.4 %collective-permute-done.15.refs_3_ = bf16[1,4,160,640]{3,2,1,0:T(8,128)(2,1)S(1)} collective-permute-done((bf16[1,4,160,640]{3,2,1,0:T(8,128)(2,1)S(1)}, bf16[1,4,160,640]{3,2,1,0:T(8,128)(2,1)S(1)}, u32[]{:S(2)}, u32[]{:S(2)}) %collective-permute-start.15) | collective-permute-done | bytes 819232 | tf_op jit(solution)/shard_map/ppermute | solution.py:461
  115.9 3.7 %collective-permute-start.17 = (bf16[128,2560]{1,0:T(8,128)(2,1)S(1)}, bf16[128,2560]{1,0:T(8,128)(2,1)S(1)}, u32[]{:S(2)}, u32[]{:S(2)}) collective-permute-start(bf16[128,2560]{1,0:T(8,128)(2,1)S(1)} %get-tuple-element.116.refs_1_), channel_id=1, source_target_pairs={{0,8},{2,10},{4,12},{6,14},{8,0},{10,2},{12,4},{14,6},{16,24},{18,... | collective-permute-start | bytes 1966088 | tf_op jit(solution)/shard_map/ppermute | solution.py:461
  120.0 1.5 collective-permute-start.25
  121.5 9.9 %collective-permute-done.16.refs_2_ = bf16[128,2560]{1,0:T(8,128)(2,1)S(1)} collective-permute-done((bf16[128,2560]{1,0:T(8,128)(2,1)S(1)}, bf16[128,2560]{1,0:T(8,128)(2,1)S(1)}, u32[]{:S(2)}, u32[]{:S(2)}) %collective-permute-start.16) | collective-permute-done | bytes 655392 | tf_op jit(solution)/shard_map/ppermute | solution.py:461
  131.7 1.6 collective-permute-done.17.refs_5_
  133.4 2.0 collective-permute-start.21
  135.4 11.0 %collective-permute-done.20.refs_3_ = bf16[128,2560]{1,0:T(8,128)(2,1)S(1)} collective-permute-done((bf16[128,2560]{1,0:T(8,128)(2,1)S(1)}, bf16[128,2560]{1,0:T(8,128)(2,1)S(1)}, u32[]{:S(2)}, u32[]{:S(2)}) %collective-permute-start.20) | collective-permute-done | bytes 655392 | tf_op jit(solution)/shard_map/ppermute | solution.py:461
  146.4 2.2 collective-permute-start.18
  150.3 12.0 %collective-permute-done.18.refs_6_ = bf16[128,2560]{1,0:T(8,128)(2,1)S(1)} collective-permute-done((bf16[128,2560]{1,0:T(8,128)(2,1)S(1)}, bf16[128,2560]{1,0:T(8,128)(2,1)S(1)}, u32[]{:S(2)}, u32[]{:S(2)}) %collective-permute-start.18) | collective-permute-done | bytes 655392 | tf_op jit(solution)/shard_map/ppermute | solution.py:461
  163.1 2.0 collective-permute-start.29
  167.2 20.2 %gate_up.1 = (bf16[1024,640]{1,0:T(8,128)(2,1)}, bf16[1024,640]{1,0:T(8,128)(2,1)}) custom-call(s32[1]{0:T(128)} %bitcast.20.me, bf16[128,2560]{1,0:T(8,128)(2,1)S(1)} %get-tuple-element.115.refs_0_, bf16[128,2560]{1,0:T(8,128)(2,1)S(1)} %get-tuple-element.116.refs_1_, bf16[128,2560]{1,0:T(8,128)(2,1)S(1)} %collective-permute-done.16.refs_2_, ...), custom_call_target="tpu_custom_call" | custom-call | flops 1024 | bytes 1024 | tf_op jit(solution)/shard_map/gate_up/pallas_call | solution.py:348
  187.4 6.9 %down.2 = (f32[256,1280]{1,0:T(8,128)}, bf16[256,1280]{1,0:T(8,128)(2,1)S(1)}, bf16[256,1280]{1,0:T(8,128)(2,1)S(1)}, f32[128,1280]{1,0:T(8,128)S(1)}, f32[128,1280]{1,0:T(8,128)S(1)}) custom-call(s32[1]{0:T(128)} %bitcast.20.me, bf16[1024,640]{1,0:T(8,128)(2,1)} %get-tuple-element.138.refs_0_, bf16[1024,640]{1,0:T(8,128)(2,1)} %get-tuple-element.139.refs_1_, ...), custom_call_target="tpu_custom_call" | custom-call | flops 1024 | bytes 1024 | tf_op jit(solution)/shard_map/down/pallas_call | solution.py:415
  194.3 7.8 %collective-permute-done.29.refs_2_ = bf16[1,4,160,640]{3,2,1,0:T(8,128)(2,1)S(1)} collective-permute-done((bf16[1,4,160,640]{3,2,1,0:T(8,128)(2,1)S(1)}, bf16[1,4,160,640]{3,2,1,0:T(8,128)(2,1)S(1)}, u32[]{:S(2)}, u32[]{:S(2)}) %collective-permute-start.29) | collective-permute-done | bytes 819232 | tf_op jit(solution)/shard_map/ppermute | solution.py:461
  202.1 1.5 collective-permute-start.30
  203.6 1.5 collective-permute-start.32
  205.1 13.4 %collective-permute-done.30.refs_1_ = bf16[256,1280]{1,0:T(8,128)(2,1)S(1)} collective-permute-done((bf16[256,1280]{1,0:T(8,128)(2,1)S(1)}, bf16[256,1280]{1,0:T(8,128)(2,1)S(1)}, u32[]{:S(2)}, u32[]{:S(2)}) %collective-permute-start.30) | collective-permute-done | bytes 655392 | tf_op jit(solution)/shard_map/ppermute | solution.py:461
  218.6 1.4 collective-permute-done.31.refs_2_
  220.1 3.5 %collective-permute-done.32.refs_3_ = bf16[1,4,160,640]{3,2,1,0:T(8,128)(2,1)S(1)} collective-permute-done((bf16[1,4,160,640]{3,2,1,0:T(8,128)(2,1)S(1)}, bf16[1,4,160,640]{3,2,1,0:T(8,128)(2,1)S(1)}, u32[]{:S(2)}, u32[]{:S(2)}) %collective-permute-start.32) | collective-permute-done | bytes 819232 | tf_op jit(solution)/shard_map/ppermute | solution.py:461
  224.0 1.7 collective-permute-start.35
  227.0 6.8 %down.3 = (f32[256,1280]{1,0:T(8,128)}, bf16[256,1280]{1,0:T(8,128)(2,1)S(1)}, bf16[256,1280]{1,0:T(8,128)(2,1)S(1)}, f32[128,1280]{1,0:T(8,128)S(1)}, f32[128,1280]{1,0:T(8,128)S(1)}) custom-call(s32[1]{0:T(128)} %bitcast.20.me, bf16[1024,640]{1,0:T(8,128)(2,1)} %get-tuple-element.138.refs_0_, bf16[1024,640]{1,0:T(8,128)(2,1)} %get-tuple-element.139.refs_1_, ...), custom_call_target="tpu_custom_call" | custom-call | flops 1024 | bytes 1024 | tf_op jit(solution)/shard_map/down/pallas_call | solution.py:415
  236.0 14.7 %collective-permute-done.37.refs_6_ = bf16[256,1280]{1,0:T(8,128)(2,1)S(1)} collective-permute-done((bf16[256,1280]{1,0:T(8,128)(2,1)S(1)}, bf16[256,1280]{1,0:T(8,128)(2,1)S(1)}, u32[]{:S(2)}, u32[]{:S(2)}) %collective-permute-start.37) | collective-permute-done | bytes 655392 | tf_op jit(solution)/shard_map/ppermute | solution.py:461
  251.5 1.7 collective-permute-start.40
  254.3 6.4 %collective-permute-done.40.refs_9_ = bf16[128,1280]{1,0:T(8,128)(2,1)} collective-permute-done((bf16[128,1280]{1,0:T(8,128)(2,1)}, bf16[128,1280]{1,0:T(8,128)(2,1)}, u32[]{:S(2)}, u32[]{:S(2)}) %collective-permute-start.40) | collective-permute-done | bytes 327712 | tf_op jit(solution)/shard_map/ppermute | solution.py:461
  260.8 2.2 collective-permute-done.39.refs_8_
  264.3 3.5 %finish.1 = bf16[256,2560]{1,0:T(8,128)(2,1)} custom-call(s32[1]{0:T(128)} %bitcast.upper, bf16[256,2560]{1,0:T(8,128)(2,1)S(1)} %copy-done.4, f32[256,1280]{1,0:T(8,128)} %get-tuple-element.149.refs_0_, bf16[256,1280]{1,0:T(8,128)(2,1)S(1)} %collective-permute-done.30.refs_1_, bf16[256,1280]{1,0:T(8,128)(2,1)S(1)} %collective-permute-done.31.refs_2_, ...), custom_call_target="tpu_custom_call" | custom-call | flops 1024 | bytes 1024 | tf_op jit(solution)/shard_map/finish/pallas_call | solution.py:449
  (129 shorter events, 34.8 us)
Async XLA Ops:
  0.0 12.0 %copy-start.28 = (s32[1,8]{1,0:T(1,128)S(1)}, s32[1,8]{1,0:T(1,128)}, u32[]{:S(2)}) copy-start(s32[1,8]{1,0:T(1,128)} %param.25) | copy-start | bytes 100
  0.0 12.4 %copy-start.29 = (s32[16]{0:T(128)S(1)}, s32[16]{0:T(128)}, u32[]{:S(2)}) copy-start(s32[16]{0:T(128)} %param.27) | copy-start | bytes 196
  0.0 15.4 %collective-permute-start = (bf16[2,64,512]{2,1,0:T(8,128)(2,1)}, bf16[2,64,512]{2,1,0:T(8,128)(2,1)S(1)}, u32[]{:S(2)}, u32[]{:S(2)}) collective-permute-start(bf16[2,64,512]{2,1,0:T(8,128)(2,1)} %param.16), channel_id=1, source_target_pairs={{0,8},{2,10},{4,12},{6,14},{8,0},{10,2},{12,4},{14,6},{16,24},{18,... | collective-permute-start | bytes 393224 | tf_op jit(solution)/shard_map/ppermute | solution.py:461
  3.0 13.2 %collective-permute-start.1 = (bf16[2,64,512]{2,1,0:T(8,128)(2,1)}, bf16[2,64,512]{2,1,0:T(8,128)(2,1)S(1)}, u32[]{:S(2)}, u32[]{:S(2)}) collective-permute-start(bf16[2,64,512]{2,1,0:T(8,128)(2,1)} %param.16), channel_id=1, source_target_pairs={{0,16},{2,18},{4,20},{6,22},{8,24},{10,26},{12,28},{14,30},{16,0},... | collective-permute-start | bytes 393224 | tf_op jit(solution)/shard_map/ppermute | solution.py:461
  5.6 10.6 %collective-permute-start.2 = (bf16[2,64,512]{2,1,0:T(8,128)(2,1)}, bf16[2,64,512]{2,1,0:T(8,128)(2,1)S(1)}, u32[]{:S(2)}, u32[]{:S(2)}) collective-permute-start(bf16[2,64,512]{2,1,0:T(8,128)(2,1)} %param.16), channel_id=1, source_target_pairs={{0,24},{2,26},{4,28},{6,30},{8,16},{10,18},{12,20},{14,22},{16,8},... | collective-permute-start | bytes 393224 | tf_op jit(solution)/shard_map/ppermute | solution.py:461
  8.9 12.3 %collective-permute-start.6 = (bf16[2,160,640]{2,1,0:T(8,128)(2,1)S(1)}, bf16[2,160,640]{2,1,0:T(8,128)(2,1)S(1)}, u32[]{:S(2)}, u32[]{:S(2)}) collective-permute-start(bf16[2,160,640]{2,1,0:T(8,128)(2,1)S(1)} %get-tuple-element.96), channel_id=1, source_target_pairs={{0,2},{2,0},{4,6},{6,4},{8,10},{10,8},{12,14},{14,12},{16,18},{18,... | collective-permute-start | bytes 1228808 | tf_op jit(solution)/shard_map/ppermute | solution.py:461
  10.6 15.4 %collective-permute-start.7 = (bf16[2,160,640]{2,1,0:T(8,128)(2,1)S(1)}, bf16[2,160,640]{2,1,0:T(8,128)(2,1)S(1)}, u32[]{:S(2)}, u32[]{:S(2)}) collective-permute-start(bf16[2,160,640]{2,1,0:T(8,128)(2,1)S(1)} %get-tuple-element.97), channel_id=1, source_target_pairs={{0,8},{2,10},{4,12},{6,14},{8,0},{10,2},{12,4},{14,6},{16,24},{18,... | collective-permute-start | bytes 1228808 | tf_op jit(solution)/shard_map/ppermute | solution.py:461
  16.3 27.0 %collective-permute-start.4 = (bf16[4,2,64,512]{3,2,1,0:T(8,128)(2,1)S(1)}, bf16[4,2,64,512]{3,2,1,0:T(8,128)(2,1)}, u32[]{:S(2)}, u32[]{:S(2)}) collective-permute-start(bf16[4,2,64,512]{3,2,1,0:T(8,128)(2,1)S(1)} %pad_maximum_fusion.1), channel_id=1, source_target_pairs={{0,4},{2,6},{4,0},{6,2},{8,12},{10,14},{12,8},{14,10},{16,20},{18,... | collective-permute-start | bytes 1572872 | tf_op jit(solution)/shard_map/ppermute | solution.py:461
  17.9 28.1 %collective-permute-start.5 = (bf16[4,2,64,512]{3,2,1,0:T(8,128)(2,1)S(1)}, bf16[4,2,64,512]{3,2,1,0:T(8,128)(2,1)}, u32[]{:S(2)}, u32[]{:S(2)}) collective-permute-start(bf16[4,2,64,512]{3,2,1,0:T(8,128)(2,1)S(1)} %pad_maximum_fusion.1), channel_id=1, source_target_pairs={{0,6},{2,4},{4,2},{6,0},{8,14},{10,12},{12,10},{14,8},{16,22},{18,... | collective-permute-start | bytes 1572872 | tf_op jit(solution)/shard_map/ppermute | solution.py:461
  19.3 36.1 %collective-permute-start.3 = (bf16[4,2,64,512]{3,2,1,0:T(8,128)(2,1)S(1)}, bf16[4,2,64,512]{3,2,1,0:T(8,128)(2,1)}, u32[]{:S(2)}, u32[]{:S(2)}) collective-permute-start(bf16[4,2,64,512]{3,2,1,0:T(8,128)(2,1)S(1)} %pad_maximum_fusion.1), channel_id=1, source_target_pairs={{0,2},{2,0},{4,6},{6,4},{8,10},{10,8},{12,14},{14,12},{16,18},{18,... | collective-permute-start | bytes 1572872 | tf_op jit(solution)/shard_map/ppermute | solution.py:461
  21.3 11.8 %copy-start.11 = (bf16[2,160,640]{2,1,0:T(8,128)(2,1)}, bf16[2,160,640]{2,1,0:T(8,128)(2,1)S(1)}, u32[]{:S(2)}) copy-start(bf16[2,160,640]{2,1,0:T(8,128)(2,1)S(1)} %collective-permute-done.6.refs_1_) | copy-start | bytes 1228804
  21.3 11.8 %collective-permute-start.8 = (bf16[2,160,640]{2,1,0:T(8,128)(2,1)S(1)}, bf16[2,160,640]{2,1,0:T(8,128)(2,1)S(1)}, u32[]{:S(2)}, u32[]{:S(2)}) collective-permute-start(bf16[2,160,640]{2,1,0:T(8,128)(2,1)S(1)} %get-tuple-element.98), channel_id=1, source_target_pairs={{0,10},{2,8},{4,14},{6,12},{8,2},{10,0},{12,6},{14,4},{16,26},{18,... | collective-permute-start | bytes 1228808 | tf_op jit(solution)/shard_map/ppermute | solution.py:461
  40.0 53.4 %copy-start = (bf16[2,4,160,640]{3,2,1,0:T(8,128)(2,1)}, bf16[2,4,160,640]{3,2,1,0:T(8,128)(2,1)S(1)}, u32[]{:S(2)}) copy-start(bf16[2,4,160,640]{3,2,1,0:T(8,128)(2,1)S(1)} %merge.2.refs_8_) | copy-start | bytes 4915204
  40.0 75.6 %collective-permute-start.13 = (bf16[2,4,160,640]{3,2,1,0:T(8,128)(2,1)S(1)}, bf16[2,4,160,640]{3,2,1,0:T(8,128)(2,1)}, u32[]{:S(2)}, u32[]{:S(2)}) collective-permute-start(bf16[2,4,160,640]{3,2,1,0:T(8,128)(2,1)S(1)} %merge.2.refs_8_), channel_id=1, source_target_pairs={{0,16},{2,18},{4,20},{6,22},{8,24},{10,26},{12,28},{14,30},{16,0},... | collective-permute-start | bytes 4915208 | tf_op jit(solution)/shard_map/ppermute | solution.py:461
  40.8 74.8 %collective-permute-start.14 = (bf16[2,4,160,640]{3,2,1,0:T(8,128)(2,1)S(1)}, bf16[2,4,160,640]{3,2,1,0:T(8,128)(2,1)}, u32[]{:S(2)}, u32[]{:S(2)}) collective-permute-start(bf16[2,4,160,640]{3,2,1,0:T(8,128)(2,1)S(1)} %merge.2.refs_8_), channel_id=1, source_target_pairs={{0,4},{2,6},{4,0},{6,2},{8,12},{10,14},{12,8},{14,10},{16,20},{18,... | collective-permute-start | bytes 4915208 | tf_op jit(solution)/shard_map/ppermute | solution.py:461
  43.3 16.5 %copy-start.17 = (bf16[1,160,640]{2,1,0:T(8,128)(2,1)}, bf16[1,160,640]{2,1,0:T(8,128)(2,1)S(1)}, u32[]{:S(2)}) copy-start(bf16[1,160,640]{2,1,0:T(8,128)(2,1)S(1)} %get-tuple-element.111.refs_0_) | copy-start | bytes 614404
  43.3 37.5 %collective-permute-start.10 = (bf16[1,160,640]{2,1,0:T(8,128)(2,1)}, bf16[1,160,640]{2,1,0:T(8,128)(2,1)}, u32[]{:S(2)}, u32[]{:S(2)}) collective-permute-start(bf16[1,160,640]{2,1,0:T(8,128)(2,1)} %get-tuple-element.102), channel_id=1, source_target_pairs={{0,8},{2,10},{4,12},{6,14},{8,0},{10,2},{12,4},{14,6},{16,24},{18,... | collective-permute-start | bytes 614408 | tf_op jit(solution)/shard_map/ppermute | solution.py:461
  46.0 37.0 %collective-permute-start.11 = (bf16[1,160,640]{2,1,0:T(8,128)(2,1)}, bf16[1,160,640]{2,1,0:T(8,128)(2,1)}, u32[]{:S(2)}, u32[]{:S(2)}) collective-permute-start(bf16[1,160,640]{2,1,0:T(8,128)(2,1)} %get-tuple-element.103), channel_id=1, source_target_pairs={{0,10},{2,8},{4,14},{6,12},{8,2},{10,0},{12,6},{14,4},{16,26},{18,... | collective-permute-start | bytes 614408 | tf_op jit(solution)/shard_map/ppermute | solution.py:461
  55.4 27.7 %collective-permute-start.9 = (bf16[1,160,640]{2,1,0:T(8,128)(2,1)}, bf16[1,160,640]{2,1,0:T(8,128)(2,1)}, u32[]{:S(2)}, u32[]{:S(2)}) collective-permute-start(bf16[1,160,640]{2,1,0:T(8,128)(2,1)} %get-tuple-element.101), channel_id=1, source_target_pairs={{0,2},{2,0},{4,6},{6,4},{8,10},{10,8},{12,14},{14,12},{16,18},{18,... | collective-permute-start | bytes 614408 | tf_op jit(solution)/shard_map/ppermute | solution.py:461
  83.0 10.8 %copy-start.18 = (bf16[1,160,640]{2,1,0:T(8,128)(2,1)S(1)}, bf16[1,160,640]{2,1,0:T(8,128)(2,1)}, u32[]{:S(2)}) copy-start(bf16[1,160,640]{2,1,0:T(8,128)(2,1)} %copy-done.17) | copy-start | bytes 614404
  93.4 3.5 %collective-permute-start.12 = (bf16[256,2560]{1,0:T(8,128)(2,1)S(1)}, bf16[256,2560]{1,0:T(8,128)(2,1)S(1)}, u32[]{:S(2)}, u32[]{:S(2)}) collective-permute-start(bf16[256,2560]{1,0:T(8,128)(2,1)S(1)} %get-tuple-element.106), channel_id=1, source_target_pairs={{0,1},{1,0},{2,3},{3,2},{4,5},{5,4},{6,7},{7,6},{8,9},{9,8},{10,11... | collective-permute-start | bytes 3932168 | tf_op jit(solution)/shard_map/ppermute | solution.py:461
  93.4 26.7 %collective-permute-start.22 = (bf16[2,4,160,640]{3,2,1,0:T(8,128)(2,1)S(1)}, bf16[2,4,160,640]{3,2,1,0:T(8,128)(2,1)S(1)}, u32[]{:S(2)}, u32[]{:S(2)}) collective-permute-start(bf16[2,4,160,640]{3,2,1,0:T(8,128)(2,1)S(1)} %merge.2.refs_8_), channel_id=1, source_target_pairs={{0,1},{1,0},{2,3},{3,2},{4,5},{5,4},{6,7},{7,6},{8,9},{9,8},{10,11... | collective-permute-start | bytes 4915208 | tf_op jit(solution)/shard_map/ppermute | solution.py:461
  95.3 20.3 %collective-permute-start.15 = (bf16[1,4,160,640]{3,2,1,0:T(8,128)(2,1)S(1)}, bf16[1,4,160,640]{3,2,1,0:T(8,128)(2,1)S(1)}, u32[]{:S(2)}, u32[]{:S(2)}) collective-permute-start(bf16[1,4,160,640]{3,2,1,0:T(8,128)(2,1)S(1)} %merge.3.refs_2_), channel_id=1, source_target_pairs={{0,4},{2,6},{4,0},{6,2},{8,12},{10,14},{12,8},{14,10},{16,20},{18,... | collective-permute-start | bytes 2457608 | tf_op jit(solution)/shard_map/ppermute | solution.py:461
  115.6 15.9 %collective-permute-start.16 = (bf16[128,2560]{1,0:T(8,128)(2,1)S(1)}, bf16[128,2560]{1,0:T(8,128)(2,1)S(1)}, u32[]{:S(2)}, u32[]{:S(2)}) collective-permute-start(bf16[128,2560]{1,0:T(8,128)(2,1)S(1)} %get-tuple-element.115.refs_0_), channel_id=1, source_target_pairs={{0,2},{2,0},{4,6},{6,4},{8,10},{10,8},{12,14},{14,12},{16,18},{18,... | collective-permute-start | bytes 1966088 | tf_op jit(solution)/shard_map/ppermute | solution.py:461
  115.9 17.5 %collective-permute-start.17 = (bf16[128,2560]{1,0:T(8,128)(2,1)S(1)}, bf16[128,2560]{1,0:T(8,128)(2,1)S(1)}, u32[]{:S(2)}, u32[]{:S(2)}) collective-permute-start(bf16[128,2560]{1,0:T(8,128)(2,1)S(1)} %get-tuple-element.116.refs_1_), channel_id=1, source_target_pairs={{0,8},{2,10},{4,12},{6,14},{8,0},{10,2},{12,4},{14,6},{16,24},{18,... | collective-permute-start | bytes 1966088 | tf_op jit(solution)/shard_map/ppermute | solution.py:461
  119.5 42.8 %collective-permute-start.23 = (bf16[2,4,160,640]{3,2,1,0:T(8,128)(2,1)}, bf16[2,4,160,640]{3,2,1,0:T(8,128)(2,1)S(1)}, u32[]{:S(2)}, u32[]{:S(2)}) collective-permute-start(bf16[2,4,160,640]{3,2,1,0:T(8,128)(2,1)} %collective-permute-done.14.refs_9_), channel_id=1, source_target_pairs={{0,1},{1,0},{2,3},{3,2},{4,5},{5,4},{6,7},{7,6},{8,9},{9,8},{10,11... | collective-permute-start | bytes 4915208 | tf_op jit(solution)/shard_map/ppermute | solution.py:461
  119.5 42.9 %collective-permute-start.24 = (bf16[2,4,160,640]{3,2,1,0:T(8,128)(2,1)}, bf16[2,4,160,640]{3,2,1,0:T(8,128)(2,1)S(1)}, u32[]{:S(2)}, u32[]{:S(2)}) collective-permute-start(bf16[2,4,160,640]{3,2,1,0:T(8,128)(2,1)} %collective-permute-done.13.refs_10_), channel_id=1, source_target_pairs={{0,1},{1,0},{2,3},{3,2},{4,5},{5,4},{6,7},{7,6},{8,9},{9,8},{10,11... | collective-permute-start | bytes 4915208 | tf_op jit(solution)/shard_map/ppermute | solution.py:461
  120.0 47.1 %copy-start.21 = (bf16[2,4,160,640]{3,2,1,0:T(8,128)(2,1)}, bf16[2,4,160,640]{3,2,1,0:T(8,128)(2,1)S(1)}, u32[]{:S(2)}) copy-start(bf16[2,4,160,640]{3,2,1,0:T(8,128)(2,1)S(1)} %collective-permute-done.22.refs_12_) | copy-start | bytes 4915204
  120.0 42.4 %collective-permute-start.25 = (bf16[2,4,160,640]{3,2,1,0:T(8,128)(2,1)}, bf16[2,4,160,640]{3,2,1,0:T(8,128)(2,1)S(1)}, u32[]{:S(2)}, u32[]{:S(2)}) collective-permute-start(bf16[2,4,160,640]{3,2,1,0:T(8,128)(2,1)} %collective-permute-done.13.refs_10_), channel_id=1, source_target_pairs={{0,4},{2,6},{4,0},{6,2},{8,12},{10,14},{12,8},{14,10},{16,20},{18,... | collective-permute-start | bytes 4915208 | tf_op jit(solution)/shard_map/ppermute | solution.py:461
  131.4 14.9 %collective-permute-start.20 = (bf16[128,2560]{1,0:T(8,128)(2,1)S(1)}, bf16[128,2560]{1,0:T(8,128)(2,1)S(1)}, u32[]{:S(2)}, u32[]{:S(2)}) collective-permute-start(bf16[128,2560]{1,0:T(8,128)(2,1)S(1)} %get-tuple-element.116.refs_1_), channel_id=1, source_target_pairs={{0,2},{2,0},{4,6},{6,4},{8,10},{10,8},{12,14},{14,12},{16,18},{18,... | collective-permute-start | bytes 1966088 | tf_op jit(solution)/shard_map/ppermute | solution.py:461
  133.4 16.4 %collective-permute-start.21 = (bf16[128,2560]{1,0:T(8,128)(2,1)S(1)}, bf16[128,2560]{1,0:T(8,128)(2,1)S(1)}, u32[]{:S(2)}, u32[]{:S(2)}) collective-permute-start(bf16[128,2560]{1,0:T(8,128)(2,1)S(1)} %get-tuple-element.115.refs_0_), channel_id=1, source_target_pairs={{0,8},{2,10},{4,12},{6,14},{8,0},{10,2},{12,4},{14,6},{16,24},{18,... | collective-permute-start | bytes 1966088 | tf_op jit(solution)/shard_map/ppermute | solution.py:461
  146.4 16.0 %collective-permute-start.18 = (bf16[128,2560]{1,0:T(8,128)(2,1)S(1)}, bf16[128,2560]{1,0:T(8,128)(2,1)S(1)}, u32[]{:S(2)}, u32[]{:S(2)}) collective-permute-start(bf16[128,2560]{1,0:T(8,128)(2,1)S(1)} %collective-permute-done.16.refs_2_), channel_id=1, source_target_pairs={{0,8},{2,10},{4,12},{6,14},{8,0},{10,2},{12,4},{14,6},{16,24},{18,... | collective-permute-start | bytes 1966088 | tf_op jit(solution)/shard_map/ppermute | solution.py:461
  149.7 12.6 %collective-permute-start.19 = (bf16[128,2560]{1,0:T(8,128)(2,1)S(1)}, bf16[128,2560]{1,0:T(8,128)(2,1)S(1)}, u32[]{:S(2)}, u32[]{:S(2)}) collective-permute-start(bf16[128,2560]{1,0:T(8,128)(2,1)S(1)} %collective-permute-done.17.refs_5_), channel_id=1, source_target_pairs={{0,2},{2,0},{4,6},{6,4},{8,10},{10,8},{12,14},{14,12},{16,18},{18,... | collective-permute-start | bytes 1966088 | tf_op jit(solution)/shard_map/ppermute | solution.py:461
  162.4 3.6 %collective-permute-start.26 = (bf16[2,4,160,640]{3,2,1,0:T(8,128)(2,1)S(1)}, bf16[2,4,160,640]{3,2,1,0:T(8,128)(2,1)S(1)}, u32[]{:S(2)}, u32[]{:S(2)}) collective-permute-start(bf16[2,4,160,640]{3,2,1,0:T(8,128)(2,1)S(1)} %collective-permute-done.25.refs_11_), channel_id=1, source_target_pairs={{0,1},{1,0},{2,3},{3,2},{4,5},{5,4},{6,7},{7,6},{8,9},{9,8},{10,11... | collective-permute-start | bytes 4915208 | tf_op jit(solution)/shard_map/ppermute | solution.py:461
  162.5 24.9 %collective-permute-start.27 = (bf16[1,4,160,640]{3,2,1,0:T(8,128)(2,1)S(1)}, bf16[1,4,160,640]{3,2,1,0:T(8,128)(2,1)S(1)}, u32[]{:S(2)}, u32[]{:S(2)}) collective-permute-start(bf16[1,4,160,640]{3,2,1,0:T(8,128)(2,1)S(1)} %merge.3.refs_2_), channel_id=1, source_target_pairs={{0,1},{1,0},{2,3},{3,2},{4,5},{5,4},{6,7},{7,6},{8,9},{9,8},{10,11... | collective-permute-start | bytes 2457608 | tf_op jit(solution)/shard_map/ppermute | solution.py:461
  163.0 24.4 %collective-permute-start.28 = (bf16[1,4,160,640]{3,2,1,0:T(8,128)(2,1)S(1)}, bf16[1,4,160,640]{3,2,1,0:T(8,128)(2,1)S(1)}, u32[]{:S(2)}, u32[]{:S(2)}) collective-permute-start(bf16[1,4,160,640]{3,2,1,0:T(8,128)(2,1)S(1)} %collective-permute-done.15.refs_3_), channel_id=1, source_target_pairs={{0,1},{1,0},{2,3},{3,2},{4,5},{5,4},{6,7},{7,6},{8,9},{9,8},{10,11... | collective-permute-start | bytes 2457608 | tf_op jit(solution)/shard_map/ppermute | solution.py:461
  163.1 39.0 %collective-permute-start.29 = (bf16[1,4,160,640]{3,2,1,0:T(8,128)(2,1)S(1)}, bf16[1,4,160,640]{3,2,1,0:T(8,128)(2,1)S(1)}, u32[]{:S(2)}, u32[]{:S(2)}) collective-permute-start(bf16[1,4,160,640]{3,2,1,0:T(8,128)(2,1)S(1)} %merge.3.refs_2_), channel_id=1, source_target_pairs={{0,16},{2,18},{4,20},{6,22},{8,24},{10,26},{12,28},{14,30},{16,0},... | collective-permute-start | bytes 2457608 | tf_op jit(solution)/shard_map/ppermute | solution.py:461
  202.1 16.4 %collective-permute-start.30 = (bf16[256,1280]{1,0:T(8,128)(2,1)S(1)}, bf16[256,1280]{1,0:T(8,128)(2,1)S(1)}, u32[]{:S(2)}, u32[]{:S(2)}) collective-permute-start(bf16[256,1280]{1,0:T(8,128)(2,1)S(1)} %get-tuple-element.150), channel_id=1, source_target_pairs={{0,2},{2,0},{4,6},{6,4},{8,10},{10,8},{12,14},{14,12},{16,18},{18,... | collective-permute-start | bytes 1966088 | tf_op jit(solution)/shard_map/ppermute | solution.py:461
  203.6 16.4 %collective-permute-start.31 = (bf16[256,1280]{1,0:T(8,128)(2,1)S(1)}, bf16[256,1280]{1,0:T(8,128)(2,1)S(1)}, u32[]{:S(2)}, u32[]{:S(2)}) collective-permute-start(bf16[256,1280]{1,0:T(8,128)(2,1)S(1)} %get-tuple-element.151), channel_id=1, source_target_pairs={{0,8},{2,10},{4,12},{6,14},{8,0},{10,2},{12,4},{14,6},{16,24},{18,... | collective-permute-start | bytes 1966088 | tf_op jit(solution)/shard_map/ppermute | solution.py:461
  203.6 19.9 %collective-permute-start.32 = (bf16[1,4,160,640]{3,2,1,0:T(8,128)(2,1)S(1)}, bf16[1,4,160,640]{3,2,1,0:T(8,128)(2,1)S(1)}, u32[]{:S(2)}, u32[]{:S(2)}) collective-permute-start(bf16[1,4,160,640]{3,2,1,0:T(8,128)(2,1)S(1)} %collective-permute-done.29.refs_2_), channel_id=1, source_target_pairs={{0,4},{2,6},{4,0},{6,2},{8,12},{10,14},{12,8},{14,10},{16,20},{18,... | collective-permute-start | bytes 2457608 | tf_op jit(solution)/shard_map/ppermute | solution.py:461
  223.5 2.5 collective-permute-start.33
  223.5 3.5 %collective-permute-start.34 = (bf16[1,4,160,640]{3,2,1,0:T(8,128)(2,1)S(1)}, bf16[1,4,160,640]{3,2,1,0:T(8,128)(2,1)S(1)}, u32[]{:S(2)}, u32[]{:S(2)}) collective-permute-start(bf16[1,4,160,640]{3,2,1,0:T(8,128)(2,1)S(1)} %collective-permute-done.32.refs_3_), channel_id=1, source_target_pairs={{0,1},{1,0},{2,3},{3,2},{4,5},{5,4},{6,7},{7,6},{8,9},{9,8},{10,11... | collective-permute-start | bytes 2457608 | tf_op jit(solution)/shard_map/ppermute | solution.py:461
  224.0 9.9 %collective-permute-start.35 = (bf16[128,1280]{1,0:T(8,128)(2,1)S(1)}, bf16[128,1280]{1,0:T(8,128)(2,1)S(1)}, u32[]{:S(2)}, u32[]{:S(2)}) collective-permute-start(bf16[128,1280]{1,0:T(8,128)(2,1)S(1)} %add_convert_fusion.2), channel_id=1, source_target_pairs={{0,8},{2,10},{4,12},{6,14},{8,0},{10,2},{12,4},{14,6},{16,24},{18,... | collective-permute-start | bytes 983048 | tf_op jit(solution)/shard_map/ppermute | solution.py:461
  225.8 9.3 %collective-permute-start.36 = (bf16[128,1280]{1,0:T(8,128)(2,1)S(1)}, bf16[128,1280]{1,0:T(8,128)(2,1)S(1)}, u32[]{:S(2)}, u32[]{:S(2)}) collective-permute-start(bf16[128,1280]{1,0:T(8,128)(2,1)S(1)} %add_convert_fusion.3), channel_id=1, source_target_pairs={{0,2},{2,0},{4,6},{6,4},{8,10},{10,8},{12,14},{14,12},{16,18},{18,... | collective-permute-start | bytes 983048 | tf_op jit(solution)/shard_map/ppermute | solution.py:461
  235.1 15.6 %collective-permute-start.37 = (bf16[256,1280]{1,0:T(8,128)(2,1)S(1)}, bf16[256,1280]{1,0:T(8,128)(2,1)S(1)}, u32[]{:S(2)}, u32[]{:S(2)}) collective-permute-start(bf16[256,1280]{1,0:T(8,128)(2,1)S(1)} %get-tuple-element.167), channel_id=1, source_target_pairs={{0,2},{2,0},{4,6},{6,4},{8,10},{10,8},{12,14},{14,12},{16,18},{18,... | collective-permute-start | bytes 1966088 | tf_op jit(solution)/shard_map/ppermute | solution.py:461
  235.4 17.9 %collective-permute-start.38 = (bf16[256,1280]{1,0:T(8,128)(2,1)S(1)}, bf16[256,1280]{1,0:T(8,128)(2,1)S(1)}, u32[]{:S(2)}, u32[]{:S(2)}) collective-permute-start(bf16[256,1280]{1,0:T(8,128)(2,1)S(1)} %get-tuple-element.168), channel_id=1, source_target_pairs={{0,8},{2,10},{4,12},{6,14},{8,0},{10,2},{12,4},{14,6},{16,24},{18,... | collective-permute-start | bytes 1966088 | tf_op jit(solution)/shard_map/ppermute | solution.py:461
  251.5 9.2 %collective-permute-start.40 = (bf16[128,1280]{1,0:T(8,128)(2,1)}, bf16[128,1280]{1,0:T(8,128)(2,1)}, u32[]{:S(2)}, u32[]{:S(2)}) collective-permute-start(bf16[128,1280]{1,0:T(8,128)(2,1)} %add_convert_fusion), channel_id=1, source_target_pairs={{0,8},{2,10},{4,12},{6,14},{8,0},{10,2},{12,4},{14,6},{16,24},{18,... | collective-permute-start | bytes 983048 | tf_op jit(solution)/shard_map/ppermute | solution.py:461
  254.0 9.0 %collective-permute-start.39 = (bf16[128,1280]{1,0:T(8,128)(2,1)}, bf16[128,1280]{1,0:T(8,128)(2,1)}, u32[]{:S(2)}, u32[]{:S(2)}) collective-permute-start(bf16[128,1280]{1,0:T(8,128)(2,1)} %add_convert_fusion.1), channel_id=1, source_target_pairs={{0,2},{2,0},{4,6},{6,4},{8,10},{10,8},{12,14},{14,12},{16,18},{18,... | collective-permute-start | bytes 983048 | tf_op jit(solution)/shard_map/ppermute | solution.py:461
  (23 other events, 61.9 us)

commit v6 on v5

--- a/solution.py
+++ b/solution.py
@@ -299,8 +299,8 @@
     x_all, gate_w, up_w, opened, x_sems, gate_sems, up_sems = refs
     width = outs[0].shape[1]
     half, depth = x_refs[0].shape
-    rows = 2 * half
-    places = [x_all.at[i // 2, pl.ds(i % 2 * half, half)] for i in range(2 * GROUP)]
+    rows = 4 * half
+    places = [x_all.at[i // 4, pl.ds(i % 4 * half, half)] for i in range(2 * GROUP)]
     first = weight_copies(me[0], w_refs, keys, 0, gate_w, -1, gate_sems)
     first += [
         pltpu.make_async_copy(x_ref, place, x_sems.at[i])
@@ -331,10 +331,10 @@
 
     for copy in first:
         copy.wait()
-    lax.fori_loop(0, GROUP, gate_step, 0)
+    lax.fori_loop(0, GROUP // 2, gate_step, 0)
     for copy in second:
         copy.wait()
-    lax.fori_loop(0, GROUP, up_step, 0)
+    lax.fori_loop(0, GROUP // 2, up_step, 0)
 
 
 def expand(me, normed, keys, weights):
@@ -352,10 +352,10 @@
         out_specs=[vmem] * n_parts,
         out_shape=[jax.ShapeDtypeStruct((total, width), jnp.bfloat16)] * n_parts,
         scratch_shapes=[
-            pltpu.VMEM((GROUP, rows, depth), jnp.bfloat16),
+            pltpu.VMEM((GROUP // 2, 2 * rows, depth), jnp.bfloat16),
             pltpu.VMEM(shape, jnp.bfloat16),
             pltpu.VMEM(shape, jnp.bfloat16),
-            pltpu.VMEM((GROUP, n_parts, rows, width), jnp.float32),
+            pltpu.VMEM((GROUP // 2, n_parts, 2 * rows, width), jnp.float32),
             pltpu.SemaphoreType.DMA((len(normed),)),
             pltpu.SemaphoreType.DMA((n_copies,)),
             pltpu.SemaphoreType.DMA((n_copies,)),
@@ -384,21 +384,22 @@
         copy.wait()
 
     def sums(block):
-        here = pl.ds(block * rows, rows)
+        here = pl.ds(block * rows, 2 * rows)
         if packed:
-            return dot_rows(acts[here, :], weight[...])
-        return sum(dot_rows(acts[i, here, :], weight[i]) for i in range(n_parts))
-
-    total = sums(3).astype(jnp.bfloat16)
-    to_x[half:, :] = total[:half]
-    to_y[half:, :] = total[half:]
-    total = sums(1)
-    to_x[:half, :] = total[:half].astype(jnp.bfloat16)
-    keep_x[...] = total[half:]
-    total = sums(2)
-    to_y[:half, :] = total[half:].astype(jnp.bfloat16)
-    keep_y[...] = total[:half]
-    own[...] = sums(0)
+            total = dot_rows(acts[here, :], weight[...])
+        else:
+            total = sum(dot_rows(acts[i, here, :], weight[i]) for i in range(n_parts))
+        return total[:rows], total[rows:]
+
+    near, far = sums(2)
+    to_x[half:, :] = far[:half].astype(jnp.bfloat16)
+    to_y[half:, :] = far[half:].astype(jnp.bfloat16)
+    to_y[:half, :] = near[half:].astype(jnp.bfloat16)
+    keep_y[...] = near[:half]
+    near, far = sums(0)
+    to_x[:half, :] = far[:half].astype(jnp.bfloat16)
+    keep_x[...] = far[half:]
+    own[...] = near
 
 
 def down(me, acts, keys, weights, mask):
@@ -588,7 +589,6 @@
     down_w = complete({0: down_own, last: down_last}) if n_req > 16 else {}
     near = near + single({key: v for key, v in down_w.items() if key not in (0, last)})
     parts = down(place, acts, *gather(near, top, 1), top - 1)
-    parts, down_top = tie((parts, down_top))
     down_w = complete({top: down_top})
     far = {key: v for key, v in down_w.items() if key & top}
 

time: 269 us -> 266 us (0.989)
  waiting for transfers between devices: 124 us -> 120 us
    ppermute x41, waiting for transfers between devices: 124 us -> 120 us  [swap(): return lax.ppermute(value, axis, [(i, i ^ bits) for i in range(size)])]
where the time goes in v6:
time: 266 us; the launch traced here: 265 us
  waiting for transfers between devices  120 us (45%)
  Pallas kernels  68.1 us (26%)
  starting transfers between devices  46.7 us (18%)
  local copies, waits for them, and re-layouts  17.9 us (7%)
  other arithmetic  11.9 us (4%)
    ppermute x41, waiting for transfers between devices, swap(): return lax.ppermute(value, axis, [(i, i ^ bits) for i in range(size)])  120 us
    ppermute x41, starting transfers between devices, swap(): return lax.ppermute(value, axis, [(i, i ^ bits) for i in range(size)])  46.7 us
    pallas_call x1, Pallas kernels, expand(): pl.pallas_call(functools.partial(expand_kernel, n_parts=n_parts, keys=key...  19.6 us
    pallas_call x1, Pallas kernels, attention(): pl.pallas_call(attention_kernel, grid=(count,), in_specs=[same(tok_count,...  14.6 us
    unnamed x60, local copies, waits for them, and re-layouts  13.7 us
    pallas_call x2, Pallas kernels, down(): pl.pallas_call(functools.partial(down_kernel, n_parts=n_parts, keys=keys,...  13.6 us
    pallas_call x1, Pallas kernels, project(): pl.pallas_call(functools.partial(project_kernel, n_parts=n_parts, n_mlp=n...  8.76 us
  transfers between devices with their start and end apart: 41, of which 22 were waited for; matrix products, arithmetic and copies ran while one was open for 6% of the time, Pallas kernels for 24%

profile of v6, /device:TPU:0, one launch (start us, length us, event | category | flops | bytes accessed | tf_op | source)
XLA Modules:
  0.0 265.2 jit_solution(1774775819124524719)
XLA Ops:
  0.0 3.0 %collective-permute-start = (bf16[2,64,512]{2,1,0:T(8,128)(2,1)}, bf16[2,64,512]{2,1,0:T(8,128)(2,1)S(1)}, u32[]{:S(2)}, u32[]{:S(2)}) collective-permute-start(bf16[2,64,512]{2,1,0:T(8,128)(2,1)} %param.16), channel_id=1, source_target_pairs={{0,8},{2,10},{4,12},{6,14},{8,0},{10,2},{12,4},{14,6},{16,24},{18,... | collective-permute-start | bytes 393224 | tf_op jit(solution)/shard_map/ppermute | solution.py:462
  3.0 2.6 collective-permute-start.1
  8.9 1.7 collective-permute-start.6
  13.6 1.8 fusion
  16.3 1.6 collective-permute-start.4
  17.9 1.4 collective-permute-start.5
  21.3 1.6 collective-permute-start.8
  26.8 6.2 %collective-permute-done.8.refs_3_ = bf16[2,160,640]{2,1,0:T(8,128)(2,1)S(1)} collective-permute-done((bf16[2,160,640]{2,1,0:T(8,128)(2,1)S(1)}, bf16[2,160,640]{2,1,0:T(8,128)(2,1)S(1)}, u32[]{:S(2)}, u32[]{:S(2)}) %collective-permute-start.8) | collective-permute-done | bytes 409632 | tf_op jit(solution)/shard_map/ppermute | solution.py:462
  37.8 2.2 merge.2.refs_8_
  40.8 1.5 collective-permute-start.14
  43.3 2.7 %collective-permute-start.10 = (bf16[1,160,640]{2,1,0:T(8,128)(2,1)}, bf16[1,160,640]{2,1,0:T(8,128)(2,1)}, u32[]{:S(2)}, u32[]{:S(2)}) collective-permute-start(bf16[1,160,640]{2,1,0:T(8,128)(2,1)} %get-tuple-element.96), channel_id=1, source_target_pairs={{0,8},{2,10},{4,12},{6,14},{8,0},{10,2},{12,4},{14,6},{16,24},{18,... | collective-permute-start | bytes 614408 | tf_op jit(solution)/shard_map/ppermute | solution.py:462
  46.2 9.2 %collective-permute-done.3 = bf16[4,2,64,512]{3,2,1,0:T(8,128)(2,1)} collective-permute-done((bf16[4,2,64,512]{3,2,1,0:T(8,128)(2,1)S(1)}, bf16[4,2,64,512]{3,2,1,0:T(8,128)(2,1)}, u32[]{:S(2)}, u32[]{:S(2)}) %collective-permute-start.3) | collective-permute-done | bytes 524320 | tf_op jit(solution)/shard_map/ppermute | solution.py:462
  55.4 1.5 collective-permute-start.9
  56.9 3.0 %pad_maximum_fusion = bf16[4,4,2,64,512]{4,3,2,1,0:T(8,128)(2,1)} fusion(bf16[1,4,2,64,512]{4,3,2,1,0:T(8,128)(2,1)} %bitcast.11, bf16[1,4,2,64,512]{4,3,2,1,0:T(8,128)(2,1)} %bitcast.10, bf16[1,4,2,64,512]{4,3,2,1,0:T(8,128)(2,1)} %bitcast.9, bf16[1,4,2,64,512]{4,3,2,1,0:T(8,128)(2,1)S(1)} %bitcast.28), kind=kLoop, calls=%fused_computation.1 | loop fusion | flops 3145728 | bytes 4194304 | tf_op jit(solution)/shard_map/stack | solution.py:543
  59.8 3.3 %gather_fusion = bf16[8,2,64,512]{3,2,1,0:T(8,128)(2,1)} fusion(bf16[16,2,64,512]{3,2,1,0:T(8,128)(2,1)} %bitcast.27, s32[1024]{0:T(1024)S(1)} %pad_clamp_fusion), kind=kCustom, calls=%fused_computation | custom fusion | bytes 2097184 | tf_op jit(solution)/shard_map/jit(_take)/gather | solution.py:545
  64.5 14.6 %attention.1.refs_0_ = bf16[512,2048]{1,0:T(8,128)(2,1)S(1)} custom-call(s32[512,1]{1,0:T(8,128)S(1)} %subtract_subtract_fusion.start_ref, f32[512,128]{1,0:T(8,128)S(1)} %get-tuple-element.86.cos_ref, f32[512,128]{1,0:T(8,128)S(1)} %get-tuple-element.87.sin_ref, f32[1,128]{1,0:T(1,128)S(1)} %bitcast.25, f32[1,128]{1,0:T(1,128)S(1)} %bitcast.26, ...), custom_call_target="tpu_custom_call" | custom-call | flops 1024 | bytes 1024 | tf_op jit(solution)/shard_map/attention/pallas_call | solution.py:108
  79.2 1.7 collective-permute-done.10.refs_2_
  80.8 2.2 collective-permute-done.11.refs_3_
  83.0 8.8 %project.1 = (f32[256,2560]{1,0:T(8,128)S(1)}, bf16[256,2560]{1,0:T(8,128)(2,1)S(1)}) custom-call(s32[1]{0:T(128)} %bitcast.1.core, bf16[512,2048]{1,0:T(8,128)(2,1)S(1)} %attention.1.refs_0_, bf16[2048,2560]{1,0:T(8,128)(2,1)} %refs_1_.3), custom_call_target="tpu_custom_call" | custom-call | flops 1024 | bytes 1024 | tf_op jit(solution)/shard_map/project/pallas_call | solution.py:148
  91.8 1.5 copy-done.2
  93.9 1.4 merge.3.refs_2_
  95.3 1.6 collective-permute-start.15
  96.9 3.2 %normalize.1 = (bf16[256,2560]{1,0:T(8,128)(2,1)S(1)}, bf16[128,2560]{1,0:T(8,128)(2,1)S(1)}, bf16[128,2560]{1,0:T(8,128)(2,1)S(1)}) custom-call(bf16[256,2560]{1,0:T(8,128)(2,1)S(1)} %copy-done.5, f32[1,2560]{1,0:T(1,128)S(1)} %broadcast_in_dim.56.gain, f32[256,2560]{1,0:T(8,128)} %copy-done.2, bf16[256,2560]{1,0:T(8,128)(2,1)S(1)} %collective-permute-done.12.refs_0_), custom_call_target="tpu_custom_call" | custom-call | flops 1024 | bytes 1024 | tf_op jit(solution)/shard_map/normalize/pallas_call | solution.py:199
  101.1 14.4 %collective-permute-done.15.refs_3_ = bf16[1,4,160,640]{3,2,1,0:T(8,128)(2,1)S(1)} collective-permute-done((bf16[1,4,160,640]{3,2,1,0:T(8,128)(2,1)S(1)}, bf16[1,4,160,640]{3,2,1,0:T(8,128)(2,1)S(1)}, u32[]{:S(2)}, u32[]{:S(2)}) %collective-permute-start.15) | collective-permute-done | bytes 819232 | tf_op jit(solution)/shard_map/ppermute | solution.py:462
  115.9 3.7 %collective-permute-start.17 = (bf16[128,2560]{1,0:T(8,128)(2,1)S(1)}, bf16[128,2560]{1,0:T(8,128)(2,1)S(1)}, u32[]{:S(2)}, u32[]{:S(2)}) collective-permute-start(bf16[128,2560]{1,0:T(8,128)(2,1)S(1)} %get-tuple-element.110.refs_1_), channel_id=1, source_target_pairs={{0,8},{2,10},{4,12},{6,14},{8,0},{10,2},{12,4},{14,6},{16,24},{18,... | collective-permute-start | bytes 1966088 | tf_op jit(solution)/shard_map/ppermute | solution.py:462
  120.0 1.5 collective-permute-start.25
  121.5 9.9 %collective-permute-done.16.refs_2_ = bf16[128,2560]{1,0:T(8,128)(2,1)S(1)} collective-permute-done((bf16[128,2560]{1,0:T(8,128)(2,1)S(1)}, bf16[128,2560]{1,0:T(8,128)(2,1)S(1)}, u32[]{:S(2)}, u32[]{:S(2)}) %collective-permute-start.16) | collective-permute-done | bytes 655392 | tf_op jit(solution)/shard_map/ppermute | solution.py:462
  131.7 1.6 collective-permute-done.17.refs_5_
  133.4 2.0 collective-permute-start.21
  135.4 11.0 %collective-permute-done.20.refs_3_ = bf16[128,2560]{1,0:T(8,128)(2,1)S(1)} collective-permute-done((bf16[128,2560]{1,0:T(8,128)(2,1)S(1)}, bf16[128,2560]{1,0:T(8,128)(2,1)S(1)}, u32[]{:S(2)}, u32[]{:S(2)}) %collective-permute-start.20) | collective-permute-done | bytes 655392 | tf_op jit(solution)/shard_map/ppermute | solution.py:462
  146.4 2.2 collective-permute-start.18
  150.3 12.0 %collective-permute-done.18.refs_6_ = bf16[128,2560]{1,0:T(8,128)(2,1)S(1)} collective-permute-done((bf16[128,2560]{1,0:T(8,128)(2,1)S(1)}, bf16[128,2560]{1,0:T(8,128)(2,1)S(1)}, u32[]{:S(2)}, u32[]{:S(2)}) %collective-permute-start.18) | collective-permute-done | bytes 655392 | tf_op jit(solution)/shard_map/ppermute | solution.py:462
  163.1 2.0 collective-permute-start.31
  167.2 19.6 %gate_up.1 = (bf16[1024,640]{1,0:T(8,128)(2,1)}, bf16[1024,640]{1,0:T(8,128)(2,1)}) custom-call(s32[1]{0:T(128)} %bitcast.20.me, bf16[128,2560]{1,0:T(8,128)(2,1)S(1)} %get-tuple-element.109.refs_0_, bf16[128,2560]{1,0:T(8,128)(2,1)S(1)} %get-tuple-element.110.refs_1_, bf16[128,2560]{1,0:T(8,128)(2,1)S(1)} %collective-permute-done.16.refs_2_, ...), custom_call_target="tpu_custom_call" | custom-call | flops 1024 | bytes 1024 | tf_op jit(solution)/shard_map/gate_up/pallas_call | solution.py:348
  186.8 6.8 %down.2 = (f32[256,1280]{1,0:T(8,128)}, bf16[256,1280]{1,0:T(8,128)(2,1)S(1)}, bf16[256,1280]{1,0:T(8,128)(2,1)S(1)}, f32[128,1280]{1,0:T(8,128)S(1)}, f32[128,1280]{1,0:T(8,128)S(1)}) custom-call(s32[1]{0:T(128)} %bitcast.20.me, bf16[1024,640]{1,0:T(8,128)(2,1)} %get-tuple-element.132.refs_0_, bf16[1024,640]{1,0:T(8,128)(2,1)} %get-tuple-element.133.refs_1_, ...), custom_call_target="tpu_custom_call" | custom-call | flops 1024 | bytes 1024 | tf_op jit(solution)/shard_map/down/pallas_call | solution.py:416
  193.7 1.8 collective-permute-start.29
  195.8 6.4 %collective-permute-done.31.refs_2_ = bf16[1,4,160,640]{3,2,1,0:T(8,128)(2,1)S(1)} collective-permute-done((bf16[1,4,160,640]{3,2,1,0:T(8,128)(2,1)S(1)}, bf16[1,4,160,640]{3,2,1,0:T(8,128)(2,1)S(1)}, u32[]{:S(2)}, u32[]{:S(2)}) %collective-permute-start.31) | collective-permute-done | bytes 819232 | tf_op jit(solution)/shard_map/ppermute | solution.py:462
  202.2 1.5 collective-permute-start.32
  203.7 6.8 %collective-permute-done.29.refs_1_ = bf16[256,1280]{1,0:T(8,128)(2,1)S(1)} collective-permute-done((bf16[256,1280]{1,0:T(8,128)(2,1)S(1)}, bf16[256,1280]{1,0:T(8,128)(2,1)S(1)}, u32[]{:S(2)}, u32[]{:S(2)}) %collective-permute-start.29) | collective-permute-done | bytes 655392 | tf_op jit(solution)/shard_map/ppermute | solution.py:462
  210.6 5.6 %collective-permute-done.30.refs_2_ = bf16[256,1280]{1,0:T(8,128)(2,1)S(1)} collective-permute-done((bf16[256,1280]{1,0:T(8,128)(2,1)S(1)}, bf16[256,1280]{1,0:T(8,128)(2,1)S(1)}, u32[]{:S(2)}, u32[]{:S(2)}) %collective-permute-start.30) | collective-permute-done | bytes 655392 | tf_op jit(solution)/shard_map/ppermute | solution.py:462
  216.2 5.7 %collective-permute-done.32.refs_3_ = bf16[1,4,160,640]{3,2,1,0:T(8,128)(2,1)S(1)} collective-permute-done((bf16[1,4,160,640]{3,2,1,0:T(8,128)(2,1)S(1)}, bf16[1,4,160,640]{3,2,1,0:T(8,128)(2,1)S(1)}, u32[]{:S(2)}, u32[]{:S(2)}) %collective-permute-start.32) | collective-permute-done | bytes 819232 | tf_op jit(solution)/shard_map/ppermute | solution.py:462
  222.5 1.9 collective-permute-start.36
  225.5 6.8 %down.3 = (f32[256,1280]{1,0:T(8,128)}, bf16[256,1280]{1,0:T(8,128)(2,1)S(1)}, bf16[256,1280]{1,0:T(8,128)(2,1)S(1)}, f32[128,1280]{1,0:T(8,128)S(1)}, f32[128,1280]{1,0:T(8,128)S(1)}) custom-call(s32[1]{0:T(128)} %bitcast.20.me, bf16[1024,640]{1,0:T(8,128)(2,1)} %get-tuple-element.132.refs_0_, bf16[1024,640]{1,0:T(8,128)(2,1)} %get-tuple-element.133.refs_1_, ...), custom_call_target="tpu_custom_call" | custom-call | flops 1024 | bytes 1024 | tf_op jit(solution)/shard_map/down/pallas_call | solution.py:416
  232.3 1.9 collective-permute-start.37
  234.2 1.5 collective-permute-start.38
  235.7 13.5 %collective-permute-done.37.refs_6_ = bf16[256,1280]{1,0:T(8,128)(2,1)S(1)} collective-permute-done((bf16[256,1280]{1,0:T(8,128)(2,1)S(1)}, bf16[256,1280]{1,0:T(8,128)(2,1)S(1)}, u32[]{:S(2)}, u32[]{:S(2)}) %collective-permute-start.37) | collective-permute-done | bytes 655392 | tf_op jit(solution)/shard_map/ppermute | solution.py:462
  252.7 6.7 %collective-permute-done.40.refs_9_ = bf16[128,1280]{1,0:T(8,128)(2,1)} collective-permute-done((bf16[128,1280]{1,0:T(8,128)(2,1)}, bf16[128,1280]{1,0:T(8,128)(2,1)}, u32[]{:S(2)}, u32[]{:S(2)}) %collective-permute-start.40) | collective-permute-done | bytes 327712 | tf_op jit(solution)/shard_map/ppermute | solution.py:462
  261.7 3.5 %finish.1 = bf16[256,2560]{1,0:T(8,128)(2,1)} custom-call(s32[1]{0:T(128)} %bitcast.upper, bf16[256,2560]{1,0:T(8,128)(2,1)S(1)} %copy-done.4, f32[256,1280]{1,0:T(8,128)} %get-tuple-element.138.refs_0_, bf16[256,1280]{1,0:T(8,128)(2,1)S(1)} %collective-permute-done.29.refs_1_, bf16[256,1280]{1,0:T(8,128)(2,1)S(1)} %collective-permute-done.30.refs_2_, ...), custom_call_target="tpu_custom_call" | custom-call | flops 1024 | bytes 1024 | tf_op jit(solution)/shard_map/finish/pallas_call | solution.py:450
  (129 shorter events, 35.5 us)
Async XLA Ops:
  0.0 12.0 %copy-start.28 = (s32[1,8]{1,0:T(1,128)S(1)}, s32[1,8]{1,0:T(1,128)}, u32[]{:S(2)}) copy-start(s32[1,8]{1,0:T(1,128)} %param.25) | copy-start | bytes 100
  0.0 12.4 %copy-start.29 = (s32[16]{0:T(128)S(1)}, s32[16]{0:T(128)}, u32[]{:S(2)}) copy-start(s32[16]{0:T(128)} %param.27) | copy-start | bytes 196
  0.0 15.4 %collective-permute-start = (bf16[2,64,512]{2,1,0:T(8,128)(2,1)}, bf16[2,64,512]{2,1,0:T(8,128)(2,1)S(1)}, u32[]{:S(2)}, u32[]{:S(2)}) collective-permute-start(bf16[2,64,512]{2,1,0:T(8,128)(2,1)} %param.16), channel_id=1, source_target_pairs={{0,8},{2,10},{4,12},{6,14},{8,0},{10,2},{12,4},{14,6},{16,24},{18,... | collective-permute-start | bytes 393224 | tf_op jit(solution)/shard_map/ppermute | solution.py:462
  3.0 13.2 %collective-permute-start.1 = (bf16[2,64,512]{2,1,0:T(8,128)(2,1)}, bf16[2,64,512]{2,1,0:T(8,128)(2,1)S(1)}, u32[]{:S(2)}, u32[]{:S(2)}) collective-permute-start(bf16[2,64,512]{2,1,0:T(8,128)(2,1)} %param.16), channel_id=1, source_target_pairs={{0,16},{2,18},{4,20},{6,22},{8,24},{10,26},{12,28},{14,30},{16,0},... | collective-permute-start | bytes 393224 | tf_op jit(solution)/shard_map/ppermute | solution.py:462
  5.6 10.6 %collective-permute-start.2 = (bf16[2,64,512]{2,1,0:T(8,128)(2,1)}, bf16[2,64,512]{2,1,0:T(8,128)(2,1)S(1)}, u32[]{:S(2)}, u32[]{:S(2)}) collective-permute-start(bf16[2,64,512]{2,1,0:T(8,128)(2,1)} %param.16), channel_id=1, source_target_pairs={{0,24},{2,26},{4,28},{6,30},{8,16},{10,18},{12,20},{14,22},{16,8},... | collective-permute-start | bytes 393224 | tf_op jit(solution)/shard_map/ppermute | solution.py:462
  8.9 12.3 %collective-permute-start.6 = (bf16[2,160,640]{2,1,0:T(8,128)(2,1)S(1)}, bf16[2,160,640]{2,1,0:T(8,128)(2,1)S(1)}, u32[]{:S(2)}, u32[]{:S(2)}) collective-permute-start(bf16[2,160,640]{2,1,0:T(8,128)(2,1)S(1)} %get-tuple-element.90), channel_id=1, source_target_pairs={{0,2},{2,0},{4,6},{6,4},{8,10},{10,8},{12,14},{14,12},{16,18},{18,... | collective-permute-start | bytes 1228808 | tf_op jit(solution)/shard_map/ppermute | solution.py:462
  10.6 15.4 %collective-permute-start.7 = (bf16[2,160,640]{2,1,0:T(8,128)(2,1)S(1)}, bf16[2,160,640]{2,1,0:T(8,128)(2,1)S(1)}, u32[]{:S(2)}, u32[]{:S(2)}) collective-permute-start(bf16[2,160,640]{2,1,0:T(8,128)(2,1)S(1)} %get-tuple-element.91), channel_id=1, source_target_pairs={{0,8},{2,10},{4,12},{6,14},{8,0},{10,2},{12,4},{14,6},{16,24},{18,... | collective-permute-start | bytes 1228808 | tf_op jit(solution)/shard_map/ppermute | solution.py:462
  16.3 27.0 %collective-permute-start.4 = (bf16[4,2,64,512]{3,2,1,0:T(8,128)(2,1)S(1)}, bf16[4,2,64,512]{3,2,1,0:T(8,128)(2,1)}, u32[]{:S(2)}, u32[]{:S(2)}) collective-permute-start(bf16[4,2,64,512]{3,2,1,0:T(8,128)(2,1)S(1)} %pad_maximum_fusion.1), channel_id=1, source_target_pairs={{0,4},{2,6},{4,0},{6,2},{8,12},{10,14},{12,8},{14,10},{16,20},{18,... | collective-permute-start | bytes 1572872 | tf_op jit(solution)/shard_map/ppermute | solution.py:462
  17.9 28.1 %collective-permute-start.5 = (bf16[4,2,64,512]{3,2,1,0:T(8,128)(2,1)S(1)}, bf16[4,2,64,512]{3,2,1,0:T(8,128)(2,1)}, u32[]{:S(2)}, u32[]{:S(2)}) collective-permute-start(bf16[4,2,64,512]{3,2,1,0:T(8,128)(2,1)S(1)} %pad_maximum_fusion.1), channel_id=1, source_target_pairs={{0,6},{2,4},{4,2},{6,0},{8,14},{10,12},{12,10},{14,8},{16,22},{18,... | collective-permute-start | bytes 1572872 | tf_op jit(solution)/shard_map/ppermute | solution.py:462
  19.3 36.1 %collective-permute-start.3 = (bf16[4,2,64,512]{3,2,1,0:T(8,128)(2,1)S(1)}, bf16[4,2,64,512]{3,2,1,0:T(8,128)(2,1)}, u32[]{:S(2)}, u32[]{:S(2)}) collective-permute-start(bf16[4,2,64,512]{3,2,1,0:T(8,128)(2,1)S(1)} %pad_maximum_fusion.1), channel_id=1, source_target_pairs={{0,2},{2,0},{4,6},{6,4},{8,10},{10,8},{12,14},{14,12},{16,18},{18,... | collective-permute-start | bytes 1572872 | tf_op jit(solution)/shard_map/ppermute | solution.py:462
  21.3 11.8 %copy-start.11 = (bf16[2,160,640]{2,1,0:T(8,128)(2,1)}, bf16[2,160,640]{2,1,0:T(8,128)(2,1)S(1)}, u32[]{:S(2)}) copy-start(bf16[2,160,640]{2,1,0:T(8,128)(2,1)S(1)} %collective-permute-done.6.refs_1_) | copy-start | bytes 1228804
  21.3 11.8 %collective-permute-start.8 = (bf16[2,160,640]{2,1,0:T(8,128)(2,1)S(1)}, bf16[2,160,640]{2,1,0:T(8,128)(2,1)S(1)}, u32[]{:S(2)}, u32[]{:S(2)}) collective-permute-start(bf16[2,160,640]{2,1,0:T(8,128)(2,1)S(1)} %get-tuple-element.92), channel_id=1, source_target_pairs={{0,10},{2,8},{4,14},{6,12},{8,2},{10,0},{12,6},{14,4},{16,26},{18,... | collective-permute-start | bytes 1228808 | tf_op jit(solution)/shard_map/ppermute | solution.py:462
  40.0 53.4 %copy-start = (bf16[2,4,160,640]{3,2,1,0:T(8,128)(2,1)}, bf16[2,4,160,640]{3,2,1,0:T(8,128)(2,1)S(1)}, u32[]{:S(2)}) copy-start(bf16[2,4,160,640]{3,2,1,0:T(8,128)(2,1)S(1)} %merge.2.refs_8_) | copy-start | bytes 4915204
  40.0 75.6 %collective-permute-start.13 = (bf16[2,4,160,640]{3,2,1,0:T(8,128)(2,1)S(1)}, bf16[2,4,160,640]{3,2,1,0:T(8,128)(2,1)}, u32[]{:S(2)}, u32[]{:S(2)}) collective-permute-start(bf16[2,4,160,640]{3,2,1,0:T(8,128)(2,1)S(1)} %merge.2.refs_8_), channel_id=1, source_target_pairs={{0,16},{2,18},{4,20},{6,22},{8,24},{10,26},{12,28},{14,30},{16,0},... | collective-permute-start | bytes 4915208 | tf_op jit(solution)/shard_map/ppermute | solution.py:462
  40.8 74.8 %collective-permute-start.14 = (bf16[2,4,160,640]{3,2,1,0:T(8,128)(2,1)S(1)}, bf16[2,4,160,640]{3,2,1,0:T(8,128)(2,1)}, u32[]{:S(2)}, u32[]{:S(2)}) collective-permute-start(bf16[2,4,160,640]{3,2,1,0:T(8,128)(2,1)S(1)} %merge.2.refs_8_), channel_id=1, source_target_pairs={{0,4},{2,6},{4,0},{6,2},{8,12},{10,14},{12,8},{14,10},{16,20},{18,... | collective-permute-start | bytes 4915208 | tf_op jit(solution)/shard_map/ppermute | solution.py:462
  43.3 16.5 %copy-start.17 = (bf16[1,160,640]{2,1,0:T(8,128)(2,1)}, bf16[1,160,640]{2,1,0:T(8,128)(2,1)S(1)}, u32[]{:S(2)}) copy-start(bf16[1,160,640]{2,1,0:T(8,128)(2,1)S(1)} %get-tuple-element.105.refs_0_) | copy-start | bytes 614404
  43.3 37.5 %collective-permute-start.10 = (bf16[1,160,640]{2,1,0:T(8,128)(2,1)}, bf16[1,160,640]{2,1,0:T(8,128)(2,1)}, u32[]{:S(2)}, u32[]{:S(2)}) collective-permute-start(bf16[1,160,640]{2,1,0:T(8,128)(2,1)} %get-tuple-element.96), channel_id=1, source_target_pairs={{0,8},{2,10},{4,12},{6,14},{8,0},{10,2},{12,4},{14,6},{16,24},{18,... | collective-permute-start | bytes 614408 | tf_op jit(solution)/shard_map/ppermute | solution.py:462
  46.0 37.0 %collective-permute-start.11 = (bf16[1,160,640]{2,1,0:T(8,128)(2,1)}, bf16[1,160,640]{2,1,0:T(8,128)(2,1)}, u32[]{:S(2)}, u32[]{:S(2)}) collective-permute-start(bf16[1,160,640]{2,1,0:T(8,128)(2,1)} %get-tuple-element.97), channel_id=1, source_target_pairs={{0,10},{2,8},{4,14},{6,12},{8,2},{10,0},{12,6},{14,4},{16,26},{18,... | collective-permute-start | bytes 614408 | tf_op jit(solution)/shard_map/ppermute | solution.py:462
  55.4 27.7 %collective-permute-start.9 = (bf16[1,160,640]{2,1,0:T(8,128)(2,1)}, bf16[1,160,640]{2,1,0:T(8,128)(2,1)}, u32[]{:S(2)}, u32[]{:S(2)}) collective-permute-start(bf16[1,160,640]{2,1,0:T(8,128)(2,1)} %get-tuple-element.95), channel_id=1, source_target_pairs={{0,2},{2,0},{4,6},{6,4},{8,10},{10,8},{12,14},{14,12},{16,18},{18,... | collective-permute-start | bytes 614408 | tf_op jit(solution)/shard_map/ppermute | solution.py:462
  83.0 10.8 %copy-start.18 = (bf16[1,160,640]{2,1,0:T(8,128)(2,1)S(1)}, bf16[1,160,640]{2,1,0:T(8,128)(2,1)}, u32[]{:S(2)}) copy-start(bf16[1,160,640]{2,1,0:T(8,128)(2,1)} %copy-done.17) | copy-start | bytes 614404
  93.4 3.5 %collective-permute-start.12 = (bf16[256,2560]{1,0:T(8,128)(2,1)S(1)}, bf16[256,2560]{1,0:T(8,128)(2,1)S(1)}, u32[]{:S(2)}, u32[]{:S(2)}) collective-permute-start(bf16[256,2560]{1,0:T(8,128)(2,1)S(1)} %get-tuple-element.100), channel_id=1, source_target_pairs={{0,1},{1,0},{2,3},{3,2},{4,5},{5,4},{6,7},{7,6},{8,9},{9,8},{10,11... | collective-permute-start | bytes 3932168 | tf_op jit(solution)/shard_map/ppermute | solution.py:462
  93.4 26.7 %collective-permute-start.22 = (bf16[2,4,160,640]{3,2,1,0:T(8,128)(2,1)S(1)}, bf16[2,4,160,640]{3,2,1,0:T(8,128)(2,1)S(1)}, u32[]{:S(2)}, u32[]{:S(2)}) collective-permute-start(bf16[2,4,160,640]{3,2,1,0:T(8,128)(2,1)S(1)} %merge.2.refs_8_), channel_id=1, source_target_pairs={{0,1},{1,0},{2,3},{3,2},{4,5},{5,4},{6,7},{7,6},{8,9},{9,8},{10,11... | collective-permute-start | bytes 4915208 | tf_op jit(solution)/shard_map/ppermute | solution.py:462
  95.3 20.3 %collective-permute-start.15 = (bf16[1,4,160,640]{3,2,1,0:T(8,128)(2,1)S(1)}, bf16[1,4,160,640]{3,2,1,0:T(8,128)(2,1)S(1)}, u32[]{:S(2)}, u32[]{:S(2)}) collective-permute-start(bf16[1,4,160,640]{3,2,1,0:T(8,128)(2,1)S(1)} %merge.3.refs_2_), channel_id=1, source_target_pairs={{0,4},{2,6},{4,0},{6,2},{8,12},{10,14},{12,8},{14,10},{16,20},{18,... | collective-permute-start | bytes 2457608 | tf_op jit(solution)/shard_map/ppermute | solution.py:462
  115.6 15.9 %collective-permute-start.16 = (bf16[128,2560]{1,0:T(8,128)(2,1)S(1)}, bf16[128,2560]{1,0:T(8,128)(2,1)S(1)}, u32[]{:S(2)}, u32[]{:S(2)}) collective-permute-start(bf16[128,2560]{1,0:T(8,128)(2,1)S(1)} %get-tuple-element.109.refs_0_), channel_id=1, source_target_pairs={{0,2},{2,0},{4,6},{6,4},{8,10},{10,8},{12,14},{14,12},{16,18},{18,... | collective-permute-start | bytes 1966088 | tf_op jit(solution)/shard_map/ppermute | solution.py:462
  115.9 17.5 %collective-permute-start.17 = (bf16[128,2560]{1,0:T(8,128)(2,1)S(1)}, bf16[128,2560]{1,0:T(8,128)(2,1)S(1)}, u32[]{:S(2)}, u32[]{:S(2)}) collective-permute-start(bf16[128,2560]{1,0:T(8,128)(2,1)S(1)} %get-tuple-element.110.refs_1_), channel_id=1, source_target_pairs={{0,8},{2,10},{4,12},{6,14},{8,0},{10,2},{12,4},{14,6},{16,24},{18,... | collective-permute-start | bytes 1966088 | tf_op jit(solution)/shard_map/ppermute | solution.py:462
  119.5 42.8 %collective-permute-start.23 = (bf16[2,4,160,640]{3,2,1,0:T(8,128)(2,1)}, bf16[2,4,160,640]{3,2,1,0:T(8,128)(2,1)S(1)}, u32[]{:S(2)}, u32[]{:S(2)}) collective-permute-start(bf16[2,4,160,640]{3,2,1,0:T(8,128)(2,1)} %collective-permute-done.14.refs_9_), channel_id=1, source_target_pairs={{0,1},{1,0},{2,3},{3,2},{4,5},{5,4},{6,7},{7,6},{8,9},{9,8},{10,11... | collective-permute-start | bytes 4915208 | tf_op jit(solution)/shard_map/ppermute | solution.py:462
  119.5 42.9 %collective-permute-start.24 = (bf16[2,4,160,640]{3,2,1,0:T(8,128)(2,1)}, bf16[2,4,160,640]{3,2,1,0:T(8,128)(2,1)S(1)}, u32[]{:S(2)}, u32[]{:S(2)}) collective-permute-start(bf16[2,4,160,640]{3,2,1,0:T(8,128)(2,1)} %collective-permute-done.13.refs_10_), channel_id=1, source_target_pairs={{0,1},{1,0},{2,3},{3,2},{4,5},{5,4},{6,7},{7,6},{8,9},{9,8},{10,11... | collective-permute-start | bytes 4915208 | tf_op jit(solution)/shard_map/ppermute | solution.py:462
  120.0 47.1 %copy-start.21 = (bf16[2,4,160,640]{3,2,1,0:T(8,128)(2,1)}, bf16[2,4,160,640]{3,2,1,0:T(8,128)(2,1)S(1)}, u32[]{:S(2)}) copy-start(bf16[2,4,160,640]{3,2,1,0:T(8,128)(2,1)S(1)} %collective-permute-done.22.refs_12_) | copy-start | bytes 4915204
  120.0 42.4 %collective-permute-start.25 = (bf16[2,4,160,640]{3,2,1,0:T(8,128)(2,1)}, bf16[2,4,160,640]{3,2,1,0:T(8,128)(2,1)S(1)}, u32[]{:S(2)}, u32[]{:S(2)}) collective-permute-start(bf16[2,4,160,640]{3,2,1,0:T(8,128)(2,1)} %collective-permute-done.13.refs_10_), channel_id=1, source_target_pairs={{0,4},{2,6},{4,0},{6,2},{8,12},{10,14},{12,8},{14,10},{16,20},{18,... | collective-permute-start | bytes 4915208 | tf_op jit(solution)/shard_map/ppermute | solution.py:462
  131.4 14.9 %collective-permute-start.20 = (bf16[128,2560]{1,0:T(8,128)(2,1)S(1)}, bf16[128,2560]{1,0:T(8,128)(2,1)S(1)}, u32[]{:S(2)}, u32[]{:S(2)}) collective-permute-start(bf16[128,2560]{1,0:T(8,128)(2,1)S(1)} %get-tuple-element.110.refs_1_), channel_id=1, source_target_pairs={{0,2},{2,0},{4,6},{6,4},{8,10},{10,8},{12,14},{14,12},{16,18},{18,... | collective-permute-start | bytes 1966088 | tf_op jit(solution)/shard_map/ppermute | solution.py:462
  133.4 16.4 %collective-permute-start.21 = (bf16[128,2560]{1,0:T(8,128)(2,1)S(1)}, bf16[128,2560]{1,0:T(8,128)(2,1)S(1)}, u32[]{:S(2)}, u32[]{:S(2)}) collective-permute-start(bf16[128,2560]{1,0:T(8,128)(2,1)S(1)} %get-tuple-element.109.refs_0_), channel_id=1, source_target_pairs={{0,8},{2,10},{4,12},{6,14},{8,0},{10,2},{12,4},{14,6},{16,24},{18,... | collective-permute-start | bytes 1966088 | tf_op jit(solution)/shard_map/ppermute | solution.py:462
  146.4 16.0 %collective-permute-start.18 = (bf16[128,2560]{1,0:T(8,128)(2,1)S(1)}, bf16[128,2560]{1,0:T(8,128)(2,1)S(1)}, u32[]{:S(2)}, u32[]{:S(2)}) collective-permute-start(bf16[128,2560]{1,0:T(8,128)(2,1)S(1)} %collective-permute-done.16.refs_2_), channel_id=1, source_target_pairs={{0,8},{2,10},{4,12},{6,14},{8,0},{10,2},{12,4},{14,6},{16,24},{18,... | collective-permute-start | bytes 1966088 | tf_op jit(solution)/shard_map/ppermute | solution.py:462
  149.7 12.6 %collective-permute-start.19 = (bf16[128,2560]{1,0:T(8,128)(2,1)S(1)}, bf16[128,2560]{1,0:T(8,128)(2,1)S(1)}, u32[]{:S(2)}, u32[]{:S(2)}) collective-permute-start(bf16[128,2560]{1,0:T(8,128)(2,1)S(1)} %collective-permute-done.17.refs_5_), channel_id=1, source_target_pairs={{0,2},{2,0},{4,6},{6,4},{8,10},{10,8},{12,14},{14,12},{16,18},{18,... | collective-permute-start | bytes 1966088 | tf_op jit(solution)/shard_map/ppermute | solution.py:462
  162.4 3.6 %collective-permute-start.26 = (bf16[2,4,160,640]{3,2,1,0:T(8,128)(2,1)S(1)}, bf16[2,4,160,640]{3,2,1,0:T(8,128)(2,1)S(1)}, u32[]{:S(2)}, u32[]{:S(2)}) collective-permute-start(bf16[2,4,160,640]{3,2,1,0:T(8,128)(2,1)S(1)} %collective-permute-done.25.refs_11_), channel_id=1, source_target_pairs={{0,1},{1,0},{2,3},{3,2},{4,5},{5,4},{6,7},{7,6},{8,9},{9,8},{10,11... | collective-permute-start | bytes 4915208 | tf_op jit(solution)/shard_map/ppermute | solution.py:462
  162.5 24.3 %collective-permute-start.27 = (bf16[1,4,160,640]{3,2,1,0:T(8,128)(2,1)S(1)}, bf16[1,4,160,640]{3,2,1,0:T(8,128)(2,1)S(1)}, u32[]{:S(2)}, u32[]{:S(2)}) collective-permute-start(bf16[1,4,160,640]{3,2,1,0:T(8,128)(2,1)S(1)} %merge.3.refs_2_), channel_id=1, source_target_pairs={{0,1},{1,0},{2,3},{3,2},{4,5},{5,4},{6,7},{7,6},{8,9},{9,8},{10,11... | collective-permute-start | bytes 2457608 | tf_op jit(solution)/shard_map/ppermute | solution.py:462
  163.0 23.8 %collective-permute-start.28 = (bf16[1,4,160,640]{3,2,1,0:T(8,128)(2,1)S(1)}, bf16[1,4,160,640]{3,2,1,0:T(8,128)(2,1)S(1)}, u32[]{:S(2)}, u32[]{:S(2)}) collective-permute-start(bf16[1,4,160,640]{3,2,1,0:T(8,128)(2,1)S(1)} %collective-permute-done.15.refs_3_), channel_id=1, source_target_pairs={{0,1},{1,0},{2,3},{3,2},{4,5},{5,4},{6,7},{7,6},{8,9},{9,8},{10,11... | collective-permute-start | bytes 2457608 | tf_op jit(solution)/shard_map/ppermute | solution.py:462
  163.1 39.2 %collective-permute-start.31 = (bf16[1,4,160,640]{3,2,1,0:T(8,128)(2,1)S(1)}, bf16[1,4,160,640]{3,2,1,0:T(8,128)(2,1)S(1)}, u32[]{:S(2)}, u32[]{:S(2)}) collective-permute-start(bf16[1,4,160,640]{3,2,1,0:T(8,128)(2,1)S(1)} %merge.3.refs_2_), channel_id=1, source_target_pairs={{0,16},{2,18},{4,20},{6,22},{8,24},{10,26},{12,28},{14,30},{16,0},... | collective-permute-start | bytes 2457608 | tf_op jit(solution)/shard_map/ppermute | solution.py:462
  193.7 16.8 %collective-permute-start.29 = (bf16[256,1280]{1,0:T(8,128)(2,1)S(1)}, bf16[256,1280]{1,0:T(8,128)(2,1)S(1)}, u32[]{:S(2)}, u32[]{:S(2)}) collective-permute-start(bf16[256,1280]{1,0:T(8,128)(2,1)S(1)} %get-tuple-element.139), channel_id=1, source_target_pairs={{0,2},{2,0},{4,6},{6,4},{8,10},{10,8},{12,14},{14,12},{16,18},{18,... | collective-permute-start | bytes 1966088 | tf_op jit(solution)/shard_map/ppermute | solution.py:462
  195.5 20.7 %collective-permute-start.30 = (bf16[256,1280]{1,0:T(8,128)(2,1)S(1)}, bf16[256,1280]{1,0:T(8,128)(2,1)S(1)}, u32[]{:S(2)}, u32[]{:S(2)}) collective-permute-start(bf16[256,1280]{1,0:T(8,128)(2,1)S(1)} %get-tuple-element.140), channel_id=1, source_target_pairs={{0,8},{2,10},{4,12},{6,14},{8,0},{10,2},{12,4},{14,6},{16,24},{18,... | collective-permute-start | bytes 1966088 | tf_op jit(solution)/shard_map/ppermute | solution.py:462
  202.2 19.7 %collective-permute-start.32 = (bf16[1,4,160,640]{3,2,1,0:T(8,128)(2,1)S(1)}, bf16[1,4,160,640]{3,2,1,0:T(8,128)(2,1)S(1)}, u32[]{:S(2)}, u32[]{:S(2)}) collective-permute-start(bf16[1,4,160,640]{3,2,1,0:T(8,128)(2,1)S(1)} %collective-permute-done.31.refs_2_), channel_id=1, source_target_pairs={{0,4},{2,6},{4,0},{6,2},{8,12},{10,14},{12,8},{14,10},{16,20},{18,... | collective-permute-start | bytes 2457608 | tf_op jit(solution)/shard_map/ppermute | solution.py:462
  222.0 2.4 collective-permute-start.33
  222.0 3.5 %collective-permute-start.34 = (bf16[1,4,160,640]{3,2,1,0:T(8,128)(2,1)S(1)}, bf16[1,4,160,640]{3,2,1,0:T(8,128)(2,1)S(1)}, u32[]{:S(2)}, u32[]{:S(2)}) collective-permute-start(bf16[1,4,160,640]{3,2,1,0:T(8,128)(2,1)S(1)} %collective-permute-done.32.refs_3_), channel_id=1, source_target_pairs={{0,1},{1,0},{2,3},{3,2},{4,5},{5,4},{6,7},{7,6},{8,9},{9,8},{10,11... | collective-permute-start | bytes 2457608 | tf_op jit(solution)/shard_map/ppermute | solution.py:462
  222.5 9.8 %collective-permute-start.35 = (bf16[128,1280]{1,0:T(8,128)(2,1)S(1)}, bf16[128,1280]{1,0:T(8,128)(2,1)S(1)}, u32[]{:S(2)}, u32[]{:S(2)}) collective-permute-start(bf16[128,1280]{1,0:T(8,128)(2,1)S(1)} %add_convert_fusion.2), channel_id=1, source_target_pairs={{0,8},{2,10},{4,12},{6,14},{8,0},{10,2},{12,4},{14,6},{16,24},{18,... | collective-permute-start | bytes 983048 | tf_op jit(solution)/shard_map/ppermute | solution.py:462
  222.5 9.8 %collective-permute-start.36 = (bf16[128,1280]{1,0:T(8,128)(2,1)S(1)}, bf16[128,1280]{1,0:T(8,128)(2,1)S(1)}, u32[]{:S(2)}, u32[]{:S(2)}) collective-permute-start(bf16[128,1280]{1,0:T(8,128)(2,1)S(1)} %add_convert_fusion.3), channel_id=1, source_target_pairs={{0,2},{2,0},{4,6},{6,4},{8,10},{10,8},{12,14},{14,12},{16,18},{18,... | collective-permute-start | bytes 983048 | tf_op jit(solution)/shard_map/ppermute | solution.py:462
  232.3 17.0 %collective-permute-start.37 = (bf16[256,1280]{1,0:T(8,128)(2,1)S(1)}, bf16[256,1280]{1,0:T(8,128)(2,1)S(1)}, u32[]{:S(2)}, u32[]{:S(2)}) collective-permute-start(bf16[256,1280]{1,0:T(8,128)(2,1)S(1)} %get-tuple-element.155), channel_id=1, source_target_pairs={{0,2},{2,0},{4,6},{6,4},{8,10},{10,8},{12,14},{14,12},{16,18},{18,... | collective-permute-start | bytes 1966088 | tf_op jit(solution)/shard_map/ppermute | solution.py:462
  234.2 16.5 %collective-permute-start.38 = (bf16[256,1280]{1,0:T(8,128)(2,1)S(1)}, bf16[256,1280]{1,0:T(8,128)(2,1)S(1)}, u32[]{:S(2)}, u32[]{:S(2)}) collective-permute-start(bf16[256,1280]{1,0:T(8,128)(2,1)S(1)} %get-tuple-element.156), channel_id=1, source_target_pairs={{0,8},{2,10},{4,12},{6,14},{8,0},{10,2},{12,4},{14,6},{16,24},{18,... | collective-permute-start | bytes 1966088 | tf_op jit(solution)/shard_map/ppermute | solution.py:462
  250.0 9.4 %collective-permute-start.40 = (bf16[128,1280]{1,0:T(8,128)(2,1)}, bf16[128,1280]{1,0:T(8,128)(2,1)}, u32[]{:S(2)}, u32[]{:S(2)}) collective-permute-start(bf16[128,1280]{1,0:T(8,128)(2,1)} %add_convert_fusion), channel_id=1, source_target_pairs={{0,8},{2,10},{4,12},{6,14},{8,0},{10,2},{12,4},{14,6},{16,24},{18,... | collective-permute-start | bytes 983048 | tf_op jit(solution)/shard_map/ppermute | solution.py:462
  251.5 8.9 %collective-permute-start.39 = (bf16[128,1280]{1,0:T(8,128)(2,1)}, bf16[128,1280]{1,0:T(8,128)(2,1)}, u32[]{:S(2)}, u32[]{:S(2)}) collective-permute-start(bf16[128,1280]{1,0:T(8,128)(2,1)} %add_convert_fusion.1), channel_id=1, source_target_pairs={{0,2},{2,0},{4,6},{6,4},{8,10},{10,8},{12,14},{14,12},{16,18},{18,... | collective-permute-start | bytes 983048 | tf_op jit(solution)/shard_map/ppermute | solution.py:462
  (23 other events, 61.9 us)

commit v7 on v6

--- a/solution.py
+++ b/solution.py
@@ -430,32 +430,32 @@
     )(me, *acts, *[array for part in weights for array in part])
 
 
-def finish_kernel(upper, resid, *refs):
-    out_ref = refs[-1]
-    half, width = resid.shape[0] // 2, resid.shape[1] // 2
-    for piece in range(2):
-        own, from_x, from_y, late_x, late_y = refs[5 * piece : 5 * piece + 5]
-        here = pl.ds(pl.multiple_of((upper[0] ^ piece) * width, 128), width)
-        for rows, first, late in (
-            (pl.ds(0, half), from_x, late_y),
-            (pl.ds(half, half), from_y, late_x),
-        ):
-            total = resid[rows, here].astype(jnp.float32) + own[rows, :]
-            total = total + first[:half, :].astype(jnp.float32) + late[...].astype(jnp.float32)
-            out_ref[rows, here] = total.astype(out_ref.dtype)
-
-
-def finish(upper, resid, pieces):
-    vmem = pl.BlockSpec(memory_space=pltpu.VMEM)
+def finish_kernel(place, resid, own, from_x, from_y, late_x, late_y, out_ref):
+    half = resid.shape[0] // 2
+    for rows, first, late in (
+        (pl.ds(0, half), from_x, late_y),
+        (pl.ds(half, half), from_y, late_x),
+    ):
+        total = resid[rows, :].astype(jnp.float32) + own[rows, :]
+        total = total + first[:half, :].astype(jnp.float32) + late[...].astype(jnp.float32)
+        out_ref[rows, :] = total.astype(out_ref.dtype)
+
+
+def finish(place, out, parts):
+    rows, width = out.shape[0], out.shape[1] // 2
+    placed = pl.BlockSpec((rows, width), lambda i, place: (0, place[0]))
+    specs = [pl.BlockSpec(part.shape, lambda i, place: (0, 0)) for part in parts]
     return pl.pallas_call(
         finish_kernel,
-        in_specs=[pl.BlockSpec(memory_space=pltpu.SMEM)] + [vmem] * 11,
-        out_specs=vmem,
-        out_shape=jax.ShapeDtypeStruct(resid.shape, resid.dtype),
+        grid_spec=pltpu.PrefetchScalarGridSpec(
+            num_scalar_prefetch=1, grid=(1,), in_specs=[placed] + specs, out_specs=placed
+        ),
+        out_shape=jax.ShapeDtypeStruct(out.shape, out.dtype),
+        input_output_aliases={1: 0},
         compiler_params=pltpu.CompilerParams(vmem_limit_bytes=VMEM_LIMIT),
         cost_estimate=SHORT,
         name="finish",
-    )(upper, resid, *[part for piece in pieces for part in piece])
+    )(place, out, *parts)
 
 
 def swap(value, axis, size, bits):
@@ -592,10 +592,12 @@
     down_w = complete({top: down_top})
     far = {key: v for key, v in down_w.items() if key & top}
 
-    sums = []
+    out = resid
     for piece in range(2):
         own, to_x, to_y, keep_x, keep_y = parts
         from_x, from_y = req(to_x, key_x), req(to_y, key_y)
+        if piece == 1:
+            out, from_x, from_y = tie((out, from_x, from_y))
         late_y = (keep_y + from_x[half:].astype(jnp.float32)).astype(jnp.bfloat16)
         late_x = (keep_x + from_y[half:].astype(jnp.float32)).astype(jnp.bfloat16)
         if piece == 0:
@@ -604,8 +606,8 @@
         late_y, late_x = req(late_y, key_y), req(late_x, key_x)
         if piece == 0:
             parts, late_y, late_x = tie((parts, late_y, late_x))
-        sums.append([own, from_x, from_y, late_x, late_y])
-    return finish(upper, resid, sums)
+        out = finish(upper ^ piece, out, [own, from_x, from_y, late_x, late_y])
+    return out
 
 
 def solution(mesh):

time: 266 us -> 266 us (level)
  local copies, waits for them, and re-layouts: 17.9 us -> 21.1 us
    unnamed x60 -> x72, local copies, waits for them, and re-layouts: 13.7 us -> 17 us
  transfers between devices with their start and end apart: 41 -> 41, of which waited for: 22 -> 22; matrix products, arithmetic and copies ran while one was open for 6% -> 5% of each run, Pallas kernels for 24% -> 26%
where the time goes in v7:
time: 266 us; the launch traced here: 265 us
  waiting for transfers between devices  118 us (44%)
  Pallas kernels  70.6 us (27%)
  starting transfers between devices  44.2 us (17%)
  local copies, waits for them, and re-layouts  21.1 us (8%)
  other arithmetic  10.4 us (4%)
    ppermute x41, waiting for transfers between devices, swap(): return lax.ppermute(value, axis, [(i, i ^ bits) for i in range(size)])  118 us
    ppermute x41, starting transfers between devices, swap(): return lax.ppermute(value, axis, [(i, i ^ bits) for i in range(size)])  44.2 us
    pallas_call x1, Pallas kernels, expand(): pl.pallas_call(functools.partial(expand_kernel, n_parts=n_parts, keys=key...  19.6 us
    unnamed x72, local copies, waits for them, and re-layouts  17 us
    pallas_call x1, Pallas kernels, attention(): pl.pallas_call(attention_kernel, grid=(count,), in_specs=[same(tok_count,...  14.6 us
    pallas_call x2, Pallas kernels, down(): pl.pallas_call(functools.partial(down_kernel, n_parts=n_parts, keys=keys,...  14 us
    pallas_call x1, Pallas kernels, project(): pl.pallas_call(functools.partial(project_kernel, n_parts=n_parts, n_mlp=n...  8.76 us
  transfers between devices with their start and end apart: 41, of which 22 were waited for; matrix products, arithmetic and copies ran while one was open for 5% of the time, Pallas kernels for 26%

profile of v7, /device:TPU:0, one launch (start us, length us, event | category | flops | bytes accessed | tf_op | source)
XLA Modules:
  0.0 265.1 jit_solution(17109474394020867759)
XLA Ops:
  0.0 3.0 %collective-permute-start = (bf16[2,64,512]{2,1,0:T(8,128)(2,1)}, bf16[2,64,512]{2,1,0:T(8,128)(2,1)S(1)}, u32[]{:S(2)}, u32[]{:S(2)}) collective-permute-start(bf16[2,64,512]{2,1,0:T(8,128)(2,1)} %param.16), channel_id=1, source_target_pairs={{0,8},{2,10},{4,12},{6,14},{8,0},{10,2},{12,4},{14,6},{16,24},{18,... | collective-permute-start | bytes 393224 | tf_op jit(solution)/shard_map/ppermute | solution.py:462
  3.0 2.6 collective-permute-start.1
  8.9 1.7 collective-permute-start.6
  13.6 1.8 fusion
  16.3 1.6 collective-permute-start.4
  21.2 1.6 collective-permute-start.8
  26.8 6.2 %collective-permute-done.8.refs_3_ = bf16[2,160,640]{2,1,0:T(8,128)(2,1)S(1)} collective-permute-done((bf16[2,160,640]{2,1,0:T(8,128)(2,1)S(1)}, bf16[2,160,640]{2,1,0:T(8,128)(2,1)S(1)}, u32[]{:S(2)}, u32[]{:S(2)}) %collective-permute-start.8) | collective-permute-done | bytes 409632 | tf_op jit(solution)/shard_map/ppermute | solution.py:462
  37.8 2.2 merge.2.refs_8_
  40.8 1.5 collective-permute-start.14
  43.3 2.7 %collective-permute-start.10 = (bf16[1,160,640]{2,1,0:T(8,128)(2,1)}, bf16[1,160,640]{2,1,0:T(8,128)(2,1)}, u32[]{:S(2)}, u32[]{:S(2)}) collective-permute-start(bf16[1,160,640]{2,1,0:T(8,128)(2,1)} %get-tuple-element.99), channel_id=1, source_target_pairs={{0,8},{2,10},{4,12},{6,14},{8,0},{10,2},{12,4},{14,6},{16,24},{18,... | collective-permute-start | bytes 614408 | tf_op jit(solution)/shard_map/ppermute | solution.py:462
  46.2 9.2 %collective-permute-done.3 = bf16[4,2,64,512]{3,2,1,0:T(8,128)(2,1)} collective-permute-done((bf16[4,2,64,512]{3,2,1,0:T(8,128)(2,1)S(1)}, bf16[4,2,64,512]{3,2,1,0:T(8,128)(2,1)}, u32[]{:S(2)}, u32[]{:S(2)}) %collective-permute-start.3) | collective-permute-done | bytes 524320 | tf_op jit(solution)/shard_map/ppermute | solution.py:462
  55.4 1.5 collective-permute-start.9
  56.9 2.9 %pad_maximum_fusion = bf16[4,4,2,64,512]{4,3,2,1,0:T(8,128)(2,1)} fusion(bf16[1,4,2,64,512]{4,3,2,1,0:T(8,128)(2,1)} %bitcast.11, bf16[1,4,2,64,512]{4,3,2,1,0:T(8,128)(2,1)} %bitcast.10, bf16[1,4,2,64,512]{4,3,2,1,0:T(8,128)(2,1)} %bitcast.9, bf16[1,4,2,64,512]{4,3,2,1,0:T(8,128)(2,1)S(1)} %bitcast.28), kind=kLoop, calls=%fused_computation.1 | loop fusion | flops 3145728 | bytes 4194304 | tf_op jit(solution)/shard_map/stack | solution.py:543
  59.8 3.3 %gather_fusion = bf16[8,2,64,512]{3,2,1,0:T(8,128)(2,1)} fusion(bf16[16,2,64,512]{3,2,1,0:T(8,128)(2,1)} %bitcast.27, s32[1024]{0:T(1024)S(1)} %pad_clamp_fusion), kind=kCustom, calls=%fused_computation | custom fusion | bytes 2097184 | tf_op jit(solution)/shard_map/jit(_take)/gather | solution.py:545
  64.5 14.6 %attention.1.refs_0_ = bf16[512,2048]{1,0:T(8,128)(2,1)S(1)} custom-call(s32[512,1]{1,0:T(8,128)S(1)} %subtract_subtract_fusion.start_ref, f32[512,128]{1,0:T(8,128)S(1)} %get-tuple-element.89.cos_ref, f32[512,128]{1,0:T(8,128)S(1)} %get-tuple-element.90.sin_ref, f32[1,128]{1,0:T(1,128)S(1)} %bitcast.25, f32[1,128]{1,0:T(1,128)S(1)} %bitcast.26, ...), custom_call_target="tpu_custom_call" | custom-call | flops 1024 | bytes 1024 | tf_op jit(solution)/shard_map/attention/pallas_call | solution.py:108
  79.1 1.8 collective-permute-done.10.refs_2_
  80.9 2.2 collective-permute-done.11.refs_3_
  83.1 8.8 %project.1 = (f32[256,2560]{1,0:T(8,128)S(1)}, bf16[256,2560]{1,0:T(8,128)(2,1)S(1)}) custom-call(s32[1]{0:T(128)} %bitcast.1.core, bf16[512,2048]{1,0:T(8,128)(2,1)S(1)} %attention.1.refs_0_, bf16[2048,2560]{1,0:T(8,128)(2,1)} %refs_1_.3), custom_call_target="tpu_custom_call" | custom-call | flops 1024 | bytes 1024 | tf_op jit(solution)/shard_map/project/pallas_call | solution.py:148
  91.9 1.6 copy-done.2
  94.0 1.4 merge.3.refs_2_
  95.4 1.6 collective-permute-start.15
  97.0 4.3 %normalize.1 = (bf16[256,2560]{1,0:T(8,128)(2,1)}, bf16[128,2560]{1,0:T(8,128)(2,1)S(1)}, bf16[128,2560]{1,0:T(8,128)(2,1)S(1)}) custom-call(bf16[256,2560]{1,0:T(8,128)(2,1)S(1)} %copy-done.3, f32[1,2560]{1,0:T(1,128)S(1)} %broadcast_in_dim.56.gain, f32[256,2560]{1,0:T(8,128)} %copy-done.2, bf16[256,2560]{1,0:T(8,128)(2,1)S(1)} %collective-permute-done.12.refs_0_), custom_call_target="tpu_custom_call" | custom-call | flops 1024 | bytes 1024 | tf_op jit(solution)/shard_map/normalize/pallas_call | solution.py:199
  101.3 14.4 %collective-permute-done.15.refs_3_ = bf16[1,4,160,640]{3,2,1,0:T(8,128)(2,1)S(1)} collective-permute-done((bf16[1,4,160,640]{3,2,1,0:T(8,128)(2,1)S(1)}, bf16[1,4,160,640]{3,2,1,0:T(8,128)(2,1)S(1)}, u32[]{:S(2)}, u32[]{:S(2)}) %collective-permute-start.15) | collective-permute-done | bytes 819232 | tf_op jit(solution)/shard_map/ppermute | solution.py:462
  115.9 3.7 %collective-permute-start.17 = (bf16[128,2560]{1,0:T(8,128)(2,1)S(1)}, bf16[128,2560]{1,0:T(8,128)(2,1)S(1)}, u32[]{:S(2)}, u32[]{:S(2)}) collective-permute-start(bf16[128,2560]{1,0:T(8,128)(2,1)S(1)} %get-tuple-element.113.refs_1_), channel_id=1, source_target_pairs={{0,8},{2,10},{4,12},{6,14},{8,0},{10,2},{12,4},{14,6},{16,24},{18,... | collective-permute-start | bytes 1966088 | tf_op jit(solution)/shard_map/ppermute | solution.py:462
  120.1 1.5 collective-permute-start.25
  121.6 9.9 %collective-permute-done.16.refs_2_ = bf16[128,2560]{1,0:T(8,128)(2,1)S(1)} collective-permute-done((bf16[128,2560]{1,0:T(8,128)(2,1)S(1)}, bf16[128,2560]{1,0:T(8,128)(2,1)S(1)}, u32[]{:S(2)}, u32[]{:S(2)}) %collective-permute-start.16) | collective-permute-done | bytes 655392 | tf_op jit(solution)/shard_map/ppermute | solution.py:462
  131.8 1.6 collective-permute-done.17.refs_5_
  133.5 2.0 collective-permute-start.21
  135.5 11.0 %collective-permute-done.20.refs_3_ = bf16[128,2560]{1,0:T(8,128)(2,1)S(1)} collective-permute-done((bf16[128,2560]{1,0:T(8,128)(2,1)S(1)}, bf16[128,2560]{1,0:T(8,128)(2,1)S(1)}, u32[]{:S(2)}, u32[]{:S(2)}) %collective-permute-start.20) | collective-permute-done | bytes 655392 | tf_op jit(solution)/shard_map/ppermute | solution.py:462
  146.5 2.2 collective-permute-start.18
  150.4 12.0 %collective-permute-done.18.refs_6_ = bf16[128,2560]{1,0:T(8,128)(2,1)S(1)} collective-permute-done((bf16[128,2560]{1,0:T(8,128)(2,1)S(1)}, bf16[128,2560]{1,0:T(8,128)(2,1)S(1)}, u32[]{:S(2)}, u32[]{:S(2)}) %collective-permute-start.18) | collective-permute-done | bytes 655392 | tf_op jit(solution)/shard_map/ppermute | solution.py:462
  163.2 1.9 collective-permute-start.31
  167.3 19.6 %gate_up.1 = (bf16[1024,640]{1,0:T(8,128)(2,1)}, bf16[1024,640]{1,0:T(8,128)(2,1)}) custom-call(s32[1]{0:T(128)} %bitcast.20.me, bf16[128,2560]{1,0:T(8,128)(2,1)S(1)} %get-tuple-element.112.refs_0_, bf16[128,2560]{1,0:T(8,128)(2,1)S(1)} %get-tuple-element.113.refs_1_, bf16[128,2560]{1,0:T(8,128)(2,1)S(1)} %collective-permute-done.16.refs_2_, ...), custom_call_target="tpu_custom_call" | custom-call | flops 1024 | bytes 1024 | tf_op jit(solution)/shard_map/gate_up/pallas_call | solution.py:348
  187.0 6.8 %down.2 = (f32[256,1280]{1,0:T(8,128)}, bf16[256,1280]{1,0:T(8,128)(2,1)S(1)}, bf16[256,1280]{1,0:T(8,128)(2,1)S(1)}, f32[128,1280]{1,0:T(8,128)S(1)}, f32[128,1280]{1,0:T(8,128)S(1)}) custom-call(s32[1]{0:T(128)} %bitcast.20.me, bf16[1024,640]{1,0:T(8,128)(2,1)} %get-tuple-element.135.refs_0_, bf16[1024,640]{1,0:T(8,128)(2,1)} %get-tuple-element.136.refs_1_, ...), custom_call_target="tpu_custom_call" | custom-call | flops 1024 | bytes 1024 | tf_op jit(solution)/shard_map/down/pallas_call | solution.py:416
  193.8 1.7 collective-permute-start.29
  195.9 6.5 %collective-permute-done.31.refs_2_ = bf16[1,4,160,640]{3,2,1,0:T(8,128)(2,1)S(1)} collective-permute-done((bf16[1,4,160,640]{3,2,1,0:T(8,128)(2,1)S(1)}, bf16[1,4,160,640]{3,2,1,0:T(8,128)(2,1)S(1)}, u32[]{:S(2)}, u32[]{:S(2)}) %collective-permute-start.31) | collective-permute-done | bytes 819232 | tf_op jit(solution)/shard_map/ppermute | solution.py:462
  202.3 1.5 collective-permute-start.32
  203.8 6.8 %collective-permute-done.29.from_x = bf16[256,1280]{1,0:T(8,128)(2,1)S(1)} collective-permute-done((bf16[256,1280]{1,0:T(8,128)(2,1)S(1)}, bf16[256,1280]{1,0:T(8,128)(2,1)S(1)}, u32[]{:S(2)}, u32[]{:S(2)}) %collective-permute-start.29) | collective-permute-done | bytes 655392 | tf_op jit(solution)/shard_map/ppermute | solution.py:462
  210.7 5.6 %collective-permute-done.30.from_y = bf16[256,1280]{1,0:T(8,128)(2,1)S(1)} collective-permute-done((bf16[256,1280]{1,0:T(8,128)(2,1)S(1)}, bf16[256,1280]{1,0:T(8,128)(2,1)S(1)}, u32[]{:S(2)}, u32[]{:S(2)}) %collective-permute-start.30) | collective-permute-done | bytes 655392 | tf_op jit(solution)/shard_map/ppermute | solution.py:462
  216.3 5.7 %collective-permute-done.32.refs_3_ = bf16[1,4,160,640]{3,2,1,0:T(8,128)(2,1)S(1)} collective-permute-done((bf16[1,4,160,640]{3,2,1,0:T(8,128)(2,1)S(1)}, bf16[1,4,160,640]{3,2,1,0:T(8,128)(2,1)S(1)}, u32[]{:S(2)}, u32[]{:S(2)}) %collective-permute-start.32) | collective-permute-done | bytes 819232 | tf_op jit(solution)/shard_map/ppermute | solution.py:462
  222.6 1.9 collective-permute-start.36
  225.6 7.2 %down.3 = (f32[256,1280]{1,0:T(8,128)}, bf16[256,1280]{1,0:T(8,128)(2,1)}, bf16[256,1280]{1,0:T(8,128)(2,1)}, f32[128,1280]{1,0:T(8,128)S(1)}, f32[128,1280]{1,0:T(8,128)S(1)}) custom-call(s32[1]{0:T(128)} %bitcast.20.me, bf16[1024,640]{1,0:T(8,128)(2,1)} %get-tuple-element.135.refs_0_, bf16[1024,640]{1,0:T(8,128)(2,1)} %get-tuple-element.136.refs_1_, ...), custom_call_target="tpu_custom_call" | custom-call | flops 1024 | bytes 1024 | tf_op jit(solution)/shard_map/down/pallas_call | solution.py:416
  235.1 1.9 collective-permute-start.37
  240.2 2.3 finish.2.resid
  242.5 9.7 %collective-permute-done.37.from_x = bf16[256,1280]{1,0:T(8,128)(2,1)S(1)} collective-permute-done((bf16[256,1280]{1,0:T(8,128)(2,1)}, bf16[256,1280]{1,0:T(8,128)(2,1)S(1)}, u32[]{:S(2)}, u32[]{:S(2)}) %collective-permute-start.37) | collective-permute-done | bytes 655392 | tf_op jit(solution)/shard_map/ppermute | solution.py:462
  252.2 1.5 collective-permute-done.38.from_y
  254.5 7.9 %collective-permute-done.40.late_y = bf16[128,1280]{1,0:T(8,128)(2,1)S(1)} collective-permute-done((bf16[128,1280]{1,0:T(8,128)(2,1)S(1)}, bf16[128,1280]{1,0:T(8,128)(2,1)S(1)}, u32[]{:S(2)}, u32[]{:S(2)}) %collective-permute-start.40) | collective-permute-done | bytes 327712 | tf_op jit(solution)/shard_map/ppermute | solution.py:462
  262.9 2.2 finish.3
  (142 shorter events, 37.0 us)
Async XLA Ops:
  0.0 12.0 %copy-start.34 = (s32[1,8]{1,0:T(1,128)S(1)}, s32[1,8]{1,0:T(1,128)}, u32[]{:S(2)}) copy-start(s32[1,8]{1,0:T(1,128)} %param.25) | copy-start | bytes 100
  0.0 12.4 %copy-start.35 = (s32[16]{0:T(128)S(1)}, s32[16]{0:T(128)}, u32[]{:S(2)}) copy-start(s32[16]{0:T(128)} %param.27) | copy-start | bytes 196
  0.0 15.5 %collective-permute-start = (bf16[2,64,512]{2,1,0:T(8,128)(2,1)}, bf16[2,64,512]{2,1,0:T(8,128)(2,1)S(1)}, u32[]{:S(2)}, u32[]{:S(2)}) collective-permute-start(bf16[2,64,512]{2,1,0:T(8,128)(2,1)} %param.16), channel_id=1, source_target_pairs={{0,8},{2,10},{4,12},{6,14},{8,0},{10,2},{12,4},{14,6},{16,24},{18,... | collective-permute-start | bytes 393224 | tf_op jit(solution)/shard_map/ppermute | solution.py:462
  3.0 13.2 %collective-permute-start.1 = (bf16[2,64,512]{2,1,0:T(8,128)(2,1)}, bf16[2,64,512]{2,1,0:T(8,128)(2,1)S(1)}, u32[]{:S(2)}, u32[]{:S(2)}) collective-permute-start(bf16[2,64,512]{2,1,0:T(8,128)(2,1)} %param.16), channel_id=1, source_target_pairs={{0,16},{2,18},{4,20},{6,22},{8,24},{10,26},{12,28},{14,30},{16,0},... | collective-permute-start | bytes 393224 | tf_op jit(solution)/shard_map/ppermute | solution.py:462
  5.6 10.6 %collective-permute-start.2 = (bf16[2,64,512]{2,1,0:T(8,128)(2,1)}, bf16[2,64,512]{2,1,0:T(8,128)(2,1)S(1)}, u32[]{:S(2)}, u32[]{:S(2)}) collective-permute-start(bf16[2,64,512]{2,1,0:T(8,128)(2,1)} %param.16), channel_id=1, source_target_pairs={{0,24},{2,26},{4,28},{6,30},{8,16},{10,18},{12,20},{14,22},{16,8},... | collective-permute-start | bytes 393224 | tf_op jit(solution)/shard_map/ppermute | solution.py:462
  8.9 12.3 %collective-permute-start.6 = (bf16[2,160,640]{2,1,0:T(8,128)(2,1)S(1)}, bf16[2,160,640]{2,1,0:T(8,128)(2,1)S(1)}, u32[]{:S(2)}, u32[]{:S(2)}) collective-permute-start(bf16[2,160,640]{2,1,0:T(8,128)(2,1)S(1)} %get-tuple-element.93), channel_id=1, source_target_pairs={{0,2},{2,0},{4,6},{6,4},{8,10},{10,8},{12,14},{14,12},{16,18},{18,... | collective-permute-start | bytes 1228808 | tf_op jit(solution)/shard_map/ppermute | solution.py:462
  10.6 15.4 %collective-permute-start.7 = (bf16[2,160,640]{2,1,0:T(8,128)(2,1)S(1)}, bf16[2,160,640]{2,1,0:T(8,128)(2,1)S(1)}, u32[]{:S(2)}, u32[]{:S(2)}) collective-permute-start(bf16[2,160,640]{2,1,0:T(8,128)(2,1)S(1)} %get-tuple-element.94), channel_id=1, source_target_pairs={{0,8},{2,10},{4,12},{6,14},{8,0},{10,2},{12,4},{14,6},{16,24},{18,... | collective-permute-start | bytes 1228808 | tf_op jit(solution)/shard_map/ppermute | solution.py:462
  16.3 27.0 %collective-permute-start.4 = (bf16[4,2,64,512]{3,2,1,0:T(8,128)(2,1)S(1)}, bf16[4,2,64,512]{3,2,1,0:T(8,128)(2,1)}, u32[]{:S(2)}, u32[]{:S(2)}) collective-permute-start(bf16[4,2,64,512]{3,2,1,0:T(8,128)(2,1)S(1)} %pad_maximum_fusion.1), channel_id=1, source_target_pairs={{0,4},{2,6},{4,0},{6,2},{8,12},{10,14},{12,8},{14,10},{16,20},{18,... | collective-permute-start | bytes 1572872 | tf_op jit(solution)/shard_map/ppermute | solution.py:462
  17.9 28.1 %collective-permute-start.5 = (bf16[4,2,64,512]{3,2,1,0:T(8,128)(2,1)S(1)}, bf16[4,2,64,512]{3,2,1,0:T(8,128)(2,1)}, u32[]{:S(2)}, u32[]{:S(2)}) collective-permute-start(bf16[4,2,64,512]{3,2,1,0:T(8,128)(2,1)S(1)} %pad_maximum_fusion.1), channel_id=1, source_target_pairs={{0,6},{2,4},{4,2},{6,0},{8,14},{10,12},{12,10},{14,8},{16,22},{18,... | collective-permute-start | bytes 1572872 | tf_op jit(solution)/shard_map/ppermute | solution.py:462
  19.3 36.1 %collective-permute-start.3 = (bf16[4,2,64,512]{3,2,1,0:T(8,128)(2,1)S(1)}, bf16[4,2,64,512]{3,2,1,0:T(8,128)(2,1)}, u32[]{:S(2)}, u32[]{:S(2)}) collective-permute-start(bf16[4,2,64,512]{3,2,1,0:T(8,128)(2,1)S(1)} %pad_maximum_fusion.1), channel_id=1, source_target_pairs={{0,2},{2,0},{4,6},{6,4},{8,10},{10,8},{12,14},{14,12},{16,18},{18,... | collective-permute-start | bytes 1572872 | tf_op jit(solution)/shard_map/ppermute | solution.py:462
  21.2 11.8 %collective-permute-start.8 = (bf16[2,160,640]{2,1,0:T(8,128)(2,1)S(1)}, bf16[2,160,640]{2,1,0:T(8,128)(2,1)S(1)}, u32[]{:S(2)}, u32[]{:S(2)}) collective-permute-start(bf16[2,160,640]{2,1,0:T(8,128)(2,1)S(1)} %get-tuple-element.95), channel_id=1, source_target_pairs={{0,10},{2,8},{4,14},{6,12},{8,2},{10,0},{12,6},{14,4},{16,26},{18,... | collective-permute-start | bytes 1228808 | tf_op jit(solution)/shard_map/ppermute | solution.py:462
  40.0 53.4 %copy-start = (bf16[2,4,160,640]{3,2,1,0:T(8,128)(2,1)}, bf16[2,4,160,640]{3,2,1,0:T(8,128)(2,1)S(1)}, u32[]{:S(2)}) copy-start(bf16[2,4,160,640]{3,2,1,0:T(8,128)(2,1)S(1)} %merge.2.refs_8_) | copy-start | bytes 4915204
  40.0 75.6 %collective-permute-start.13 = (bf16[2,4,160,640]{3,2,1,0:T(8,128)(2,1)S(1)}, bf16[2,4,160,640]{3,2,1,0:T(8,128)(2,1)}, u32[]{:S(2)}, u32[]{:S(2)}) collective-permute-start(bf16[2,4,160,640]{3,2,1,0:T(8,128)(2,1)S(1)} %merge.2.refs_8_), channel_id=1, source_target_pairs={{0,16},{2,18},{4,20},{6,22},{8,24},{10,26},{12,28},{14,30},{16,0},... | collective-permute-start | bytes 4915208 | tf_op jit(solution)/shard_map/ppermute | solution.py:462
  40.8 74.9 %collective-permute-start.14 = (bf16[2,4,160,640]{3,2,1,0:T(8,128)(2,1)S(1)}, bf16[2,4,160,640]{3,2,1,0:T(8,128)(2,1)}, u32[]{:S(2)}, u32[]{:S(2)}) collective-permute-start(bf16[2,4,160,640]{3,2,1,0:T(8,128)(2,1)S(1)} %merge.2.refs_8_), channel_id=1, source_target_pairs={{0,4},{2,6},{4,0},{6,2},{8,12},{10,14},{12,8},{14,10},{16,20},{18,... | collective-permute-start | bytes 4915208 | tf_op jit(solution)/shard_map/ppermute | solution.py:462
  43.3 16.5 %copy-start.23 = (bf16[1,160,640]{2,1,0:T(8,128)(2,1)}, bf16[1,160,640]{2,1,0:T(8,128)(2,1)S(1)}, u32[]{:S(2)}) copy-start(bf16[1,160,640]{2,1,0:T(8,128)(2,1)S(1)} %get-tuple-element.108.refs_0_) | copy-start | bytes 614404
  43.3 37.6 %collective-permute-start.10 = (bf16[1,160,640]{2,1,0:T(8,128)(2,1)}, bf16[1,160,640]{2,1,0:T(8,128)(2,1)}, u32[]{:S(2)}, u32[]{:S(2)}) collective-permute-start(bf16[1,160,640]{2,1,0:T(8,128)(2,1)} %get-tuple-element.99), channel_id=1, source_target_pairs={{0,8},{2,10},{4,12},{6,14},{8,0},{10,2},{12,4},{14,6},{16,24},{18,... | collective-permute-start | bytes 614408 | tf_op jit(solution)/shard_map/ppermute | solution.py:462
  46.0 37.0 %collective-permute-start.11 = (bf16[1,160,640]{2,1,0:T(8,128)(2,1)}, bf16[1,160,640]{2,1,0:T(8,128)(2,1)}, u32[]{:S(2)}, u32[]{:S(2)}) collective-permute-start(bf16[1,160,640]{2,1,0:T(8,128)(2,1)} %get-tuple-element.100), channel_id=1, source_target_pairs={{0,10},{2,8},{4,14},{6,12},{8,2},{10,0},{12,6},{14,4},{16,26},{18,... | collective-permute-start | bytes 614408 | tf_op jit(solution)/shard_map/ppermute | solution.py:462
  55.4 27.7 %collective-permute-start.9 = (bf16[1,160,640]{2,1,0:T(8,128)(2,1)}, bf16[1,160,640]{2,1,0:T(8,128)(2,1)}, u32[]{:S(2)}, u32[]{:S(2)}) collective-permute-start(bf16[1,160,640]{2,1,0:T(8,128)(2,1)} %get-tuple-element.98), channel_id=1, source_target_pairs={{0,2},{2,0},{4,6},{6,4},{8,10},{10,8},{12,14},{14,12},{16,18},{18,... | collective-permute-start | bytes 614408 | tf_op jit(solution)/shard_map/ppermute | solution.py:462
  93.4 3.5 %collective-permute-start.12 = (bf16[256,2560]{1,0:T(8,128)(2,1)S(1)}, bf16[256,2560]{1,0:T(8,128)(2,1)S(1)}, u32[]{:S(2)}, u32[]{:S(2)}) collective-permute-start(bf16[256,2560]{1,0:T(8,128)(2,1)S(1)} %get-tuple-element.103), channel_id=1, source_target_pairs={{0,1},{1,0},{2,3},{3,2},{4,5},{5,4},{6,7},{7,6},{8,9},{9,8},{10,11... | collective-permute-start | bytes 3932168 | tf_op jit(solution)/shard_map/ppermute | solution.py:462
  93.4 26.7 %collective-permute-start.22 = (bf16[2,4,160,640]{3,2,1,0:T(8,128)(2,1)S(1)}, bf16[2,4,160,640]{3,2,1,0:T(8,128)(2,1)S(1)}, u32[]{:S(2)}, u32[]{:S(2)}) collective-permute-start(bf16[2,4,160,640]{3,2,1,0:T(8,128)(2,1)S(1)} %merge.2.refs_8_), channel_id=1, source_target_pairs={{0,1},{1,0},{2,3},{3,2},{4,5},{5,4},{6,7},{7,6},{8,9},{9,8},{10,11... | collective-permute-start | bytes 4915208 | tf_op jit(solution)/shard_map/ppermute | solution.py:462
  95.4 20.3 %collective-permute-start.15 = (bf16[1,4,160,640]{3,2,1,0:T(8,128)(2,1)S(1)}, bf16[1,4,160,640]{3,2,1,0:T(8,128)(2,1)S(1)}, u32[]{:S(2)}, u32[]{:S(2)}) collective-permute-start(bf16[1,4,160,640]{3,2,1,0:T(8,128)(2,1)S(1)} %merge.3.refs_2_), channel_id=1, source_target_pairs={{0,4},{2,6},{4,0},{6,2},{8,12},{10,14},{12,8},{14,10},{16,20},{18,... | collective-permute-start | bytes 2457608 | tf_op jit(solution)/shard_map/ppermute | solution.py:462
  115.7 15.9 %collective-permute-start.16 = (bf16[128,2560]{1,0:T(8,128)(2,1)S(1)}, bf16[128,2560]{1,0:T(8,128)(2,1)S(1)}, u32[]{:S(2)}, u32[]{:S(2)}) collective-permute-start(bf16[128,2560]{1,0:T(8,128)(2,1)S(1)} %get-tuple-element.112.refs_0_), channel_id=1, source_target_pairs={{0,2},{2,0},{4,6},{6,4},{8,10},{10,8},{12,14},{14,12},{16,18},{18,... | collective-permute-start | bytes 1966088 | tf_op jit(solution)/shard_map/ppermute | solution.py:462
  115.9 17.5 %collective-permute-start.17 = (bf16[128,2560]{1,0:T(8,128)(2,1)S(1)}, bf16[128,2560]{1,0:T(8,128)(2,1)S(1)}, u32[]{:S(2)}, u32[]{:S(2)}) collective-permute-start(bf16[128,2560]{1,0:T(8,128)(2,1)S(1)} %get-tuple-element.113.refs_1_), channel_id=1, source_target_pairs={{0,8},{2,10},{4,12},{6,14},{8,0},{10,2},{12,4},{14,6},{16,24},{18,... | collective-permute-start | bytes 1966088 | tf_op jit(solution)/shard_map/ppermute | solution.py:462
  119.6 42.9 %collective-permute-start.23 = (bf16[2,4,160,640]{3,2,1,0:T(8,128)(2,1)}, bf16[2,4,160,640]{3,2,1,0:T(8,128)(2,1)S(1)}, u32[]{:S(2)}, u32[]{:S(2)}) collective-permute-start(bf16[2,4,160,640]{3,2,1,0:T(8,128)(2,1)} %collective-permute-done.14.refs_9_), channel_id=1, source_target_pairs={{0,1},{1,0},{2,3},{3,2},{4,5},{5,4},{6,7},{7,6},{8,9},{9,8},{10,11... | collective-permute-start | bytes 4915208 | tf_op jit(solution)/shard_map/ppermute | solution.py:462
  119.6 42.9 %collective-permute-start.24 = (bf16[2,4,160,640]{3,2,1,0:T(8,128)(2,1)}, bf16[2,4,160,640]{3,2,1,0:T(8,128)(2,1)S(1)}, u32[]{:S(2)}, u32[]{:S(2)}) collective-permute-start(bf16[2,4,160,640]{3,2,1,0:T(8,128)(2,1)} %collective-permute-done.13.refs_10_), channel_id=1, source_target_pairs={{0,1},{1,0},{2,3},{3,2},{4,5},{5,4},{6,7},{7,6},{8,9},{9,8},{10,11... | collective-permute-start | bytes 4915208 | tf_op jit(solution)/shard_map/ppermute | solution.py:462
  120.1 47.2 %copy-start.27 = (bf16[2,4,160,640]{3,2,1,0:T(8,128)(2,1)}, bf16[2,4,160,640]{3,2,1,0:T(8,128)(2,1)S(1)}, u32[]{:S(2)}) copy-start(bf16[2,4,160,640]{3,2,1,0:T(8,128)(2,1)S(1)} %collective-permute-done.22.refs_12_) | copy-start | bytes 4915204
  120.1 42.4 %collective-permute-start.25 = (bf16[2,4,160,640]{3,2,1,0:T(8,128)(2,1)}, bf16[2,4,160,640]{3,2,1,0:T(8,128)(2,1)S(1)}, u32[]{:S(2)}, u32[]{:S(2)}) collective-permute-start(bf16[2,4,160,640]{3,2,1,0:T(8,128)(2,1)} %collective-permute-done.13.refs_10_), channel_id=1, source_target_pairs={{0,4},{2,6},{4,0},{6,2},{8,12},{10,14},{12,8},{14,10},{16,20},{18,... | collective-permute-start | bytes 4915208 | tf_op jit(solution)/shard_map/ppermute | solution.py:462
  131.5 14.9 %collective-permute-start.20 = (bf16[128,2560]{1,0:T(8,128)(2,1)S(1)}, bf16[128,2560]{1,0:T(8,128)(2,1)S(1)}, u32[]{:S(2)}, u32[]{:S(2)}) collective-permute-start(bf16[128,2560]{1,0:T(8,128)(2,1)S(1)} %get-tuple-element.113.refs_1_), channel_id=1, source_target_pairs={{0,2},{2,0},{4,6},{6,4},{8,10},{10,8},{12,14},{14,12},{16,18},{18,... | collective-permute-start | bytes 1966088 | tf_op jit(solution)/shard_map/ppermute | solution.py:462
  133.5 16.3 %collective-permute-start.21 = (bf16[128,2560]{1,0:T(8,128)(2,1)S(1)}, bf16[128,2560]{1,0:T(8,128)(2,1)S(1)}, u32[]{:S(2)}, u32[]{:S(2)}) collective-permute-start(bf16[128,2560]{1,0:T(8,128)(2,1)S(1)} %get-tuple-element.112.refs_0_), channel_id=1, source_target_pairs={{0,8},{2,10},{4,12},{6,14},{8,0},{10,2},{12,4},{14,6},{16,24},{18,... | collective-permute-start | bytes 1966088 | tf_op jit(solution)/shard_map/ppermute | solution.py:462
  146.5 16.0 %collective-permute-start.18 = (bf16[128,2560]{1,0:T(8,128)(2,1)S(1)}, bf16[128,2560]{1,0:T(8,128)(2,1)S(1)}, u32[]{:S(2)}, u32[]{:S(2)}) collective-permute-start(bf16[128,2560]{1,0:T(8,128)(2,1)S(1)} %collective-permute-done.16.refs_2_), channel_id=1, source_target_pairs={{0,8},{2,10},{4,12},{6,14},{8,0},{10,2},{12,4},{14,6},{16,24},{18,... | collective-permute-start | bytes 1966088 | tf_op jit(solution)/shard_map/ppermute | solution.py:462
  149.8 12.7 %collective-permute-start.19 = (bf16[128,2560]{1,0:T(8,128)(2,1)S(1)}, bf16[128,2560]{1,0:T(8,128)(2,1)S(1)}, u32[]{:S(2)}, u32[]{:S(2)}) collective-permute-start(bf16[128,2560]{1,0:T(8,128)(2,1)S(1)} %collective-permute-done.17.refs_5_), channel_id=1, source_target_pairs={{0,2},{2,0},{4,6},{6,4},{8,10},{10,8},{12,14},{14,12},{16,18},{18,... | collective-permute-start | bytes 1966088 | tf_op jit(solution)/shard_map/ppermute | solution.py:462
  162.5 3.6 %collective-permute-start.26 = (bf16[2,4,160,640]{3,2,1,0:T(8,128)(2,1)S(1)}, bf16[2,4,160,640]{3,2,1,0:T(8,128)(2,1)S(1)}, u32[]{:S(2)}, u32[]{:S(2)}) collective-permute-start(bf16[2,4,160,640]{3,2,1,0:T(8,128)(2,1)S(1)} %collective-permute-done.25.refs_11_), channel_id=1, source_target_pairs={{0,1},{1,0},{2,3},{3,2},{4,5},{5,4},{6,7},{7,6},{8,9},{9,8},{10,11... | collective-permute-start | bytes 4915208 | tf_op jit(solution)/shard_map/ppermute | solution.py:462
  162.6 24.3 %collective-permute-start.27 = (bf16[1,4,160,640]{3,2,1,0:T(8,128)(2,1)S(1)}, bf16[1,4,160,640]{3,2,1,0:T(8,128)(2,1)S(1)}, u32[]{:S(2)}, u32[]{:S(2)}) collective-permute-start(bf16[1,4,160,640]{3,2,1,0:T(8,128)(2,1)S(1)} %merge.3.refs_2_), channel_id=1, source_target_pairs={{0,1},{1,0},{2,3},{3,2},{4,5},{5,4},{6,7},{7,6},{8,9},{9,8},{10,11... | collective-permute-start | bytes 2457608 | tf_op jit(solution)/shard_map/ppermute | solution.py:462
  163.1 23.8 %collective-permute-start.28 = (bf16[1,4,160,640]{3,2,1,0:T(8,128)(2,1)S(1)}, bf16[1,4,160,640]{3,2,1,0:T(8,128)(2,1)S(1)}, u32[]{:S(2)}, u32[]{:S(2)}) collective-permute-start(bf16[1,4,160,640]{3,2,1,0:T(8,128)(2,1)S(1)} %collective-permute-done.15.refs_3_), channel_id=1, source_target_pairs={{0,1},{1,0},{2,3},{3,2},{4,5},{5,4},{6,7},{7,6},{8,9},{9,8},{10,11... | collective-permute-start | bytes 2457608 | tf_op jit(solution)/shard_map/ppermute | solution.py:462
  163.2 39.2 %collective-permute-start.31 = (bf16[1,4,160,640]{3,2,1,0:T(8,128)(2,1)S(1)}, bf16[1,4,160,640]{3,2,1,0:T(8,128)(2,1)S(1)}, u32[]{:S(2)}, u32[]{:S(2)}) collective-permute-start(bf16[1,4,160,640]{3,2,1,0:T(8,128)(2,1)S(1)} %merge.3.refs_2_), channel_id=1, source_target_pairs={{0,16},{2,18},{4,20},{6,22},{8,24},{10,26},{12,28},{14,30},{16,0},... | collective-permute-start | bytes 2457608 | tf_op jit(solution)/shard_map/ppermute | solution.py:462
  193.8 16.8 %collective-permute-start.29 = (bf16[256,1280]{1,0:T(8,128)(2,1)S(1)}, bf16[256,1280]{1,0:T(8,128)(2,1)S(1)}, u32[]{:S(2)}, u32[]{:S(2)}) collective-permute-start(bf16[256,1280]{1,0:T(8,128)(2,1)S(1)} %get-tuple-element.142), channel_id=1, source_target_pairs={{0,2},{2,0},{4,6},{6,4},{8,10},{10,8},{12,14},{14,12},{16,18},{18,... | collective-permute-start | bytes 1966088 | tf_op jit(solution)/shard_map/ppermute | solution.py:462
  195.5 20.8 %collective-permute-start.30 = (bf16[256,1280]{1,0:T(8,128)(2,1)S(1)}, bf16[256,1280]{1,0:T(8,128)(2,1)S(1)}, u32[]{:S(2)}, u32[]{:S(2)}) collective-permute-start(bf16[256,1280]{1,0:T(8,128)(2,1)S(1)} %get-tuple-element.143), channel_id=1, source_target_pairs={{0,8},{2,10},{4,12},{6,14},{8,0},{10,2},{12,4},{14,6},{16,24},{18,... | collective-permute-start | bytes 1966088 | tf_op jit(solution)/shard_map/ppermute | solution.py:462
  202.3 19.7 %collective-permute-start.32 = (bf16[1,4,160,640]{3,2,1,0:T(8,128)(2,1)S(1)}, bf16[1,4,160,640]{3,2,1,0:T(8,128)(2,1)S(1)}, u32[]{:S(2)}, u32[]{:S(2)}) collective-permute-start(bf16[1,4,160,640]{3,2,1,0:T(8,128)(2,1)S(1)} %collective-permute-done.31.refs_2_), channel_id=1, source_target_pairs={{0,4},{2,6},{4,0},{6,2},{8,12},{10,14},{12,8},{14,10},{16,20},{18,... | collective-permute-start | bytes 2457608 | tf_op jit(solution)/shard_map/ppermute | solution.py:462
  222.1 2.4 collective-permute-start.33
  222.1 3.5 %collective-permute-start.34 = (bf16[1,4,160,640]{3,2,1,0:T(8,128)(2,1)S(1)}, bf16[1,4,160,640]{3,2,1,0:T(8,128)(2,1)S(1)}, u32[]{:S(2)}, u32[]{:S(2)}) collective-permute-start(bf16[1,4,160,640]{3,2,1,0:T(8,128)(2,1)S(1)} %collective-permute-done.32.refs_3_), channel_id=1, source_target_pairs={{0,1},{1,0},{2,3},{3,2},{4,5},{5,4},{6,7},{7,6},{8,9},{9,8},{10,11... | collective-permute-start | bytes 2457608 | tf_op jit(solution)/shard_map/ppermute | solution.py:462
  222.6 11.0 %collective-permute-start.35 = (bf16[128,1280]{1,0:T(8,128)(2,1)S(1)}, bf16[128,1280]{1,0:T(8,128)(2,1)S(1)}, u32[]{:S(2)}, u32[]{:S(2)}) collective-permute-start(bf16[128,1280]{1,0:T(8,128)(2,1)S(1)} %add_convert_fusion.2), channel_id=1, source_target_pairs={{0,8},{2,10},{4,12},{6,14},{8,0},{10,2},{12,4},{14,6},{16,24},{18,... | collective-permute-start | bytes 983048 | tf_op jit(solution)/shard_map/ppermute | solution.py:462
  222.6 11.8 %collective-permute-start.36 = (bf16[128,1280]{1,0:T(8,128)(2,1)S(1)}, bf16[128,1280]{1,0:T(8,128)(2,1)S(1)}, u32[]{:S(2)}, u32[]{:S(2)}) collective-permute-start(bf16[128,1280]{1,0:T(8,128)(2,1)S(1)} %add_convert_fusion.3), channel_id=1, source_target_pairs={{0,2},{2,0},{4,6},{6,4},{8,10},{10,8},{12,14},{14,12},{16,18},{18,... | collective-permute-start | bytes 983048 | tf_op jit(solution)/shard_map/ppermute | solution.py:462
  235.1 17.1 %collective-permute-start.37 = (bf16[256,1280]{1,0:T(8,128)(2,1)}, bf16[256,1280]{1,0:T(8,128)(2,1)S(1)}, u32[]{:S(2)}, u32[]{:S(2)}) collective-permute-start(bf16[256,1280]{1,0:T(8,128)(2,1)} %get-tuple-element.157), channel_id=1, source_target_pairs={{0,2},{2,0},{4,6},{6,4},{8,10},{10,8},{12,14},{14,12},{16,18},{18,... | collective-permute-start | bytes 1966088 | tf_op jit(solution)/shard_map/ppermute | solution.py:462
  237.0 16.7 %collective-permute-start.38 = (bf16[256,1280]{1,0:T(8,128)(2,1)}, bf16[256,1280]{1,0:T(8,128)(2,1)S(1)}, u32[]{:S(2)}, u32[]{:S(2)}) collective-permute-start(bf16[256,1280]{1,0:T(8,128)(2,1)} %get-tuple-element.158), channel_id=1, source_target_pairs={{0,8},{2,10},{4,12},{6,14},{8,0},{10,2},{12,4},{14,6},{16,24},{18,... | collective-permute-start | bytes 1966088 | tf_op jit(solution)/shard_map/ppermute | solution.py:462
  240.2 13.4 %copy-start.10 = (f32[128,1280]{1,0:T(8,128)S(1)}, f32[128,1280]{1,0:T(8,128)}, u32[]{:S(2)}) copy-start(f32[128,1280]{1,0:T(8,128)} %copy-done.9) | copy-start | bytes 1966084
  242.5 20.4 %copy-start.5 = (f32[256,1280]{1,0:T(8,128)S(1)}, f32[256,1280]{1,0:T(8,128)}, u32[]{:S(2)}) copy-start(f32[256,1280]{1,0:T(8,128)} %get-tuple-element.160.own) | copy-start | bytes 3932164
  253.7 8.7 %collective-permute-start.40 = (bf16[128,1280]{1,0:T(8,128)(2,1)S(1)}, bf16[128,1280]{1,0:T(8,128)(2,1)S(1)}, u32[]{:S(2)}, u32[]{:S(2)}) collective-permute-start(bf16[128,1280]{1,0:T(8,128)(2,1)S(1)} %add_convert_fusion), channel_id=1, source_target_pairs={{0,8},{2,10},{4,12},{6,14},{8,0},{10,2},{12,4},{14,6},{16,24},{18,... | collective-permute-start | bytes 983048 | tf_op jit(solution)/shard_map/ppermute | solution.py:462
  254.1 8.7 %collective-permute-start.39 = (bf16[128,1280]{1,0:T(8,128)(2,1)S(1)}, bf16[128,1280]{1,0:T(8,128)(2,1)S(1)}, u32[]{:S(2)}, u32[]{:S(2)}) collective-permute-start(bf16[128,1280]{1,0:T(8,128)(2,1)S(1)} %add_convert_fusion.1), channel_id=1, source_target_pairs={{0,2},{2,0},{4,6},{6,4},{8,10},{10,8},{12,14},{14,12},{16,18},{18,... | collective-permute-start | bytes 983048 | tf_op jit(solution)/shard_map/ppermute | solution.py:462
  (29 other events, 87.8 us)
